TPU v7x, 32 devices: a whole 2x2x4 slice. The times are simulated.
32 devices in a mesh: seq: 8 (over z, y), head: 4 (over x, core).
Axes of the slice: x: 2, y: 2, z: 4, core: 2. Of those that a mesh axis runs over, the one named last changes fastest.
Arguments:
- queries: bfloat16 [4096, 64, 128], P(('seq', 'head')), may hold values from -6 to 6
- key_heads: bfloat16 [4096, 64, 128], P(('seq', 'head')), may hold values from -6 to 6
- value_heads: bfloat16 [4096, 64, 128], P(('seq', 'head')), may hold values from -6 to 6
- grad_output: bfloat16 [4096, 64, 128], P(('seq', 'head')), may hold values from -6 to 6
- doc_lengths: int32 [16], replicated, may hold values from 1 to 2048, 4096 in all
Outputs:
- query_gradient: bfloat16 [4096, 64, 128], P(('seq', 'head'))
- lookup_derivative: bfloat16 [4096, 64, 128], P(('seq', 'head'))
- content_derivative: bfloat16 [4096, 64, 128], P(('seq', 'head'))
Inputs may be any that keep to these rules, and one draw needn't show every extreme that they name: `doc_lengths`: the lengths sum to 4096; the longest is exactly 2048.
All inputs are finite; a program needn't handle non-finite values.
Results may differ from a plain program's by a relative error of at most 0.005.
Values may be sent and summed in bfloat16 or wider, within the bound.
No kernel may reach another device: no remote copies, remote signals or barrier semaphores. Data moves between devices by JAX's collectives and lax.ppermute only.
A program may use at most 128 MiB of HBM per device.

v0:
```python
import functools
import math

import jax
import jax.numpy as jnp
from jax import lax
from jax.experimental import pallas as pl
from jax.experimental.pallas import tpu as pltpu
from jax.sharding import PartitionSpec as P

CHUNKS = 4
VMEM = 56 * 1024 * 1024
F32 = jnp.float32
B16 = jnp.bfloat16


def _log2(n):
    k = n.bit_length() - 1
    assert 1 << k == n
    return k


def _same(len_ref, *pairs):
    total = jnp.int32(0)
    split = [jnp.bool_(False)] * len(pairs)
    for k in range(len_ref.shape[0]):
        total = total + len_ref[k]
        split = [s | ((total > p) & (total <= q)) for s, (p, q) in zip(split, pairs)]
    return [jnp.where(s, F32(0.0), F32(1.0)) for s in split]


def _edges(len_ref, first, last):
    start, stop, total = jnp.int32(0), jnp.int32(2**30), jnp.int32(0)
    for k in range(len_ref.shape[0]):
        total = total + len_ref[k]
        start = jnp.where(total <= last, jnp.maximum(start, total), start)
        stop = jnp.where(total > first, jnp.minimum(stop, total), stop)
    return start, stop


def _dot(a, b, ca, cb):
    return lax.dot_general(
        a, b, (((ca,), (cb,)), ((), ())), preferred_element_type=F32
    )


def _pick(rows, d, start, stop, first):
    row = lax.broadcasted_iota(jnp.int32, (rows, d), 0)
    token, odd = first + (row >> 1), row & 1
    last, lead = token >= start, token < stop
    return [
        jnp.where(ok & (odd == parity), F32(1.0), F32(0.0)).astype(B16)
        for ok in (last, lead)
        for parity in (0, 1)
    ]


def states_kernel(
    steps, place_ref, len_ref, q_ref, k_ref, v_ref, g_ref, *rest
):
    keep_ref, send_ref, pick = rest[-3:]
    n, width, _, d = q_ref.shape
    rows = 2 * n
    step = pl.program_id(0)
    first = place_ref[0] * n

    @pl.when(step == 0)
    def _():
        start, stop = _edges(len_ref, first, first + n - 1)
        for i, w in enumerate(_pick(rows, d, start, stop, first)):
            pick[i] = w

    def fill(out_ref):
        for p in range(width):
            query, key, value, grad = (
                ref[:, p].reshape(rows, d) for ref in (q_ref, k_ref, v_ref, g_ref)
            )
            keys = jnp.concatenate([key * pick[0], key * pick[1]], axis=1)
            grads = jnp.concatenate([grad * pick[2], grad * pick[3]], axis=1)
            out_ref[0, p] = _dot(value, keys, 0, 0).astype(out_ref.dtype)
            out_ref[1, p] = _dot(query, grads, 0, 0).astype(out_ref.dtype)

    @pl.when(step < steps // 2)
    def _():
        fill(keep_ref)

    @pl.when(step >= steps // 2)
    def _():
        fill(send_ref)


def grads_kernel(
    scaling,
    steps,
    place_ref,
    len_ref,
    q_ref,
    k_ref,
    v_ref,
    g_ref,
    mine_ref,
    got_ref,
    *rest,
):
    dq_ref, dk_ref, dv_ref, pick, down, across = rest[-6:]
    n, width, _, d = q_ref.shape
    rows = 2 * n
    step = pl.program_id(0)
    first = place_ref[0] * n

    @pl.when(step == 0)
    def _():
        start, stop = _edges(len_ref, first, first + n - 1)
        for i, w in enumerate(_pick(rows, d, start, stop, first)):
            pick[i] = w
        for ref, later, earlier in ((down, 0, 1), (across, 1, 0)):
            t = lax.broadcasted_iota(jnp.int32, (rows, rows), later)
            s = lax.broadcasted_iota(jnp.int32, (rows, rows), earlier)
            same_head = ((t ^ s) & 1) == 0
            t, s = first + (t >> 1), first + (s >> 1)
            begin = jnp.zeros((rows, rows), jnp.int32)
            total = jnp.int32(0)
            for k in range(len_ref.shape[0]):
                total = total + len_ref[k]
                begin = jnp.where(t >= total, total, begin)
            live = same_head & (s <= t) & (s >= begin)
            ref[...] = jnp.where(live, F32(scaling), F32(0.0)).astype(B16)

    def fill(state_ref):
        for p in range(width):
            query, key, value, grad = (
                ref[:, p].reshape(rows, d) for ref in (q_ref, k_ref, v_ref, g_ref)
            )
            state_a = state_ref[0, p]
            state_b = state_ref[1, p]
            last0, last1, lead0, lead1 = (pick[i] for i in range(4))
            ts = _dot(grad, value, 1, 1).astype(B16) * down[...]
            st = _dot(value, grad, 1, 1).astype(B16) * across[...]
            sc = _dot(key, query, 1, 1).astype(B16) * across[...]
            cat = jnp.concatenate
            dq = _dot(ts, key, 1, 0) + _dot(
                cat([grad * lead0, grad * lead1], axis=1),
                cat([state_a[:, :d], state_a[:, d:]], axis=0),
                1,
                0,
            )
            dk = _dot(st, query, 1, 0) + _dot(
                cat([value * last0, value * last1], axis=1), state_b, 1, 1
            )
            dv = _dot(sc, grad, 1, 0) + _dot(
                cat([key * last0, key * last1], axis=1),
                cat([state_b[:, :d], state_b[:, d:]], axis=0),
                1,
                0,
            )
            for ref, x in ((dq_ref, dq), (dk_ref, dk), (dv_ref, dv)):
                ref[:, p] = x.astype(B16).reshape(n, 2, d)

    @pl.when(step < steps // 2)
    def _():
        fill(mine_ref)

    @pl.when(step >= steps // 2)
    def _():
        fill(got_ref)


class Plan:
    def __init__(self, seq_size, head_size, n, heads, d, place, lengths):
        self.n, self.d, self.seq_size, self.head_size = n, d, seq_size, head_size
        self.head_bits, self.seq_bits = _log2(head_size), _log2(seq_size)
        self.scaling = 1.0 / math.sqrt(d * (n * seq_size * head_size // 2))
        pairs = heads // 2
        self.part = max(pairs // CHUNKS, min(pairs, head_size))
        self.chunks = pairs // self.part
        self.width = min(2, self.part >> self.head_bits)
        self.steps = self.part // self.width
        self.total = pairs
        self.place, self.lengths = place, lengths

    def token_spec(self, chunk):
        n, d, width, steps = self.n, self.d, self.width, self.steps
        return pl.BlockSpec(
            (n, width, 2, d),
            lambda i, place, _: (0, chunk * steps + (i ^ place[1]), 0, 0),
        )

    def half_specs(self):
        half = self.steps // 2
        shape = (2, self.width, self.d, 2 * self.d)
        low = pl.BlockSpec(shape, lambda i, *_: (0, jnp.minimum(i, half - 1), 0, 0))
        high = pl.BlockSpec(shape, lambda i, *_: (0, jnp.maximum(i - half, 0), 0, 0))
        return [low, high]

    def call(self, body, name, grid, ins, in_specs, outs, out_specs, scratch, cost, **kw):
        return pl.pallas_call(
            body,
            grid_spec=pltpu.PrefetchScalarGridSpec(
                num_scalar_prefetch=2,
                grid=grid,
                in_specs=in_specs,
                out_specs=out_specs,
                scratch_shapes=scratch,
            ),
            out_shape=outs,
            compiler_params=pltpu.CompilerParams(vmem_limit_bytes=VMEM),
            cost_estimate=pl.CostEstimate(
                flops=cost[0], bytes_accessed=cost[1], transcendentals=0
            ),
            name=name,
            **kw,
        )(self.place, self.lengths, *ins)

    def states(self, chunk, arrays, after):
        rows, d = 2 * self.n, self.d
        shape = (2, self.part // 2, d, 2 * d)
        return self.call(
            functools.partial(states_kernel, self.steps),
            "states",
            (self.steps,),
            [*arrays, *after],
            [self.token_spec(chunk)] * 4 + [pl.BlockSpec(memory_space=pl.ANY)] * len(after),
            (jax.ShapeDtypeStruct(shape, F32), jax.ShapeDtypeStruct(shape, B16)),
            self.half_specs(),
            [pltpu.VMEM((4, rows, d), B16)],
            (8 * rows * d * d * self.part, 8 * rows * d * self.part),
        )

    def grads(self, chunk, arrays, mine, got, before, after):
        rows, d = 2 * self.n, self.d
        token = self.token_spec(chunk)
        anywhere = pl.BlockSpec(memory_space=pl.ANY)
        out = jax.ShapeDtypeStruct((self.n, self.total, 2, d), B16)
        return self.call(
            functools.partial(grads_kernel, self.scaling, self.steps),
            "grads",
            (self.steps,),
            [*arrays, mine, got, *before, *after],
            [token] * 4 + self.half_specs() + [anywhere] * (len(before) + len(after)),
            (out, out, out),
            [token] * 3,
            [
                pltpu.VMEM((4, rows, d), B16),
                pltpu.VMEM((rows, rows), B16),
                pltpu.VMEM((rows, rows), B16),
            ],
            (20 * rows * d * d * self.part, 16 * rows * d * self.part),
            input_output_aliases={8 + i: i for i in range(len(before))},
        )

    def combine(self, name, body, ins, outs, after):
        specs = [
            pl.BlockSpec((1, *x.shape[1:]), (lambda i, *_: (i, 0, 0, 0)) if x.shape[0] == 2
                         else (lambda i, *_: (0, 0, 0, 0)))
            for x in (*ins, *outs)
        ]
        count = len(ins)
        moved = sum(math.prod(x.shape) * jnp.dtype(x.dtype).itemsize for x in (*ins, *outs))

        def kernel(place_ref, len_ref, *refs):
            device = place_ref[0]
            body(pl.program_id(0), device, len_ref, refs[:count], refs[-len(outs):])

        return self.call(
            kernel,
            name,
            (2,),
            [*ins, *after],
            specs[:count] + [pl.BlockSpec(memory_space=pl.ANY)] * len(after),
            tuple(outs),
            specs[count:],
            [],
            (moved, moved),
        )

    def level(self, device, len_ref, level):
        n = self.n
        group = (device >> (level + 1)) << (level + 1)
        middle = (group + (1 << level)) * n
        begin, end = group * n, (group + (2 << level)) * n
        lasts, firsts, join = _same(
            len_ref, (middle - 1, end - 1), (begin, middle), (middle - 1, middle)
        )
        return (device >> level) & 1 == 1, lasts, firsts, join

    def up_weights(self, which, device, len_ref, level):
        hi, lasts, firsts, _ = self.level(device, len_ref, level)
        one = F32(1.0)
        own = jnp.where(which == 0, jnp.where(hi, one, lasts), jnp.where(hi, firsts, one))
        got = jnp.where(which == 0, jnp.where(hi, lasts, one), jnp.where(hi, one, firsts))
        return own, got

    def down_weights(self, which, device, len_ref, level):
        hi, lasts, firsts, join = self.level(device, len_ref, level)
        one, zero = F32(1.0), F32(0.0)
        through = jnp.where(which == 0, firsts, lasts)
        mine_far = hi == (which == 0)
        m_in = jnp.where(mine_far, through, one)
        m_got = jnp.where(mine_far, join, zero)
        s_in = jnp.where(mine_far, one, through)
        s_own = jnp.where(mine_far, zero, join)
        return m_in, m_got, s_in, s_own

    def unit_weight(self, which, device, len_ref, level):
        n, bits = self.n, self.head_bits
        begin = ((device >> bits) << bits) * n
        end = begin + (n << bits)
        middle = (((device >> (level + 1)) << (level + 1)) + (1 << level)) * n
        hi = (device >> level) & 1 == 1
        ahead, behind = _same(len_ref, (middle - 1, begin), (end - 1, middle))
        return jnp.where(
            which == 0, jnp.where(hi, ahead, F32(0.0)), jnp.where(hi, F32(0.0), behind)
        )

    def swap(self, x, level):
        if level < self.head_bits:
            moves = [(i, i ^ (1 << level)) for i in range(self.head_size)]
            return lax.ppermute(x, "head", moves)
        bit = 1 << (level - self.head_bits)
        return lax.ppermute(x, "seq", [(i, i ^ bit) for i in range(self.seq_size)])

    def stages(self, chunk, arrays):
        d, bits, last = self.d, self.head_bits, self.head_bits + self.seq_bits - 1
        own, got, here = [], [], {}

        def shaped(pairs, dtype, lead=2):
            return jax.ShapeDtypeStruct((lead, pairs, d, 2 * d), dtype)

        def first(after):
            keep, send = self.states(chunk, arrays, after)
            own.append(keep)
            here["got"] = self.swap(send, 0)
            return keep

        def up(level, after):
            got.append(here["got"])
            pairs = own[-1].shape[1]
            if level + 1 < bits:
                half = pairs // 2

                def body(which, device, len_ref, ins, outs):
                    o, g = self.up_weights(which, device, len_ref, level)
                    x = o * ins[0][0] + g * ins[1][0].astype(F32)
                    outs[0][0] = x[:half]
                    outs[1][0] = x[half:].astype(B16)

                outs = [shaped(half, F32), shaped(half, B16)]
                keep, send = self.combine("up", body, [own[-1], got[-1]], outs, after)
                own.append(keep)
            else:

                def body(which, device, len_ref, ins, outs):
                    o, g = self.up_weights(which, device, len_ref, level)
                    x = o * ins[0][0] + g * ins[1][0].astype(F32)
                    outs[0][0] = x
                    outs[1][0] = x.astype(B16)

                outs = [shaped(pairs, F32), shaped(pairs, B16)]
                keep, send = self.combine("total", body, [own[-1], got[-1]], outs, after)
                here["total"] = keep
            here["got"] = self.swap(send, level + 1)
            return keep

        def across(level, after):
            ins = [here["total"], here["got"]]
            if "state" in here:
                ins.append(here["state"])
            pairs = ins[0].shape[1]
            final = level + 1 == last

            def body(which, device, len_ref, ins, outs):
                o, g = self.up_weights(which, device, len_ref, level)
                other = ins[1][0].astype(F32)
                x = o * ins[0][0] + g * other
                y = self.unit_weight(which, device, len_ref, level) * other
                if len(ins) > 2:
                    y = y + ins[2][0]
                outs[0][0] = y
                if final:

                    @pl.when(which == ((device >> last) & 1))
                    def _():
                        outs[1][0] = x.astype(B16)

                else:
                    outs[1][0] = x.astype(B16)
                    outs[2][0] = x

            outs = [shaped(pairs, F32), shaped(pairs, B16, 1 if final else 2)]
            if not final:
                outs.append(shaped(pairs, F32))
            state, send, *total = self.combine("across", body, ins, outs, after)
            here["state"] = state
            here["total"] = total[0] if total else None
            here["got"] = self.swap(send, level + 1)
            return state

        def down(level, after):
            top = level == bits - 1
            ins = [here["state"], here["got"], own[level], got[level]]
            pairs = own[level].shape[1]
            half = pairs // 2
            factor = self.scaling if level == 0 else 1.0

            def body(which, device, len_ref, ins, outs):
                m_in, m_got, s_in, s_own = self.down_weights(which, device, len_ref, level)
                m_in, m_got, s_in, s_own = (
                    factor * w for w in (m_in, m_got, s_in, s_own)
                )
                if top:
                    w = self.unit_weight(which, device, len_ref, last)
                    parts = [(slice(None), ins[0][0] + w * ins[1][0].astype(F32))]
                else:
                    parts = [
                        (slice(0, half), ins[0][0]),
                        (slice(half, pairs), ins[1][0].astype(F32)),
                    ]
                for at, x in parts:
                    own_x, got_x = ins[2][0, at], ins[3][0, at].astype(F32)
                    outs[0][0, at] = (m_in * x + m_got * got_x).astype(outs[0].dtype)
                    outs[1][0, at] = (s_in * x + s_own * own_x).astype(B16)

            outs = [shaped(pairs, B16 if level == 0 else F32), shaped(pairs, B16)]
            here["state"], send = self.combine("down", body, ins, outs, after)
            here["got"] = self.swap(send, level)
            return here["state"]

        def final(before, after):
            return self.grads(chunk, arrays, here["state"], here["got"], before, after)

        steps = [first]
        steps += [functools.partial(up, level) for level in range(bits)]
        steps += [functools.partial(across, level) for level in range(bits, last)]
        steps += [functools.partial(down, level) for level in reversed(range(bits))]
        return steps + [final]


def local(seq_size, head_size, queries, key_heads, value_heads, grad_output, doc_lengths):
    n, heads, d = queries.shape
    arrays = tuple(
        x.reshape(n, heads // 2, 2, d)
        for x in (queries, key_heads, value_heads, grad_output)
    )
    device = (lax.axis_index("seq") * head_size + lax.axis_index("head")).astype(jnp.int32)
    plan = Plan(seq_size, head_size, n, heads, d, None, doc_lengths)
    flip = sum(
        ((device >> level) & 1) * (plan.steps >> (level + 1))
        for level in range(plan.head_bits)
    )
    plan.place = jnp.stack([device, flip]).astype(jnp.int32)
    stages = [plan.stages(chunk, arrays) for chunk in range(plan.chunks)]
    count = len(stages[0])
    outs, after = (), ()
    for wave in range(count + plan.chunks - 1):
        for chunk in reversed(range(plan.chunks)):
            stage = wave - chunk
            if not 0 <= stage < count:
                continue
            if stage + 1 < count:
                after = (stages[chunk][stage](after),)
            else:
                outs = stages[chunk][stage](outs, after)
    return tuple(x.reshape(n, heads, d) for x in outs)


def solution(mesh):
    placed = P(("seq", "head"), None, None)
    return jax.shard_map(
        functools.partial(local, mesh.shape["seq"], mesh.shape["head"]),
        mesh=mesh,
        in_specs=(placed, placed, placed, placed, P()),
        out_specs=(placed, placed, placed),
        check_vma=False,
    )
```

profile of v0, /device:TPU:0, one launch (start us, length us, event | category | flops | bytes accessed | tf_op | source)
XLA Modules:
  0.0 186.9 jit_solution(11040255224224152278)
XLA Ops:
  1.2 6.7 %states.4 = (f32[2,4,128,256]{3,2,1,0:T(8,128)}, bf16[2,4,128,256]{3,2,1,0:T(8,128)(2,1)}) custom-call(s32[2]{0:T(128)} %pad_add_fusion.place_ref, s32[16]{0:T(128)} %len_ref.63, bf16[128,32,2,128]{3,2,1,0:T(2,128)(2,1)} %bitcast.9, bf16[128,32,2,128]{3,2,1,0:T(2,128)(2,1)} %bitcast.17, bf16[128,32,2,128]{3,2,1,0:T(2,128)(2,1)} %bitcast.25, ...), custom_call_target="tpu_custom_call" | custom-call | flops 268435456 | bytes 2097152 | tf_op jit(solution)/shard_map/states/pallas_call | solution.py:196
  8.4 6.7 %states.5 = (f32[2,4,128,256]{3,2,1,0:T(8,128)}, bf16[2,4,128,256]{3,2,1,0:T(8,128)(2,1)}) custom-call(s32[2]{0:T(128)} %pad_add_fusion.place_ref, s32[16]{0:T(128)} %len_ref.63, bf16[128,32,2,128]{3,2,1,0:T(2,128)(2,1)} %bitcast.10, bf16[128,32,2,128]{3,2,1,0:T(2,128)(2,1)} %bitcast.18, bf16[128,32,2,128]{3,2,1,0:T(2,128)(2,1)} %bitcast.26, ...), custom_call_target="tpu_custom_call" | custom-call | flops 268435456 | bytes 2097152 | tf_op jit(solution)/shard_map/states/pallas_call | solution.py:196
  16.0 2.9 %up.4 = (f32[2,2,128,256]{3,2,1,0:T(8,128)}, bf16[2,2,128,256]{3,2,1,0:T(8,128)(2,1)}) custom-call(s32[2]{0:T(128)} %pad_add_fusion.place_ref, s32[16]{0:T(128)} %len_ref.63, f32[2,4,128,256]{3,2,1,0:T(8,128)} %get-tuple-element.75.rest_0_.refs_0_.refs_2_, bf16[2,4,128,256]{3,2,1,0:T(8,128)(2,1)} %copy-done.2, ...), custom_call_target="tpu_custom_call" | custom-call | flops 2359296 | bytes 2359296 | tf_op jit(solution)/shard_map/up/pallas_call | solution.py:196
  18.8 2.9 %collective-permute-start.1 = (bf16[2,2,128,256]{3,2,1,0:T(8,128)(2,1)}, bf16[2,2,128,256]{3,2,1,0:T(8,128)(2,1)S(1)}, u32[]{:S(2)}, u32[]{:S(2)}) collective-permute-start(bf16[2,2,128,256]{3,2,1,0:T(8,128)(2,1)} %get-tuple-element.79), channel_id=1, source_target_pairs={{0,2},{1,3},{2,0},{3,1},{4,6},{5,7},{6,4},{7,5},{8,10},{9,11},{10,... | collective-permute-start | bytes 786440 | tf_op jit(solution)/shard_map/ppermute | solution.py:318
  21.8 6.7 %states.6 = (f32[2,4,128,256]{3,2,1,0:T(8,128)}, bf16[2,4,128,256]{3,2,1,0:T(8,128)(2,1)}) custom-call(s32[2]{0:T(128)} %pad_add_fusion.place_ref, s32[16]{0:T(128)} %len_ref.63, bf16[128,32,2,128]{3,2,1,0:T(2,128)(2,1)} %bitcast.11, bf16[128,32,2,128]{3,2,1,0:T(2,128)(2,1)} %bitcast.19, bf16[128,32,2,128]{3,2,1,0:T(2,128)(2,1)} %bitcast.27, ...), custom_call_target="tpu_custom_call" | custom-call | flops 268435456 | bytes 2097152 | tf_op jit(solution)/shard_map/states/pallas_call | solution.py:196
  29.3 2.9 %up.5 = (f32[2,2,128,256]{3,2,1,0:T(8,128)}, bf16[2,2,128,256]{3,2,1,0:T(8,128)(2,1)}) custom-call(s32[2]{0:T(128)} %pad_add_fusion.place_ref, s32[16]{0:T(128)} %len_ref.63, f32[2,4,128,256]{3,2,1,0:T(8,128)} %get-tuple-element.77.refs_2_.refs_0_, bf16[2,4,128,256]{3,2,1,0:T(8,128)(2,1)} %copy-done.1, f32[2,4,128,256]{3,2,1,0:T(8,128)} %get-tuple-element.81.refs_2_.refs_0_), custom_call_target="tpu_custom_call" | custom-call | flops 2359296 | bytes 2359296 | tf_op jit(solution)/shard_map/up/pallas_call | solution.py:196
  32.9 2.7 %total.4 = (f32[2,2,128,256]{3,2,1,0:T(8,128)}, bf16[2,2,128,256]{3,2,1,0:T(8,128)(2,1)}) custom-call(s32[2]{0:T(128)} %pad_add_fusion.place_ref, s32[16]{0:T(128)} %len_ref.63, f32[2,2,128,256]{3,2,1,0:T(8,128)} %get-tuple-element.78.rest_0_.refs_0_.refs_2_, bf16[2,2,128,256]{3,2,1,0:T(8,128)(2,1)} %copy-done.7, ...), custom_call_target="tpu_custom_call" | custom-call | flops 1572864 | bytes 1572864 | tf_op jit(solution)/shard_map/total/pallas_call | solution.py:196
  35.6 6.9 %states.7 = (f32[2,4,128,256]{3,2,1,0:T(8,128)}, bf16[2,4,128,256]{3,2,1,0:T(8,128)(2,1)}) custom-call(s32[2]{0:T(128)} %pad_add_fusion.place_ref, s32[16]{0:T(128)} %len_ref.63, bf16[128,32,2,128]{3,2,1,0:T(2,128)(2,1)} %bitcast.12, bf16[128,32,2,128]{3,2,1,0:T(2,128)(2,1)} %bitcast.20, bf16[128,32,2,128]{3,2,1,0:T(2,128)(2,1)} %bitcast.28, ...), custom_call_target="tpu_custom_call" | custom-call | flops 268435456 | bytes 2097152 | tf_op jit(solution)/shard_map/states/pallas_call | solution.py:196
  45.8 2.9 %up.6 = (f32[2,2,128,256]{3,2,1,0:T(8,128)}, bf16[2,2,128,256]{3,2,1,0:T(8,128)(2,1)}) custom-call(s32[2]{0:T(128)} %pad_add_fusion.place_ref, s32[16]{0:T(128)} %len_ref.63, f32[2,4,128,256]{3,2,1,0:T(8,128)} %get-tuple-element.81.refs_2_.refs_0_, bf16[2,4,128,256]{3,2,1,0:T(8,128)(2,1)} %copy-done, f32[2,4,128,256]{3,2,1,0:T(8,128)} %get-tuple-element.84.refs_2_.refs_0_), custom_call_target="tpu_custom_call" | custom-call | flops 2359296 | bytes 2359296 | tf_op jit(solution)/shard_map/up/pallas_call | solution.py:196
  57.7 2.9 %across.8 = (f32[2,2,128,256]{3,2,1,0:T(8,128)}, bf16[2,2,128,256]{3,2,1,0:T(8,128)(2,1)}, f32[2,2,128,256]{3,2,1,0:T(8,128)}) custom-call(s32[2]{0:T(128)} %pad_add_fusion.place_ref, s32[16]{0:T(128)} %len_ref.63, f32[2,2,128,256]{3,2,1,0:T(8,128)} %get-tuple-element.83.rest_0_.refs_0_, bf16[2,2,128,256]{3,2,1,0:T(8,128)(2,1)} %copy-done.19, ...), custom_call_target="tpu_custom_call" | custom-call | flops 2097152 | bytes 2097152 | tf_op jit(solution)/shard_map/across/pallas_call | solution.py:196
  63.0 2.9 %up.7 = (f32[2,2,128,256]{3,2,1,0:T(8,128)}, bf16[2,2,128,256]{3,2,1,0:T(8,128)(2,1)}) custom-call(s32[2]{0:T(128)} %pad_add_fusion.place_ref, s32[16]{0:T(128)} %len_ref.63, f32[2,4,128,256]{3,2,1,0:T(8,128)} %get-tuple-element.84.refs_2_.refs_0_, bf16[2,4,128,256]{3,2,1,0:T(8,128)(2,1)} %copy-done.3, f32[2,2,128,256]{3,2,1,0:T(8,128)} %get-tuple-element.91.refs_2_), custom_call_target="tpu_custom_call" | custom-call | flops 2359296 | bytes 2359296 | tf_op jit(solution)/shard_map/up/pallas_call | solution.py:196
  66.5 2.6 %total.6 = (f32[2,2,128,256]{3,2,1,0:T(8,128)}, bf16[2,2,128,256]{3,2,1,0:T(8,128)(2,1)}) custom-call(s32[2]{0:T(128)} %pad_add_fusion.place_ref, s32[16]{0:T(128)} %len_ref.63, f32[2,2,128,256]{3,2,1,0:T(8,128)} %get-tuple-element.89.refs_2_.refs_0_, bf16[2,2,128,256]{3,2,1,0:T(8,128)(2,1)} %copy-done.4, f32[2,2,128,256]{3,2,1,0:T(8,128)} %get-tuple-element.92.refs_2_.refs_0_), custom_call_target="tpu_custom_call" | custom-call | flops 1572864 | bytes 1572864 | tf_op jit(solution)/shard_map/total/pallas_call | solution.py:196
  70.1 2.9 %across.9 = (f32[2,2,128,256]{3,2,1,0:T(8,128)}, bf16[2,2,128,256]{3,2,1,0:T(8,128)(2,1)}, f32[2,2,128,256]{3,2,1,0:T(8,128)}) custom-call(s32[2]{0:T(128)} %pad_add_fusion.place_ref, s32[16]{0:T(128)} %len_ref.63, f32[2,2,128,256]{3,2,1,0:T(8,128)} %get-tuple-element.90.refs_2_.refs_0_, bf16[2,2,128,256]{3,2,1,0:T(8,128)(2,1)} %copy-done.18, ...), custom_call_target="tpu_custom_call" | custom-call | flops 2097152 | bytes 2097152 | tf_op jit(solution)/shard_map/across/pallas_call | solution.py:196
  74.0 2.8 %across.10 = (f32[2,2,128,256]{3,2,1,0:T(8,128)}, bf16[1,2,128,256]{3,2,1,0:T(8,128)(2,1)}) custom-call(s32[2]{0:T(128)} %pad_add_fusion.place_ref, s32[16]{0:T(128)} %len_ref.63, f32[2,2,128,256]{3,2,1,0:T(8,128)} %get-tuple-element.94.refs_0_, bf16[2,2,128,256]{3,2,1,0:T(8,128)(2,1)} %copy-done.15, f32[2,2,128,256]{3,2,1,0:T(8,128)} %get-tuple-element.91.refs_2_, ...), custom_call_target="tpu_custom_call" | custom-call | flops 1966080 | bytes 1966080 | tf_op jit(solution)/shard_map/across/pallas_call | solution.py:196
  77.5 2.6 %total.7 = (f32[2,2,128,256]{3,2,1,0:T(8,128)}, bf16[2,2,128,256]{3,2,1,0:T(8,128)(2,1)}) custom-call(s32[2]{0:T(128)} %pad_add_fusion.place_ref, s32[16]{0:T(128)} %len_ref.63, f32[2,2,128,256]{3,2,1,0:T(8,128)} %get-tuple-element.92.refs_2_.refs_0_, bf16[2,2,128,256]{3,2,1,0:T(8,128)(2,1)} %copy-done.5, f32[2,2,128,256]{3,2,1,0:T(8,128)} %get-tuple-element.100.refs_2_.refs_0_), custom_call_target="tpu_custom_call" | custom-call | flops 1572864 | bytes 1572864 | tf_op jit(solution)/shard_map/total/pallas_call | solution.py:196
  85.5 2.9 %across.11 = (f32[2,2,128,256]{3,2,1,0:T(8,128)}, bf16[2,2,128,256]{3,2,1,0:T(8,128)(2,1)}, f32[2,2,128,256]{3,2,1,0:T(8,128)}) custom-call(s32[2]{0:T(128)} %pad_add_fusion.place_ref, s32[16]{0:T(128)} %len_ref.63, f32[2,2,128,256]{3,2,1,0:T(8,128)} %get-tuple-element.98.refs_2_.refs_0_, bf16[2,2,128,256]{3,2,1,0:T(8,128)(2,1)} %copy-done.17, ...), custom_call_target="tpu_custom_call" | custom-call | flops 2097152 | bytes 2097152 | tf_op jit(solution)/shard_map/across/pallas_call | solution.py:196
  90.7 2.8 %across.12 = (f32[2,2,128,256]{3,2,1,0:T(8,128)}, bf16[1,2,128,256]{3,2,1,0:T(8,128)(2,1)}) custom-call(s32[2]{0:T(128)} %pad_add_fusion.place_ref, s32[16]{0:T(128)} %len_ref.63, f32[2,2,128,256]{3,2,1,0:T(8,128)} %get-tuple-element.104.refs_0_, bf16[2,2,128,256]{3,2,1,0:T(8,128)(2,1)} %copy-done.14, f32[2,2,128,256]{3,2,1,0:T(8,128)} %get-tuple-element.99.refs_3_.refs_2_, ...), custom_call_target="tpu_custom_call" | custom-call | flops 1966080 | bytes 1966080 | tf_op jit(solution)/shard_map/across/pallas_call | solution.py:196
  94.1 3.0 %down.8 = (f32[2,2,128,256]{3,2,1,0:T(8,128)}, bf16[2,2,128,256]{3,2,1,0:T(8,128)(2,1)}) custom-call(s32[2]{0:T(128)} %pad_add_fusion.place_ref, s32[16]{0:T(128)} %len_ref.63, f32[2,2,128,256]{3,2,1,0:T(8,128)} %get-tuple-element.100.refs_2_.refs_0_, bf16[1,2,128,256]{3,2,1,0:T(8,128)(2,1)} %copy-done.26, ...), custom_call_target="tpu_custom_call" | custom-call | flops 2228224 | bytes 2228224 | tf_op jit(solution)/shard_map/down/pallas_call | solution.py:196
  100.2 2.8 %across.13 = (f32[2,2,128,256]{3,2,1,0:T(8,128)}, bf16[2,2,128,256]{3,2,1,0:T(8,128)(2,1)}, f32[2,2,128,256]{3,2,1,0:T(8,128)}) custom-call(s32[2]{0:T(128)} %pad_add_fusion.place_ref, s32[16]{0:T(128)} %len_ref.63, f32[2,2,128,256]{3,2,1,0:T(8,128)} %get-tuple-element.101.refs_2_.refs_0_, bf16[2,2,128,256]{3,2,1,0:T(8,128)(2,1)} %copy-done.16, ...), custom_call_target="tpu_custom_call" | custom-call | flops 2097152 | bytes 2097152 | tf_op jit(solution)/shard_map/across/pallas_call | solution.py:196
  104.2 2.8 %across.14 = (f32[2,2,128,256]{3,2,1,0:T(8,128)}, bf16[1,2,128,256]{3,2,1,0:T(8,128)(2,1)}) custom-call(s32[2]{0:T(128)} %pad_add_fusion.place_ref, s32[16]{0:T(128)} %len_ref.63, f32[2,2,128,256]{3,2,1,0:T(8,128)} %get-tuple-element.115.refs_0_, bf16[2,2,128,256]{3,2,1,0:T(8,128)(2,1)} %copy-done.12, f32[2,2,128,256]{3,2,1,0:T(8,128)} %get-tuple-element.107.refs_3_.refs_2_, ...), custom_call_target="tpu_custom_call" | custom-call | flops 1966080 | bytes 1966080 | tf_op jit(solution)/shard_map/across/pallas_call | solution.py:196
  107.7 3.1 %down.9 = (f32[2,2,128,256]{3,2,1,0:T(8,128)}, bf16[2,2,128,256]{3,2,1,0:T(8,128)(2,1)}) custom-call(s32[2]{0:T(128)} %pad_add_fusion.place_ref, s32[16]{0:T(128)} %len_ref.63, f32[2,2,128,256]{3,2,1,0:T(8,128)} %get-tuple-element.108.refs_4_.refs_0_, bf16[1,2,128,256]{3,2,1,0:T(8,128)(2,1)} %copy-done.27, ...), custom_call_target="tpu_custom_call" | custom-call | flops 2228224 | bytes 2228224 | tf_op jit(solution)/shard_map/down/pallas_call | solution.py:196
  114.2 3.3 %down.10 = (bf16[2,4,128,256]{3,2,1,0:T(8,128)(2,1)}, bf16[2,4,128,256]{3,2,1,0:T(8,128)(2,1)}) custom-call(s32[2]{0:T(128)} %pad_add_fusion.place_ref, s32[16]{0:T(128)} %len_ref.63, f32[2,2,128,256]{3,2,1,0:T(8,128)} %get-tuple-element.109.refs_2_.refs_0_, bf16[2,2,128,256]{3,2,1,0:T(8,128)(2,1)} %copy-done.20, ...), custom_call_target="tpu_custom_call" | custom-call | flops 3407872 | bytes 3407872 | tf_op jit(solution)/shard_map/down/pallas_call | solution.py:196
  118.2 2.8 %across.15 = (f32[2,2,128,256]{3,2,1,0:T(8,128)}, bf16[1,2,128,256]{3,2,1,0:T(8,128)(2,1)}) custom-call(s32[2]{0:T(128)} %pad_add_fusion.place_ref, s32[16]{0:T(128)} %len_ref.63, f32[2,2,128,256]{3,2,1,0:T(8,128)} %get-tuple-element.110.refs_0_, bf16[2,2,128,256]{3,2,1,0:T(8,128)(2,1)} %copy-done.13, f32[2,2,128,256]{3,2,1,0:T(8,128)} %get-tuple-element.112.refs_3_.refs_2_, ...), custom_call_target="tpu_custom_call" | custom-call | flops 1966080 | bytes 1966080 | tf_op jit(solution)/shard_map/across/pallas_call | solution.py:196
  122.0 3.0 %down.11 = (f32[2,2,128,256]{3,2,1,0:T(8,128)}, bf16[2,2,128,256]{3,2,1,0:T(8,128)(2,1)}) custom-call(s32[2]{0:T(128)} %pad_add_fusion.place_ref, s32[16]{0:T(128)} %len_ref.63, f32[2,2,128,256]{3,2,1,0:T(8,128)} %get-tuple-element.117.refs_4_.refs_0_, bf16[1,2,128,256]{3,2,1,0:T(8,128)(2,1)} %copy-done.24, ...), custom_call_target="tpu_custom_call" | custom-call | flops 2228224 | bytes 2228224 | tf_op jit(solution)/shard_map/down/pallas_call | solution.py:196
  127.7 3.4 %down.12 = (bf16[2,4,128,256]{3,2,1,0:T(8,128)(2,1)}, bf16[2,4,128,256]{3,2,1,0:T(8,128)(2,1)}) custom-call(s32[2]{0:T(128)} %pad_add_fusion.place_ref, s32[16]{0:T(128)} %len_ref.63, f32[2,2,128,256]{3,2,1,0:T(8,128)} %get-tuple-element.118.refs_4_.refs_0_, bf16[2,2,128,256]{3,2,1,0:T(8,128)(2,1)} %copy-done.21, ...), custom_call_target="tpu_custom_call" | custom-call | flops 3407872 | bytes 3407872 | tf_op jit(solution)/shard_map/down/pallas_call | solution.py:196
  131.8 3.0 %down.13 = (f32[2,2,128,256]{3,2,1,0:T(8,128)}, bf16[2,2,128,256]{3,2,1,0:T(8,128)(2,1)}) custom-call(s32[2]{0:T(128)} %pad_add_fusion.place_ref, s32[16]{0:T(128)} %len_ref.63, f32[2,2,128,256]{3,2,1,0:T(8,128)} %get-tuple-element.120.refs_4_.refs_0_, bf16[1,2,128,256]{3,2,1,0:T(8,128)(2,1)} %copy-done.25, ...), custom_call_target="tpu_custom_call" | custom-call | flops 2228224 | bytes 2228224 | tf_op jit(solution)/shard_map/down/pallas_call | solution.py:196
  136.1 3.3 %down.14 = (bf16[2,4,128,256]{3,2,1,0:T(8,128)(2,1)}, bf16[2,4,128,256]{3,2,1,0:T(8,128)(2,1)}) custom-call(s32[2]{0:T(128)} %pad_add_fusion.place_ref, s32[16]{0:T(128)} %len_ref.63, f32[2,2,128,256]{3,2,1,0:T(8,128)} %get-tuple-element.124.refs_4_.refs_0_, bf16[2,2,128,256]{3,2,1,0:T(8,128)(2,1)} %copy-done.22, ...), custom_call_target="tpu_custom_call" | custom-call | flops 3407872 | bytes 3407872 | tf_op jit(solution)/shard_map/down/pallas_call | solution.py:196
  142.1 3.3 %down.15 = (bf16[2,4,128,256]{3,2,1,0:T(8,128)(2,1)}, bf16[2,4,128,256]{3,2,1,0:T(8,128)(2,1)}) custom-call(s32[2]{0:T(128)} %pad_add_fusion.place_ref, s32[16]{0:T(128)} %len_ref.63, f32[2,2,128,256]{3,2,1,0:T(8,128)} %get-tuple-element.126.refs_4_.refs_0_, bf16[2,2,128,256]{3,2,1,0:T(8,128)(2,1)} %copy-done.23, ...), custom_call_target="tpu_custom_call" | custom-call | flops 3407872 | bytes 3407872 | tf_op jit(solution)/shard_map/down/pallas_call | solution.py:196
  146.2 9.5 %grads.4 = (bf16[128,32,2,128]{3,2,1,0:T(2,128)(2,1)}, bf16[128,32,2,128]{3,2,1,0:T(2,128)(2,1)}, bf16[128,32,2,128]{3,2,1,0:T(2,128)(2,1)}) custom-call(s32[2]{0:T(128)} %pad_add_fusion.place_ref, s32[16]{0:T(128)} %len_ref.63, bf16[128,32,2,128]{3,2,1,0:T(2,128)(2,1)} %bitcast.13, bf16[128,32,2,128]{3,2,1,0:T(2,128)(2,1)} %bitcast.21, ...), custom_call_target="tpu_custom_call" | custom-call | flops 671088640 | bytes 4194304 | tf_op jit(solution)/shard_map/grads/pallas_call | solution.py:196
  156.5 9.5 %grads.5 = (bf16[128,32,2,128]{3,2,1,0:T(2,128)(2,1)}, bf16[128,32,2,128]{3,2,1,0:T(2,128)(2,1)}, bf16[128,32,2,128]{3,2,1,0:T(2,128)(2,1)}) custom-call(s32[2]{0:T(128)} %pad_add_fusion.place_ref, s32[16]{0:T(128)} %len_ref.63, bf16[128,32,2,128]{3,2,1,0:T(2,128)(2,1)} %bitcast.14, ...), custom_call_target="tpu_custom_call", output_to_operand_aliasing={{0}: (8, {}), {1}: (9, {}), {2}: (10, {})} | custom-call | flops 671088640 | bytes 4194304 | tf_op jit(solution)/shard_map/grads/pallas_call | solution.py:196
  166.9 9.7 %grads.6 = (bf16[128,32,2,128]{3,2,1,0:T(2,128)(2,1)}, bf16[128,32,2,128]{3,2,1,0:T(2,128)(2,1)}, bf16[128,32,2,128]{3,2,1,0:T(2,128)(2,1)}) custom-call(s32[2]{0:T(128)} %pad_add_fusion.place_ref, s32[16]{0:T(128)} %len_ref.63, bf16[128,32,2,128]{3,2,1,0:T(2,128)(2,1)} %bitcast.15, ...), custom_call_target="tpu_custom_call", output_to_operand_aliasing={{0}: (8, {}), {1}: (9, {}), {2}: (10, {})} | custom-call | flops 671088640 | bytes 4194304 | tf_op jit(solution)/shard_map/grads/pallas_call | solution.py:196
  177.4 9.5 %grads.7 = (bf16[128,32,2,128]{3,2,1,0:T(2,128)(2,1)}, bf16[128,32,2,128]{3,2,1,0:T(2,128)(2,1)}, bf16[128,32,2,128]{3,2,1,0:T(2,128)(2,1)}) custom-call(s32[2]{0:T(128)} %pad_add_fusion.place_ref, s32[16]{0:T(128)} %len_ref.63, bf16[128,32,2,128]{3,2,1,0:T(2,128)(2,1)} %bitcast.16, ...), custom_call_target="tpu_custom_call", output_to_operand_aliasing={{0}: (8, {}), {1}: (9, {}), {2}: (10, {})} | custom-call | flops 671088640 | bytes 4194304 | tf_op jit(solution)/shard_map/grads/pallas_call | solution.py:196
  (119 shorter events, 50.0 us)
Async XLA Ops:
  7.9 7.3 %collective-permute-start = (bf16[2,4,128,256]{3,2,1,0:T(8,128)(2,1)}, bf16[2,4,128,256]{3,2,1,0:T(8,128)(2,1)S(1)}, u32[]{:S(2)}, u32[]{:S(2)}) collective-permute-start(bf16[2,4,128,256]{3,2,1,0:T(8,128)(2,1)} %get-tuple-element.76), channel_id=1, source_target_pairs={{0,1},{1,0},{2,3},{3,2},{4,5},{5,4},{6,7},{7,6},{8,9},{9,8},{10,11... | collective-permute-start | bytes 1572872 | tf_op jit(solution)/shard_map/ppermute | solution.py:318
  15.1 13.4 %collective-permute-start.2 = (bf16[2,4,128,256]{3,2,1,0:T(8,128)(2,1)}, bf16[2,4,128,256]{3,2,1,0:T(8,128)(2,1)S(1)}, u32[]{:S(2)}, u32[]{:S(2)}) collective-permute-start(bf16[2,4,128,256]{3,2,1,0:T(8,128)(2,1)} %get-tuple-element.80), channel_id=1, source_target_pairs={{0,1},{1,0},{2,3},{3,2},{4,5},{5,4},{6,7},{7,6},{8,9},{9,8},{10,11... | collective-permute-start | bytes 1572872 | tf_op jit(solution)/shard_map/ppermute | solution.py:318
  18.8 13.4 %collective-permute-start.1 = (bf16[2,2,128,256]{3,2,1,0:T(8,128)(2,1)}, bf16[2,2,128,256]{3,2,1,0:T(8,128)(2,1)S(1)}, u32[]{:S(2)}, u32[]{:S(2)}) collective-permute-start(bf16[2,2,128,256]{3,2,1,0:T(8,128)(2,1)} %get-tuple-element.79), channel_id=1, source_target_pairs={{0,2},{1,3},{2,0},{3,1},{4,6},{5,7},{6,4},{7,5},{8,10},{9,11},{10,... | collective-permute-start | bytes 786440 | tf_op jit(solution)/shard_map/ppermute | solution.py:318
  28.5 16.5 %collective-permute-start.6 = (bf16[2,4,128,256]{3,2,1,0:T(8,128)(2,1)}, bf16[2,4,128,256]{3,2,1,0:T(8,128)(2,1)S(1)}, u32[]{:S(2)}, u32[]{:S(2)}) collective-permute-start(bf16[2,4,128,256]{3,2,1,0:T(8,128)(2,1)} %get-tuple-element.88), channel_id=1, source_target_pairs={{0,1},{1,0},{2,3},{3,2},{4,5},{5,4},{6,7},{7,6},{8,9},{9,8},{10,11... | collective-permute-start | bytes 1572872 | tf_op jit(solution)/shard_map/ppermute | solution.py:318
  35.6 7.4 %copy-start.30 = (bf16[2,2,128,256]{3,2,1,0:T(8,128)(2,1)S(1)}, bf16[2,2,128,256]{3,2,1,0:T(8,128)(2,1)}, u32[]{:S(2)}) copy-start(bf16[2,2,128,256]{3,2,1,0:T(8,128)(2,1)} %get-tuple-element.87) | copy-start | bytes 786436
  35.6 7.4 %copy-start.29 = (bf16[2,2,128,256]{3,2,1,0:T(8,128)(2,1)S(1)}, bf16[2,2,128,256]{3,2,1,0:T(8,128)(2,1)}, u32[]{:S(2)}) copy-start(bf16[2,2,128,256]{3,2,1,0:T(8,128)(2,1)} %get-tuple-element.86) | copy-start | bytes 786436
  42.5 19.7 %collective-permute-start.3 = (bf16[2,4,128,256]{3,2,1,0:T(8,128)(2,1)}, bf16[2,4,128,256]{3,2,1,0:T(8,128)(2,1)S(1)}, u32[]{:S(2)}, u32[]{:S(2)}) collective-permute-start(bf16[2,4,128,256]{3,2,1,0:T(8,128)(2,1)} %get-tuple-element.85), channel_id=1, source_target_pairs={{0,1},{1,0},{2,3},{3,2},{4,5},{5,4},{6,7},{7,6},{8,9},{9,8},{10,11... | collective-permute-start | bytes 1572872 | tf_op jit(solution)/shard_map/ppermute | solution.py:318
  43.0 8.4 %collective-permute-start.5 = (bf16[2,2,128,256]{3,2,1,0:T(8,128)(2,1)S(1)}, bf16[2,2,128,256]{3,2,1,0:T(8,128)(2,1)S(1)}, u32[]{:S(2)}, u32[]{:S(2)}) collective-permute-start(bf16[2,2,128,256]{3,2,1,0:T(8,128)(2,1)S(1)} %copy-done.30), channel_id=1, source_target_pairs={{0,2},{1,3},{2,0},{3,1},{4,6},{5,7},{6,4},{7,5},{8,10},{9,11},{10,... | collective-permute-start | bytes 786440 | tf_op jit(solution)/shard_map/ppermute | solution.py:318
  43.0 14.0 %collective-permute-start.4 = (bf16[2,2,128,256]{3,2,1,0:T(8,128)(2,1)S(1)}, bf16[2,2,128,256]{3,2,1,0:T(8,128)(2,1)S(1)}, u32[]{:S(2)}, u32[]{:S(2)}) collective-permute-start(bf16[2,2,128,256]{3,2,1,0:T(8,128)(2,1)S(1)} %copy-done.29), channel_id=1, source_target_pairs={{0,4},{4,0},{8,12},{12,8},{16,20},{20,16},{24,28},{28,24},{1,5},{5... | collective-permute-start | bytes 786440 | tf_op jit(solution)/shard_map/ppermute | solution.py:320
  48.7 17.1 %collective-permute-start.10 = (bf16[2,2,128,256]{3,2,1,0:T(8,128)(2,1)}, bf16[2,2,128,256]{3,2,1,0:T(8,128)(2,1)S(1)}, u32[]{:S(2)}, u32[]{:S(2)}) collective-permute-start(bf16[2,2,128,256]{3,2,1,0:T(8,128)(2,1)} %get-tuple-element.97), channel_id=1, source_target_pairs={{0,2},{1,3},{2,0},{3,1},{4,6},{5,7},{6,4},{7,5},{8,10},{9,11},{10,... | collective-permute-start | bytes 786440 | tf_op jit(solution)/shard_map/ppermute | solution.py:318
  54.7 14.7 %collective-permute-start.9 = (bf16[2,2,128,256]{3,2,1,0:T(8,128)(2,1)}, bf16[2,2,128,256]{3,2,1,0:T(8,128)(2,1)S(1)}, u32[]{:S(2)}, u32[]{:S(2)}) collective-permute-start(bf16[2,2,128,256]{3,2,1,0:T(8,128)(2,1)} %get-tuple-element.96), channel_id=1, source_target_pairs={{0,4},{4,0},{8,12},{12,8},{16,20},{20,16},{24,28},{28,24},{1,5},{5... | collective-permute-start | bytes 786440 | tf_op jit(solution)/shard_map/ppermute | solution.py:320
  60.6 12.7 %collective-permute-start.8 = (bf16[2,2,128,256]{3,2,1,0:T(8,128)(2,1)}, bf16[2,2,128,256]{3,2,1,0:T(8,128)(2,1)S(1)}, u32[]{:S(2)}, u32[]{:S(2)}) collective-permute-start(bf16[2,2,128,256]{3,2,1,0:T(8,128)(2,1)} %get-tuple-element.95), channel_id=1, source_target_pairs={{0,8},{4,12},{8,0},{12,4},{16,24},{20,28},{24,16},{28,20},{1,9},{5... | collective-permute-start | bytes 786440 | tf_op jit(solution)/shard_map/ppermute | solution.py:320
  65.8 11.0 %collective-permute-start.7 = (bf16[2,2,128,256]{3,2,1,0:T(8,128)(2,1)}, bf16[2,2,128,256]{3,2,1,0:T(8,128)(2,1)S(1)}, u32[]{:S(2)}, u32[]{:S(2)}) collective-permute-start(bf16[2,2,128,256]{3,2,1,0:T(8,128)(2,1)} %get-tuple-element.93), channel_id=1, source_target_pairs={{0,2},{1,3},{2,0},{3,1},{4,6},{5,7},{6,4},{7,5},{8,10},{9,11},{10,... | collective-permute-start | bytes 786440 | tf_op jit(solution)/shard_map/ppermute | solution.py:318
  69.2 15.6 %collective-permute-start.14 = (bf16[2,2,128,256]{3,2,1,0:T(8,128)(2,1)}, bf16[2,2,128,256]{3,2,1,0:T(8,128)(2,1)S(1)}, u32[]{:S(2)}, u32[]{:S(2)}) collective-permute-start(bf16[2,2,128,256]{3,2,1,0:T(8,128)(2,1)} %get-tuple-element.106), channel_id=1, source_target_pairs={{0,4},{4,0},{8,12},{12,8},{16,20},{20,16},{24,28},{28,24},{1,5},{5... | collective-permute-start | bytes 786440 | tf_op jit(solution)/shard_map/ppermute | solution.py:320
  72.9 17.0 %collective-permute-start.13 = (bf16[2,2,128,256]{3,2,1,0:T(8,128)(2,1)}, bf16[2,2,128,256]{3,2,1,0:T(8,128)(2,1)S(1)}, u32[]{:S(2)}, u32[]{:S(2)}) collective-permute-start(bf16[2,2,128,256]{3,2,1,0:T(8,128)(2,1)} %get-tuple-element.105), channel_id=1, source_target_pairs={{0,8},{4,12},{8,0},{12,4},{16,24},{20,28},{24,16},{28,20},{1,9},{5... | collective-permute-start | bytes 786440 | tf_op jit(solution)/shard_map/ppermute | solution.py:320
  80.2 19.4 %collective-permute-start.11 = (bf16[2,2,128,256]{3,2,1,0:T(8,128)(2,1)}, bf16[2,2,128,256]{3,2,1,0:T(8,128)(2,1)S(1)}, u32[]{:S(2)}, u32[]{:S(2)}) collective-permute-start(bf16[2,2,128,256]{3,2,1,0:T(8,128)(2,1)} %get-tuple-element.102), channel_id=1, source_target_pairs={{0,4},{4,0},{8,12},{12,8},{16,20},{20,16},{24,28},{28,24},{1,5},{5... | collective-permute-start | bytes 786440 | tf_op jit(solution)/shard_map/ppermute | solution.py:320
  82.2 11.3 %collective-permute-start.12 = (bf16[1,2,128,256]{3,2,1,0:T(8,128)(2,1)}, bf16[1,2,128,256]{3,2,1,0:T(8,128)(2,1)S(1)}, u32[]{:S(2)}, u32[]{:S(2)}) collective-permute-start(bf16[1,2,128,256]{3,2,1,0:T(8,128)(2,1)} %get-tuple-element.103), channel_id=1, source_target_pairs={{0,16},{4,20},{8,24},{12,28},{16,0},{20,4},{24,8},{28,12},{1,17},{... | collective-permute-start | bytes 393224 | tf_op jit(solution)/shard_map/ppermute | solution.py:320
  88.4 15.2 %collective-permute-start.18 = (bf16[2,2,128,256]{3,2,1,0:T(8,128)(2,1)}, bf16[2,2,128,256]{3,2,1,0:T(8,128)(2,1)S(1)}, u32[]{:S(2)}, u32[]{:S(2)}) collective-permute-start(bf16[2,2,128,256]{3,2,1,0:T(8,128)(2,1)} %get-tuple-element.116), channel_id=1, source_target_pairs={{0,8},{4,12},{8,0},{12,4},{16,24},{20,28},{24,16},{28,20},{1,9},{5... | collective-permute-start | bytes 786440 | tf_op jit(solution)/shard_map/ppermute | solution.py:320
  97.2 16.3 %collective-permute-start.16 = (bf16[2,2,128,256]{3,2,1,0:T(8,128)(2,1)}, bf16[2,2,128,256]{3,2,1,0:T(8,128)(2,1)S(1)}, u32[]{:S(2)}, u32[]{:S(2)}) collective-permute-start(bf16[2,2,128,256]{3,2,1,0:T(8,128)(2,1)} %get-tuple-element.113), channel_id=1, source_target_pairs={{0,2},{1,3},{2,0},{3,1},{4,6},{5,7},{6,4},{7,5},{8,10},{9,11},{10,... | collective-permute-start | bytes 786440 | tf_op jit(solution)/shard_map/ppermute | solution.py:318
  99.2 7.8 %collective-permute-start.17 = (bf16[1,2,128,256]{3,2,1,0:T(8,128)(2,1)}, bf16[1,2,128,256]{3,2,1,0:T(8,128)(2,1)S(1)}, u32[]{:S(2)}, u32[]{:S(2)}) collective-permute-start(bf16[1,2,128,256]{3,2,1,0:T(8,128)(2,1)} %get-tuple-element.114), channel_id=1, source_target_pairs={{0,16},{4,20},{8,24},{12,28},{16,0},{20,4},{24,8},{28,12},{1,17},{... | collective-permute-start | bytes 393224 | tf_op jit(solution)/shard_map/ppermute | solution.py:320
  103.1 14.4 %collective-permute-start.15 = (bf16[2,2,128,256]{3,2,1,0:T(8,128)(2,1)}, bf16[2,2,128,256]{3,2,1,0:T(8,128)(2,1)S(1)}, u32[]{:S(2)}, u32[]{:S(2)}) collective-permute-start(bf16[2,2,128,256]{3,2,1,0:T(8,128)(2,1)} %get-tuple-element.111), channel_id=1, source_target_pairs={{0,8},{4,12},{8,0},{12,4},{16,24},{20,28},{24,16},{28,20},{1,9},{5... | collective-permute-start | bytes 786440 | tf_op jit(solution)/shard_map/ppermute | solution.py:320
  110.8 16.2 %collective-permute-start.20 = (bf16[2,2,128,256]{3,2,1,0:T(8,128)(2,1)}, bf16[2,2,128,256]{3,2,1,0:T(8,128)(2,1)S(1)}, u32[]{:S(2)}, u32[]{:S(2)}) collective-permute-start(bf16[2,2,128,256]{3,2,1,0:T(8,128)(2,1)} %get-tuple-element.122), channel_id=1, source_target_pairs={{0,2},{1,3},{2,0},{3,1},{4,6},{5,7},{6,4},{7,5},{8,10},{9,11},{10,... | collective-permute-start | bytes 786440 | tf_op jit(solution)/shard_map/ppermute | solution.py:318
  110.8 10.5 %collective-permute-start.21 = (bf16[1,2,128,256]{3,2,1,0:T(8,128)(2,1)}, bf16[1,2,128,256]{3,2,1,0:T(8,128)(2,1)S(1)}, u32[]{:S(2)}, u32[]{:S(2)}) collective-permute-start(bf16[1,2,128,256]{3,2,1,0:T(8,128)(2,1)} %get-tuple-element.123), channel_id=1, source_target_pairs={{0,16},{4,20},{8,24},{12,28},{16,0},{20,4},{24,8},{28,12},{1,17},{... | collective-permute-start | bytes 393224 | tf_op jit(solution)/shard_map/ppermute | solution.py:320
  121.0 10.1 %collective-permute-start.19 = (bf16[1,2,128,256]{3,2,1,0:T(8,128)(2,1)}, bf16[1,2,128,256]{3,2,1,0:T(8,128)(2,1)S(1)}, u32[]{:S(2)}, u32[]{:S(2)}) collective-permute-start(bf16[1,2,128,256]{3,2,1,0:T(8,128)(2,1)} %get-tuple-element.121), channel_id=1, source_target_pairs={{0,16},{4,20},{8,24},{12,28},{16,0},{20,4},{24,8},{28,12},{1,17},{... | collective-permute-start | bytes 393224 | tf_op jit(solution)/shard_map/ppermute | solution.py:320
  125.0 10.4 %collective-permute-start.23 = (bf16[2,2,128,256]{3,2,1,0:T(8,128)(2,1)}, bf16[2,2,128,256]{3,2,1,0:T(8,128)(2,1)S(1)}, u32[]{:S(2)}, u32[]{:S(2)}) collective-permute-start(bf16[2,2,128,256]{3,2,1,0:T(8,128)(2,1)} %get-tuple-element.128), channel_id=1, source_target_pairs={{0,2},{1,3},{2,0},{3,1},{4,6},{5,7},{6,4},{7,5},{8,10},{9,11},{10,... | collective-permute-start | bytes 786440 | tf_op jit(solution)/shard_map/ppermute | solution.py:318
  127.7 7.2 %copy-start.28 = (bf16[2,4,128,256]{3,2,1,0:T(8,128)(2,1)S(1)}, bf16[2,4,128,256]{3,2,1,0:T(8,128)(2,1)}, u32[]{:S(2)}) copy-start(bf16[2,4,128,256]{3,2,1,0:T(8,128)(2,1)} %get-tuple-element.134) | copy-start | bytes 1572868
  134.8 6.6 %collective-permute-start.22 = (bf16[2,2,128,256]{3,2,1,0:T(8,128)(2,1)}, bf16[2,2,128,256]{3,2,1,0:T(8,128)(2,1)S(1)}, u32[]{:S(2)}, u32[]{:S(2)}) collective-permute-start(bf16[2,2,128,256]{3,2,1,0:T(8,128)(2,1)} %get-tuple-element.127), channel_id=1, source_target_pairs={{0,2},{1,3},{2,0},{3,1},{4,6},{5,7},{6,4},{7,5},{8,10},{9,11},{10,... | collective-permute-start | bytes 786440 | tf_op jit(solution)/shard_map/ppermute | solution.py:318
  134.9 10.5 %collective-permute-start.27 = (bf16[2,4,128,256]{3,2,1,0:T(8,128)(2,1)S(1)}, bf16[2,4,128,256]{3,2,1,0:T(8,128)(2,1)S(1)}, u32[]{:S(2)}, u32[]{:S(2)}) collective-permute-start(bf16[2,4,128,256]{3,2,1,0:T(8,128)(2,1)S(1)} %copy-done.28), channel_id=1, source_target_pairs={{0,1},{1,0},{2,3},{3,2},{4,5},{5,4},{6,7},{7,6},{8,9},{9,8},{10,11... | collective-permute-start | bytes 1572872 | tf_op jit(solution)/shard_map/ppermute | solution.py:318
  134.9 20.8 %collective-permute-start.26 = (bf16[2,4,128,256]{3,2,1,0:T(8,128)(2,1)}, bf16[2,4,128,256]{3,2,1,0:T(8,128)(2,1)S(1)}, u32[]{:S(2)}, u32[]{:S(2)}) collective-permute-start(bf16[2,4,128,256]{3,2,1,0:T(8,128)(2,1)} %get-tuple-element.133), channel_id=1, source_target_pairs={{0,1},{1,0},{2,3},{3,2},{4,5},{5,4},{6,7},{7,6},{8,9},{9,8},{10,11... | collective-permute-start | bytes 1572872 | tf_op jit(solution)/shard_map/ppermute | solution.py:318
  139.4 26.6 %collective-permute-start.25 = (bf16[2,4,128,256]{3,2,1,0:T(8,128)(2,1)}, bf16[2,4,128,256]{3,2,1,0:T(8,128)(2,1)S(1)}, u32[]{:S(2)}, u32[]{:S(2)}) collective-permute-start(bf16[2,4,128,256]{3,2,1,0:T(8,128)(2,1)} %get-tuple-element.132), channel_id=1, source_target_pairs={{0,1},{1,0},{2,3},{3,2},{4,5},{5,4},{6,7},{7,6},{8,9},{9,8},{10,11... | collective-permute-start | bytes 1572872 | tf_op jit(solution)/shard_map/ppermute | solution.py:318
  145.4 31.2 %collective-permute-start.24 = (bf16[2,4,128,256]{3,2,1,0:T(8,128)(2,1)}, bf16[2,4,128,256]{3,2,1,0:T(8,128)(2,1)S(1)}, u32[]{:S(2)}, u32[]{:S(2)}) collective-permute-start(bf16[2,4,128,256]{3,2,1,0:T(8,128)(2,1)} %get-tuple-element.131), channel_id=1, source_target_pairs={{0,1},{1,0},{2,3},{3,2},{4,5},{5,4},{6,7},{7,6},{8,9},{9,8},{10,11... | collective-permute-start | bytes 1572872 | tf_op jit(solution)/shard_map/ppermute | solution.py:318
  166.0 0.8 copy-start.9
  (27 other events, 19.5 us)
where the time goes:
time: 188 us; the launch traced here: 187 us
  Pallas kernels  136 us (72%)
  starting transfers between devices  26.4 us (14%)
  local copies, waits for them, and re-layouts  20.3 us (11%)
  waiting for transfers between devices  3.09 us (2%)
    pallas_call x32, Pallas kernels, call(): pl.pallas_call(body, grid_spec=pltpu.PrefetchScalarGridSpec(num_scalar_pr...  136 us
    unnamed x62, local copies, waits for them, and re-layouts  20.3 us
    ppermute x12, starting transfers between devices, swap(): return lax.ppermute(x, 'seq', [(i, i ^ bit) for i in range(self.seq_size)])  16.3 us
    ppermute x16, starting transfers between devices, swap(): return lax.ppermute(x, 'head', moves)  10.1 us
  transfers between devices with their start and end apart: 28, of which 2 were waited for; matrix products, arithmetic and copies ran while one was open for 0% of the time, Pallas kernels for 64%

commit v1 on v0

v1 whole, which is shorter than its diff:
```python
import functools
import math

import jax
import jax.numpy as jnp
from jax import lax
from jax.experimental import pallas as pl
from jax.experimental.pallas import tpu as pltpu
from jax.sharding import PartitionSpec as P

CHUNKS = 4
VMEM = 24 * 1024 * 1024
F32 = jnp.float32
B16 = jnp.bfloat16
IN_VMEM = pl.BlockSpec(memory_space=pltpu.VMEM)
IN_SMEM = pl.BlockSpec(memory_space=pltpu.SMEM)
IN_HBM = pl.BlockSpec(memory_space=pltpu.HBM)
ANYWHERE = pl.BlockSpec(memory_space=pl.ANY)


def _log2(n):
    k = n.bit_length() - 1
    assert 1 << k == n
    return k


def _same(len_ref, pairs):
    total = jnp.int32(0)
    split = [jnp.bool_(False)] * len(pairs)
    for k in range(len_ref.shape[0]):
        total = total + len_ref[k]
        split = [s | ((total > p) & (total <= q)) for s, (p, q) in zip(split, pairs)]
    return [jnp.where(s, F32(0.0), F32(1.0)) for s in split]


def _edges(len_ref, first, last):
    start, stop, total = jnp.int32(0), jnp.int32(2**30), jnp.int32(0)
    for k in range(len_ref.shape[0]):
        total = total + len_ref[k]
        start = jnp.where(total <= last, jnp.maximum(start, total), start)
        stop = jnp.where(total > first, jnp.minimum(stop, total), stop)
    return start, stop


def _dot(a, b, ca, cb):
    return lax.dot_general(
        a, b, (((ca,), (cb,)), ((), ())), preferred_element_type=F32
    )


def states_kernel(chunk, place_ref, len_ref, *refs):
    tokens, (keep_ref, send_ref, head_ref) = refs[:4], refs[-10:-7]
    slabs, wide, sems = refs[-7:-3], refs[-3:-1], refs[-1]
    n, _, d = tokens[0].shape
    heads = slabs[0].shape[1]
    half = heads // 2
    copies = [
        pltpu.make_async_copy(
            ref.at[:, pl.ds(chunk * heads, heads), :], slab, sems.at[i]
        )
        for i, (ref, slab) in enumerate(zip(tokens, slabs))
    ]
    for copy in copies:
        copy.start()
    first = place_ref[0] * n
    flip = place_ref[1]
    start, stop = _edges(len_ref, first, first + n - 1)
    row = lax.broadcasted_iota(jnp.int32, (n, d), 0) + first
    weights = (
        jnp.where(row < stop, F32(1.0), F32(0.0)).astype(B16),
        jnp.where(row >= start, F32(1.0), F32(0.0)).astype(B16),
    )
    for i, (copy, slab) in enumerate(zip(copies, slabs)):
        scr = wide[i % 2]
        copy.wait()
        scr[...] = slab[...].astype(F32).reshape(n * heads, d)
        for h in range(heads):
            head_ref[i, h] = scr[pl.ds(h, n, stride=heads), :].astype(B16)
    for r in range(heads):
        h = r ^ flip
        out, o = (keep_ref, r) if r < half else (send_ref, r - half)
        query, key, value, grad = (head_ref[i, h] for i in range(4))
        out[0, o] = _dot(key * weights[1], value, 0, 0).astype(out.dtype)
        out[1, o] = _dot(query, grad * weights[0], 0, 0).astype(out.dtype)


def grads_kernel(chunk, scaling, place_ref, len_ref, head_ref, mine_ref, got_ref, *refs):
    outs, token_ref = refs[-11:-8], refs[-8]
    wide, slabs, sems = refs[-7:-4], refs[-4:-1], refs[-1]
    token_ref[...] = jnp.zeros(token_ref.shape, token_ref.dtype)
    _, heads, n, d = head_ref.shape
    half = heads // 2
    first = place_ref[0] * n
    flip = place_ref[1]
    start, stop = _edges(len_ref, first, first + n - 1)
    row = lax.broadcasted_iota(jnp.int32, (n, d), 0) + first
    lead = jnp.where(row < stop, F32(1.0), F32(0.0))
    last = jnp.where(row >= start, F32(1.0), F32(0.0))
    last16 = last.astype(B16)

    def live(later):
        t = lax.broadcasted_iota(jnp.int32, (n, n), later) + first
        s = lax.broadcasted_iota(jnp.int32, (n, n), 1 - later) + first
        begin = jnp.zeros((n, n), jnp.int32)
        total = jnp.int32(0)
        for k in range(len_ref.shape[0]):
            total = total + len_ref[k]
            begin = jnp.where(t >= total, total, begin)
        return jnp.where((s <= t) & (s >= begin), F32(scaling), F32(0.0))

    down, across = live(0), live(1)
    cat = jnp.concatenate
    for r in range(heads):
        h = r ^ flip
        ref, o = (mine_ref, r) if r < half else (got_ref, r - half)
        state_a, state_b = ref[0, o], ref[1, o]
        query, key, value, grad = (head_ref[i, h] for i in range(4))
        x = _dot(grad, cat([value, state_a], axis=0), 1, 1)
        y = _dot(value, cat([grad, state_b], axis=0), 1, 1)
        z = _dot(key, query, 1, 1)
        ts = (x[:, :n] * down).astype(B16)
        st = (y[:, :n] * across).astype(B16)
        sc = (z * across).astype(B16)
        at = pl.ds(h, n, stride=heads)
        wide[0][at, :] = _dot(ts, key, 1, 0) + x[:, n:] * lead
        wide[1][at, :] = _dot(st, query, 1, 0) + y[:, n:] * last
        wide[2][at, :] = _dot(
            cat([sc, key * last16], axis=1), cat([grad, state_b], axis=0), 1, 0
        )
    copies = []
    for i, (scr, slab, out) in enumerate(zip(wide, slabs, outs)):
        slab[...] = scr[...].reshape(n, heads, d).astype(B16)
        copy = pltpu.make_async_copy(
            slab, out.at[:, pl.ds(chunk * heads, heads), :], sems.at[i]
        )
        copy.start()
        copies.append(copy)
    for copy in copies:
        copy.wait()


class Plan:
    def __init__(self, seq_size, head_size, n, heads, d, lengths):
        self.n, self.d, self.seq_size, self.head_size = n, d, seq_size, head_size
        self.head_bits, self.seq_bits = _log2(head_size), _log2(seq_size)
        self.levels = self.head_bits + self.seq_bits
        self.scaling = 1.0 / math.sqrt(d * (n * seq_size * head_size // 2))
        self.part = max(heads // CHUNKS, min(heads, head_size))
        self.chunks = heads // self.part
        self.total = heads
        self.lengths = lengths
        device = lax.axis_index("seq") * head_size + lax.axis_index("head")
        device = device.astype(jnp.int32)
        flip = sum(
            ((device >> level) & 1) * (self.part >> (level + 1))
            for level in range(self.head_bits)
        )
        self.place = jnp.stack([device, flip]).astype(jnp.int32)
        self.index = {}
        for level in range(self.levels):
            names = ["up_own", "up_got"]
            if level < self.head_bits:
                names += ["m_in", "m_got", "s_in", "s_own"]
            else:
                names += ["unit"]
            for name in names + (["pick"] if level + 1 == self.levels else []):
                self.index[name, level] = len(self.index)

    def call(self, body, name, ins, in_specs, outs, out_specs, scratch, cost, **kw):
        return pl.pallas_call(
            body,
            in_specs=in_specs,
            out_specs=out_specs,
            out_shape=outs,
            scratch_shapes=scratch,
            compiler_params=pltpu.CompilerParams(vmem_limit_bytes=VMEM),
            cost_estimate=pl.CostEstimate(
                flops=cost[0], bytes_accessed=cost[1], transcendentals=0
            ),
            name=name,
            **kw,
        )(*ins)

    def states(self, chunk, arrays, after):
        n, d, part = self.n, self.d, self.part
        shape = (2, part // 2, d, d)
        return self.call(
            functools.partial(states_kernel, chunk),
            "states",
            [self.place, self.lengths, *arrays, *after],
            [IN_SMEM] * 2 + [IN_HBM] * 4 + [ANYWHERE] * len(after),
            (
                jax.ShapeDtypeStruct(shape, F32),
                jax.ShapeDtypeStruct(shape, B16),
                jax.ShapeDtypeStruct((4, part, n, d), B16),
            ),
            [IN_VMEM] * 3,
            [pltpu.VMEM((n, part, d), B16)] * 4
            + [pltpu.VMEM((n * part, d), F32)] * 2
            + [pltpu.SemaphoreType.DMA((4,))],
            (4 * n * d * d * part, 16 * n * d * part),
        )

    def grads(self, chunk, heads, mine, got, before, after):
        n, d, part = self.n, self.d, self.part
        out = jax.ShapeDtypeStruct((n, self.total, d), B16)
        return self.call(
            functools.partial(grads_kernel, chunk, self.scaling),
            "grads",
            [self.place, self.lengths, heads, mine, got, *before, *after],
            [IN_SMEM] * 2
            + [IN_VMEM] * 3
            + [IN_HBM] * len(before)
            + [ANYWHERE] * len(after),
            (out, out, out, jax.ShapeDtypeStruct((8, 128), F32)),
            [IN_HBM] * 3 + [IN_VMEM],
            [pltpu.VMEM((n * part, d), F32)] * 3
            + [pltpu.VMEM((n, part, d), B16)] * 3
            + [pltpu.SemaphoreType.DMA((3,))],
            (16 * n * d * d * part, 16 * n * d * part),
            input_output_aliases={5 + i: i for i in range(len(before))},
        )

    def weights(self, after):
        n, bits = self.n, self.head_bits

        def kernel(place_ref, len_ref, *refs):
            out = refs[-1]
            device = place_ref[0]
            begin = ((device >> bits) << bits) * n
            end = begin + (n << bits)
            pairs = []
            for level in range(self.levels):
                group = (device >> (level + 1)) << (level + 1)
                low, high = group * n, (group + (2 << level)) * n
                middle = (group + (1 << level)) * n
                pairs += [(middle - 1, high - 1), (low, middle)]
                if level < bits:
                    pairs += [(middle - 1, middle)]
                else:
                    pairs += [(middle - 1, begin), (end - 1, middle)]
            same = _same(len_ref, pairs)
            one, zero = F32(1.0), F32(0.0)

            def put(name, level, a, b):
                out[2 * self.index[name, level]] = a
                out[2 * self.index[name, level] + 1] = b

            for level in range(self.levels):
                hi = (device >> level) & 1 == 1
                lasts, firsts = same[0], same[1]
                put("up_own", level, jnp.where(hi, one, lasts), jnp.where(hi, firsts, one))
                put("up_got", level, jnp.where(hi, lasts, one), jnp.where(hi, one, firsts))
                if level < bits:
                    join = same[2]
                    same = same[3:]
                    put("m_in", level, jnp.where(hi, firsts, one), jnp.where(hi, one, lasts))
                    put("m_got", level, jnp.where(hi, join, zero), jnp.where(hi, zero, join))
                    put("s_in", level, jnp.where(hi, one, firsts), jnp.where(hi, lasts, one))
                    put("s_own", level, jnp.where(hi, zero, join), jnp.where(hi, join, zero))
                else:
                    ahead, behind = same[2], same[3]
                    same = same[4:]
                    put("unit", level, jnp.where(hi, ahead, zero), jnp.where(hi, zero, behind))
                if level + 1 == self.levels:
                    put("pick", level, jnp.where(hi, zero, one), jnp.where(hi, one, zero))

        self.scalars = self.call(
            kernel,
            "weights",
            [self.place, self.lengths, *after],
            [IN_SMEM] * 2 + [ANYWHERE] * len(after),
            jax.ShapeDtypeStruct((2 * len(self.index),), F32),
            IN_SMEM,
            [],
            (1000, 1000),
        )

    def combine(self, name, body, ins, outs, after):
        moved = sum(math.prod(x.shape) * jnp.dtype(x.dtype).itemsize for x in (*ins, *outs))

        def kernel(scalar_ref, *refs):
            body(
                lambda name, level, which: scalar_ref[2 * self.index[name, level] + which],
                refs[: len(ins)],
                refs[len(refs) - len(outs) :],
            )

        return self.call(
            kernel,
            name,
            [self.scalars, *ins, *after],
            [IN_SMEM] + [IN_VMEM] * len(ins) + [ANYWHERE] * len(after),
            tuple(outs),
            [IN_VMEM] * len(outs),
            [],
            (moved, moved),
        )

    def swap(self, x, level):
        if level < self.head_bits:
            moves = [(i, i ^ (1 << level)) for i in range(self.head_size)]
            return lax.ppermute(x, "head", moves)
        bit = 1 << (level - self.head_bits)
        return lax.ppermute(x, "seq", [(i, i ^ bit) for i in range(self.seq_size)])

    def stages(self, chunk, arrays):
        d, bits, last = self.d, self.head_bits, self.levels - 1
        own, got, here = [], [], {}

        def shaped(heads, dtype, lead=2):
            return jax.ShapeDtypeStruct((lead, heads, d, d), dtype)

        def first(after):
            keep, send, here["heads"] = self.states(chunk, arrays, after)
            own.append(keep)
            here["got"] = self.swap(send, 0)
            if chunk == 0:
                self.weights((keep,))
            return keep

        def up(level, after):
            got.append(here["got"])
            heads = own[-1].shape[1]
            half = heads // 2 if level + 1 < bits else heads

            def body(w, ins, outs):
                for which in range(2):
                    o, g = w("up_own", level, which), w("up_got", level, which)
                    for h in range(heads):
                        x = o * ins[0][which, h] + g * ins[1][which, h].astype(F32)
                        if h < half:
                            outs[0][which, h] = x
                        if half == heads:
                            outs[1][which, h] = x.astype(B16)
                        elif h >= half:
                            outs[1][which, h - half] = x.astype(B16)

            outs = [shaped(half, F32), shaped(half, B16)]
            keep, send = self.combine("up", body, [own[-1], got[-1]], outs, after)
            if half < heads:
                own.append(keep)
            else:
                here["total"] = keep
            here["got"] = self.swap(send, level + 1)
            return keep

        def across(level, after):
            ins = [here["total"], here["got"]]
            if "state" in here:
                ins.append(here["state"])
            heads = ins[0].shape[1]
            final = level + 1 == last

            def body(w, ins, outs):
                for h in range(heads):
                    totals = []
                    for which in range(2):
                        other = ins[1][which, h].astype(F32)
                        x = w("up_own", level, which) * ins[0][which, h]
                        x = x + w("up_got", level, which) * other
                        y = w("unit", level, which) * other
                        if len(ins) > 2:
                            y = y + ins[2][which, h]
                        outs[0][which, h] = y
                        totals.append(x)
                        if not final:
                            outs[1][which, h] = x.astype(B16)
                            outs[2][which, h] = x
                    if final:
                        x = w("pick", last, 0) * totals[0] + w("pick", last, 1) * totals[1]
                        outs[1][0, h] = x.astype(B16)

            outs = [shaped(heads, F32), shaped(heads, B16, 1 if final else 2)]
            if not final:
                outs.append(shaped(heads, F32))
            state, send, *total = self.combine("across", body, ins, outs, after)
            here["state"] = state
            here["total"] = total[0] if total else None
            here["got"] = self.swap(send, level + 1)
            return state

        def down(level, after):
            top = level == bits - 1
            ins = [here["state"], here["got"], own[level], got[level]]
            heads = own[level].shape[1]
            half = heads // 2
            factor = self.scaling if level == 0 else 1.0

            def body(w, ins, outs):
                for which in range(2):
                    m_in, m_got, s_in, s_own = (
                        factor * w(name, level, which)
                        for name in ("m_in", "m_got", "s_in", "s_own")
                    )
                    for h in range(heads):
                        if top:
                            x = w("unit", last, which) * ins[1][0, h].astype(F32)
                            x = x + ins[0][which, h]
                        elif h < half:
                            x = ins[0][which, h]
                        else:
                            x = ins[1][which, h - half].astype(F32)
                        mine = m_in * x + m_got * ins[3][which, h].astype(F32)
                        theirs = s_in * x + s_own * ins[2][which, h]
                        outs[0][which, h] = mine.astype(outs[0].dtype)
                        outs[1][which, h] = theirs.astype(B16)

            outs = [shaped(heads, B16 if level == 0 else F32), shaped(heads, B16)]
            here["state"], send = self.combine("down", body, ins, outs, after)
            here["got"] = self.swap(send, level)
            return here["state"]

        def final(before, after):
            *outs, token = self.grads(
                chunk, here["heads"], here["state"], here["got"], before, after
            )
            return outs, token

        steps = [first]
        steps += [functools.partial(up, level) for level in range(bits)]
        steps += [functools.partial(across, level) for level in range(bits, last)]
        steps += [functools.partial(down, level) for level in reversed(range(bits))]
        return steps + [final]


def local(seq_size, head_size, queries, key_heads, value_heads, grad_output, doc_lengths):
    n, heads, d = queries.shape
    arrays = (queries, key_heads, value_heads, grad_output)
    plan = Plan(seq_size, head_size, n, heads, d, doc_lengths)
    stages = [plan.stages(chunk, arrays) for chunk in range(plan.chunks)]
    count = len(stages[0])
    outs, after = (), ()
    for wave in range(count + plan.chunks - 1):
        for chunk in reversed(range(plan.chunks)):
            stage = wave - chunk
            if not 0 <= stage < count:
                continue
            if stage + 1 < count:
                after = (stages[chunk][stage](after),)
            else:
                outs, token = stages[chunk][stage](outs, after)
                after = (token,)
    return tuple(outs)


def solution(mesh):
    placed = P(("seq", "head"), None, None)
    return jax.shard_map(
        functools.partial(local, mesh.shape["seq"], mesh.shape["head"]),
        mesh=mesh,
        in_specs=(placed, placed, placed, placed, P()),
        out_specs=(placed, placed, placed),
        check_vma=False,
    )
```

time: 188 us -> 115 us (0.61)
  Pallas kernels: 136 us -> 53.7 us
  waiting for transfers between devices: 3.09 us -> 20.4 us
  local copies, waits for them, and re-layouts: 20.3 us -> 7.03 us
  starting transfers between devices: 26.4 us -> 32.5 us
    pallas_call x32 -> x33, Pallas kernels: 136 us -> 53.7 us  [call(): pl.pallas_call(body, in_specs=in_specs, out_specs=out_specs, out_shape=ou...]
    unnamed x62 -> x16, local copies, waits for them, and re-layouts: 20.3 us -> 7.03 us
    ppermute x12, waiting for transfers between devices: 0.03 us -> 12.7 us  [swap(): return lax.ppermute(x, 'seq', [(i, i ^ bit) for i in range(self.seq_size)])]
    ppermute x16, waiting for transfers between devices: 3.06 us -> 7.72 us  [swap(): return lax.ppermute(x, 'head', moves)]
    ppermute x12, starting transfers between devices: 16.3 us -> 19.7 us  [swap(): return lax.ppermute(x, 'seq', [(i, i ^ bit) for i in range(self.seq_size)])]
    ppermute x16, starting transfers between devices: 10.1 us -> 12.8 us  [swap(): return lax.ppermute(x, 'head', moves)]
  transfers between devices with their start and end apart: 28 -> 28, of which waited for: 2 -> 7; matrix products, arithmetic and copies ran while one was open for 0% -> 0% of each run, Pallas kernels for 64% -> 39%
where the time goes in v1:
time: 115 us
  Pallas kernels  53.7 us (47%)
  starting transfers between devices  32.5 us (28%)
  waiting for transfers between devices  20.4 us (18%)
  local copies, waits for them, and re-layouts  7.03 us (6%)
  between operations  1.18 us (1%)
    pallas_call x33, Pallas kernels, call(): pl.pallas_call(body, in_specs=in_specs, out_specs=out_specs, out_shape=ou...  53.7 us
    ppermute x12, starting transfers between devices, swap(): return lax.ppermute(x, 'seq', [(i, i ^ bit) for i in range(self.seq_size)])  19.7 us
    ppermute x16, starting transfers between devices, swap(): return lax.ppermute(x, 'head', moves)  12.8 us
    ppermute x12, waiting for transfers between devices, swap(): return lax.ppermute(x, 'seq', [(i, i ^ bit) for i in range(self.seq_size)])  12.7 us
    ppermute x16, waiting for transfers between devices, swap(): return lax.ppermute(x, 'head', moves)  7.72 us
    unnamed x16, local copies, waits for them, and re-layouts  7.03 us
  transfers between devices with their start and end apart: 28, of which 7 were waited for; matrix products, arithmetic and copies ran while one was open for 0% of the time, Pallas kernels for 39%

profile of v1, /device:TPU:0, one launch (start us, length us, event | category | flops | bytes accessed | tf_op | source)
XLA Modules:
  0.0 114.9 jit_solution(12729506132132147121)
XLA Ops:
  0.7 1.6 %copy-done = bf16[128,64,128]{2,1,0:T(8,128)(2,1)S(1)} copy-done((bf16[128,64,128]{2,1,0:T(8,128)(2,1)S(1)}, bf16[128,64,128]{2,1,0:T(8,128)(2,1)}, u32[]{:S(2)}) %copy-start) | copy-done | bytes 2097176
  2.3 1.6 %copy-done.2 = bf16[128,64,128]{2,1,0:T(8,128)(2,1)S(1)} copy-done((bf16[128,64,128]{2,1,0:T(8,128)(2,1)S(1)}, bf16[128,64,128]{2,1,0:T(8,128)(2,1)}, u32[]{:S(2)}) %copy-start.2) | copy-done | bytes 2097176
  3.9 1.6 %copy-done.4 = bf16[128,64,128]{2,1,0:T(8,128)(2,1)S(1)} copy-done((bf16[128,64,128]{2,1,0:T(8,128)(2,1)S(1)}, bf16[128,64,128]{2,1,0:T(8,128)(2,1)}, u32[]{:S(2)}) %copy-start.4) | copy-done | bytes 2097176
  5.5 1.6 %copy-done.5 = bf16[128,64,128]{2,1,0:T(8,128)(2,1)S(1)} copy-done((bf16[128,64,128]{2,1,0:T(8,128)(2,1)S(1)}, bf16[128,64,128]{2,1,0:T(8,128)(2,1)}, u32[]{:S(2)}) %copy-start.5) | copy-done | bytes 2097176
  7.7 3.1 %states.4 = (f32[2,8,128,128]{3,2,1,0:T(8,128)S(1)}, bf16[2,8,128,128]{3,2,1,0:T(8,128)(2,1)S(1)}, bf16[4,16,128,128]{3,2,1,0:T(8,128)(2,1)S(1)}) custom-call(s32[2]{0:T(128)S(1)} %pad_add_fusion.place_ref, s32[16]{0:T(128)S(1)} %copy-done.6, bf16[128,64,128]{2,1,0:T(8,128)(2,1)S(1)} %copy-done, bf16[128,64,128]{2,1,0:T(8,128)(2,1)S(1)} %copy-done.2, ...), custom_call_target="tpu_custom_call" | custom-call | flops 134217728 | bytes 4194304 | tf_op jit(solution)/shard_map/states/pallas_call | solution.py:170
  11.3 3.1 %states.5 = (f32[2,8,128,128]{3,2,1,0:T(8,128)S(1)}, bf16[2,8,128,128]{3,2,1,0:T(8,128)(2,1)S(1)}, bf16[4,16,128,128]{3,2,1,0:T(8,128)(2,1)S(1)}) custom-call(s32[2]{0:T(128)S(1)} %pad_add_fusion.place_ref, s32[16]{0:T(128)S(1)} %copy-done.6, bf16[128,64,128]{2,1,0:T(8,128)(2,1)S(1)} %copy-done, bf16[128,64,128]{2,1,0:T(8,128)(2,1)S(1)} %copy-done.2, ...), custom_call_target="tpu_custom_call" | custom-call | flops 134217728 | bytes 4194304 | tf_op jit(solution)/shard_map/states/pallas_call | solution.py:170
  14.6 1.9 %weights.1.scalar_ref = f32[44]{0:T(128)S(1)} custom-call(s32[2]{0:T(128)S(1)} %pad_add_fusion.place_ref, s32[16]{0:T(128)S(1)} %copy-done.6, f32[2,8,128,128]{3,2,1,0:T(8,128)S(1)} %get-tuple-element.82.refs_0_.refs_4_.refs_2_), custom_call_target="tpu_custom_call" | custom-call | flops 1000 | bytes 1000 | tf_op jit(solution)/shard_map/weights/pallas_call | solution.py:170
  17.2 3.0 %collective-permute-start.1 = (bf16[2,4,128,128]{3,2,1,0:T(8,128)(2,1)S(1)}, bf16[2,4,128,128]{3,2,1,0:T(8,128)(2,1)S(1)}, u32[]{:S(2)}, u32[]{:S(2)}) collective-permute-start(bf16[2,4,128,128]{3,2,1,0:T(8,128)(2,1)S(1)} %get-tuple-element.86), channel_id=1, source_target_pairs={{0,2},{1,3},{2,0},{3,1},{4,6},{5,7},{6,4},{7,5},{8,10},{9,11},{10,... | collective-permute-start | bytes 786440 | tf_op jit(solution)/shard_map/ppermute | solution.py:303
  20.2 3.1 %states.6 = (f32[2,8,128,128]{3,2,1,0:T(8,128)S(1)}, bf16[2,8,128,128]{3,2,1,0:T(8,128)(2,1)S(1)}, bf16[4,16,128,128]{3,2,1,0:T(8,128)(2,1)S(1)}) custom-call(s32[2]{0:T(128)S(1)} %pad_add_fusion.place_ref, s32[16]{0:T(128)S(1)} %copy-done.6, bf16[128,64,128]{2,1,0:T(8,128)(2,1)S(1)} %copy-done.1, bf16[128,64,128]{2,1,0:T(8,128)(2,1)S(1)} %copy-done.3, ...), custom_call_target="tpu_custom_call" | custom-call | flops 134217728 | bytes 4194304 | tf_op jit(solution)/shard_map/states/pallas_call | solution.py:170
  24.0 2.6 %collective-permute-done.1.refs_1_.refs_3_ = bf16[2,4,128,128]{3,2,1,0:T(8,128)(2,1)S(1)} collective-permute-done((bf16[2,4,128,128]{3,2,1,0:T(8,128)(2,1)S(1)}, bf16[2,4,128,128]{3,2,1,0:T(8,128)(2,1)S(1)}, u32[]{:S(2)}, u32[]{:S(2)}) %collective-permute-start.1) | collective-permute-done | bytes 262176 | tf_op jit(solution)/shard_map/ppermute | solution.py:303
  27.3 3.2 %states.7 = (f32[2,8,128,128]{3,2,1,0:T(8,128)S(1)}, bf16[2,8,128,128]{3,2,1,0:T(8,128)(2,1)S(1)}, bf16[4,16,128,128]{3,2,1,0:T(8,128)(2,1)S(1)}) custom-call(s32[2]{0:T(128)S(1)} %pad_add_fusion.place_ref, s32[16]{0:T(128)S(1)} %copy-done.6, bf16[128,64,128]{2,1,0:T(8,128)(2,1)S(1)} %copy-done.1, bf16[128,64,128]{2,1,0:T(8,128)(2,1)S(1)} %copy-done.3, ...), custom_call_target="tpu_custom_call" | custom-call | flops 134217728 | bytes 4194304 | tf_op jit(solution)/shard_map/states/pallas_call | solution.py:170
  30.6 1.8 %collective-permute-start.5 = (bf16[2,4,128,128]{3,2,1,0:T(8,128)(2,1)S(1)}, bf16[2,4,128,128]{3,2,1,0:T(8,128)(2,1)S(1)}, u32[]{:S(2)}, u32[]{:S(2)}) collective-permute-start(bf16[2,4,128,128]{3,2,1,0:T(8,128)(2,1)S(1)} %get-tuple-element.95), channel_id=1, source_target_pairs={{0,2},{1,3},{2,0},{3,1},{4,6},{5,7},{6,4},{7,5},{8,10},{9,11},{10,... | collective-permute-start | bytes 786440 | tf_op jit(solution)/shard_map/ppermute | solution.py:303
  32.4 1.5 %collective-permute-start.4 = (bf16[2,4,128,128]{3,2,1,0:T(8,128)(2,1)S(1)}, bf16[2,4,128,128]{3,2,1,0:T(8,128)(2,1)S(1)}, u32[]{:S(2)}, u32[]{:S(2)}) collective-permute-start(bf16[2,4,128,128]{3,2,1,0:T(8,128)(2,1)S(1)} %get-tuple-element.94), channel_id=1, source_target_pairs={{0,4},{4,0},{8,12},{12,8},{16,20},{20,16},{24,28},{28,24},{1,5},{5... | collective-permute-start | bytes 786440 | tf_op jit(solution)/shard_map/ppermute | solution.py:305
  35.3 4.5 %collective-permute-done.5.refs_1_.refs_3_ = bf16[2,4,128,128]{3,2,1,0:T(8,128)(2,1)S(1)} collective-permute-done((bf16[2,4,128,128]{3,2,1,0:T(8,128)(2,1)S(1)}, bf16[2,4,128,128]{3,2,1,0:T(8,128)(2,1)S(1)}, u32[]{:S(2)}, u32[]{:S(2)}) %collective-permute-start.5) | collective-permute-done | bytes 262176 | tf_op jit(solution)/shard_map/ppermute | solution.py:303
  40.4 1.8 %collective-permute-start.9 = (bf16[2,4,128,128]{3,2,1,0:T(8,128)(2,1)S(1)}, bf16[2,4,128,128]{3,2,1,0:T(8,128)(2,1)S(1)}, u32[]{:S(2)}, u32[]{:S(2)}) collective-permute-start(bf16[2,4,128,128]{3,2,1,0:T(8,128)(2,1)S(1)} %get-tuple-element.104), channel_id=1, source_target_pairs={{0,4},{4,0},{8,12},{12,8},{16,20},{20,16},{24,28},{28,24},{1,5},{5... | collective-permute-start | bytes 786440 | tf_op jit(solution)/shard_map/ppermute | solution.py:305
  42.9 1.7 %collective-permute-start.8 = (bf16[2,4,128,128]{3,2,1,0:T(8,128)(2,1)S(1)}, bf16[2,4,128,128]{3,2,1,0:T(8,128)(2,1)S(1)}, u32[]{:S(2)}, u32[]{:S(2)}) collective-permute-start(bf16[2,4,128,128]{3,2,1,0:T(8,128)(2,1)S(1)} %get-tuple-element.103), channel_id=1, source_target_pairs={{0,8},{4,12},{8,0},{12,4},{16,24},{20,28},{24,16},{28,20},{1,9},{5... | collective-permute-start | bytes 786440 | tf_op jit(solution)/shard_map/ppermute | solution.py:305
  45.3 1.5 %collective-permute-start.7 = (bf16[2,4,128,128]{3,2,1,0:T(8,128)(2,1)S(1)}, bf16[2,4,128,128]{3,2,1,0:T(8,128)(2,1)S(1)}, u32[]{:S(2)}, u32[]{:S(2)}) collective-permute-start(bf16[2,4,128,128]{3,2,1,0:T(8,128)(2,1)S(1)} %get-tuple-element.101), channel_id=1, source_target_pairs={{0,2},{1,3},{2,0},{3,1},{4,6},{5,7},{6,4},{7,5},{8,10},{9,11},{10,... | collective-permute-start | bytes 786440 | tf_op jit(solution)/shard_map/ppermute | solution.py:303
  48.7 1.8 %collective-permute-start.13 = (bf16[2,4,128,128]{3,2,1,0:T(8,128)(2,1)S(1)}, bf16[2,4,128,128]{3,2,1,0:T(8,128)(2,1)S(1)}, u32[]{:S(2)}, u32[]{:S(2)}) collective-permute-start(bf16[2,4,128,128]{3,2,1,0:T(8,128)(2,1)S(1)} %get-tuple-element.113), channel_id=1, source_target_pairs={{0,8},{4,12},{8,0},{12,4},{16,24},{20,28},{24,16},{28,20},{1,9},{5... | collective-permute-start | bytes 786440 | tf_op jit(solution)/shard_map/ppermute | solution.py:305
  51.1 2.7 %collective-permute-start.12 = (bf16[1,4,128,128]{3,2,1,0:T(8,128)(2,1)S(1)}, bf16[1,4,128,128]{3,2,1,0:T(8,128)(2,1)S(1)}, u32[]{:S(2)}, u32[]{:S(2)}) collective-permute-start(bf16[1,4,128,128]{3,2,1,0:T(8,128)(2,1)S(1)} %get-tuple-element.111), channel_id=1, source_target_pairs={{0,16},{4,20},{8,24},{12,28},{16,0},{20,4},{24,8},{28,12},{1,17},{... | collective-permute-start | bytes 393224 | tf_op jit(solution)/shard_map/ppermute | solution.py:305
  54.4 1.6 %collective-permute-start.11 = (bf16[2,4,128,128]{3,2,1,0:T(8,128)(2,1)S(1)}, bf16[2,4,128,128]{3,2,1,0:T(8,128)(2,1)S(1)}, u32[]{:S(2)}, u32[]{:S(2)}) collective-permute-start(bf16[2,4,128,128]{3,2,1,0:T(8,128)(2,1)S(1)} %get-tuple-element.110), channel_id=1, source_target_pairs={{0,4},{4,0},{8,12},{12,8},{16,20},{20,16},{24,28},{28,24},{1,5},{5... | collective-permute-start | bytes 786440 | tf_op jit(solution)/shard_map/ppermute | solution.py:305
  57.2 2.2 %collective-permute-done.13.refs_1_ = bf16[2,4,128,128]{3,2,1,0:T(8,128)(2,1)S(1)} collective-permute-done((bf16[2,4,128,128]{3,2,1,0:T(8,128)(2,1)S(1)}, bf16[2,4,128,128]{3,2,1,0:T(8,128)(2,1)S(1)}, u32[]{:S(2)}, u32[]{:S(2)}) %collective-permute-start.13) | collective-permute-done | bytes 262176 | tf_op jit(solution)/shard_map/ppermute | solution.py:305
  60.8 1.6 %collective-permute-start.16 = (bf16[2,4,128,128]{3,2,1,0:T(8,128)(2,1)S(1)}, bf16[2,4,128,128]{3,2,1,0:T(8,128)(2,1)S(1)}, u32[]{:S(2)}, u32[]{:S(2)}) collective-permute-start(bf16[2,4,128,128]{3,2,1,0:T(8,128)(2,1)S(1)} %get-tuple-element.121), channel_id=1, source_target_pairs={{0,2},{1,3},{2,0},{3,1},{4,6},{5,7},{6,4},{7,5},{8,10},{9,11},{10,... | collective-permute-start | bytes 786440 | tf_op jit(solution)/shard_map/ppermute | solution.py:303
  62.4 3.3 %collective-permute-start.17 = (bf16[1,4,128,128]{3,2,1,0:T(8,128)(2,1)S(1)}, bf16[1,4,128,128]{3,2,1,0:T(8,128)(2,1)S(1)}, u32[]{:S(2)}, u32[]{:S(2)}) collective-permute-start(bf16[1,4,128,128]{3,2,1,0:T(8,128)(2,1)S(1)} %get-tuple-element.122), channel_id=1, source_target_pairs={{0,16},{4,20},{8,24},{12,28},{16,0},{20,4},{24,8},{28,12},{1,17},{... | collective-permute-start | bytes 393224 | tf_op jit(solution)/shard_map/ppermute | solution.py:305
  66.4 1.6 %collective-permute-start.15 = (bf16[2,4,128,128]{3,2,1,0:T(8,128)(2,1)S(1)}, bf16[2,4,128,128]{3,2,1,0:T(8,128)(2,1)S(1)}, u32[]{:S(2)}, u32[]{:S(2)}) collective-permute-start(bf16[2,4,128,128]{3,2,1,0:T(8,128)(2,1)S(1)} %get-tuple-element.119), channel_id=1, source_target_pairs={{0,8},{4,12},{8,0},{12,4},{16,24},{20,28},{24,16},{28,20},{1,9},{5... | collective-permute-start | bytes 786440 | tf_op jit(solution)/shard_map/ppermute | solution.py:305
  70.3 1.5 %collective-permute-start.21 = (bf16[2,4,128,128]{3,2,1,0:T(8,128)(2,1)S(1)}, bf16[2,4,128,128]{3,2,1,0:T(8,128)(2,1)S(1)}, u32[]{:S(2)}, u32[]{:S(2)}) collective-permute-start(bf16[2,4,128,128]{3,2,1,0:T(8,128)(2,1)S(1)} %get-tuple-element.132), channel_id=1, source_target_pairs={{0,2},{1,3},{2,0},{3,1},{4,6},{5,7},{6,4},{7,5},{8,10},{9,11},{10,... | collective-permute-start | bytes 786440 | tf_op jit(solution)/shard_map/ppermute | solution.py:303
  72.7 2.6 %collective-permute-start.22 = (bf16[1,4,128,128]{3,2,1,0:T(8,128)(2,1)S(1)}, bf16[1,4,128,128]{3,2,1,0:T(8,128)(2,1)S(1)}, u32[]{:S(2)}, u32[]{:S(2)}) collective-permute-start(bf16[1,4,128,128]{3,2,1,0:T(8,128)(2,1)S(1)} %get-tuple-element.133), channel_id=1, source_target_pairs={{0,16},{4,20},{8,24},{12,28},{16,0},{20,4},{24,8},{28,12},{1,17},{... | collective-permute-start | bytes 393224 | tf_op jit(solution)/shard_map/ppermute | solution.py:305
  76.1 6.3 %collective-permute-done.22.refs_1_ = bf16[1,4,128,128]{3,2,1,0:T(8,128)(2,1)S(1)} collective-permute-done((bf16[1,4,128,128]{3,2,1,0:T(8,128)(2,1)S(1)}, bf16[1,4,128,128]{3,2,1,0:T(8,128)(2,1)S(1)}, u32[]{:S(2)}, u32[]{:S(2)}) %collective-permute-start.22) | collective-permute-done | bytes 131104 | tf_op jit(solution)/shard_map/ppermute | solution.py:305
  84.9 5.4 %grads.4 = (bf16[128,64,128]{2,1,0:T(8,128)(2,1)}, bf16[128,64,128]{2,1,0:T(8,128)(2,1)}, bf16[128,64,128]{2,1,0:T(8,128)(2,1)}, f32[8,128]{1,0:T(8,128)S(1)}) custom-call(s32[2]{0:T(128)S(1)} %pad_add_fusion.place_ref, s32[16]{0:T(128)S(1)} %copy-done.7, bf16[4,16,128,128]{3,2,1,0:T(8,128)(2,1)S(1)} %get-tuple-element.130.head_ref, ...), custom_call_target="tpu_custom_call" | custom-call | flops 536870912 | bytes 4194304 | tf_op jit(solution)/shard_map/grads/pallas_call | solution.py:170
  90.4 3.3 %collective-permute-done.19.refs_1_ = bf16[1,4,128,128]{3,2,1,0:T(8,128)(2,1)S(1)} collective-permute-done((bf16[1,4,128,128]{3,2,1,0:T(8,128)(2,1)S(1)}, bf16[1,4,128,128]{3,2,1,0:T(8,128)(2,1)S(1)}, u32[]{:S(2)}, u32[]{:S(2)}) %collective-permute-start.19) | collective-permute-done | bytes 131104 | tf_op jit(solution)/shard_map/ppermute | solution.py:305
  96.2 5.6 %grads.5 = (bf16[128,64,128]{2,1,0:T(8,128)(2,1)}, bf16[128,64,128]{2,1,0:T(8,128)(2,1)}, bf16[128,64,128]{2,1,0:T(8,128)(2,1)}, f32[8,128]{1,0:T(8,128)S(1)}) custom-call(s32[2]{0:T(128)S(1)} %pad_add_fusion.place_ref, s32[16]{0:T(128)S(1)} %copy-done.7, ...), custom_call_target="tpu_custom_call", output_to_operand_aliasing={{0}: (5, {}), {1}: (6, {}), {2}: (7, {})} | custom-call | flops 536870912 | bytes 4194304 | tf_op jit(solution)/shard_map/grads/pallas_call | solution.py:170
  103.3 5.4 %grads.6 = (bf16[128,64,128]{2,1,0:T(8,128)(2,1)}, bf16[128,64,128]{2,1,0:T(8,128)(2,1)}, bf16[128,64,128]{2,1,0:T(8,128)(2,1)}, f32[8,128]{1,0:T(8,128)S(1)}) custom-call(s32[2]{0:T(128)S(1)} %pad_add_fusion.place_ref, s32[16]{0:T(128)S(1)} %copy-done.7, ...), custom_call_target="tpu_custom_call", output_to_operand_aliasing={{0}: (5, {}), {1}: (6, {}), {2}: (7, {})} | custom-call | flops 536870912 | bytes 4194304 | tf_op jit(solution)/shard_map/grads/pallas_call | solution.py:170
  108.7 6.0 %grads.7 = (bf16[128,64,128]{2,1,0:T(8,128)(2,1)}, bf16[128,64,128]{2,1,0:T(8,128)(2,1)}, bf16[128,64,128]{2,1,0:T(8,128)(2,1)}, f32[8,128]{1,0:T(8,128)}) custom-call(s32[2]{0:T(128)S(1)} %pad_add_fusion.place_ref, s32[16]{0:T(128)S(1)} %copy-done.7, ...), custom_call_target="tpu_custom_call", output_to_operand_aliasing={{0}: (5, {}), {1}: (6, {}), {2}: (7, {})} | custom-call | flops 536870912 | bytes 4194304 | tf_op jit(solution)/shard_map/grads/pallas_call | solution.py:170
  (74 shorter events, 23.5 us)
Async XLA Ops:
  0.7 1.6 %copy-start = (bf16[128,64,128]{2,1,0:T(8,128)(2,1)S(1)}, bf16[128,64,128]{2,1,0:T(8,128)(2,1)}, u32[]{:S(2)}) copy-start(bf16[128,64,128]{2,1,0:T(8,128)(2,1)} %refs_0_.7) | copy-start | bytes 6291460
  10.8 5.7 %collective-permute-start = (bf16[2,8,128,128]{3,2,1,0:T(8,128)(2,1)S(1)}, bf16[2,8,128,128]{3,2,1,0:T(8,128)(2,1)S(1)}, u32[]{:S(2)}, u32[]{:S(2)}) collective-permute-start(bf16[2,8,128,128]{3,2,1,0:T(8,128)(2,1)S(1)} %get-tuple-element.83), channel_id=1, source_target_pairs={{0,1},{1,0},{2,3},{3,2},{4,5},{5,4},{6,7},{7,6},{8,9},{9,8},{10,11... | collective-permute-start | bytes 1572872 | tf_op jit(solution)/shard_map/ppermute | solution.py:303
  11.3 8.9 %copy-start.3 = (bf16[128,64,128]{2,1,0:T(8,128)(2,1)S(1)}, bf16[128,64,128]{2,1,0:T(8,128)(2,1)}, u32[]{:S(2)}) copy-start(bf16[128,64,128]{2,1,0:T(8,128)(2,1)} %refs_1_.7) | copy-start | bytes 6291460
  14.4 5.8 %copy-start.1 = (bf16[128,64,128]{2,1,0:T(8,128)(2,1)S(1)}, bf16[128,64,128]{2,1,0:T(8,128)(2,1)}, u32[]{:S(2)}) copy-start(bf16[128,64,128]{2,1,0:T(8,128)(2,1)} %refs_0_.7) | copy-start | bytes 6291460
  14.4 8.9 %collective-permute-start.2 = (bf16[2,8,128,128]{3,2,1,0:T(8,128)(2,1)S(1)}, bf16[2,8,128,128]{3,2,1,0:T(8,128)(2,1)S(1)}, u32[]{:S(2)}, u32[]{:S(2)}) collective-permute-start(bf16[2,8,128,128]{3,2,1,0:T(8,128)(2,1)S(1)} %get-tuple-element.87), channel_id=1, source_target_pairs={{0,1},{1,0},{2,3},{3,2},{4,5},{5,4},{6,7},{7,6},{8,9},{9,8},{10,11... | collective-permute-start | bytes 1572872 | tf_op jit(solution)/shard_map/ppermute | solution.py:303
  17.2 9.5 %collective-permute-start.1 = (bf16[2,4,128,128]{3,2,1,0:T(8,128)(2,1)S(1)}, bf16[2,4,128,128]{3,2,1,0:T(8,128)(2,1)S(1)}, u32[]{:S(2)}, u32[]{:S(2)}) collective-permute-start(bf16[2,4,128,128]{3,2,1,0:T(8,128)(2,1)S(1)} %get-tuple-element.86), channel_id=1, source_target_pairs={{0,2},{1,3},{2,0},{3,1},{4,6},{5,7},{6,4},{7,5},{8,10},{9,11},{10,... | collective-permute-start | bytes 786440 | tf_op jit(solution)/shard_map/ppermute | solution.py:303
  23.3 10.7 %collective-permute-start.6 = (bf16[2,8,128,128]{3,2,1,0:T(8,128)(2,1)S(1)}, bf16[2,8,128,128]{3,2,1,0:T(8,128)(2,1)S(1)}, u32[]{:S(2)}, u32[]{:S(2)}) collective-permute-start(bf16[2,8,128,128]{3,2,1,0:T(8,128)(2,1)S(1)} %get-tuple-element.96), channel_id=1, source_target_pairs={{0,1},{1,0},{2,3},{3,2},{4,5},{5,4},{6,7},{7,6},{8,9},{9,8},{10,11... | collective-permute-start | bytes 1572872 | tf_op jit(solution)/shard_map/ppermute | solution.py:303
  30.5 14.0 %collective-permute-start.3 = (bf16[2,8,128,128]{3,2,1,0:T(8,128)(2,1)S(1)}, bf16[2,8,128,128]{3,2,1,0:T(8,128)(2,1)S(1)}, u32[]{:S(2)}, u32[]{:S(2)}) collective-permute-start(bf16[2,8,128,128]{3,2,1,0:T(8,128)(2,1)S(1)} %get-tuple-element.93), channel_id=1, source_target_pairs={{0,1},{1,0},{2,3},{3,2},{4,5},{5,4},{6,7},{7,6},{8,9},{9,8},{10,11... | collective-permute-start | bytes 1572872 | tf_op jit(solution)/shard_map/ppermute | solution.py:303
  30.6 9.2 %collective-permute-start.5 = (bf16[2,4,128,128]{3,2,1,0:T(8,128)(2,1)S(1)}, bf16[2,4,128,128]{3,2,1,0:T(8,128)(2,1)S(1)}, u32[]{:S(2)}, u32[]{:S(2)}) collective-permute-start(bf16[2,4,128,128]{3,2,1,0:T(8,128)(2,1)S(1)} %get-tuple-element.95), channel_id=1, source_target_pairs={{0,2},{1,3},{2,0},{3,1},{4,6},{5,7},{6,4},{7,5},{8,10},{9,11},{10,... | collective-permute-start | bytes 786440 | tf_op jit(solution)/shard_map/ppermute | solution.py:303
  32.4 9.8 %collective-permute-start.4 = (bf16[2,4,128,128]{3,2,1,0:T(8,128)(2,1)S(1)}, bf16[2,4,128,128]{3,2,1,0:T(8,128)(2,1)S(1)}, u32[]{:S(2)}, u32[]{:S(2)}) collective-permute-start(bf16[2,4,128,128]{3,2,1,0:T(8,128)(2,1)S(1)} %get-tuple-element.94), channel_id=1, source_target_pairs={{0,4},{4,0},{8,12},{12,8},{16,20},{20,16},{24,28},{28,24},{1,5},{5... | collective-permute-start | bytes 786440 | tf_op jit(solution)/shard_map/ppermute | solution.py:305
  34.7 12.2 %collective-permute-start.10 = (bf16[2,4,128,128]{3,2,1,0:T(8,128)(2,1)S(1)}, bf16[2,4,128,128]{3,2,1,0:T(8,128)(2,1)S(1)}, u32[]{:S(2)}, u32[]{:S(2)}) collective-permute-start(bf16[2,4,128,128]{3,2,1,0:T(8,128)(2,1)S(1)} %get-tuple-element.105), channel_id=1, source_target_pairs={{0,2},{1,3},{2,0},{3,1},{4,6},{5,7},{6,4},{7,5},{8,10},{9,11},{10,... | collective-permute-start | bytes 786440 | tf_op jit(solution)/shard_map/ppermute | solution.py:303
  40.4 7.6 %collective-permute-start.9 = (bf16[2,4,128,128]{3,2,1,0:T(8,128)(2,1)S(1)}, bf16[2,4,128,128]{3,2,1,0:T(8,128)(2,1)S(1)}, u32[]{:S(2)}, u32[]{:S(2)}) collective-permute-start(bf16[2,4,128,128]{3,2,1,0:T(8,128)(2,1)S(1)} %get-tuple-element.104), channel_id=1, source_target_pairs={{0,4},{4,0},{8,12},{12,8},{16,20},{20,16},{24,28},{28,24},{1,5},{5... | collective-permute-start | bytes 786440 | tf_op jit(solution)/shard_map/ppermute | solution.py:305
  42.9 7.5 %collective-permute-start.8 = (bf16[2,4,128,128]{3,2,1,0:T(8,128)(2,1)S(1)}, bf16[2,4,128,128]{3,2,1,0:T(8,128)(2,1)S(1)}, u32[]{:S(2)}, u32[]{:S(2)}) collective-permute-start(bf16[2,4,128,128]{3,2,1,0:T(8,128)(2,1)S(1)} %get-tuple-element.103), channel_id=1, source_target_pairs={{0,8},{4,12},{8,0},{12,4},{16,24},{20,28},{24,16},{28,20},{1,9},{5... | collective-permute-start | bytes 786440 | tf_op jit(solution)/shard_map/ppermute | solution.py:305
  45.3 8.5 %collective-permute-start.7 = (bf16[2,4,128,128]{3,2,1,0:T(8,128)(2,1)S(1)}, bf16[2,4,128,128]{3,2,1,0:T(8,128)(2,1)S(1)}, u32[]{:S(2)}, u32[]{:S(2)}) collective-permute-start(bf16[2,4,128,128]{3,2,1,0:T(8,128)(2,1)S(1)} %get-tuple-element.101), channel_id=1, source_target_pairs={{0,2},{1,3},{2,0},{3,1},{4,6},{5,7},{6,4},{7,5},{8,10},{9,11},{10,... | collective-permute-start | bytes 786440 | tf_op jit(solution)/shard_map/ppermute | solution.py:303
  47.5 8.6 %collective-permute-start.14 = (bf16[2,4,128,128]{3,2,1,0:T(8,128)(2,1)S(1)}, bf16[2,4,128,128]{3,2,1,0:T(8,128)(2,1)S(1)}, u32[]{:S(2)}, u32[]{:S(2)}) collective-permute-start(bf16[2,4,128,128]{3,2,1,0:T(8,128)(2,1)S(1)} %get-tuple-element.114), channel_id=1, source_target_pairs={{0,4},{4,0},{8,12},{12,8},{16,20},{20,16},{24,28},{28,24},{1,5},{5... | collective-permute-start | bytes 786440 | tf_op jit(solution)/shard_map/ppermute | solution.py:305
  48.7 10.7 %collective-permute-start.13 = (bf16[2,4,128,128]{3,2,1,0:T(8,128)(2,1)S(1)}, bf16[2,4,128,128]{3,2,1,0:T(8,128)(2,1)S(1)}, u32[]{:S(2)}, u32[]{:S(2)}) collective-permute-start(bf16[2,4,128,128]{3,2,1,0:T(8,128)(2,1)S(1)} %get-tuple-element.113), channel_id=1, source_target_pairs={{0,8},{4,12},{8,0},{12,4},{16,24},{20,28},{24,16},{28,20},{1,9},{5... | collective-permute-start | bytes 786440 | tf_op jit(solution)/shard_map/ppermute | solution.py:305
  51.1 8.9 %collective-permute-start.12 = (bf16[1,4,128,128]{3,2,1,0:T(8,128)(2,1)S(1)}, bf16[1,4,128,128]{3,2,1,0:T(8,128)(2,1)S(1)}, u32[]{:S(2)}, u32[]{:S(2)}) collective-permute-start(bf16[1,4,128,128]{3,2,1,0:T(8,128)(2,1)S(1)} %get-tuple-element.111), channel_id=1, source_target_pairs={{0,16},{4,20},{8,24},{12,28},{16,0},{20,4},{24,8},{28,12},{1,17},{... | collective-permute-start | bytes 393224 | tf_op jit(solution)/shard_map/ppermute | solution.py:305
  54.4 11.3 %collective-permute-start.11 = (bf16[2,4,128,128]{3,2,1,0:T(8,128)(2,1)S(1)}, bf16[2,4,128,128]{3,2,1,0:T(8,128)(2,1)S(1)}, u32[]{:S(2)}, u32[]{:S(2)}) collective-permute-start(bf16[2,4,128,128]{3,2,1,0:T(8,128)(2,1)S(1)} %get-tuple-element.110), channel_id=1, source_target_pairs={{0,4},{4,0},{8,12},{12,8},{16,20},{20,16},{24,28},{28,24},{1,5},{5... | collective-permute-start | bytes 786440 | tf_op jit(solution)/shard_map/ppermute | solution.py:305
  56.7 12.1 %collective-permute-start.18 = (bf16[2,4,128,128]{3,2,1,0:T(8,128)(2,1)S(1)}, bf16[2,4,128,128]{3,2,1,0:T(8,128)(2,1)S(1)}, u32[]{:S(2)}, u32[]{:S(2)}) collective-permute-start(bf16[2,4,128,128]{3,2,1,0:T(8,128)(2,1)S(1)} %get-tuple-element.124), channel_id=1, source_target_pairs={{0,8},{4,12},{8,0},{12,4},{16,24},{20,28},{24,16},{28,20},{1,9},{5... | collective-permute-start | bytes 786440 | tf_op jit(solution)/shard_map/ppermute | solution.py:305
  60.8 11.0 %collective-permute-start.16 = (bf16[2,4,128,128]{3,2,1,0:T(8,128)(2,1)S(1)}, bf16[2,4,128,128]{3,2,1,0:T(8,128)(2,1)S(1)}, u32[]{:S(2)}, u32[]{:S(2)}) collective-permute-start(bf16[2,4,128,128]{3,2,1,0:T(8,128)(2,1)S(1)} %get-tuple-element.121), channel_id=1, source_target_pairs={{0,2},{1,3},{2,0},{3,1},{4,6},{5,7},{6,4},{7,5},{8,10},{9,11},{10,... | collective-permute-start | bytes 786440 | tf_op jit(solution)/shard_map/ppermute | solution.py:303
  62.4 7.1 %collective-permute-start.17 = (bf16[1,4,128,128]{3,2,1,0:T(8,128)(2,1)S(1)}, bf16[1,4,128,128]{3,2,1,0:T(8,128)(2,1)S(1)}, u32[]{:S(2)}, u32[]{:S(2)}) collective-permute-start(bf16[1,4,128,128]{3,2,1,0:T(8,128)(2,1)S(1)} %get-tuple-element.122), channel_id=1, source_target_pairs={{0,16},{4,20},{8,24},{12,28},{16,0},{20,4},{24,8},{28,12},{1,17},{... | collective-permute-start | bytes 393224 | tf_op jit(solution)/shard_map/ppermute | solution.py:305
  66.4 9.0 %collective-permute-start.15 = (bf16[2,4,128,128]{3,2,1,0:T(8,128)(2,1)S(1)}, bf16[2,4,128,128]{3,2,1,0:T(8,128)(2,1)S(1)}, u32[]{:S(2)}, u32[]{:S(2)}) collective-permute-start(bf16[2,4,128,128]{3,2,1,0:T(8,128)(2,1)S(1)} %get-tuple-element.119), channel_id=1, source_target_pairs={{0,8},{4,12},{8,0},{12,4},{16,24},{20,28},{24,16},{28,20},{1,9},{5... | collective-permute-start | bytes 786440 | tf_op jit(solution)/shard_map/ppermute | solution.py:305
  70.3 12.8 %collective-permute-start.21 = (bf16[2,4,128,128]{3,2,1,0:T(8,128)(2,1)S(1)}, bf16[2,4,128,128]{3,2,1,0:T(8,128)(2,1)S(1)}, u32[]{:S(2)}, u32[]{:S(2)}) collective-permute-start(bf16[2,4,128,128]{3,2,1,0:T(8,128)(2,1)S(1)} %get-tuple-element.132), channel_id=1, source_target_pairs={{0,2},{1,3},{2,0},{3,1},{4,6},{5,7},{6,4},{7,5},{8,10},{9,11},{10,... | collective-permute-start | bytes 786440 | tf_op jit(solution)/shard_map/ppermute | solution.py:303
  72.7 12.3 %collective-permute-start.20 = (bf16[2,8,128,128]{3,2,1,0:T(8,128)(2,1)S(1)}, bf16[2,8,128,128]{3,2,1,0:T(8,128)(2,1)S(1)}, u32[]{:S(2)}, u32[]{:S(2)}) collective-permute-start(bf16[2,8,128,128]{3,2,1,0:T(8,128)(2,1)S(1)} %get-tuple-element.131), channel_id=1, source_target_pairs={{0,1},{1,0},{2,3},{3,2},{4,5},{5,4},{6,7},{7,6},{8,9},{9,8},{10,11... | collective-permute-start | bytes 1572872 | tf_op jit(solution)/shard_map/ppermute | solution.py:303
  72.7 9.6 %collective-permute-start.22 = (bf16[1,4,128,128]{3,2,1,0:T(8,128)(2,1)S(1)}, bf16[1,4,128,128]{3,2,1,0:T(8,128)(2,1)S(1)}, u32[]{:S(2)}, u32[]{:S(2)}) collective-permute-start(bf16[1,4,128,128]{3,2,1,0:T(8,128)(2,1)S(1)} %get-tuple-element.133), channel_id=1, source_target_pairs={{0,16},{4,20},{8,24},{12,28},{16,0},{20,4},{24,8},{28,12},{1,17},{... | collective-permute-start | bytes 393224 | tf_op jit(solution)/shard_map/ppermute | solution.py:305
  82.4 2.6 %copy-start.7 = (s32[16]{0:T(128)S(1)}, s32[16]{0:T(128)}, u32[]{:S(2)}) copy-start(s32[16]{0:T(128)} %len_ref.17) | copy-start | bytes 196
  84.0 12.2 %collective-permute-start.24 = (bf16[2,8,128,128]{3,2,1,0:T(8,128)(2,1)S(1)}, bf16[2,8,128,128]{3,2,1,0:T(8,128)(2,1)S(1)}, u32[]{:S(2)}, u32[]{:S(2)}) collective-permute-start(bf16[2,8,128,128]{3,2,1,0:T(8,128)(2,1)S(1)} %get-tuple-element.140), channel_id=1, source_target_pairs={{0,1},{1,0},{2,3},{3,2},{4,5},{5,4},{6,7},{7,6},{8,9},{9,8},{10,11... | collective-permute-start | bytes 1572872 | tf_op jit(solution)/shard_map/ppermute | solution.py:303
  84.0 9.6 %collective-permute-start.19 = (bf16[1,4,128,128]{3,2,1,0:T(8,128)(2,1)S(1)}, bf16[1,4,128,128]{3,2,1,0:T(8,128)(2,1)S(1)}, u32[]{:S(2)}, u32[]{:S(2)}) collective-permute-start(bf16[1,4,128,128]{3,2,1,0:T(8,128)(2,1)S(1)} %get-tuple-element.129), channel_id=1, source_target_pairs={{0,16},{4,20},{8,24},{12,28},{16,0},{20,4},{24,8},{28,12},{1,17},{... | collective-permute-start | bytes 393224 | tf_op jit(solution)/shard_map/ppermute | solution.py:305
  84.1 11.1 %collective-permute-start.25 = (bf16[2,4,128,128]{3,2,1,0:T(8,128)(2,1)S(1)}, bf16[2,4,128,128]{3,2,1,0:T(8,128)(2,1)S(1)}, u32[]{:S(2)}, u32[]{:S(2)}) collective-permute-start(bf16[2,4,128,128]{3,2,1,0:T(8,128)(2,1)S(1)} %get-tuple-element.144), channel_id=1, source_target_pairs={{0,2},{1,3},{2,0},{3,1},{4,6},{5,7},{6,4},{7,5},{8,10},{9,11},{10,... | collective-permute-start | bytes 786440 | tf_op jit(solution)/shard_map/ppermute | solution.py:303
  94.4 7.9 %collective-permute-start.23 = (bf16[2,4,128,128]{3,2,1,0:T(8,128)(2,1)S(1)}, bf16[2,4,128,128]{3,2,1,0:T(8,128)(2,1)S(1)}, u32[]{:S(2)}, u32[]{:S(2)}) collective-permute-start(bf16[2,4,128,128]{3,2,1,0:T(8,128)(2,1)S(1)} %get-tuple-element.138), channel_id=1, source_target_pairs={{0,2},{1,3},{2,0},{3,1},{4,6},{5,7},{6,4},{7,5},{8,10},{9,11},{10,... | collective-permute-start | bytes 786440 | tf_op jit(solution)/shard_map/ppermute | solution.py:303
  96.1 7.2 %collective-permute-start.27 = (bf16[2,8,128,128]{3,2,1,0:T(8,128)(2,1)S(1)}, bf16[2,8,128,128]{3,2,1,0:T(8,128)(2,1)S(1)}, u32[]{:S(2)}, u32[]{:S(2)}) collective-permute-start(bf16[2,8,128,128]{3,2,1,0:T(8,128)(2,1)S(1)} %get-tuple-element.150), channel_id=1, source_target_pairs={{0,1},{1,0},{2,3},{3,2},{4,5},{5,4},{6,7},{7,6},{8,9},{9,8},{10,11... | collective-permute-start | bytes 1572872 | tf_op jit(solution)/shard_map/ppermute | solution.py:303
  103.2 5.5 %collective-permute-start.26 = (bf16[2,8,128,128]{3,2,1,0:T(8,128)(2,1)S(1)}, bf16[2,8,128,128]{3,2,1,0:T(8,128)(2,1)S(1)}, u32[]{:S(2)}, u32[]{:S(2)}) collective-permute-start(bf16[2,8,128,128]{3,2,1,0:T(8,128)(2,1)S(1)} %get-tuple-element.148), channel_id=1, source_target_pairs={{0,1},{1,0},{2,3},{3,2},{4,5},{5,4},{6,7},{7,6},{8,9},{9,8},{10,11... | collective-permute-start | bytes 1572872 | tf_op jit(solution)/shard_map/ppermute | solution.py:303
  (4 other events, 5.4 us)

commit v2 on v1

--- a/solution.py
+++ b/solution.py
@@ -10,6 +10,8 @@
 
 CHUNKS = 4
 VMEM = 24 * 1024 * 1024
+VMEM_STATES = 59 * 1024 * 1024
+VMEM_CHUNK = 18 * 1024 * 1024
 F32 = jnp.float32
 B16 = jnp.bfloat16
 IN_VMEM = pl.BlockSpec(memory_space=pltpu.VMEM)
@@ -166,17 +168,15 @@
             for name in names + (["pick"] if level + 1 == self.levels else []):
                 self.index[name, level] = len(self.index)
 
-    def call(self, body, name, ins, in_specs, outs, out_specs, scratch, cost, **kw):
+    def call(self, body, name, ins, in_specs, outs, out_specs, scratch, vmem=VMEM, **kw):
         return pl.pallas_call(
             body,
             in_specs=in_specs,
             out_specs=out_specs,
             out_shape=outs,
             scratch_shapes=scratch,
-            compiler_params=pltpu.CompilerParams(vmem_limit_bytes=VMEM),
-            cost_estimate=pl.CostEstimate(
-                flops=cost[0], bytes_accessed=cost[1], transcendentals=0
-            ),
+            compiler_params=pltpu.CompilerParams(vmem_limit_bytes=vmem),
+            cost_estimate=pl.CostEstimate(flops=1, bytes_accessed=1, transcendentals=0),
             name=name,
             **kw,
         )(*ins)
@@ -198,7 +198,7 @@
             [pltpu.VMEM((n, part, d), B16)] * 4
             + [pltpu.VMEM((n * part, d), F32)] * 2
             + [pltpu.SemaphoreType.DMA((4,))],
-            (4 * n * d * d * part, 16 * n * d * part),
+            VMEM_STATES - chunk * (VMEM_CHUNK // self.chunks),
         )
 
     def grads(self, chunk, heads, mine, got, before, after):
@@ -217,7 +217,6 @@
             [pltpu.VMEM((n * part, d), F32)] * 3
             + [pltpu.VMEM((n, part, d), B16)] * 3
             + [pltpu.SemaphoreType.DMA((3,))],
-            (16 * n * d * d * part, 16 * n * d * part),
             input_output_aliases={5 + i: i for i in range(len(before))},
         )
 
@@ -273,12 +272,9 @@
             jax.ShapeDtypeStruct((2 * len(self.index),), F32),
             IN_SMEM,
             [],
-            (1000, 1000),
         )
 
     def combine(self, name, body, ins, outs, after):
-        moved = sum(math.prod(x.shape) * jnp.dtype(x.dtype).itemsize for x in (*ins, *outs))
-
         def kernel(scalar_ref, *refs):
             body(
                 lambda name, level, which: scalar_ref[2 * self.index[name, level] + which],
@@ -294,7 +290,6 @@
             tuple(outs),
             [IN_VMEM] * len(outs),
             [],
-            (moved, moved),
         )
 
     def swap(self, x, level):
@@ -431,16 +426,17 @@
     stages = [plan.stages(chunk, arrays) for chunk in range(plan.chunks)]
     count = len(stages[0])
     outs, after = (), ()
-    for wave in range(count + plan.chunks - 1):
+    order = [(0, chunk) for chunk in range(plan.chunks)]
+    for wave in range(1, count + plan.chunks - 1):
         for chunk in reversed(range(plan.chunks)):
-            stage = wave - chunk
-            if not 0 <= stage < count:
-                continue
-            if stage + 1 < count:
-                after = (stages[chunk][stage](after),)
-            else:
-                outs, token = stages[chunk][stage](outs, after)
-                after = (token,)
+            if 1 <= wave - chunk < count:
+                order.append((wave - chunk, chunk))
+    for stage, chunk in order:
+        if stage + 1 < count:
+            after = (stages[chunk][stage](after),)
+        else:
+            outs, token = stages[chunk][stage](outs, after)
+            after = (token,)
     return tuple(outs)
 
 

time: 115 us -> 117 us (1.017)
  Pallas kernels: 53.7 us -> 61.1 us
  local copies, waits for them, and re-layouts: 7.03 us -> 1.29 us
  waiting for transfers between devices: 20.4 us -> 19.2 us
    pallas_call x33, Pallas kernels: 53.7 us -> 61.1 us  [call(): pl.pallas_call(body, in_specs=in_specs, out_specs=out_specs, out_shape=ou...]
    unnamed x16 -> x18, local copies, waits for them, and re-layouts: 7.03 us -> 1.29 us
  transfers between devices with their start and end apart: 28 -> 28, of which waited for: 7 -> 8; matrix products, arithmetic and copies ran while one was open for 0% -> 0% of each run, Pallas kernels for 39% -> 42%
where the time goes in v2:
time: 117 us
  Pallas kernels  61.1 us (52%)
  starting transfers between devices  33.6 us (29%)
  waiting for transfers between devices  19.2 us (16%)
  local copies, waits for them, and re-layouts  1.29 us (1%)
  between operations  1.17 us (1%)
    pallas_call x33, Pallas kernels, call(): pl.pallas_call(body, in_specs=in_specs, out_specs=out_specs, out_shape=ou...  61.1 us
    ppermute x12, starting transfers between devices, swap(): return lax.ppermute(x, 'seq', [(i, i ^ bit) for i in range(self.seq_size)])  20.8 us
    ppermute x16, starting transfers between devices, swap(): return lax.ppermute(x, 'head', moves)  12.9 us
    ppermute x12, waiting for transfers between devices, swap(): return lax.ppermute(x, 'seq', [(i, i ^ bit) for i in range(self.seq_size)])  12 us
    ppermute x16, waiting for transfers between devices, swap(): return lax.ppermute(x, 'head', moves)  7.18 us
  transfers between devices with their start and end apart: 28, of which 8 were waited for; matrix products, arithmetic and copies ran while one was open for 0% of the time, Pallas kernels for 42%

profile of v2, /device:TPU:0, one launch (start us, length us, event | category | flops | bytes accessed | tf_op | source)
XLA Modules:
  0.0 117.1 jit_solution(16097108482749550912)
XLA Ops:
  1.3 5.6 %states.4 = (f32[2,8,128,128]{3,2,1,0:T(8,128)}, bf16[2,8,128,128]{3,2,1,0:T(8,128)(2,1)}, bf16[4,16,128,128]{3,2,1,0:T(8,128)(2,1)}) custom-call(s32[2]{0:T(128)} %pad_add_fusion.place_ref, s32[16]{0:T(128)} %len_ref.17, bf16[128,64,128]{2,1,0:T(8,128)(2,1)} %refs_0_.7, bf16[128,64,128]{2,1,0:T(8,128)(2,1)} %refs_1_.7, bf16[128,64,128]{2,1,0:T(8,128)(2,1)} %refs_2_.7, ...), custom_call_target="tpu_custom_call" | custom-call | flops 1 | bytes 1 | tf_op jit(solution)/shard_map/states/pallas_call | solution.py:172
  7.4 5.7 %states.5 = (f32[2,8,128,128]{3,2,1,0:T(8,128)}, bf16[2,8,128,128]{3,2,1,0:T(8,128)(2,1)}, bf16[4,16,128,128]{3,2,1,0:T(8,128)(2,1)}) custom-call(s32[2]{0:T(128)} %pad_add_fusion.place_ref, s32[16]{0:T(128)} %len_ref.17, bf16[128,64,128]{2,1,0:T(8,128)(2,1)} %refs_0_.7, bf16[128,64,128]{2,1,0:T(8,128)(2,1)} %refs_1_.7, bf16[128,64,128]{2,1,0:T(8,128)(2,1)} %refs_2_.7, ...), custom_call_target="tpu_custom_call" | custom-call | flops 1 | bytes 1 | tf_op jit(solution)/shard_map/states/pallas_call | solution.py:172
  13.3 1.2 %copy-done.2 = f32[2,8,128,128]{3,2,1,0:T(8,128)S(1)} copy-done((f32[2,8,128,128]{3,2,1,0:T(8,128)S(1)}, f32[2,8,128,128]{3,2,1,0:T(8,128)}, u32[]{:S(2)}) %copy-start.2) | copy-done | bytes 1048600
  14.5 5.0 %states.6 = (f32[2,8,128,128]{3,2,1,0:T(8,128)S(1)}, bf16[2,8,128,128]{3,2,1,0:T(8,128)(2,1)S(1)}, bf16[4,16,128,128]{3,2,1,0:T(8,128)(2,1)}) custom-call(s32[2]{0:T(128)S(1)} %copy-done.8, s32[16]{0:T(128)S(1)} %copy-done.7, bf16[128,64,128]{2,1,0:T(8,128)(2,1)} %refs_0_.7, bf16[128,64,128]{2,1,0:T(8,128)(2,1)} %refs_1_.7, bf16[128,64,128]{2,1,0:T(8,128)(2,1)} %refs_2_.7, ...), custom_call_target="tpu_custom_call" | custom-call | flops 1 | bytes 1 | tf_op jit(solution)/shard_map/states/pallas_call | solution.py:172
  20.0 1.9 %weights.1.scalar_ref = f32[44]{0:T(128)S(1)} custom-call(s32[2]{0:T(128)S(1)} %copy-done.8, s32[16]{0:T(128)S(1)} %copy-done.7, f32[2,8,128,128]{3,2,1,0:T(8,128)S(1)} %copy-done.1), custom_call_target="tpu_custom_call" | custom-call | flops 1 | bytes 1 | tf_op jit(solution)/shard_map/weights/pallas_call | solution.py:172
  21.9 3.6 %states.7 = (f32[2,8,128,128]{3,2,1,0:T(8,128)S(1)}, bf16[2,8,128,128]{3,2,1,0:T(8,128)(2,1)S(1)}, bf16[4,16,128,128]{3,2,1,0:T(8,128)(2,1)S(1)}) custom-call(s32[2]{0:T(128)S(1)} %copy-done.8, s32[16]{0:T(128)S(1)} %copy-done.7, bf16[128,64,128]{2,1,0:T(8,128)(2,1)S(1)} %copy-done, bf16[128,64,128]{2,1,0:T(8,128)(2,1)} %refs_1_.7, ...), custom_call_target="tpu_custom_call" | custom-call | flops 1 | bytes 1 | tf_op jit(solution)/shard_map/states/pallas_call | solution.py:172
  26.3 2.6 %collective-permute-start.2 = (bf16[2,4,128,128]{3,2,1,0:T(8,128)(2,1)S(1)}, bf16[2,4,128,128]{3,2,1,0:T(8,128)(2,1)S(1)}, u32[]{:S(2)}, u32[]{:S(2)}) collective-permute-start(bf16[2,4,128,128]{3,2,1,0:T(8,128)(2,1)S(1)} %get-tuple-element.90), channel_id=1, source_target_pairs={{0,2},{1,3},{2,0},{3,1},{4,6},{5,7},{6,4},{7,5},{8,10},{9,11},{10,... | collective-permute-start | bytes 786440 | tf_op jit(solution)/shard_map/ppermute | solution.py:298
  30.2 5.8 %collective-permute-done.2.refs_1_.refs_3_ = bf16[2,4,128,128]{3,2,1,0:T(8,128)(2,1)S(1)} collective-permute-done((bf16[2,4,128,128]{3,2,1,0:T(8,128)(2,1)S(1)}, bf16[2,4,128,128]{3,2,1,0:T(8,128)(2,1)S(1)}, u32[]{:S(2)}, u32[]{:S(2)}) %collective-permute-start.2) | collective-permute-done | bytes 262176 | tf_op jit(solution)/shard_map/ppermute | solution.py:298
  36.6 2.0 %collective-permute-start.4 = (bf16[2,4,128,128]{3,2,1,0:T(8,128)(2,1)S(1)}, bf16[2,4,128,128]{3,2,1,0:T(8,128)(2,1)S(1)}, u32[]{:S(2)}, u32[]{:S(2)}) collective-permute-start(bf16[2,4,128,128]{3,2,1,0:T(8,128)(2,1)S(1)} %get-tuple-element.94), channel_id=1, source_target_pairs={{0,4},{4,0},{8,12},{12,8},{16,20},{20,16},{24,28},{28,24},{1,5},{5... | collective-permute-start | bytes 786440 | tf_op jit(solution)/shard_map/ppermute | solution.py:300
  39.3 1.6 %collective-permute-start.10 = (bf16[2,4,128,128]{3,2,1,0:T(8,128)(2,1)S(1)}, bf16[2,4,128,128]{3,2,1,0:T(8,128)(2,1)S(1)}, u32[]{:S(2)}, u32[]{:S(2)}) collective-permute-start(bf16[2,4,128,128]{3,2,1,0:T(8,128)(2,1)S(1)} %get-tuple-element.105), channel_id=1, source_target_pairs={{0,2},{1,3},{2,0},{3,1},{4,6},{5,7},{6,4},{7,5},{8,10},{9,11},{10,... | collective-permute-start | bytes 786440 | tf_op jit(solution)/shard_map/ppermute | solution.py:298
  42.3 2.0 %collective-permute-start.9 = (bf16[2,4,128,128]{3,2,1,0:T(8,128)(2,1)S(1)}, bf16[2,4,128,128]{3,2,1,0:T(8,128)(2,1)S(1)}, u32[]{:S(2)}, u32[]{:S(2)}) collective-permute-start(bf16[2,4,128,128]{3,2,1,0:T(8,128)(2,1)S(1)} %get-tuple-element.104), channel_id=1, source_target_pairs={{0,4},{4,0},{8,12},{12,8},{16,20},{20,16},{24,28},{28,24},{1,5},{5... | collective-permute-start | bytes 786440 | tf_op jit(solution)/shard_map/ppermute | solution.py:300
  45.2 1.7 %collective-permute-start.8 = (bf16[2,4,128,128]{3,2,1,0:T(8,128)(2,1)S(1)}, bf16[2,4,128,128]{3,2,1,0:T(8,128)(2,1)S(1)}, u32[]{:S(2)}, u32[]{:S(2)}) collective-permute-start(bf16[2,4,128,128]{3,2,1,0:T(8,128)(2,1)S(1)} %get-tuple-element.103), channel_id=1, source_target_pairs={{0,8},{4,12},{8,0},{12,4},{16,24},{20,28},{24,16},{28,20},{1,9},{5... | collective-permute-start | bytes 786440 | tf_op jit(solution)/shard_map/ppermute | solution.py:300
  47.7 1.5 %collective-permute-start.7 = (bf16[2,4,128,128]{3,2,1,0:T(8,128)(2,1)S(1)}, bf16[2,4,128,128]{3,2,1,0:T(8,128)(2,1)S(1)}, u32[]{:S(2)}, u32[]{:S(2)}) collective-permute-start(bf16[2,4,128,128]{3,2,1,0:T(8,128)(2,1)S(1)} %get-tuple-element.101), channel_id=1, source_target_pairs={{0,2},{1,3},{2,0},{3,1},{4,6},{5,7},{6,4},{7,5},{8,10},{9,11},{10,... | collective-permute-start | bytes 786440 | tf_op jit(solution)/shard_map/ppermute | solution.py:298
  49.8 1.6 %collective-permute-start.14 = (bf16[2,4,128,128]{3,2,1,0:T(8,128)(2,1)S(1)}, bf16[2,4,128,128]{3,2,1,0:T(8,128)(2,1)S(1)}, u32[]{:S(2)}, u32[]{:S(2)}) collective-permute-start(bf16[2,4,128,128]{3,2,1,0:T(8,128)(2,1)S(1)} %get-tuple-element.114), channel_id=1, source_target_pairs={{0,4},{4,0},{8,12},{12,8},{16,20},{20,16},{24,28},{28,24},{1,5},{5... | collective-permute-start | bytes 786440 | tf_op jit(solution)/shard_map/ppermute | solution.py:300
  53.4 2.6 %collective-permute-start.12 = (bf16[1,4,128,128]{3,2,1,0:T(8,128)(2,1)S(1)}, bf16[1,4,128,128]{3,2,1,0:T(8,128)(2,1)S(1)}, u32[]{:S(2)}, u32[]{:S(2)}) collective-permute-start(bf16[1,4,128,128]{3,2,1,0:T(8,128)(2,1)S(1)} %get-tuple-element.111), channel_id=1, source_target_pairs={{0,16},{4,20},{8,24},{12,28},{16,0},{20,4},{24,8},{28,12},{1,17},{... | collective-permute-start | bytes 393224 | tf_op jit(solution)/shard_map/ppermute | solution.py:300
  56.6 1.5 %collective-permute-start.11 = (bf16[2,4,128,128]{3,2,1,0:T(8,128)(2,1)S(1)}, bf16[2,4,128,128]{3,2,1,0:T(8,128)(2,1)S(1)}, u32[]{:S(2)}, u32[]{:S(2)}) collective-permute-start(bf16[2,4,128,128]{3,2,1,0:T(8,128)(2,1)S(1)} %get-tuple-element.110), channel_id=1, source_target_pairs={{0,4},{4,0},{8,12},{12,8},{16,20},{20,16},{24,28},{28,24},{1,5},{5... | collective-permute-start | bytes 786440 | tf_op jit(solution)/shard_map/ppermute | solution.py:300
  58.8 1.1 collective-permute-start.18
  59.8 1.8 %collective-permute-done.13.refs_1_ = bf16[2,4,128,128]{3,2,1,0:T(8,128)(2,1)S(1)} collective-permute-done((bf16[2,4,128,128]{3,2,1,0:T(8,128)(2,1)S(1)}, bf16[2,4,128,128]{3,2,1,0:T(8,128)(2,1)S(1)}, u32[]{:S(2)}, u32[]{:S(2)}) %collective-permute-start.13) | collective-permute-done | bytes 262176 | tf_op jit(solution)/shard_map/ppermute | solution.py:300
  63.0 1.5 %collective-permute-start.16 = (bf16[2,4,128,128]{3,2,1,0:T(8,128)(2,1)S(1)}, bf16[2,4,128,128]{3,2,1,0:T(8,128)(2,1)S(1)}, u32[]{:S(2)}, u32[]{:S(2)}) collective-permute-start(bf16[2,4,128,128]{3,2,1,0:T(8,128)(2,1)S(1)} %get-tuple-element.121), channel_id=1, source_target_pairs={{0,2},{1,3},{2,0},{3,1},{4,6},{5,7},{6,4},{7,5},{8,10},{9,11},{10,... | collective-permute-start | bytes 786440 | tf_op jit(solution)/shard_map/ppermute | solution.py:298
  64.5 3.4 %collective-permute-start.17 = (bf16[1,4,128,128]{3,2,1,0:T(8,128)(2,1)S(1)}, bf16[1,4,128,128]{3,2,1,0:T(8,128)(2,1)S(1)}, u32[]{:S(2)}, u32[]{:S(2)}) collective-permute-start(bf16[1,4,128,128]{3,2,1,0:T(8,128)(2,1)S(1)} %get-tuple-element.122), channel_id=1, source_target_pairs={{0,16},{4,20},{8,24},{12,28},{16,0},{20,4},{24,8},{28,12},{1,17},{... | collective-permute-start | bytes 393224 | tf_op jit(solution)/shard_map/ppermute | solution.py:300
  68.6 1.4 %collective-permute-start.15 = (bf16[2,4,128,128]{3,2,1,0:T(8,128)(2,1)S(1)}, bf16[2,4,128,128]{3,2,1,0:T(8,128)(2,1)S(1)}, u32[]{:S(2)}, u32[]{:S(2)}) collective-permute-start(bf16[2,4,128,128]{3,2,1,0:T(8,128)(2,1)S(1)} %get-tuple-element.119), channel_id=1, source_target_pairs={{0,8},{4,12},{8,0},{12,4},{16,24},{20,28},{24,16},{28,20},{1,9},{5... | collective-permute-start | bytes 786440 | tf_op jit(solution)/shard_map/ppermute | solution.py:300
  71.7 2.2 %collective-permute-start.21 = (bf16[2,4,128,128]{3,2,1,0:T(8,128)(2,1)S(1)}, bf16[2,4,128,128]{3,2,1,0:T(8,128)(2,1)S(1)}, u32[]{:S(2)}, u32[]{:S(2)}) collective-permute-start(bf16[2,4,128,128]{3,2,1,0:T(8,128)(2,1)S(1)} %get-tuple-element.132), channel_id=1, source_target_pairs={{0,2},{1,3},{2,0},{3,1},{4,6},{5,7},{6,4},{7,5},{8,10},{9,11},{10,... | collective-permute-start | bytes 786440 | tf_op jit(solution)/shard_map/ppermute | solution.py:298
  73.9 0.8 down.10
  74.8 2.8 %collective-permute-start.22 = (bf16[1,4,128,128]{3,2,1,0:T(8,128)(2,1)S(1)}, bf16[1,4,128,128]{3,2,1,0:T(8,128)(2,1)S(1)}, u32[]{:S(2)}, u32[]{:S(2)}) collective-permute-start(bf16[1,4,128,128]{3,2,1,0:T(8,128)(2,1)S(1)} %get-tuple-element.133), channel_id=1, source_target_pairs={{0,16},{4,20},{8,24},{12,28},{16,0},{20,4},{24,8},{28,12},{1,17},{... | collective-permute-start | bytes 393224 | tf_op jit(solution)/shard_map/ppermute | solution.py:300
  78.3 6.2 %collective-permute-done.22.refs_1_ = bf16[1,4,128,128]{3,2,1,0:T(8,128)(2,1)S(1)} collective-permute-done((bf16[1,4,128,128]{3,2,1,0:T(8,128)(2,1)S(1)}, bf16[1,4,128,128]{3,2,1,0:T(8,128)(2,1)S(1)}, u32[]{:S(2)}, u32[]{:S(2)}) %collective-permute-start.22) | collective-permute-done | bytes 131104 | tf_op jit(solution)/shard_map/ppermute | solution.py:300
  85.3 0.8 down.12
  87.0 5.4 %grads.4 = (bf16[128,64,128]{2,1,0:T(8,128)(2,1)}, bf16[128,64,128]{2,1,0:T(8,128)(2,1)}, bf16[128,64,128]{2,1,0:T(8,128)(2,1)}, f32[8,128]{1,0:T(8,128)S(1)}) custom-call(s32[2]{0:T(128)S(1)} %copy-done.8, s32[16]{0:T(128)S(1)} %copy-done.7, bf16[4,16,128,128]{3,2,1,0:T(8,128)(2,1)S(1)} %copy-done.6, ...), custom_call_target="tpu_custom_call" | custom-call | flops 1 | bytes 1 | tf_op jit(solution)/shard_map/grads/pallas_call | solution.py:172
  92.4 3.4 %collective-permute-done.19.refs_1_ = bf16[1,4,128,128]{3,2,1,0:T(8,128)(2,1)S(1)} collective-permute-done((bf16[1,4,128,128]{3,2,1,0:T(8,128)(2,1)S(1)}, bf16[1,4,128,128]{3,2,1,0:T(8,128)(2,1)S(1)}, u32[]{:S(2)}, u32[]{:S(2)}) %collective-permute-start.19) | collective-permute-done | bytes 131104 | tf_op jit(solution)/shard_map/ppermute | solution.py:300
  97.3 0.8 down.14
  98.2 5.6 %grads.5 = (bf16[128,64,128]{2,1,0:T(8,128)(2,1)}, bf16[128,64,128]{2,1,0:T(8,128)(2,1)}, bf16[128,64,128]{2,1,0:T(8,128)(2,1)}, f32[8,128]{1,0:T(8,128)S(1)}) custom-call(s32[2]{0:T(128)S(1)} %copy-done.8, s32[16]{0:T(128)S(1)} %copy-done.7, bf16[4,16,128,128]{3,2,1,0:T(8,128)(2,1)S(1)} %copy-done.5, ...), custom_call_target="tpu_custom_call", output_to_operand_aliasing={{0}: (5, {}), {1}: (6, {}), {2}: (7, {})} | custom-call | flops 1 | bytes 1 | tf_op jit(solution)/shard_map/grads/pallas_call | solution.py:172
  105.5 5.4 %grads.6 = (bf16[128,64,128]{2,1,0:T(8,128)(2,1)}, bf16[128,64,128]{2,1,0:T(8,128)(2,1)}, bf16[128,64,128]{2,1,0:T(8,128)(2,1)}, f32[8,128]{1,0:T(8,128)S(1)}) custom-call(s32[2]{0:T(128)S(1)} %copy-done.8, s32[16]{0:T(128)S(1)} %copy-done.7, bf16[4,16,128,128]{3,2,1,0:T(8,128)(2,1)S(1)} %copy-done.4, ...), custom_call_target="tpu_custom_call", output_to_operand_aliasing={{0}: (5, {}), {1}: (6, {}), {2}: (7, {})} | custom-call | flops 1 | bytes 1 | tf_op jit(solution)/shard_map/grads/pallas_call | solution.py:172
  110.9 6.0 %grads.7 = (bf16[128,64,128]{2,1,0:T(8,128)(2,1)}, bf16[128,64,128]{2,1,0:T(8,128)(2,1)}, bf16[128,64,128]{2,1,0:T(8,128)(2,1)}, f32[8,128]{1,0:T(8,128)}) custom-call(s32[2]{0:T(128)S(1)} %copy-done.8, s32[16]{0:T(128)S(1)} %copy-done.7, ...), custom_call_target="tpu_custom_call", output_to_operand_aliasing={{0}: (5, {}), {1}: (6, {}), {2}: (7, {})} | custom-call | flops 1 | bytes 1 | tf_op jit(solution)/shard_map/grads/pallas_call | solution.py:172
  (76 shorter events, 21.4 us)
Async XLA Ops:
  6.9 18.7 %collective-permute-start.1 = (bf16[2,8,128,128]{3,2,1,0:T(8,128)(2,1)}, bf16[2,8,128,128]{3,2,1,0:T(8,128)(2,1)S(1)}, u32[]{:S(2)}, u32[]{:S(2)}) collective-permute-start(bf16[2,8,128,128]{3,2,1,0:T(8,128)(2,1)} %get-tuple-element.88), channel_id=1, source_target_pairs={{0,1},{1,0},{2,3},{3,2},{4,5},{5,4},{6,7},{7,6},{8,9},{9,8},{10,11... | collective-permute-start | bytes 1572872 | tf_op jit(solution)/shard_map/ppermute | solution.py:298
  7.4 5.8 %copy-start.7 = (s32[16]{0:T(128)S(1)}, s32[16]{0:T(128)}, u32[]{:S(2)}) copy-start(s32[16]{0:T(128)} %len_ref.17) | copy-start | bytes 196
  7.4 5.8 %copy-start.8 = (s32[2]{0:T(128)S(1)}, s32[2]{0:T(128)}, u32[]{:S(2)}) copy-start(s32[2]{0:T(128)} %pad_add_fusion.place_ref) | copy-start | bytes 28
  13.2 15.9 %collective-permute-start.3 = (bf16[2,8,128,128]{3,2,1,0:T(8,128)(2,1)}, bf16[2,8,128,128]{3,2,1,0:T(8,128)(2,1)S(1)}, u32[]{:S(2)}, u32[]{:S(2)}) collective-permute-start(bf16[2,8,128,128]{3,2,1,0:T(8,128)(2,1)} %get-tuple-element.91), channel_id=1, source_target_pairs={{0,1},{1,0},{2,3},{3,2},{4,5},{5,4},{6,7},{7,6},{8,9},{9,8},{10,11... | collective-permute-start | bytes 1572872 | tf_op jit(solution)/shard_map/ppermute | solution.py:298
  14.5 5.5 %copy-start.1 = (f32[2,8,128,128]{3,2,1,0:T(8,128)S(1)}, f32[2,8,128,128]{3,2,1,0:T(8,128)}, u32[]{:S(2)}) copy-start(f32[2,8,128,128]{3,2,1,0:T(8,128)} %get-tuple-element.82.refs_4_.refs_0_.refs_2_) | copy-start | bytes 3145732
  14.5 7.4 %copy-start = (bf16[128,64,128]{2,1,0:T(8,128)(2,1)S(1)}, bf16[128,64,128]{2,1,0:T(8,128)(2,1)}, u32[]{:S(2)}) copy-start(bf16[128,64,128]{2,1,0:T(8,128)(2,1)} %refs_0_.7) | copy-start | bytes 6291460
  19.5 19.2 %collective-permute-start.6 = (bf16[2,8,128,128]{3,2,1,0:T(8,128)(2,1)S(1)}, bf16[2,8,128,128]{3,2,1,0:T(8,128)(2,1)S(1)}, u32[]{:S(2)}, u32[]{:S(2)}) collective-permute-start(bf16[2,8,128,128]{3,2,1,0:T(8,128)(2,1)S(1)} %get-tuple-element.96), channel_id=1, source_target_pairs={{0,1},{1,0},{2,3},{3,2},{4,5},{5,4},{6,7},{7,6},{8,9},{9,8},{10,11... | collective-permute-start | bytes 1572872 | tf_op jit(solution)/shard_map/ppermute | solution.py:298
  26.3 9.7 %collective-permute-start.2 = (bf16[2,4,128,128]{3,2,1,0:T(8,128)(2,1)S(1)}, bf16[2,4,128,128]{3,2,1,0:T(8,128)(2,1)S(1)}, u32[]{:S(2)}, u32[]{:S(2)}) collective-permute-start(bf16[2,4,128,128]{3,2,1,0:T(8,128)(2,1)S(1)} %get-tuple-element.90), channel_id=1, source_target_pairs={{0,2},{1,3},{2,0},{3,1},{4,6},{5,7},{6,4},{7,5},{8,10},{9,11},{10,... | collective-permute-start | bytes 786440 | tf_op jit(solution)/shard_map/ppermute | solution.py:298
  28.9 18.1 %collective-permute-start = (bf16[2,8,128,128]{3,2,1,0:T(8,128)(2,1)S(1)}, bf16[2,8,128,128]{3,2,1,0:T(8,128)(2,1)S(1)}, u32[]{:S(2)}, u32[]{:S(2)}) collective-permute-start(bf16[2,8,128,128]{3,2,1,0:T(8,128)(2,1)S(1)} %get-tuple-element.87), channel_id=1, source_target_pairs={{0,1},{1,0},{2,3},{3,2},{4,5},{5,4},{6,7},{7,6},{8,9},{9,8},{10,11... | collective-permute-start | bytes 1572872 | tf_op jit(solution)/shard_map/ppermute | solution.py:298
  29.7 11.9 %collective-permute-start.5 = (bf16[2,4,128,128]{3,2,1,0:T(8,128)(2,1)S(1)}, bf16[2,4,128,128]{3,2,1,0:T(8,128)(2,1)S(1)}, u32[]{:S(2)}, u32[]{:S(2)}) collective-permute-start(bf16[2,4,128,128]{3,2,1,0:T(8,128)(2,1)S(1)} %get-tuple-element.95), channel_id=1, source_target_pairs={{0,2},{1,3},{2,0},{3,1},{4,6},{5,7},{6,4},{7,5},{8,10},{9,11},{10,... | collective-permute-start | bytes 786440 | tf_op jit(solution)/shard_map/ppermute | solution.py:298
  36.6 7.9 %collective-permute-start.4 = (bf16[2,4,128,128]{3,2,1,0:T(8,128)(2,1)S(1)}, bf16[2,4,128,128]{3,2,1,0:T(8,128)(2,1)S(1)}, u32[]{:S(2)}, u32[]{:S(2)}) collective-permute-start(bf16[2,4,128,128]{3,2,1,0:T(8,128)(2,1)S(1)} %get-tuple-element.94), channel_id=1, source_target_pairs={{0,4},{4,0},{8,12},{12,8},{16,20},{20,16},{24,28},{28,24},{1,5},{5... | collective-permute-start | bytes 786440 | tf_op jit(solution)/shard_map/ppermute | solution.py:300
  39.3 9.9 %collective-permute-start.10 = (bf16[2,4,128,128]{3,2,1,0:T(8,128)(2,1)S(1)}, bf16[2,4,128,128]{3,2,1,0:T(8,128)(2,1)S(1)}, u32[]{:S(2)}, u32[]{:S(2)}) collective-permute-start(bf16[2,4,128,128]{3,2,1,0:T(8,128)(2,1)S(1)} %get-tuple-element.105), channel_id=1, source_target_pairs={{0,2},{1,3},{2,0},{3,1},{4,6},{5,7},{6,4},{7,5},{8,10},{9,11},{10,... | collective-permute-start | bytes 786440 | tf_op jit(solution)/shard_map/ppermute | solution.py:298
  42.3 9.1 %collective-permute-start.9 = (bf16[2,4,128,128]{3,2,1,0:T(8,128)(2,1)S(1)}, bf16[2,4,128,128]{3,2,1,0:T(8,128)(2,1)S(1)}, u32[]{:S(2)}, u32[]{:S(2)}) collective-permute-start(bf16[2,4,128,128]{3,2,1,0:T(8,128)(2,1)S(1)} %get-tuple-element.104), channel_id=1, source_target_pairs={{0,4},{4,0},{8,12},{12,8},{16,20},{20,16},{24,28},{28,24},{1,5},{5... | collective-permute-start | bytes 786440 | tf_op jit(solution)/shard_map/ppermute | solution.py:300
  45.2 7.5 %collective-permute-start.8 = (bf16[2,4,128,128]{3,2,1,0:T(8,128)(2,1)S(1)}, bf16[2,4,128,128]{3,2,1,0:T(8,128)(2,1)S(1)}, u32[]{:S(2)}, u32[]{:S(2)}) collective-permute-start(bf16[2,4,128,128]{3,2,1,0:T(8,128)(2,1)S(1)} %get-tuple-element.103), channel_id=1, source_target_pairs={{0,8},{4,12},{8,0},{12,4},{16,24},{20,28},{24,16},{28,20},{1,9},{5... | collective-permute-start | bytes 786440 | tf_op jit(solution)/shard_map/ppermute | solution.py:300
  47.7 8.3 %collective-permute-start.7 = (bf16[2,4,128,128]{3,2,1,0:T(8,128)(2,1)S(1)}, bf16[2,4,128,128]{3,2,1,0:T(8,128)(2,1)S(1)}, u32[]{:S(2)}, u32[]{:S(2)}) collective-permute-start(bf16[2,4,128,128]{3,2,1,0:T(8,128)(2,1)S(1)} %get-tuple-element.101), channel_id=1, source_target_pairs={{0,2},{1,3},{2,0},{3,1},{4,6},{5,7},{6,4},{7,5},{8,10},{9,11},{10,... | collective-permute-start | bytes 786440 | tf_op jit(solution)/shard_map/ppermute | solution.py:298
  49.8 8.3 %collective-permute-start.14 = (bf16[2,4,128,128]{3,2,1,0:T(8,128)(2,1)S(1)}, bf16[2,4,128,128]{3,2,1,0:T(8,128)(2,1)S(1)}, u32[]{:S(2)}, u32[]{:S(2)}) collective-permute-start(bf16[2,4,128,128]{3,2,1,0:T(8,128)(2,1)S(1)} %get-tuple-element.114), channel_id=1, source_target_pairs={{0,4},{4,0},{8,12},{12,8},{16,20},{20,16},{24,28},{28,24},{1,5},{5... | collective-permute-start | bytes 786440 | tf_op jit(solution)/shard_map/ppermute | solution.py:300
  52.0 9.6 %collective-permute-start.13 = (bf16[2,4,128,128]{3,2,1,0:T(8,128)(2,1)S(1)}, bf16[2,4,128,128]{3,2,1,0:T(8,128)(2,1)S(1)}, u32[]{:S(2)}, u32[]{:S(2)}) collective-permute-start(bf16[2,4,128,128]{3,2,1,0:T(8,128)(2,1)S(1)} %get-tuple-element.113), channel_id=1, source_target_pairs={{0,8},{4,12},{8,0},{12,4},{16,24},{20,28},{24,16},{28,20},{1,9},{5... | collective-permute-start | bytes 786440 | tf_op jit(solution)/shard_map/ppermute | solution.py:300
  53.4 8.9 %collective-permute-start.12 = (bf16[1,4,128,128]{3,2,1,0:T(8,128)(2,1)S(1)}, bf16[1,4,128,128]{3,2,1,0:T(8,128)(2,1)S(1)}, u32[]{:S(2)}, u32[]{:S(2)}) collective-permute-start(bf16[1,4,128,128]{3,2,1,0:T(8,128)(2,1)S(1)} %get-tuple-element.111), channel_id=1, source_target_pairs={{0,16},{4,20},{8,24},{12,28},{16,0},{20,4},{24,8},{28,12},{1,17},{... | collective-permute-start | bytes 393224 | tf_op jit(solution)/shard_map/ppermute | solution.py:300
  56.6 11.3 %collective-permute-start.11 = (bf16[2,4,128,128]{3,2,1,0:T(8,128)(2,1)S(1)}, bf16[2,4,128,128]{3,2,1,0:T(8,128)(2,1)S(1)}, u32[]{:S(2)}, u32[]{:S(2)}) collective-permute-start(bf16[2,4,128,128]{3,2,1,0:T(8,128)(2,1)S(1)} %get-tuple-element.110), channel_id=1, source_target_pairs={{0,4},{4,0},{8,12},{12,8},{16,20},{20,16},{24,28},{28,24},{1,5},{5... | collective-permute-start | bytes 786440 | tf_op jit(solution)/shard_map/ppermute | solution.py:300
  58.8 11.2 %collective-permute-start.18 = (bf16[2,4,128,128]{3,2,1,0:T(8,128)(2,1)S(1)}, bf16[2,4,128,128]{3,2,1,0:T(8,128)(2,1)S(1)}, u32[]{:S(2)}, u32[]{:S(2)}) collective-permute-start(bf16[2,4,128,128]{3,2,1,0:T(8,128)(2,1)S(1)} %get-tuple-element.124), channel_id=1, source_target_pairs={{0,8},{4,12},{8,0},{12,4},{16,24},{20,28},{24,16},{28,20},{1,9},{5... | collective-permute-start | bytes 786440 | tf_op jit(solution)/shard_map/ppermute | solution.py:300
  63.0 10.8 %collective-permute-start.16 = (bf16[2,4,128,128]{3,2,1,0:T(8,128)(2,1)S(1)}, bf16[2,4,128,128]{3,2,1,0:T(8,128)(2,1)S(1)}, u32[]{:S(2)}, u32[]{:S(2)}) collective-permute-start(bf16[2,4,128,128]{3,2,1,0:T(8,128)(2,1)S(1)} %get-tuple-element.121), channel_id=1, source_target_pairs={{0,2},{1,3},{2,0},{3,1},{4,6},{5,7},{6,4},{7,5},{8,10},{9,11},{10,... | collective-permute-start | bytes 786440 | tf_op jit(solution)/shard_map/ppermute | solution.py:298
  64.5 6.4 %collective-permute-start.17 = (bf16[1,4,128,128]{3,2,1,0:T(8,128)(2,1)S(1)}, bf16[1,4,128,128]{3,2,1,0:T(8,128)(2,1)S(1)}, u32[]{:S(2)}, u32[]{:S(2)}) collective-permute-start(bf16[1,4,128,128]{3,2,1,0:T(8,128)(2,1)S(1)} %get-tuple-element.122), channel_id=1, source_target_pairs={{0,16},{4,20},{8,24},{12,28},{16,0},{20,4},{24,8},{28,12},{1,17},{... | collective-permute-start | bytes 393224 | tf_op jit(solution)/shard_map/ppermute | solution.py:300
  68.6 9.0 %collective-permute-start.15 = (bf16[2,4,128,128]{3,2,1,0:T(8,128)(2,1)S(1)}, bf16[2,4,128,128]{3,2,1,0:T(8,128)(2,1)S(1)}, u32[]{:S(2)}, u32[]{:S(2)}) collective-permute-start(bf16[2,4,128,128]{3,2,1,0:T(8,128)(2,1)S(1)} %get-tuple-element.119), channel_id=1, source_target_pairs={{0,8},{4,12},{8,0},{12,4},{16,24},{20,28},{24,16},{28,20},{1,9},{5... | collective-permute-start | bytes 786440 | tf_op jit(solution)/shard_map/ppermute | solution.py:300
  71.7 13.5 %collective-permute-start.21 = (bf16[2,4,128,128]{3,2,1,0:T(8,128)(2,1)S(1)}, bf16[2,4,128,128]{3,2,1,0:T(8,128)(2,1)S(1)}, u32[]{:S(2)}, u32[]{:S(2)}) collective-permute-start(bf16[2,4,128,128]{3,2,1,0:T(8,128)(2,1)S(1)} %get-tuple-element.132), channel_id=1, source_target_pairs={{0,2},{1,3},{2,0},{3,1},{4,6},{5,7},{6,4},{7,5},{8,10},{9,11},{10,... | collective-permute-start | bytes 786440 | tf_op jit(solution)/shard_map/ppermute | solution.py:298
  74.7 12.3 %collective-permute-start.20 = (bf16[2,8,128,128]{3,2,1,0:T(8,128)(2,1)S(1)}, bf16[2,8,128,128]{3,2,1,0:T(8,128)(2,1)S(1)}, u32[]{:S(2)}, u32[]{:S(2)}) collective-permute-start(bf16[2,8,128,128]{3,2,1,0:T(8,128)(2,1)S(1)} %get-tuple-element.131), channel_id=1, source_target_pairs={{0,1},{1,0},{2,3},{3,2},{4,5},{5,4},{6,7},{7,6},{8,9},{9,8},{10,11... | collective-permute-start | bytes 1572872 | tf_op jit(solution)/shard_map/ppermute | solution.py:298
  74.8 9.7 %collective-permute-start.22 = (bf16[1,4,128,128]{3,2,1,0:T(8,128)(2,1)S(1)}, bf16[1,4,128,128]{3,2,1,0:T(8,128)(2,1)S(1)}, u32[]{:S(2)}, u32[]{:S(2)}) collective-permute-start(bf16[1,4,128,128]{3,2,1,0:T(8,128)(2,1)S(1)} %get-tuple-element.133), channel_id=1, source_target_pairs={{0,16},{4,20},{8,24},{12,28},{16,0},{20,4},{24,8},{28,12},{1,17},{... | collective-permute-start | bytes 393224 | tf_op jit(solution)/shard_map/ppermute | solution.py:300
  86.1 12.1 %collective-permute-start.24 = (bf16[2,8,128,128]{3,2,1,0:T(8,128)(2,1)S(1)}, bf16[2,8,128,128]{3,2,1,0:T(8,128)(2,1)S(1)}, u32[]{:S(2)}, u32[]{:S(2)}) collective-permute-start(bf16[2,8,128,128]{3,2,1,0:T(8,128)(2,1)S(1)} %get-tuple-element.140), channel_id=1, source_target_pairs={{0,1},{1,0},{2,3},{3,2},{4,5},{5,4},{6,7},{7,6},{8,9},{9,8},{10,11... | collective-permute-start | bytes 1572872 | tf_op jit(solution)/shard_map/ppermute | solution.py:298
  86.2 9.6 %collective-permute-start.19 = (bf16[1,4,128,128]{3,2,1,0:T(8,128)(2,1)S(1)}, bf16[1,4,128,128]{3,2,1,0:T(8,128)(2,1)S(1)}, u32[]{:S(2)}, u32[]{:S(2)}) collective-permute-start(bf16[1,4,128,128]{3,2,1,0:T(8,128)(2,1)S(1)} %get-tuple-element.129), channel_id=1, source_target_pairs={{0,16},{4,20},{8,24},{12,28},{16,0},{20,4},{24,8},{28,12},{1,17},{... | collective-permute-start | bytes 393224 | tf_op jit(solution)/shard_map/ppermute | solution.py:300
  86.3 11.0 %collective-permute-start.25 = (bf16[2,4,128,128]{3,2,1,0:T(8,128)(2,1)S(1)}, bf16[2,4,128,128]{3,2,1,0:T(8,128)(2,1)S(1)}, u32[]{:S(2)}, u32[]{:S(2)}) collective-permute-start(bf16[2,4,128,128]{3,2,1,0:T(8,128)(2,1)S(1)} %get-tuple-element.144), channel_id=1, source_target_pairs={{0,2},{1,3},{2,0},{3,1},{4,6},{5,7},{6,4},{7,5},{8,10},{9,11},{10,... | collective-permute-start | bytes 786440 | tf_op jit(solution)/shard_map/ppermute | solution.py:298
  96.5 7.9 %collective-permute-start.23 = (bf16[2,4,128,128]{3,2,1,0:T(8,128)(2,1)S(1)}, bf16[2,4,128,128]{3,2,1,0:T(8,128)(2,1)S(1)}, u32[]{:S(2)}, u32[]{:S(2)}) collective-permute-start(bf16[2,4,128,128]{3,2,1,0:T(8,128)(2,1)S(1)} %get-tuple-element.138), channel_id=1, source_target_pairs={{0,2},{1,3},{2,0},{3,1},{4,6},{5,7},{6,4},{7,5},{8,10},{9,11},{10,... | collective-permute-start | bytes 786440 | tf_op jit(solution)/shard_map/ppermute | solution.py:298
  98.1 7.3 %collective-permute-start.27 = (bf16[2,8,128,128]{3,2,1,0:T(8,128)(2,1)S(1)}, bf16[2,8,128,128]{3,2,1,0:T(8,128)(2,1)S(1)}, u32[]{:S(2)}, u32[]{:S(2)}) collective-permute-start(bf16[2,8,128,128]{3,2,1,0:T(8,128)(2,1)S(1)} %get-tuple-element.150), channel_id=1, source_target_pairs={{0,1},{1,0},{2,3},{3,2},{4,5},{5,4},{6,7},{7,6},{8,9},{9,8},{10,11... | collective-permute-start | bytes 1572872 | tf_op jit(solution)/shard_map/ppermute | solution.py:298
  105.3 5.6 %collective-permute-start.26 = (bf16[2,8,128,128]{3,2,1,0:T(8,128)(2,1)S(1)}, bf16[2,8,128,128]{3,2,1,0:T(8,128)(2,1)S(1)}, u32[]{:S(2)}, u32[]{:S(2)}) collective-permute-start(bf16[2,8,128,128]{3,2,1,0:T(8,128)(2,1)S(1)} %get-tuple-element.148), channel_id=1, source_target_pairs={{0,1},{1,0},{2,3},{3,2},{4,5},{5,4},{6,7},{7,6},{8,9},{9,8},{10,11... | collective-permute-start | bytes 1572872 | tf_op jit(solution)/shard_map/ppermute | solution.py:298
  (5 other events, 11.2 us)

commit v3 on v2

--- a/solution.py
+++ b/solution.py
@@ -10,8 +10,8 @@
 
 CHUNKS = 4
 VMEM = 24 * 1024 * 1024
-VMEM_STATES = 59 * 1024 * 1024
-VMEM_CHUNK = 18 * 1024 * 1024
+VMEM_FIRST = 56 * 1024 * 1024
+VMEM_NEXT = 46 * 1024 * 1024
 F32 = jnp.float32
 B16 = jnp.bfloat16
 IN_VMEM = pl.BlockSpec(memory_space=pltpu.VMEM)
@@ -50,40 +50,53 @@
     )
 
 
-def states_kernel(chunk, place_ref, len_ref, *refs):
-    tokens, (keep_ref, send_ref, head_ref) = refs[:4], refs[-10:-7]
-    slabs, wide, sems = refs[-7:-3], refs[-3:-1], refs[-1]
+def states_kernel(chunks, weights, place_ref, len_ref, *refs):
+    count = len(chunks)
+    tokens, refs = refs[:4], refs[len(refs) - 2 * count - (weights is not None) - 5 :]
+    if weights is not None:
+        weights(place_ref, len_ref, refs[0])
+        refs = refs[1:]
+    keeps, head_refs, send_ref = refs[:count], refs[count : 2 * count], refs[2 * count]
+    slab, wide, sems = refs[2 * count + 1], refs[-3:-1], refs[-1]
     n, _, d = tokens[0].shape
-    heads = slabs[0].shape[1]
+    heads = slab.shape[3]
     half = heads // 2
     copies = [
-        pltpu.make_async_copy(
-            ref.at[:, pl.ds(chunk * heads, heads), :], slab, sems.at[i]
-        )
-        for i, (ref, slab) in enumerate(zip(tokens, slabs))
+        [
+            pltpu.make_async_copy(
+                ref.at[:, pl.ds(chunk * heads, heads), :], slab.at[j, i], sems.at[j, i]
+            )
+            for i, ref in enumerate(tokens)
+        ]
+        for j, chunk in enumerate(chunks)
     ]
-    for copy in copies:
-        copy.start()
+    for some in copies:
+        for copy in some:
+            copy.start()
     first = place_ref[0] * n
     flip = place_ref[1]
     start, stop = _edges(len_ref, first, first + n - 1)
     row = lax.broadcasted_iota(jnp.int32, (n, d), 0) + first
-    weights = (
-        jnp.where(row < stop, F32(1.0), F32(0.0)).astype(B16),
-        jnp.where(row >= start, F32(1.0), F32(0.0)).astype(B16),
-    )
-    for i, (copy, slab) in enumerate(zip(copies, slabs)):
-        scr = wide[i % 2]
-        copy.wait()
-        scr[...] = slab[...].astype(F32).reshape(n * heads, d)
-        for h in range(heads):
-            head_ref[i, h] = scr[pl.ds(h, n, stride=heads), :].astype(B16)
-    for r in range(heads):
-        h = r ^ flip
-        out, o = (keep_ref, r) if r < half else (send_ref, r - half)
-        query, key, value, grad = (head_ref[i, h] for i in range(4))
-        out[0, o] = _dot(key * weights[1], value, 0, 0).astype(out.dtype)
-        out[1, o] = _dot(query, grad * weights[0], 0, 0).astype(out.dtype)
+    lead = jnp.where(row < stop, F32(1.0), F32(0.0)).astype(B16)
+    last = jnp.where(row >= start, F32(1.0), F32(0.0)).astype(B16)
+    for j in range(count):
+        for i in range(4):
+            scr = wide[i % 2]
+            copies[j][i].wait()
+            scr[...] = slab[j, i].astype(F32).reshape(n * heads, d)
+            for h in range(heads):
+                head_refs[j][i, h] = scr[pl.ds(h, n, stride=heads), :].astype(B16)
+        for r in range(heads):
+            h = r ^ flip
+            query, key, value, grad = (head_refs[j][i, h] for i in range(4))
+            state_a = _dot(key * last, value, 0, 0)
+            state_b = _dot(query, grad * lead, 0, 0)
+            if r < half:
+                keeps[j][0, r] = state_a
+                keeps[j][1, r] = state_b
+            else:
+                send_ref[j, 0, r - half] = state_a.astype(B16)
+                send_ref[j, 1, r - half] = state_b.astype(B16)
 
 
 def grads_kernel(chunk, scaling, place_ref, len_ref, head_ref, mine_ref, got_ref, *refs):
@@ -181,25 +194,32 @@
             **kw,
         )(*ins)
 
-    def states(self, chunk, arrays, after):
-        n, d, part = self.n, self.d, self.part
+    def states(self, chunks, arrays, after):
+        n, d, part, count = self.n, self.d, self.part, len(chunks)
         shape = (2, part // 2, d, d)
-        return self.call(
-            functools.partial(states_kernel, chunk),
+        first = chunks[0] == 0
+        outs = [jax.ShapeDtypeStruct(shape, F32)] * count
+        outs += [jax.ShapeDtypeStruct((4, part, n, d), B16)] * count
+        outs += [jax.ShapeDtypeStruct((count, *shape), B16)]
+        specs = [IN_VMEM] * len(outs)
+        if first:
+            outs = [jax.ShapeDtypeStruct((2 * len(self.index),), F32)] + outs
+            specs = [IN_SMEM] + specs
+        got = self.call(
+            functools.partial(states_kernel, chunks, self.weights if first else None),
             "states",
             [self.place, self.lengths, *arrays, *after],
             [IN_SMEM] * 2 + [IN_HBM] * 4 + [ANYWHERE] * len(after),
-            (
-                jax.ShapeDtypeStruct(shape, F32),
-                jax.ShapeDtypeStruct(shape, B16),
-                jax.ShapeDtypeStruct((4, part, n, d), B16),
-            ),
-            [IN_VMEM] * 3,
-            [pltpu.VMEM((n, part, d), B16)] * 4
+            tuple(outs),
+            specs,
+            [pltpu.VMEM((count, 4, n, part, d), B16)]
             + [pltpu.VMEM((n * part, d), F32)] * 2
-            + [pltpu.SemaphoreType.DMA((4,))],
-            VMEM_STATES - chunk * (VMEM_CHUNK // self.chunks),
-        )
+            + [pltpu.SemaphoreType.DMA((count, 4))],
+            VMEM_FIRST if first else VMEM_NEXT,
+        )
+        if first:
+            self.scalars, *got = got
+        return got[:count], got[count : 2 * count], self.swap(got[-1], 0)
 
     def grads(self, chunk, heads, mine, got, before, after):
         n, d, part = self.n, self.d, self.part
@@ -220,59 +240,47 @@
             input_output_aliases={5 + i: i for i in range(len(before))},
         )
 
-    def weights(self, after):
+    def weights(self, place_ref, len_ref, out):
         n, bits = self.n, self.head_bits
-
-        def kernel(place_ref, len_ref, *refs):
-            out = refs[-1]
-            device = place_ref[0]
-            begin = ((device >> bits) << bits) * n
-            end = begin + (n << bits)
-            pairs = []
-            for level in range(self.levels):
-                group = (device >> (level + 1)) << (level + 1)
-                low, high = group * n, (group + (2 << level)) * n
-                middle = (group + (1 << level)) * n
-                pairs += [(middle - 1, high - 1), (low, middle)]
-                if level < bits:
-                    pairs += [(middle - 1, middle)]
-                else:
-                    pairs += [(middle - 1, begin), (end - 1, middle)]
-            same = _same(len_ref, pairs)
-            one, zero = F32(1.0), F32(0.0)
-
-            def put(name, level, a, b):
-                out[2 * self.index[name, level]] = a
-                out[2 * self.index[name, level] + 1] = b
-
-            for level in range(self.levels):
-                hi = (device >> level) & 1 == 1
-                lasts, firsts = same[0], same[1]
-                put("up_own", level, jnp.where(hi, one, lasts), jnp.where(hi, firsts, one))
-                put("up_got", level, jnp.where(hi, lasts, one), jnp.where(hi, one, firsts))
-                if level < bits:
-                    join = same[2]
-                    same = same[3:]
-                    put("m_in", level, jnp.where(hi, firsts, one), jnp.where(hi, one, lasts))
-                    put("m_got", level, jnp.where(hi, join, zero), jnp.where(hi, zero, join))
-                    put("s_in", level, jnp.where(hi, one, firsts), jnp.where(hi, lasts, one))
-                    put("s_own", level, jnp.where(hi, zero, join), jnp.where(hi, join, zero))
-                else:
-                    ahead, behind = same[2], same[3]
-                    same = same[4:]
-                    put("unit", level, jnp.where(hi, ahead, zero), jnp.where(hi, zero, behind))
-                if level + 1 == self.levels:
-                    put("pick", level, jnp.where(hi, zero, one), jnp.where(hi, one, zero))
-
-        self.scalars = self.call(
-            kernel,
-            "weights",
-            [self.place, self.lengths, *after],
-            [IN_SMEM] * 2 + [ANYWHERE] * len(after),
-            jax.ShapeDtypeStruct((2 * len(self.index),), F32),
-            IN_SMEM,
-            [],
-        )
+        device = place_ref[0]
+        begin = ((device >> bits) << bits) * n
+        end = begin + (n << bits)
+        pairs = []
+        for level in range(self.levels):
+            group = (device >> (level + 1)) << (level + 1)
+            low, high = group * n, (group + (2 << level)) * n
+            middle = (group + (1 << level)) * n
+            pairs += [(middle - 1, high - 1), (low, middle)]
+            if level < bits:
+                pairs += [(middle - 1, middle)]
+            else:
+                pairs += [(middle - 1, begin), (end - 1, middle)]
+        same = _same(len_ref, pairs)
+        one, zero = F32(1.0), F32(0.0)
+
+        def put(name, level, a, b):
+            out[2 * self.index[name, level]] = a
+            out[2 * self.index[name, level] + 1] = b
+
+        for level in range(self.levels):
+            hi = (device >> level) & 1 == 1
+            lasts, firsts = same[0], same[1]
+            put("up_own", level, jnp.where(hi, one, lasts), jnp.where(hi, firsts, one))
+            put("up_got", level, jnp.where(hi, lasts, one), jnp.where(hi, one, firsts))
+            if level < bits:
+                join = same[2]
+                same = same[3:]
+                put("m_in", level, jnp.where(hi, firsts, one), jnp.where(hi, one, lasts))
+                put("m_got", level, jnp.where(hi, join, zero), jnp.where(hi, zero, join))
+                put("s_in", level, jnp.where(hi, one, firsts), jnp.where(hi, lasts, one))
+                put("s_own", level, jnp.where(hi, zero, join), jnp.where(hi, join, zero))
+            else:
+                ahead, behind = same[2], same[3]
+                same = same[4:]
+                put("unit", level, jnp.where(hi, ahead, zero), jnp.where(hi, zero, behind))
+            if level + 1 == self.levels:
+                put("pick", level, jnp.where(hi, zero, one), jnp.where(hi, one, zero))
+
 
     def combine(self, name, body, ins, outs, after):
         def kernel(scalar_ref, *refs):
@@ -292,6 +300,40 @@
             [],
         )
 
+    def order(self):
+        bits = self.head_bits
+        links = [0] + list(range(1, self.levels)) + list(reversed(range(bits)))
+        count = len(links)
+        size = max(1, self.chunks // 2)
+        step, grads, hop = 1.7, 5.5, [2.0] + [5.4] * (self.levels - 1)
+        lasts = [step] * (count - 1) + [grads]
+        left = [sum(lasts[i:]) + sum(hop[k] for k in links[i:]) for i in range(count)]
+
+        def run(patience, sign):
+            now, free, line = 0.0, [0.0] * self.levels, []
+            nexts = [0] * self.chunks
+            ready = [-6.0 if chunk < size else 2.0 for chunk in range(self.chunks)]
+            while any(i < count for i in nexts):
+                open_ = [c for c in range(self.chunks) if nexts[c] < count]
+
+                def rank(c):
+                    late = patience if nexts[c] + 1 == count else 0.0
+                    return max(now, ready[c] + late), sign * left[nexts[c]], c
+
+                chunk = min(open_, key=rank)
+                i = nexts[chunk]
+                now = max(now, ready[chunk]) + lasts[i]
+                line.append((chunk, i))
+                nexts[chunk] += 1
+                if i + 1 < count:
+                    k = links[i + 1]
+                    free[k] = max(now, free[k]) + hop[k]
+                    ready[chunk] = free[k]
+            return now, line
+
+        tries = [run(p, sign) for sign in (-1.0, 1.0) for p in (0.0, 2.0, 4.0, 8.0, 16.0)]
+        return min(tries, key=lambda one: one[0])[1]
+
     def swap(self, x, level):
         if level < self.head_bits:
             moves = [(i, i ^ (1 << level)) for i in range(self.head_size)]
@@ -299,31 +341,27 @@
         bit = 1 << (level - self.head_bits)
         return lax.ppermute(x, "seq", [(i, i ^ bit) for i in range(self.seq_size)])
 
-    def stages(self, chunk, arrays):
+    def stages(self, chunk, keep, tokens, swapped, spot):
         d, bits, last = self.d, self.head_bits, self.levels - 1
         own, got, here = [], [], {}
 
         def shaped(heads, dtype, lead=2):
             return jax.ShapeDtypeStruct((lead, heads, d, d), dtype)
 
-        def first(after):
-            keep, send, here["heads"] = self.states(chunk, arrays, after)
-            own.append(keep)
-            here["got"] = self.swap(send, 0)
-            if chunk == 0:
-                self.weights((keep,))
-            return keep
+        own.append(keep)
+        here["heads"], here["got"] = tokens, swapped
 
         def up(level, after):
             got.append(here["got"])
             heads = own[-1].shape[1]
             half = heads // 2 if level + 1 < bits else heads
+            at = (spot,) if level == 0 else ()
 
             def body(w, ins, outs):
                 for which in range(2):
                     o, g = w("up_own", level, which), w("up_got", level, which)
                     for h in range(heads):
-                        x = o * ins[0][which, h] + g * ins[1][which, h].astype(F32)
+                        x = o * ins[0][which, h] + g * ins[1][(*at, which, h)].astype(F32)
                         if h < half:
                             outs[0][which, h] = x
                         if half == heads:
@@ -381,6 +419,7 @@
             heads = own[level].shape[1]
             half = heads // 2
             factor = self.scaling if level == 0 else 1.0
+            at = (spot,) if level == 0 else ()
 
             def body(w, ins, outs):
                 for which in range(2):
@@ -396,7 +435,7 @@
                             x = ins[0][which, h]
                         else:
                             x = ins[1][which, h - half].astype(F32)
-                        mine = m_in * x + m_got * ins[3][which, h].astype(F32)
+                        mine = m_in * x + m_got * ins[3][(*at, which, h)].astype(F32)
                         theirs = s_in * x + s_own * ins[2][which, h]
                         outs[0][which, h] = mine.astype(outs[0].dtype)
                         outs[1][which, h] = theirs.astype(B16)
@@ -412,8 +451,7 @@
             )
             return outs, token
 
-        steps = [first]
-        steps += [functools.partial(up, level) for level in range(bits)]
+        steps = [functools.partial(up, level) for level in range(bits)]
         steps += [functools.partial(across, level) for level in range(bits, last)]
         steps += [functools.partial(down, level) for level in reversed(range(bits))]
         return steps + [final]
@@ -423,15 +461,16 @@
     n, heads, d = queries.shape
     arrays = (queries, key_heads, value_heads, grad_output)
     plan = Plan(seq_size, head_size, n, heads, d, doc_lengths)
-    stages = [plan.stages(chunk, arrays) for chunk in range(plan.chunks)]
-    count = len(stages[0])
-    outs, after = (), ()
-    order = [(0, chunk) for chunk in range(plan.chunks)]
-    for wave in range(1, count + plan.chunks - 1):
-        for chunk in reversed(range(plan.chunks)):
-            if 1 <= wave - chunk < count:
-                order.append((wave - chunk, chunk))
-    for stage, chunk in order:
+    stages, after = [], ()
+    size = max(1, plan.chunks // 2)
+    for begin in range(0, plan.chunks, size):
+        chunks = list(range(begin, begin + size))
+        keeps, tokens, swapped = plan.states(chunks, arrays, after)
+        after = (keeps[0],)
+        for spot, chunk in enumerate(chunks):
+            stages.append(plan.stages(chunk, keeps[spot], tokens[spot], swapped, spot))
+    outs, count = (), len(stages[0])
+    for chunk, stage in plan.order():
         if stage + 1 < count:
             after = (stages[chunk][stage](after),)
         else:

time: 117 us -> 111 us (0.949)
  Pallas kernels: 61.1 us -> 56.3 us
    pallas_call x33 -> x30, Pallas kernels: 61.1 us -> 56.3 us  [call(): pl.pallas_call(body, in_specs=in_specs, out_specs=out_specs, out_shape=ou...]
    ppermute x16 -> x14, starting transfers between devices: 12.9 us -> 12 us  [swap(): return lax.ppermute(x, 'head', moves)]
    ppermute x16 -> x14, waiting for transfers between devices: 7.18 us -> 7.1 us  [swap(): return lax.ppermute(x, 'head', moves)]
  transfers between devices with their start and end apart: 28 -> 26, of which waited for: 8 -> 6; matrix products, arithmetic and copies ran while one was open for 0% -> 0% of each run, Pallas kernels for 42% -> 37%
where the time goes in v3:
time: 111 us
  Pallas kernels  56.3 us (51%)
  starting transfers between devices  33.7 us (30%)
  waiting for transfers between devices  18.3 us (16%)
  local copies, waits for them, and re-layouts  1.26 us (1%)
  between operations  1.14 us (1%)
    pallas_call x30, Pallas kernels, call(): pl.pallas_call(body, in_specs=in_specs, out_specs=out_specs, out_shape=ou...  56.3 us
    ppermute x12, starting transfers between devices, swap(): return lax.ppermute(x, 'seq', [(i, i ^ bit) for i in range(self.seq_size)])  21.8 us
    ppermute x14, starting transfers between devices, swap(): return lax.ppermute(x, 'head', moves)  12 us
    ppermute x12, waiting for transfers between devices, swap(): return lax.ppermute(x, 'seq', [(i, i ^ bit) for i in range(self.seq_size)])  11.2 us
    ppermute x14, waiting for transfers between devices, swap(): return lax.ppermute(x, 'head', moves)  7.1 us
  transfers between devices with their start and end apart: 26, of which 6 were waited for; matrix products, arithmetic and copies ran while one was open for 0% of the time, Pallas kernels for 37%

profile of v3, /device:TPU:0, one launch (start us, length us, event | category | flops | bytes accessed | tf_op | source)
XLA Modules:
  0.0 111.2 jit_solution(14436155847430966221)
XLA Ops:
  1.2 9.5 %states.2 = (f32[44]{0:T(128)}, f32[2,8,128,128]{3,2,1,0:T(8,128)}, f32[2,8,128,128]{3,2,1,0:T(8,128)}, bf16[4,16,128,128]{3,2,1,0:T(8,128)(2,1)}, bf16[4,16,128...) custom-call(s32[2]{0:T(128)} %pad_add_fusion.place_ref, s32[16]{0:T(128)} %len_ref.11, ...), custom_call_target="tpu_custom_call" | custom-call | flops 1 | bytes 1 | tf_op jit(solution)/shard_map/states/pallas_call | solution.py:185
  11.2 1.2 %copy-done = f32[2,8,128,128]{3,2,1,0:T(8,128)S(1)} copy-done((f32[2,8,128,128]{3,2,1,0:T(8,128)S(1)}, f32[2,8,128,128]{3,2,1,0:T(8,128)}, u32[]{:S(2)}) %copy-start) | copy-done | bytes 1048600
  12.5 7.2 %states.3 = (f32[2,8,128,128]{3,2,1,0:T(8,128)S(1)}, f32[2,8,128,128]{3,2,1,0:T(8,128)S(1)}, bf16[4,16,128,128]{3,2,1,0:T(8,128)(2,1)S(1)}, bf16[4,16,128,128]{3...) custom-call(s32[2]{0:T(128)S(1)} %copy-done.7, s32[16]{0:T(128)S(1)} %copy-done.6, bf16[128,64,128]{2,1,0:T(8,128)(2,1)} %refs_0_.3, ...), custom_call_target="tpu_custom_call" | custom-call | flops 1 | bytes 1 | tf_op jit(solution)/shard_map/states/pallas_call | solution.py:185
  20.5 3.0 %collective-permute-start.3 = (bf16[2,4,128,128]{3,2,1,0:T(8,128)(2,1)S(1)}, bf16[2,4,128,128]{3,2,1,0:T(8,128)(2,1)S(1)}, u32[]{:S(2)}, u32[]{:S(2)}) collective-permute-start(bf16[2,4,128,128]{3,2,1,0:T(8,128)(2,1)S(1)} %get-tuple-element.94), channel_id=1, source_target_pairs={{0,2},{1,3},{2,0},{3,1},{4,6},{5,7},{6,4},{7,5},{8,10},{9,11},{10,... | collective-permute-start | bytes 786440 | tf_op jit(solution)/shard_map/ppermute | solution.py:340
  25.7 4.9 %collective-permute-done.3.refs_1_.refs_3_ = bf16[2,4,128,128]{3,2,1,0:T(8,128)(2,1)S(1)} collective-permute-done((bf16[2,4,128,128]{3,2,1,0:T(8,128)(2,1)S(1)}, bf16[2,4,128,128]{3,2,1,0:T(8,128)(2,1)S(1)}, u32[]{:S(2)}, u32[]{:S(2)}) %collective-permute-start.3) | collective-permute-done | bytes 262176 | tf_op jit(solution)/shard_map/ppermute | solution.py:340
  31.2 2.2 %collective-permute-start.4 = (bf16[2,4,128,128]{3,2,1,0:T(8,128)(2,1)S(1)}, bf16[2,4,128,128]{3,2,1,0:T(8,128)(2,1)S(1)}, u32[]{:S(2)}, u32[]{:S(2)}) collective-permute-start(bf16[2,4,128,128]{3,2,1,0:T(8,128)(2,1)S(1)} %get-tuple-element.96), channel_id=1, source_target_pairs={{0,4},{4,0},{8,12},{12,8},{16,20},{20,16},{24,28},{28,24},{1,5},{5... | collective-permute-start | bytes 786440 | tf_op jit(solution)/shard_map/ppermute | solution.py:342
  33.4 1.5 %collective-permute-start.8 = (bf16[2,4,128,128]{3,2,1,0:T(8,128)(2,1)S(1)}, bf16[2,4,128,128]{3,2,1,0:T(8,128)(2,1)S(1)}, u32[]{:S(2)}, u32[]{:S(2)}) collective-permute-start(bf16[2,4,128,128]{3,2,1,0:T(8,128)(2,1)S(1)} %get-tuple-element.103), channel_id=1, source_target_pairs={{0,2},{1,3},{2,0},{3,1},{4,6},{5,7},{6,4},{7,5},{8,10},{9,11},{10,... | collective-permute-start | bytes 786440 | tf_op jit(solution)/shard_map/ppermute | solution.py:340
  34.9 1.3 %collective-permute-done.5.refs_1_.refs_3_ = bf16[2,4,128,128]{3,2,1,0:T(8,128)(2,1)S(1)} collective-permute-done((bf16[2,4,128,128]{3,2,1,0:T(8,128)(2,1)S(1)}, bf16[2,4,128,128]{3,2,1,0:T(8,128)(2,1)S(1)}, u32[]{:S(2)}, u32[]{:S(2)}) %collective-permute-start.5) | collective-permute-done | bytes 262176 | tf_op jit(solution)/shard_map/ppermute | solution.py:340
  36.9 2.2 %collective-permute-start.7 = (bf16[2,4,128,128]{3,2,1,0:T(8,128)(2,1)S(1)}, bf16[2,4,128,128]{3,2,1,0:T(8,128)(2,1)S(1)}, u32[]{:S(2)}, u32[]{:S(2)}) collective-permute-start(bf16[2,4,128,128]{3,2,1,0:T(8,128)(2,1)S(1)} %get-tuple-element.102), channel_id=1, source_target_pairs={{0,4},{4,0},{8,12},{12,8},{16,20},{20,16},{24,28},{28,24},{1,5},{5... | collective-permute-start | bytes 786440 | tf_op jit(solution)/shard_map/ppermute | solution.py:342
  39.7 1.6 %collective-permute-start.6 = (bf16[2,4,128,128]{3,2,1,0:T(8,128)(2,1)S(1)}, bf16[2,4,128,128]{3,2,1,0:T(8,128)(2,1)S(1)}, u32[]{:S(2)}, u32[]{:S(2)}) collective-permute-start(bf16[2,4,128,128]{3,2,1,0:T(8,128)(2,1)S(1)} %get-tuple-element.100), channel_id=1, source_target_pairs={{0,8},{4,12},{8,0},{12,4},{16,24},{20,28},{24,16},{28,20},{1,9},{5... | collective-permute-start | bytes 786440 | tf_op jit(solution)/shard_map/ppermute | solution.py:342
  41.3 1.5 %collective-permute-start.2 = (bf16[2,4,128,128]{3,2,1,0:T(8,128)(2,1)S(1)}, bf16[2,4,128,128]{3,2,1,0:T(8,128)(2,1)S(1)}, u32[]{:S(2)}, u32[]{:S(2)}) collective-permute-start(bf16[2,4,128,128]{3,2,1,0:T(8,128)(2,1)S(1)} %get-tuple-element.93), channel_id=1, source_target_pairs={{0,2},{1,3},{2,0},{3,1},{4,6},{5,7},{6,4},{7,5},{8,10},{9,11},{10,... | collective-permute-start | bytes 786440 | tf_op jit(solution)/shard_map/ppermute | solution.py:340
  43.4 1.1 collective-permute-start.12
  45.2 1.7 %collective-permute-start.11 = (bf16[2,4,128,128]{3,2,1,0:T(8,128)(2,1)S(1)}, bf16[2,4,128,128]{3,2,1,0:T(8,128)(2,1)S(1)}, u32[]{:S(2)}, u32[]{:S(2)}) collective-permute-start(bf16[2,4,128,128]{3,2,1,0:T(8,128)(2,1)S(1)} %get-tuple-element.111), channel_id=1, source_target_pairs={{0,8},{4,12},{8,0},{12,4},{16,24},{20,28},{24,16},{28,20},{1,9},{5... | collective-permute-start | bytes 786440 | tf_op jit(solution)/shard_map/ppermute | solution.py:342
  46.9 0.9 across.10
  47.8 2.7 %collective-permute-start.10 = (bf16[1,4,128,128]{3,2,1,0:T(8,128)(2,1)S(1)}, bf16[1,4,128,128]{3,2,1,0:T(8,128)(2,1)S(1)}, u32[]{:S(2)}, u32[]{:S(2)}) collective-permute-start(bf16[1,4,128,128]{3,2,1,0:T(8,128)(2,1)S(1)} %get-tuple-element.109), channel_id=1, source_target_pairs={{0,16},{4,20},{8,24},{12,28},{16,0},{20,4},{24,8},{28,12},{1,17},{... | collective-permute-start | bytes 393224 | tf_op jit(solution)/shard_map/ppermute | solution.py:342
  51.1 0.9 collective-permute-start.9
  52.7 1.5 %collective-permute-start.16 = (bf16[2,4,128,128]{3,2,1,0:T(8,128)(2,1)S(1)}, bf16[2,4,128,128]{3,2,1,0:T(8,128)(2,1)S(1)}, u32[]{:S(2)}, u32[]{:S(2)}) collective-permute-start(bf16[2,4,128,128]{3,2,1,0:T(8,128)(2,1)S(1)} %get-tuple-element.122), channel_id=1, source_target_pairs={{0,8},{4,12},{8,0},{12,4},{16,24},{20,28},{24,16},{28,20},{1,9},{5... | collective-permute-start | bytes 786440 | tf_op jit(solution)/shard_map/ppermute | solution.py:342
  54.1 1.5 %collective-permute-done.11.refs_1_ = bf16[2,4,128,128]{3,2,1,0:T(8,128)(2,1)S(1)} collective-permute-done((bf16[2,4,128,128]{3,2,1,0:T(8,128)(2,1)S(1)}, bf16[2,4,128,128]{3,2,1,0:T(8,128)(2,1)S(1)}, u32[]{:S(2)}, u32[]{:S(2)}) %collective-permute-start.11) | collective-permute-done | bytes 262176 | tf_op jit(solution)/shard_map/ppermute | solution.py:342
  57.1 1.6 %collective-permute-start.14 = (bf16[2,4,128,128]{3,2,1,0:T(8,128)(2,1)S(1)}, bf16[2,4,128,128]{3,2,1,0:T(8,128)(2,1)S(1)}, u32[]{:S(2)}, u32[]{:S(2)}) collective-permute-start(bf16[2,4,128,128]{3,2,1,0:T(8,128)(2,1)S(1)} %get-tuple-element.119), channel_id=1, source_target_pairs={{0,2},{1,3},{2,0},{3,1},{4,6},{5,7},{6,4},{7,5},{8,10},{9,11},{10,... | collective-permute-start | bytes 786440 | tf_op jit(solution)/shard_map/ppermute | solution.py:340
  58.7 3.2 %collective-permute-start.15 = (bf16[1,4,128,128]{3,2,1,0:T(8,128)(2,1)S(1)}, bf16[1,4,128,128]{3,2,1,0:T(8,128)(2,1)S(1)}, u32[]{:S(2)}, u32[]{:S(2)}) collective-permute-start(bf16[1,4,128,128]{3,2,1,0:T(8,128)(2,1)S(1)} %get-tuple-element.120), channel_id=1, source_target_pairs={{0,16},{4,20},{8,24},{12,28},{16,0},{20,4},{24,8},{28,12},{1,17},{... | collective-permute-start | bytes 393224 | tf_op jit(solution)/shard_map/ppermute | solution.py:342
  62.5 1.9 %collective-permute-start.13 = (bf16[2,4,128,128]{3,2,1,0:T(8,128)(2,1)S(1)}, bf16[2,4,128,128]{3,2,1,0:T(8,128)(2,1)S(1)}, u32[]{:S(2)}, u32[]{:S(2)}) collective-permute-start(bf16[2,4,128,128]{3,2,1,0:T(8,128)(2,1)S(1)} %get-tuple-element.117), channel_id=1, source_target_pairs={{0,8},{4,12},{8,0},{12,4},{16,24},{20,28},{24,16},{28,20},{1,9},{5... | collective-permute-start | bytes 786440 | tf_op jit(solution)/shard_map/ppermute | solution.py:342
  65.8 1.9 %collective-permute-start.19 = (bf16[2,4,128,128]{3,2,1,0:T(8,128)(2,1)S(1)}, bf16[2,4,128,128]{3,2,1,0:T(8,128)(2,1)S(1)}, u32[]{:S(2)}, u32[]{:S(2)}) collective-permute-start(bf16[2,4,128,128]{3,2,1,0:T(8,128)(2,1)S(1)} %get-tuple-element.130), channel_id=1, source_target_pairs={{0,2},{1,3},{2,0},{3,1},{4,6},{5,7},{6,4},{7,5},{8,10},{9,11},{10,... | collective-permute-start | bytes 786440 | tf_op jit(solution)/shard_map/ppermute | solution.py:340
  67.8 0.8 down.10
  68.7 2.8 %collective-permute-start.20 = (bf16[1,4,128,128]{3,2,1,0:T(8,128)(2,1)S(1)}, bf16[1,4,128,128]{3,2,1,0:T(8,128)(2,1)S(1)}, u32[]{:S(2)}, u32[]{:S(2)}) collective-permute-start(bf16[1,4,128,128]{3,2,1,0:T(8,128)(2,1)S(1)} %get-tuple-element.131), channel_id=1, source_target_pairs={{0,16},{4,20},{8,24},{12,28},{16,0},{20,4},{24,8},{28,12},{1,17},{... | collective-permute-start | bytes 393224 | tf_op jit(solution)/shard_map/ppermute | solution.py:342
  72.2 6.2 %collective-permute-done.20.refs_1_ = bf16[1,4,128,128]{3,2,1,0:T(8,128)(2,1)S(1)} collective-permute-done((bf16[1,4,128,128]{3,2,1,0:T(8,128)(2,1)S(1)}, bf16[1,4,128,128]{3,2,1,0:T(8,128)(2,1)S(1)}, u32[]{:S(2)}, u32[]{:S(2)}) %collective-permute-start.20) | collective-permute-done | bytes 131104 | tf_op jit(solution)/shard_map/ppermute | solution.py:342
  79.2 0.9 down.12
  80.9 5.4 %grads.4 = (bf16[128,64,128]{2,1,0:T(8,128)(2,1)}, bf16[128,64,128]{2,1,0:T(8,128)(2,1)}, bf16[128,64,128]{2,1,0:T(8,128)(2,1)}, f32[8,128]{1,0:T(8,128)S(1)}) custom-call(s32[2]{0:T(128)S(1)} %copy-done.7, s32[16]{0:T(128)S(1)} %copy-done.6, bf16[4,16,128,128]{3,2,1,0:T(8,128)(2,1)S(1)} %copy-done.3, ...), custom_call_target="tpu_custom_call" | custom-call | flops 1 | bytes 1 | tf_op jit(solution)/shard_map/grads/pallas_call | solution.py:185
  86.3 3.4 %collective-permute-done.17.refs_1_ = bf16[1,4,128,128]{3,2,1,0:T(8,128)(2,1)S(1)} collective-permute-done((bf16[1,4,128,128]{3,2,1,0:T(8,128)(2,1)S(1)}, bf16[1,4,128,128]{3,2,1,0:T(8,128)(2,1)S(1)}, u32[]{:S(2)}, u32[]{:S(2)}) %collective-permute-start.17) | collective-permute-done | bytes 131104 | tf_op jit(solution)/shard_map/ppermute | solution.py:342
  91.2 0.8 down.14
  92.1 5.4 %grads.5 = (bf16[128,64,128]{2,1,0:T(8,128)(2,1)}, bf16[128,64,128]{2,1,0:T(8,128)(2,1)}, bf16[128,64,128]{2,1,0:T(8,128)(2,1)}, f32[8,128]{1,0:T(8,128)S(1)}) custom-call(s32[2]{0:T(128)S(1)} %copy-done.7, s32[16]{0:T(128)S(1)} %copy-done.6, bf16[4,16,128,128]{3,2,1,0:T(8,128)(2,1)S(1)} %copy-done.2, ...), custom_call_target="tpu_custom_call", output_to_operand_aliasing={{0}: (5, {}), {1}: (6, {}), {2}: (7, {})} | custom-call | flops 1 | bytes 1 | tf_op jit(solution)/shard_map/grads/pallas_call | solution.py:185
  99.3 5.6 %grads.6 = (bf16[128,64,128]{2,1,0:T(8,128)(2,1)}, bf16[128,64,128]{2,1,0:T(8,128)(2,1)}, bf16[128,64,128]{2,1,0:T(8,128)(2,1)}, f32[8,128]{1,0:T(8,128)S(1)}) custom-call(s32[2]{0:T(128)S(1)} %copy-done.7, s32[16]{0:T(128)S(1)} %copy-done.6, ...), custom_call_target="tpu_custom_call", output_to_operand_aliasing={{0}: (5, {}), {1}: (6, {}), {2}: (7, {})} | custom-call | flops 1 | bytes 1 | tf_op jit(solution)/shard_map/grads/pallas_call | solution.py:185
  105.0 6.0 %grads.7 = (bf16[128,64,128]{2,1,0:T(8,128)(2,1)}, bf16[128,64,128]{2,1,0:T(8,128)(2,1)}, bf16[128,64,128]{2,1,0:T(8,128)(2,1)}, f32[8,128]{1,0:T(8,128)}) custom-call(s32[2]{0:T(128)S(1)} %copy-done.7, s32[16]{0:T(128)S(1)} %copy-done.6, bf16[4,16,128,128]{3,2,1,0:T(8,128)(2,1)S(1)} %copy-done.4, ...), custom_call_target="tpu_custom_call", output_to_operand_aliasing={{0}: (5, {}), {1}: (6, {}), {2}: (7, {})} | custom-call | flops 1 | bytes 1 | tf_op jit(solution)/shard_map/grads/pallas_call | solution.py:185
  (67 shorter events, 17.7 us)
Async XLA Ops:
  1.2 10.0 %copy-start.6 = (s32[16]{0:T(128)S(1)}, s32[16]{0:T(128)}, u32[]{:S(2)}) copy-start(s32[16]{0:T(128)} %len_ref.11) | copy-start | bytes 196
  1.2 10.0 %copy-start.7 = (s32[2]{0:T(128)S(1)}, s32[2]{0:T(128)}, u32[]{:S(2)}) copy-start(s32[2]{0:T(128)} %pad_add_fusion.place_ref) | copy-start | bytes 28
  10.7 9.1 %collective-permute-start.1 = (bf16[2,2,8,128,128]{4,3,2,1,0:T(8,128)(2,1)}, bf16[2,2,8,128,128]{4,3,2,1,0:T(8,128)(2,1)S(1)}, u32[]{:S(2)}, u32[]{:S(2)}) collective-permute-start(bf16[2,2,8,128,128]{4,3,2,1,0:T(8,128)(2,1)} %get-tuple-element.88), channel_id=1, source_target_pairs={{0,1},{1,0},{2,3},{3,2},{4,5},{5,4},{6,7},{7,6},{8,9},{9,8},{10,11... | collective-permute-start | bytes 3145736 | tf_op jit(solution)/shard_map/ppermute | solution.py:340
  12.5 7.3 %copy-start.5 = (f32[44]{0:T(128)S(1)}, f32[44]{0:T(128)}, u32[]{:S(2)}) copy-start(f32[44]{0:T(128)} %get-tuple-element.83.scalar_ref) | copy-start | bytes 532
  19.7 3.8 %copy-start.1 = (f32[2,8,128,128]{3,2,1,0:T(8,128)S(1)}, f32[2,8,128,128]{3,2,1,0:T(8,128)}, u32[]{:S(2)}) copy-start(f32[2,8,128,128]{3,2,1,0:T(8,128)} %get-tuple-element.87.refs_0_.refs_2_) | copy-start | bytes 3145732
  19.7 4.6 %collective-permute-start = (bf16[2,2,8,128,128]{4,3,2,1,0:T(8,128)(2,1)S(1)}, bf16[2,2,8,128,128]{4,3,2,1,0:T(8,128)(2,1)S(1)}, u32[]{:S(2)}, u32[]{:S(2)}) collective-permute-start(bf16[2,2,8,128,128]{4,3,2,1,0:T(8,128)(2,1)S(1)} %get-tuple-element.85), channel_id=1, source_target_pairs={{0,1},{1,0},{2,3},{3,2},{4,5},{5,4},{6,7},{7,6},{8,9},{9,8},{10,11... | collective-permute-start | bytes 3145736 | tf_op jit(solution)/shard_map/ppermute | solution.py:340
  20.5 10.1 %collective-permute-start.3 = (bf16[2,4,128,128]{3,2,1,0:T(8,128)(2,1)S(1)}, bf16[2,4,128,128]{3,2,1,0:T(8,128)(2,1)S(1)}, u32[]{:S(2)}, u32[]{:S(2)}) collective-permute-start(bf16[2,4,128,128]{3,2,1,0:T(8,128)(2,1)S(1)} %get-tuple-element.94), channel_id=1, source_target_pairs={{0,2},{1,3},{2,0},{3,1},{4,6},{5,7},{6,4},{7,5},{8,10},{9,11},{10,... | collective-permute-start | bytes 786440 | tf_op jit(solution)/shard_map/ppermute | solution.py:340
  24.2 12.0 %collective-permute-start.5 = (bf16[2,4,128,128]{3,2,1,0:T(8,128)(2,1)S(1)}, bf16[2,4,128,128]{3,2,1,0:T(8,128)(2,1)S(1)}, u32[]{:S(2)}, u32[]{:S(2)}) collective-permute-start(bf16[2,4,128,128]{3,2,1,0:T(8,128)(2,1)S(1)} %get-tuple-element.97), channel_id=1, source_target_pairs={{0,2},{1,3},{2,0},{3,1},{4,6},{5,7},{6,4},{7,5},{8,10},{9,11},{10,... | collective-permute-start | bytes 786440 | tf_op jit(solution)/shard_map/ppermute | solution.py:340
  31.2 7.8 %collective-permute-start.4 = (bf16[2,4,128,128]{3,2,1,0:T(8,128)(2,1)S(1)}, bf16[2,4,128,128]{3,2,1,0:T(8,128)(2,1)S(1)}, u32[]{:S(2)}, u32[]{:S(2)}) collective-permute-start(bf16[2,4,128,128]{3,2,1,0:T(8,128)(2,1)S(1)} %get-tuple-element.96), channel_id=1, source_target_pairs={{0,4},{4,0},{8,12},{12,8},{16,20},{20,16},{24,28},{28,24},{1,5},{5... | collective-permute-start | bytes 786440 | tf_op jit(solution)/shard_map/ppermute | solution.py:342
  33.4 9.4 %collective-permute-start.8 = (bf16[2,4,128,128]{3,2,1,0:T(8,128)(2,1)S(1)}, bf16[2,4,128,128]{3,2,1,0:T(8,128)(2,1)S(1)}, u32[]{:S(2)}, u32[]{:S(2)}) collective-permute-start(bf16[2,4,128,128]{3,2,1,0:T(8,128)(2,1)S(1)} %get-tuple-element.103), channel_id=1, source_target_pairs={{0,2},{1,3},{2,0},{3,1},{4,6},{5,7},{6,4},{7,5},{8,10},{9,11},{10,... | collective-permute-start | bytes 786440 | tf_op jit(solution)/shard_map/ppermute | solution.py:340
  36.9 7.7 %collective-permute-start.7 = (bf16[2,4,128,128]{3,2,1,0:T(8,128)(2,1)S(1)}, bf16[2,4,128,128]{3,2,1,0:T(8,128)(2,1)S(1)}, u32[]{:S(2)}, u32[]{:S(2)}) collective-permute-start(bf16[2,4,128,128]{3,2,1,0:T(8,128)(2,1)S(1)} %get-tuple-element.102), channel_id=1, source_target_pairs={{0,4},{4,0},{8,12},{12,8},{16,20},{20,16},{24,28},{28,24},{1,5},{5... | collective-permute-start | bytes 786440 | tf_op jit(solution)/shard_map/ppermute | solution.py:342
  39.7 7.3 %collective-permute-start.6 = (bf16[2,4,128,128]{3,2,1,0:T(8,128)(2,1)S(1)}, bf16[2,4,128,128]{3,2,1,0:T(8,128)(2,1)S(1)}, u32[]{:S(2)}, u32[]{:S(2)}) collective-permute-start(bf16[2,4,128,128]{3,2,1,0:T(8,128)(2,1)S(1)} %get-tuple-element.100), channel_id=1, source_target_pairs={{0,8},{4,12},{8,0},{12,4},{16,24},{20,28},{24,16},{28,20},{1,9},{5... | collective-permute-start | bytes 786440 | tf_op jit(solution)/shard_map/ppermute | solution.py:342
  41.3 9.2 %collective-permute-start.2 = (bf16[2,4,128,128]{3,2,1,0:T(8,128)(2,1)S(1)}, bf16[2,4,128,128]{3,2,1,0:T(8,128)(2,1)S(1)}, u32[]{:S(2)}, u32[]{:S(2)}) collective-permute-start(bf16[2,4,128,128]{3,2,1,0:T(8,128)(2,1)S(1)} %get-tuple-element.93), channel_id=1, source_target_pairs={{0,2},{1,3},{2,0},{3,1},{4,6},{5,7},{6,4},{7,5},{8,10},{9,11},{10,... | collective-permute-start | bytes 786440 | tf_op jit(solution)/shard_map/ppermute | solution.py:340
  43.4 8.6 %collective-permute-start.12 = (bf16[2,4,128,128]{3,2,1,0:T(8,128)(2,1)S(1)}, bf16[2,4,128,128]{3,2,1,0:T(8,128)(2,1)S(1)}, u32[]{:S(2)}, u32[]{:S(2)}) collective-permute-start(bf16[2,4,128,128]{3,2,1,0:T(8,128)(2,1)S(1)} %get-tuple-element.112), channel_id=1, source_target_pairs={{0,4},{4,0},{8,12},{12,8},{16,20},{20,16},{24,28},{28,24},{1,5},{5... | collective-permute-start | bytes 786440 | tf_op jit(solution)/shard_map/ppermute | solution.py:342
  45.2 10.5 %collective-permute-start.11 = (bf16[2,4,128,128]{3,2,1,0:T(8,128)(2,1)S(1)}, bf16[2,4,128,128]{3,2,1,0:T(8,128)(2,1)S(1)}, u32[]{:S(2)}, u32[]{:S(2)}) collective-permute-start(bf16[2,4,128,128]{3,2,1,0:T(8,128)(2,1)S(1)} %get-tuple-element.111), channel_id=1, source_target_pairs={{0,8},{4,12},{8,0},{12,4},{16,24},{20,28},{24,16},{28,20},{1,9},{5... | collective-permute-start | bytes 786440 | tf_op jit(solution)/shard_map/ppermute | solution.py:342
  47.8 8.5 %collective-permute-start.10 = (bf16[1,4,128,128]{3,2,1,0:T(8,128)(2,1)S(1)}, bf16[1,4,128,128]{3,2,1,0:T(8,128)(2,1)S(1)}, u32[]{:S(2)}, u32[]{:S(2)}) collective-permute-start(bf16[1,4,128,128]{3,2,1,0:T(8,128)(2,1)S(1)} %get-tuple-element.109), channel_id=1, source_target_pairs={{0,16},{4,20},{8,24},{12,28},{16,0},{20,4},{24,8},{28,12},{1,17},{... | collective-permute-start | bytes 393224 | tf_op jit(solution)/shard_map/ppermute | solution.py:342
  51.1 10.8 %collective-permute-start.9 = (bf16[2,4,128,128]{3,2,1,0:T(8,128)(2,1)S(1)}, bf16[2,4,128,128]{3,2,1,0:T(8,128)(2,1)S(1)}, u32[]{:S(2)}, u32[]{:S(2)}) collective-permute-start(bf16[2,4,128,128]{3,2,1,0:T(8,128)(2,1)S(1)} %get-tuple-element.108), channel_id=1, source_target_pairs={{0,4},{4,0},{8,12},{12,8},{16,20},{20,16},{24,28},{28,24},{1,5},{5... | collective-permute-start | bytes 786440 | tf_op jit(solution)/shard_map/ppermute | solution.py:342
  52.7 11.7 %collective-permute-start.16 = (bf16[2,4,128,128]{3,2,1,0:T(8,128)(2,1)S(1)}, bf16[2,4,128,128]{3,2,1,0:T(8,128)(2,1)S(1)}, u32[]{:S(2)}, u32[]{:S(2)}) collective-permute-start(bf16[2,4,128,128]{3,2,1,0:T(8,128)(2,1)S(1)} %get-tuple-element.122), channel_id=1, source_target_pairs={{0,8},{4,12},{8,0},{12,4},{16,24},{20,28},{24,16},{28,20},{1,9},{5... | collective-permute-start | bytes 786440 | tf_op jit(solution)/shard_map/ppermute | solution.py:342
  57.1 10.7 %collective-permute-start.14 = (bf16[2,4,128,128]{3,2,1,0:T(8,128)(2,1)S(1)}, bf16[2,4,128,128]{3,2,1,0:T(8,128)(2,1)S(1)}, u32[]{:S(2)}, u32[]{:S(2)}) collective-permute-start(bf16[2,4,128,128]{3,2,1,0:T(8,128)(2,1)S(1)} %get-tuple-element.119), channel_id=1, source_target_pairs={{0,2},{1,3},{2,0},{3,1},{4,6},{5,7},{6,4},{7,5},{8,10},{9,11},{10,... | collective-permute-start | bytes 786440 | tf_op jit(solution)/shard_map/ppermute | solution.py:340
  58.7 6.4 %collective-permute-start.15 = (bf16[1,4,128,128]{3,2,1,0:T(8,128)(2,1)S(1)}, bf16[1,4,128,128]{3,2,1,0:T(8,128)(2,1)S(1)}, u32[]{:S(2)}, u32[]{:S(2)}) collective-permute-start(bf16[1,4,128,128]{3,2,1,0:T(8,128)(2,1)S(1)} %get-tuple-element.120), channel_id=1, source_target_pairs={{0,16},{4,20},{8,24},{12,28},{16,0},{20,4},{24,8},{28,12},{1,17},{... | collective-permute-start | bytes 393224 | tf_op jit(solution)/shard_map/ppermute | solution.py:342
  62.5 9.0 %collective-permute-start.13 = (bf16[2,4,128,128]{3,2,1,0:T(8,128)(2,1)S(1)}, bf16[2,4,128,128]{3,2,1,0:T(8,128)(2,1)S(1)}, u32[]{:S(2)}, u32[]{:S(2)}) collective-permute-start(bf16[2,4,128,128]{3,2,1,0:T(8,128)(2,1)S(1)} %get-tuple-element.117), channel_id=1, source_target_pairs={{0,8},{4,12},{8,0},{12,4},{16,24},{20,28},{24,16},{28,20},{1,9},{5... | collective-permute-start | bytes 786440 | tf_op jit(solution)/shard_map/ppermute | solution.py:342
  65.8 13.3 %collective-permute-start.19 = (bf16[2,4,128,128]{3,2,1,0:T(8,128)(2,1)S(1)}, bf16[2,4,128,128]{3,2,1,0:T(8,128)(2,1)S(1)}, u32[]{:S(2)}, u32[]{:S(2)}) collective-permute-start(bf16[2,4,128,128]{3,2,1,0:T(8,128)(2,1)S(1)} %get-tuple-element.130), channel_id=1, source_target_pairs={{0,2},{1,3},{2,0},{3,1},{4,6},{5,7},{6,4},{7,5},{8,10},{9,11},{10,... | collective-permute-start | bytes 786440 | tf_op jit(solution)/shard_map/ppermute | solution.py:340
  68.6 12.3 %collective-permute-start.18 = (bf16[2,8,128,128]{3,2,1,0:T(8,128)(2,1)S(1)}, bf16[2,8,128,128]{3,2,1,0:T(8,128)(2,1)S(1)}, u32[]{:S(2)}, u32[]{:S(2)}) collective-permute-start(bf16[2,8,128,128]{3,2,1,0:T(8,128)(2,1)S(1)} %get-tuple-element.129), channel_id=1, source_target_pairs={{0,1},{1,0},{2,3},{3,2},{4,5},{5,4},{6,7},{7,6},{8,9},{9,8},{10,11... | collective-permute-start | bytes 1572872 | tf_op jit(solution)/shard_map/ppermute | solution.py:340
  68.7 9.7 %collective-permute-start.20 = (bf16[1,4,128,128]{3,2,1,0:T(8,128)(2,1)S(1)}, bf16[1,4,128,128]{3,2,1,0:T(8,128)(2,1)S(1)}, u32[]{:S(2)}, u32[]{:S(2)}) collective-permute-start(bf16[1,4,128,128]{3,2,1,0:T(8,128)(2,1)S(1)} %get-tuple-element.131), channel_id=1, source_target_pairs={{0,16},{4,20},{8,24},{12,28},{16,0},{20,4},{24,8},{28,12},{1,17},{... | collective-permute-start | bytes 393224 | tf_op jit(solution)/shard_map/ppermute | solution.py:342
  80.0 12.1 %collective-permute-start.22 = (bf16[2,8,128,128]{3,2,1,0:T(8,128)(2,1)S(1)}, bf16[2,8,128,128]{3,2,1,0:T(8,128)(2,1)S(1)}, u32[]{:S(2)}, u32[]{:S(2)}) collective-permute-start(bf16[2,8,128,128]{3,2,1,0:T(8,128)(2,1)S(1)} %get-tuple-element.138), channel_id=1, source_target_pairs={{0,1},{1,0},{2,3},{3,2},{4,5},{5,4},{6,7},{7,6},{8,9},{9,8},{10,11... | collective-permute-start | bytes 1572872 | tf_op jit(solution)/shard_map/ppermute | solution.py:340
  80.1 9.6 %collective-permute-start.17 = (bf16[1,4,128,128]{3,2,1,0:T(8,128)(2,1)S(1)}, bf16[1,4,128,128]{3,2,1,0:T(8,128)(2,1)S(1)}, u32[]{:S(2)}, u32[]{:S(2)}) collective-permute-start(bf16[1,4,128,128]{3,2,1,0:T(8,128)(2,1)S(1)} %get-tuple-element.127), channel_id=1, source_target_pairs={{0,16},{4,20},{8,24},{12,28},{16,0},{20,4},{24,8},{28,12},{1,17},{... | collective-permute-start | bytes 393224 | tf_op jit(solution)/shard_map/ppermute | solution.py:342
  80.2 11.0 %collective-permute-start.23 = (bf16[2,4,128,128]{3,2,1,0:T(8,128)(2,1)S(1)}, bf16[2,4,128,128]{3,2,1,0:T(8,128)(2,1)S(1)}, u32[]{:S(2)}, u32[]{:S(2)}) collective-permute-start(bf16[2,4,128,128]{3,2,1,0:T(8,128)(2,1)S(1)} %get-tuple-element.142), channel_id=1, source_target_pairs={{0,2},{1,3},{2,0},{3,1},{4,6},{5,7},{6,4},{7,5},{8,10},{9,11},{10,... | collective-permute-start | bytes 786440 | tf_op jit(solution)/shard_map/ppermute | solution.py:340
  89.7 2.4 %copy-start.2 = (bf16[4,16,128,128]{3,2,1,0:T(8,128)(2,1)S(1)}, bf16[4,16,128,128]{3,2,1,0:T(8,128)(2,1)}, u32[]{:S(2)}) copy-start(bf16[4,16,128,128]{3,2,1,0:T(8,128)(2,1)} %get-tuple-element.137.head_ref) | copy-start | bytes 6291460
  90.5 7.9 %collective-permute-start.21 = (bf16[2,4,128,128]{3,2,1,0:T(8,128)(2,1)S(1)}, bf16[2,4,128,128]{3,2,1,0:T(8,128)(2,1)S(1)}, u32[]{:S(2)}, u32[]{:S(2)}) collective-permute-start(bf16[2,4,128,128]{3,2,1,0:T(8,128)(2,1)S(1)} %get-tuple-element.136), channel_id=1, source_target_pairs={{0,2},{1,3},{2,0},{3,1},{4,6},{5,7},{6,4},{7,5},{8,10},{9,11},{10,... | collective-permute-start | bytes 786440 | tf_op jit(solution)/shard_map/ppermute | solution.py:340
  92.0 7.3 %collective-permute-start.25 = (bf16[2,8,128,128]{3,2,1,0:T(8,128)(2,1)S(1)}, bf16[2,8,128,128]{3,2,1,0:T(8,128)(2,1)S(1)}, u32[]{:S(2)}, u32[]{:S(2)}) collective-permute-start(bf16[2,8,128,128]{3,2,1,0:T(8,128)(2,1)S(1)} %get-tuple-element.148), channel_id=1, source_target_pairs={{0,1},{1,0},{2,3},{3,2},{4,5},{5,4},{6,7},{7,6},{8,9},{9,8},{10,11... | collective-permute-start | bytes 1572872 | tf_op jit(solution)/shard_map/ppermute | solution.py:340
  99.2 5.7 %collective-permute-start.24 = (bf16[2,8,128,128]{3,2,1,0:T(8,128)(2,1)S(1)}, bf16[2,8,128,128]{3,2,1,0:T(8,128)(2,1)S(1)}, u32[]{:S(2)}, u32[]{:S(2)}) collective-permute-start(bf16[2,8,128,128]{3,2,1,0:T(8,128)(2,1)S(1)} %get-tuple-element.146), channel_id=1, source_target_pairs={{0,1},{1,0},{2,3},{3,2},{4,5},{5,4},{6,7},{7,6},{8,9},{9,8},{10,11... | collective-permute-start | bytes 1572872 | tf_op jit(solution)/shard_map/ppermute | solution.py:340
  99.3 5.7 %copy-start.4 = (bf16[4,16,128,128]{3,2,1,0:T(8,128)(2,1)S(1)}, bf16[4,16,128,128]{3,2,1,0:T(8,128)(2,1)}, u32[]{:S(2)}) copy-start(bf16[4,16,128,128]{3,2,1,0:T(8,128)(2,1)} %get-tuple-element.82.head_ref) | copy-start | bytes 6291460
  (2 other events, 3.0 us)

commit v4 on v3

--- a/solution.py
+++ b/solution.py
@@ -10,10 +10,11 @@
 
 CHUNKS = 4
 VMEM = 24 * 1024 * 1024
-VMEM_FIRST = 56 * 1024 * 1024
+VMEM_FIRST = 55 * 1024 * 1024
 VMEM_NEXT = 46 * 1024 * 1024
 F32 = jnp.float32
 B16 = jnp.bfloat16
+COST = 3690
 IN_VMEM = pl.BlockSpec(memory_space=pltpu.VMEM)
 IN_SMEM = pl.BlockSpec(memory_space=pltpu.SMEM)
 IN_HBM = pl.BlockSpec(memory_space=pltpu.HBM)
@@ -54,8 +55,7 @@
     count = len(chunks)
     tokens, refs = refs[:4], refs[len(refs) - 2 * count - (weights is not None) - 5 :]
     if weights is not None:
-        weights(place_ref, len_ref, refs[0])
-        refs = refs[1:]
+        scalar_ref, *refs = refs
     keeps, head_refs, send_ref = refs[:count], refs[count : 2 * count], refs[2 * count]
     slab, wide, sems = refs[2 * count + 1], refs[-3:-1], refs[-1]
     n, _, d = tokens[0].shape
@@ -73,6 +73,8 @@
     for some in copies:
         for copy in some:
             copy.start()
+    if weights is not None:
+        weights(place_ref, len_ref, scalar_ref)
     first = place_ref[0] * n
     flip = place_ref[1]
     start, stop = _edges(len_ref, first, first + n - 1)
@@ -99,8 +101,8 @@
                 send_ref[j, 1, r - half] = state_b.astype(B16)
 
 
-def grads_kernel(chunk, scaling, place_ref, len_ref, head_ref, mine_ref, got_ref, *refs):
-    outs, token_ref = refs[-11:-8], refs[-8]
+def grads_kernel(chunk, scaling, place_ref, len_ref, head_ref, mine_ref, *refs):
+    got, outs, token_ref = refs[:4], refs[-11:-8], refs[-8]
     wide, slabs, sems = refs[-7:-4], refs[-4:-1], refs[-1]
     token_ref[...] = jnp.zeros(token_ref.shape, token_ref.dtype)
     _, heads, n, d = head_ref.shape
@@ -125,25 +127,33 @@
 
     down, across = live(0), live(1)
     cat = jnp.concatenate
-    for r in range(heads):
-        h = r ^ flip
-        ref, o = (mine_ref, r) if r < half else (got_ref, r - half)
-        state_a, state_b = ref[0, o], ref[1, o]
-        query, key, value, grad = (head_ref[i, h] for i in range(4))
+
+    def query_part(query, key, value, grad, state_a, state_b):
         x = _dot(grad, cat([value, state_a], axis=0), 1, 1)
+        ts = (x[:, :n] * down).astype(B16)
+        return _dot(ts, key, 1, 0) + x[:, n:] * lead
+
+    def key_part(query, key, value, grad, state_a, state_b):
         y = _dot(value, cat([grad, state_b], axis=0), 1, 1)
-        z = _dot(key, query, 1, 1)
-        ts = (x[:, :n] * down).astype(B16)
         st = (y[:, :n] * across).astype(B16)
-        sc = (z * across).astype(B16)
-        at = pl.ds(h, n, stride=heads)
-        wide[0][at, :] = _dot(ts, key, 1, 0) + x[:, n:] * lead
-        wide[1][at, :] = _dot(st, query, 1, 0) + y[:, n:] * last
-        wide[2][at, :] = _dot(
-            cat([sc, key * last16], axis=1), cat([grad, state_b], axis=0), 1, 0
-        )
+        return _dot(st, query, 1, 0) + y[:, n:] * last
+
+    def value_part(query, key, value, grad, state_a, state_b):
+        sc = (_dot(key, query, 1, 1) * across).astype(B16)
+        return _dot(cat([sc, key * last16], axis=1), cat([grad, state_b], axis=0), 1, 0)
+
     copies = []
-    for i, (scr, slab, out) in enumerate(zip(wide, slabs, outs)):
+    for i, part in enumerate((query_part, key_part, value_part)):
+        scr, slab, out = wide[i], slabs[i], outs[i]
+        for r in range(heads):
+            h = r ^ flip
+            if r < half:
+                states = mine_ref[0, r], mine_ref[1, r]
+            else:
+                side, o = divmod(r - half, half // 2)
+                states = got[side][0, o], got[2 + side][0, o]
+            tokens = [head_ref[a, h] for a in range(4)]
+            scr[pl.ds(h, n, stride=heads), :] = part(*tokens, *states)
         slab[...] = scr[...].reshape(n, heads, d).astype(B16)
         copy = pltpu.make_async_copy(
             slab, out.at[:, pl.ds(chunk * heads, heads), :], sems.at[i]
@@ -181,7 +191,7 @@
             for name in names + (["pick"] if level + 1 == self.levels else []):
                 self.index[name, level] = len(self.index)
 
-    def call(self, body, name, ins, in_specs, outs, out_specs, scratch, vmem=VMEM, **kw):
+    def call(self, body, name, ins, in_specs, outs, out_specs, scratch, vmem=VMEM, cost=700, **kw):
         return pl.pallas_call(
             body,
             in_specs=in_specs,
@@ -189,7 +199,9 @@
             out_shape=outs,
             scratch_shapes=scratch,
             compiler_params=pltpu.CompilerParams(vmem_limit_bytes=vmem),
-            cost_estimate=pl.CostEstimate(flops=1, bytes_accessed=1, transcendentals=0),
+            cost_estimate=pl.CostEstimate(
+                flops=1, bytes_accessed=int(cost * COST), transcendentals=0
+            ),
             name=name,
             **kw,
         )(*ins)
@@ -216,6 +228,7 @@
             + [pltpu.VMEM((n * part, d), F32)] * 2
             + [pltpu.SemaphoreType.DMA((count, 4))],
             VMEM_FIRST if first else VMEM_NEXT,
+            3500 * count,
         )
         if first:
             self.scalars, *got = got
@@ -227,9 +240,9 @@
         return self.call(
             functools.partial(grads_kernel, chunk, self.scaling),
             "grads",
-            [self.place, self.lengths, heads, mine, got, *before, *after],
+            [self.place, self.lengths, heads, mine, *got, *before, *after],
             [IN_SMEM] * 2
-            + [IN_VMEM] * 3
+            + [IN_VMEM] * 6
             + [IN_HBM] * len(before)
             + [ANYWHERE] * len(after),
             (out, out, out, jax.ShapeDtypeStruct((8, 128), F32)),
@@ -237,7 +250,8 @@
             [pltpu.VMEM((n * part, d), F32)] * 3
             + [pltpu.VMEM((n, part, d), B16)] * 3
             + [pltpu.SemaphoreType.DMA((3,))],
-            input_output_aliases={5 + i: i for i in range(len(before))},
+            cost=5500,
+            input_output_aliases={8 + i: i for i in range(len(before))},
         )
 
     def weights(self, place_ref, len_ref, out):
@@ -300,39 +314,22 @@
             [],
         )
 
-    def order(self):
-        bits = self.head_bits
-        links = [0] + list(range(1, self.levels)) + list(reversed(range(bits)))
-        count = len(links)
-        size = max(1, self.chunks // 2)
-        step, grads, hop = 1.7, 5.5, [2.0] + [5.4] * (self.levels - 1)
-        lasts = [step] * (count - 1) + [grads]
-        left = [sum(lasts[i:]) + sum(hop[k] for k in links[i:]) for i in range(count)]
-
-        def run(patience, sign):
-            now, free, line = 0.0, [0.0] * self.levels, []
-            nexts = [0] * self.chunks
-            ready = [-6.0 if chunk < size else 2.0 for chunk in range(self.chunks)]
-            while any(i < count for i in nexts):
-                open_ = [c for c in range(self.chunks) if nexts[c] < count]
-
-                def rank(c):
-                    late = patience if nexts[c] + 1 == count else 0.0
-                    return max(now, ready[c] + late), sign * left[nexts[c]], c
-
-                chunk = min(open_, key=rank)
-                i = nexts[chunk]
-                now = max(now, ready[chunk]) + lasts[i]
-                line.append((chunk, i))
-                nexts[chunk] += 1
-                if i + 1 < count:
-                    k = links[i + 1]
-                    free[k] = max(now, free[k]) + hop[k]
-                    ready[chunk] = free[k]
-            return now, line
-
-        tries = [run(p, sign) for sign in (-1.0, 1.0) for p in (0.0, 2.0, 4.0, 8.0, 16.0)]
-        return min(tries, key=lambda one: one[0])[1]
+    def order(self, count):
+        chunks = self.chunks
+        line = []
+        for wave in range(count - 2 + chunks - 1):
+            for chunk in reversed(range(chunks)):
+                if 0 <= wave - chunk < count - 2:
+                    line.append((chunk, wave - chunk))
+        fill, final = count - 2, count - 1
+        spare = line[-2:] if chunks > 1 else []
+        line = line[: len(line) - len(spare)]
+        line += [(0, fill), *spare[:-1], (0, final), *spare[-1:]]
+        for chunk in range(1, chunks):
+            line += [(chunk, fill)] if chunk == 1 else []
+            line += [(chunk + 1, fill)] if chunk + 1 < chunks else []
+            line.append((chunk, final))
+        return line
 
     def swap(self, x, level):
         if level < self.head_bits:
@@ -438,11 +435,18 @@
                         mine = m_in * x + m_got * ins[3][(*at, which, h)].astype(F32)
                         theirs = s_in * x + s_own * ins[2][which, h]
                         outs[0][which, h] = mine.astype(outs[0].dtype)
-                        outs[1][which, h] = theirs.astype(B16)
-
-            outs = [shaped(heads, B16 if level == 0 else F32), shaped(heads, B16)]
-            here["state"], send = self.combine("down", body, ins, outs, after)
-            here["got"] = self.swap(send, level)
+                        if level:
+                            outs[1][which, h] = theirs.astype(B16)
+                        else:
+                            outs[1 + 2 * which + h // half][0, h % half] = theirs.astype(B16)
+
+            if level:
+                outs = [shaped(heads, F32), shaped(heads, B16)]
+            else:
+                outs = [shaped(heads, B16)] + [shaped(half, B16, 1)] * 4
+            here["state"], *send = self.combine("down", body, ins, outs, after)
+            moved = [self.swap(x, level) for x in send]
+            here["got"] = moved if level == 0 else moved[0]
             return here["state"]
 
         def final(before, after):
@@ -470,7 +474,7 @@
         for spot, chunk in enumerate(chunks):
             stages.append(plan.stages(chunk, keeps[spot], tokens[spot], swapped, spot))
     outs, count = (), len(stages[0])
-    for chunk, stage in plan.order():
+    for chunk, stage in plan.order(count):
         if stage + 1 < count:
             after = (stages[chunk][stage](after),)
         else:

time: 111 us -> 117 us (1.054)
  Pallas kernels: 56.3 us -> 62.9 us
  waiting for transfers between devices: 18.3 us -> 17.1 us
    pallas_call x30, Pallas kernels: 56.3 us -> 62.9 us  [call(): pl.pallas_call(body, in_specs=in_specs, out_specs=out_specs, out_shape=ou...]
    ppermute x12, starting transfers between devices: 21.8 us -> 18.5 us  [swap(): return lax.ppermute(x, 'seq', [(i, i ^ bit) for i in range(self.seq_size)])]
    ppermute x14 -> x26, starting transfers between devices: 12 us -> 14.8 us  [swap(): return lax.ppermute(x, 'head', moves)]
    ppermute x12, waiting for transfers between devices: 11.2 us -> 9.37 us  [swap(): return lax.ppermute(x, 'seq', [(i, i ^ bit) for i in range(self.seq_size)])]
    ppermute x14 -> x26, waiting for transfers between devices: 7.1 us -> 7.77 us  [swap(): return lax.ppermute(x, 'head', moves)]
  transfers between devices with their start and end apart: 26 -> 38, of which waited for: 6 -> 9; matrix products, arithmetic and copies ran while one was open for 0% -> 0% of each run, Pallas kernels for 37% -> 40%
where the time goes in v4:
time: 117 us; the launch traced here: 116 us
  Pallas kernels  62.9 us (54%)
  starting transfers between devices  33.3 us (28%)
  waiting for transfers between devices  17.1 us (15%)
  local copies, waits for them, and re-layouts  1.26 us (1%)
    pallas_call x30, Pallas kernels, call(): pl.pallas_call(body, in_specs=in_specs, out_specs=out_specs, out_shape=ou...  62.9 us
    ppermute x12, starting transfers between devices, swap(): return lax.ppermute(x, 'seq', [(i, i ^ bit) for i in range(self.seq_size)])  18.5 us
    ppermute x26, starting transfers between devices, swap(): return lax.ppermute(x, 'head', moves)  14.8 us
    ppermute x12, waiting for transfers between devices, swap(): return lax.ppermute(x, 'seq', [(i, i ^ bit) for i in range(self.seq_size)])  9.37 us
    ppermute x26, waiting for transfers between devices, swap(): return lax.ppermute(x, 'head', moves)  7.77 us
  transfers between devices with their start and end apart: 38, of which 9 were waited for; matrix products, arithmetic and copies ran while one was open for 0% of the time, Pallas kernels for 40%

profile of v4, /device:TPU:0, one launch (start us, length us, event | category | flops | bytes accessed | tf_op | source)
XLA Modules:
  0.0 116.4 jit_solution(4594631813869800465)
XLA Ops:
  1.3 8.7 %states.2 = (f32[44]{0:T(128)}, f32[2,8,128,128]{3,2,1,0:T(8,128)}, f32[2,8,128,128]{3,2,1,0:T(8,128)}, bf16[4,16,128,128]{3,2,1,0:T(8,128)(2,1)}, bf16[4,16,128...) custom-call(s32[2]{0:T(128)} %pad_add_fusion.place_ref, s32[16]{0:T(128)} %len_ref.11, ...), custom_call_target="tpu_custom_call" | custom-call | flops 1 | bytes 25830000 | tf_op jit(solution)/shard_map/states/pallas_call | solution.py:195
  10.6 1.2 %copy-done = f32[2,8,128,128]{3,2,1,0:T(8,128)S(1)} copy-done((f32[2,8,128,128]{3,2,1,0:T(8,128)S(1)}, f32[2,8,128,128]{3,2,1,0:T(8,128)}, u32[]{:S(2)}) %copy-start) | copy-done | bytes 1048600
  11.8 7.2 %states.3 = (f32[2,8,128,128]{3,2,1,0:T(8,128)S(1)}, f32[2,8,128,128]{3,2,1,0:T(8,128)S(1)}, bf16[4,16,128,128]{3,2,1,0:T(8,128)(2,1)S(1)}, bf16[4,16,128,128]{3...) custom-call(s32[2]{0:T(128)S(1)} %copy-done.7, s32[16]{0:T(128)S(1)} %copy-done.6, bf16[128,64,128]{2,1,0:T(8,128)(2,1)} %refs_0_.3, ...), custom_call_target="tpu_custom_call" | custom-call | flops 1 | bytes 25830000 | tf_op jit(solution)/shard_map/states/pallas_call | solution.py:195
  19.8 3.0 %collective-permute-start.2 = (bf16[2,4,128,128]{3,2,1,0:T(8,128)(2,1)S(1)}, bf16[2,4,128,128]{3,2,1,0:T(8,128)(2,1)S(1)}, u32[]{:S(2)}, u32[]{:S(2)}) collective-permute-start(bf16[2,4,128,128]{3,2,1,0:T(8,128)(2,1)S(1)} %get-tuple-element.101), channel_id=1, source_target_pairs={{0,2},{1,3},{2,0},{3,1},{4,6},{5,7},{6,4},{7,5},{8,10},{9,11},{10,... | collective-permute-start | bytes 786440 | tf_op jit(solution)/shard_map/ppermute | solution.py:337
  23.6 6.3 %collective-permute-done.2.refs_1_.refs_3_ = bf16[2,4,128,128]{3,2,1,0:T(8,128)(2,1)S(1)} collective-permute-done((bf16[2,4,128,128]{3,2,1,0:T(8,128)(2,1)S(1)}, bf16[2,4,128,128]{3,2,1,0:T(8,128)(2,1)S(1)}, u32[]{:S(2)}, u32[]{:S(2)}) %collective-permute-start.2) | collective-permute-done | bytes 262176 | tf_op jit(solution)/shard_map/ppermute | solution.py:337
  30.5 2.2 %collective-permute-start.3 = (bf16[2,4,128,128]{3,2,1,0:T(8,128)(2,1)S(1)}, bf16[2,4,128,128]{3,2,1,0:T(8,128)(2,1)S(1)}, u32[]{:S(2)}, u32[]{:S(2)}) collective-permute-start(bf16[2,4,128,128]{3,2,1,0:T(8,128)(2,1)S(1)} %get-tuple-element.105), channel_id=1, source_target_pairs={{0,4},{4,0},{8,12},{12,8},{16,20},{20,16},{24,28},{28,24},{1,5},{5... | collective-permute-start | bytes 786440 | tf_op jit(solution)/shard_map/ppermute | solution.py:339
  33.4 1.6 %collective-permute-start.8 = (bf16[2,4,128,128]{3,2,1,0:T(8,128)(2,1)S(1)}, bf16[2,4,128,128]{3,2,1,0:T(8,128)(2,1)S(1)}, u32[]{:S(2)}, u32[]{:S(2)}) collective-permute-start(bf16[2,4,128,128]{3,2,1,0:T(8,128)(2,1)S(1)} %get-tuple-element.115), channel_id=1, source_target_pairs={{0,2},{1,3},{2,0},{3,1},{4,6},{5,7},{6,4},{7,5},{8,10},{9,11},{10,... | collective-permute-start | bytes 786440 | tf_op jit(solution)/shard_map/ppermute | solution.py:337
  36.1 2.2 %collective-permute-start.7 = (bf16[2,4,128,128]{3,2,1,0:T(8,128)(2,1)S(1)}, bf16[2,4,128,128]{3,2,1,0:T(8,128)(2,1)S(1)}, u32[]{:S(2)}, u32[]{:S(2)}) collective-permute-start(bf16[2,4,128,128]{3,2,1,0:T(8,128)(2,1)S(1)} %get-tuple-element.114), channel_id=1, source_target_pairs={{0,4},{4,0},{8,12},{12,8},{16,20},{20,16},{24,28},{28,24},{1,5},{5... | collective-permute-start | bytes 786440 | tf_op jit(solution)/shard_map/ppermute | solution.py:339
  39.0 1.7 %collective-permute-start.6 = (bf16[2,4,128,128]{3,2,1,0:T(8,128)(2,1)S(1)}, bf16[2,4,128,128]{3,2,1,0:T(8,128)(2,1)S(1)}, u32[]{:S(2)}, u32[]{:S(2)}) collective-permute-start(bf16[2,4,128,128]{3,2,1,0:T(8,128)(2,1)S(1)} %get-tuple-element.113), channel_id=1, source_target_pairs={{0,8},{4,12},{8,0},{12,4},{16,24},{20,28},{24,16},{28,20},{1,9},{5... | collective-permute-start | bytes 786440 | tf_op jit(solution)/shard_map/ppermute | solution.py:339
  41.3 1.5 %collective-permute-start.5 = (bf16[2,4,128,128]{3,2,1,0:T(8,128)(2,1)S(1)}, bf16[2,4,128,128]{3,2,1,0:T(8,128)(2,1)S(1)}, u32[]{:S(2)}, u32[]{:S(2)}) collective-permute-start(bf16[2,4,128,128]{3,2,1,0:T(8,128)(2,1)S(1)} %get-tuple-element.111), channel_id=1, source_target_pairs={{0,2},{1,3},{2,0},{3,1},{4,6},{5,7},{6,4},{7,5},{8,10},{9,11},{10,... | collective-permute-start | bytes 786440 | tf_op jit(solution)/shard_map/ppermute | solution.py:337
  43.5 0.9 collective-permute-start.12
  45.1 1.2 collective-permute-start.11
  48.4 0.9 collective-permute-start.9
  49.3 2.6 %collective-permute-start.10 = (bf16[1,4,128,128]{3,2,1,0:T(8,128)(2,1)S(1)}, bf16[1,4,128,128]{3,2,1,0:T(8,128)(2,1)S(1)}, u32[]{:S(2)}, u32[]{:S(2)}) collective-permute-start(bf16[1,4,128,128]{3,2,1,0:T(8,128)(2,1)S(1)} %get-tuple-element.121), channel_id=1, source_target_pairs={{0,16},{4,20},{8,24},{12,28},{16,0},{20,4},{24,8},{28,12},{1,17},{... | collective-permute-start | bytes 393224 | tf_op jit(solution)/shard_map/ppermute | solution.py:339
  52.6 0.9 collective-permute-start.15
  53.5 2.1 %collective-permute-done.11.refs_1_ = bf16[2,4,128,128]{3,2,1,0:T(8,128)(2,1)S(1)} collective-permute-done((bf16[2,4,128,128]{3,2,1,0:T(8,128)(2,1)S(1)}, bf16[2,4,128,128]{3,2,1,0:T(8,128)(2,1)S(1)}, u32[]{:S(2)}, u32[]{:S(2)}) %collective-permute-start.11) | collective-permute-done | bytes 262176 | tf_op jit(solution)/shard_map/ppermute | solution.py:339
  57.8 3.3 %collective-permute-start.13 = (bf16[2,4,128,128]{3,2,1,0:T(8,128)(2,1)S(1)}, bf16[2,4,128,128]{3,2,1,0:T(8,128)(2,1)S(1)}, u32[]{:S(2)}, u32[]{:S(2)}) collective-permute-start(bf16[2,4,128,128]{3,2,1,0:T(8,128)(2,1)S(1)} %get-tuple-element.129), channel_id=1, source_target_pairs={{0,8},{4,12},{8,0},{12,4},{16,24},{20,28},{24,16},{28,20},{1,9},{5... | collective-permute-start | bytes 786440 | tf_op jit(solution)/shard_map/ppermute | solution.py:339
  62.6 2.1 %collective-permute-done.15.refs_1_ = bf16[2,4,128,128]{3,2,1,0:T(8,128)(2,1)S(1)} collective-permute-done((bf16[2,4,128,128]{3,2,1,0:T(8,128)(2,1)S(1)}, bf16[2,4,128,128]{3,2,1,0:T(8,128)(2,1)S(1)}, u32[]{:S(2)}, u32[]{:S(2)}) %collective-permute-start.15) | collective-permute-done | bytes 262176 | tf_op jit(solution)/shard_map/ppermute | solution.py:339
  66.0 3.1 %collective-permute-done.14.refs_1_ = bf16[1,4,128,128]{3,2,1,0:T(8,128)(2,1)S(1)} collective-permute-done((bf16[1,4,128,128]{3,2,1,0:T(8,128)(2,1)S(1)}, bf16[1,4,128,128]{3,2,1,0:T(8,128)(2,1)S(1)}, u32[]{:S(2)}, u32[]{:S(2)}) %collective-permute-start.14) | collective-permute-done | bytes 131104 | tf_op jit(solution)/shard_map/ppermute | solution.py:339
  70.5 0.9 down.10
  72.0 1.3 %collective-permute-start.24 = (bf16[2,4,128,128]{3,2,1,0:T(8,128)(2,1)S(1)}, bf16[2,4,128,128]{3,2,1,0:T(8,128)(2,1)S(1)}, u32[]{:S(2)}, u32[]{:S(2)}) collective-permute-start(bf16[2,4,128,128]{3,2,1,0:T(8,128)(2,1)S(1)} %get-tuple-element.151), channel_id=1, source_target_pairs={{0,2},{1,3},{2,0},{3,1},{4,6},{5,7},{6,4},{7,5},{8,10},{9,11},{10,... | collective-permute-start | bytes 786440 | tf_op jit(solution)/shard_map/ppermute | solution.py:337
  73.2 1.1 collective-permute-done.22.refs_1_
  75.0 1.4 %collective-permute-start.29 = (bf16[2,4,128,128]{3,2,1,0:T(8,128)(2,1)S(1)}, bf16[2,4,128,128]{3,2,1,0:T(8,128)(2,1)S(1)}, u32[]{:S(2)}, u32[]{:S(2)}) collective-permute-start(bf16[2,4,128,128]{3,2,1,0:T(8,128)(2,1)S(1)} %get-tuple-element.160), channel_id=1, source_target_pairs={{0,2},{1,3},{2,0},{3,1},{4,6},{5,7},{6,4},{7,5},{8,10},{9,11},{10,... | collective-permute-start | bytes 786440 | tf_op jit(solution)/shard_map/ppermute | solution.py:337
  76.4 1.4 %collective-permute-start.16 = (bf16[1,4,128,128]{3,2,1,0:T(8,128)(2,1)S(1)}, bf16[1,4,128,128]{3,2,1,0:T(8,128)(2,1)S(1)}, u32[]{:S(2)}, u32[]{:S(2)}) collective-permute-start(bf16[1,4,128,128]{3,2,1,0:T(8,128)(2,1)S(1)} %get-tuple-element.137), channel_id=1, source_target_pairs={{0,16},{4,20},{8,24},{12,28},{16,0},{20,4},{24,8},{28,12},{1,17},{... | collective-permute-start | bytes 393224 | tf_op jit(solution)/shard_map/ppermute | solution.py:339
  77.8 7.3 %grads.4 = (bf16[128,64,128]{2,1,0:T(8,128)(2,1)}, bf16[128,64,128]{2,1,0:T(8,128)(2,1)}, bf16[128,64,128]{2,1,0:T(8,128)(2,1)}, f32[8,128]{1,0:T(8,128)S(1)}) custom-call(s32[2]{0:T(128)S(1)} %copy-done.7, s32[16]{0:T(128)S(1)} %copy-done.6, bf16[4,16,128,128]{3,2,1,0:T(8,128)(2,1)S(1)} %copy-done.3, ...), custom_call_target="tpu_custom_call" | custom-call | flops 1 | bytes 20295000 | tf_op jit(solution)/shard_map/grads/pallas_call | solution.py:195
  85.2 0.8 collective-permute-done.16.refs_1_
  87.5 0.9 down.13
  89.5 0.8 down.14
  91.4 7.3 %grads.5 = (bf16[128,64,128]{2,1,0:T(8,128)(2,1)}, bf16[128,64,128]{2,1,0:T(8,128)(2,1)}, bf16[128,64,128]{2,1,0:T(8,128)(2,1)}, f32[8,128]{1,0:T(8,128)S(1)}) custom-call(s32[2]{0:T(128)S(1)} %copy-done.7, s32[16]{0:T(128)S(1)} %copy-done.6, bf16[4,16,128,128]{3,2,1,0:T(8,128)(2,1)S(1)} %copy-done.2, ...), custom_call_target="tpu_custom_call", output_to_operand_aliasing={{0}: (8, {}), {1}: (9, {}), {2}: (10, {})} | custom-call | flops 1 | bytes 20295000 | tf_op jit(solution)/shard_map/grads/pallas_call | solution.py:195
  98.8 1.1 down.15
  100.9 7.3 %grads.6 = (bf16[128,64,128]{2,1,0:T(8,128)(2,1)}, bf16[128,64,128]{2,1,0:T(8,128)(2,1)}, bf16[128,64,128]{2,1,0:T(8,128)(2,1)}, f32[8,128]{1,0:T(8,128)S(1)}) custom-call(s32[2]{0:T(128)S(1)} %copy-done.7, s32[16]{0:T(128)S(1)} %copy-done.6, ...), custom_call_target="tpu_custom_call", output_to_operand_aliasing={{0}: (8, {}), {1}: (9, {}), {2}: (10, {})} | custom-call | flops 1 | bytes 20295000 | tf_op jit(solution)/shard_map/grads/pallas_call | solution.py:195
  108.3 7.9 %grads.7 = (bf16[128,64,128]{2,1,0:T(8,128)(2,1)}, bf16[128,64,128]{2,1,0:T(8,128)(2,1)}, bf16[128,64,128]{2,1,0:T(8,128)(2,1)}, f32[8,128]{1,0:T(8,128)}) custom-call(s32[2]{0:T(128)S(1)} %copy-done.7, s32[16]{0:T(128)S(1)} %copy-done.6, bf16[4,16,128,128]{3,2,1,0:T(8,128)(2,1)S(1)} %copy-done.4, ...), custom_call_target="tpu_custom_call", output_to_operand_aliasing={{0}: (8, {}), {1}: (9, {}), {2}: (10, {})} | custom-call | flops 1 | bytes 20295000 | tf_op jit(solution)/shard_map/grads/pallas_call | solution.py:195
  (91 shorter events, 23.1 us)
Async XLA Ops:
  10.0 9.1 %collective-permute-start.1 = (bf16[2,2,8,128,128]{4,3,2,1,0:T(8,128)(2,1)}, bf16[2,2,8,128,128]{4,3,2,1,0:T(8,128)(2,1)S(1)}, u32[]{:S(2)}, u32[]{:S(2)}) collective-permute-start(bf16[2,2,8,128,128]{4,3,2,1,0:T(8,128)(2,1)} %get-tuple-element.98), channel_id=1, source_target_pairs={{0,1},{1,0},{2,3},{3,2},{4,5},{5,4},{6,7},{7,6},{8,9},{9,8},{10,11... | collective-permute-start | bytes 3145736 | tf_op jit(solution)/shard_map/ppermute | solution.py:337
  19.0 13.7 %collective-permute-start = (bf16[2,2,8,128,128]{4,3,2,1,0:T(8,128)(2,1)S(1)}, bf16[2,2,8,128,128]{4,3,2,1,0:T(8,128)(2,1)S(1)}, u32[]{:S(2)}, u32[]{:S(2)}) collective-permute-start(bf16[2,2,8,128,128]{4,3,2,1,0:T(8,128)(2,1)S(1)} %get-tuple-element.97), channel_id=1, source_target_pairs={{0,1},{1,0},{2,3},{3,2},{4,5},{5,4},{6,7},{7,6},{8,9},{9,8},{10,11... | collective-permute-start | bytes 3145736 | tf_op jit(solution)/shard_map/ppermute | solution.py:337
  19.8 10.1 %collective-permute-start.2 = (bf16[2,4,128,128]{3,2,1,0:T(8,128)(2,1)S(1)}, bf16[2,4,128,128]{3,2,1,0:T(8,128)(2,1)S(1)}, u32[]{:S(2)}, u32[]{:S(2)}) collective-permute-start(bf16[2,4,128,128]{3,2,1,0:T(8,128)(2,1)S(1)} %get-tuple-element.101), channel_id=1, source_target_pairs={{0,2},{1,3},{2,0},{3,1},{4,6},{5,7},{6,4},{7,5},{8,10},{9,11},{10,... | collective-permute-start | bytes 786440 | tf_op jit(solution)/shard_map/ppermute | solution.py:337
  23.5 12.0 %collective-permute-start.4 = (bf16[2,4,128,128]{3,2,1,0:T(8,128)(2,1)S(1)}, bf16[2,4,128,128]{3,2,1,0:T(8,128)(2,1)S(1)}, u32[]{:S(2)}, u32[]{:S(2)}) collective-permute-start(bf16[2,4,128,128]{3,2,1,0:T(8,128)(2,1)S(1)} %get-tuple-element.106), channel_id=1, source_target_pairs={{0,2},{1,3},{2,0},{3,1},{4,6},{5,7},{6,4},{7,5},{8,10},{9,11},{10,... | collective-permute-start | bytes 786440 | tf_op jit(solution)/shard_map/ppermute | solution.py:337
  30.5 7.8 %collective-permute-start.3 = (bf16[2,4,128,128]{3,2,1,0:T(8,128)(2,1)S(1)}, bf16[2,4,128,128]{3,2,1,0:T(8,128)(2,1)S(1)}, u32[]{:S(2)}, u32[]{:S(2)}) collective-permute-start(bf16[2,4,128,128]{3,2,1,0:T(8,128)(2,1)S(1)} %get-tuple-element.105), channel_id=1, source_target_pairs={{0,4},{4,0},{8,12},{12,8},{16,20},{20,16},{24,28},{28,24},{1,5},{5... | collective-permute-start | bytes 786440 | tf_op jit(solution)/shard_map/ppermute | solution.py:339
  33.4 9.5 %collective-permute-start.8 = (bf16[2,4,128,128]{3,2,1,0:T(8,128)(2,1)S(1)}, bf16[2,4,128,128]{3,2,1,0:T(8,128)(2,1)S(1)}, u32[]{:S(2)}, u32[]{:S(2)}) collective-permute-start(bf16[2,4,128,128]{3,2,1,0:T(8,128)(2,1)S(1)} %get-tuple-element.115), channel_id=1, source_target_pairs={{0,2},{1,3},{2,0},{3,1},{4,6},{5,7},{6,4},{7,5},{8,10},{9,11},{10,... | collective-permute-start | bytes 786440 | tf_op jit(solution)/shard_map/ppermute | solution.py:337
  36.1 8.3 %collective-permute-start.7 = (bf16[2,4,128,128]{3,2,1,0:T(8,128)(2,1)S(1)}, bf16[2,4,128,128]{3,2,1,0:T(8,128)(2,1)S(1)}, u32[]{:S(2)}, u32[]{:S(2)}) collective-permute-start(bf16[2,4,128,128]{3,2,1,0:T(8,128)(2,1)S(1)} %get-tuple-element.114), channel_id=1, source_target_pairs={{0,4},{4,0},{8,12},{12,8},{16,20},{20,16},{24,28},{28,24},{1,5},{5... | collective-permute-start | bytes 786440 | tf_op jit(solution)/shard_map/ppermute | solution.py:339
  39.0 7.3 %collective-permute-start.6 = (bf16[2,4,128,128]{3,2,1,0:T(8,128)(2,1)S(1)}, bf16[2,4,128,128]{3,2,1,0:T(8,128)(2,1)S(1)}, u32[]{:S(2)}, u32[]{:S(2)}) collective-permute-start(bf16[2,4,128,128]{3,2,1,0:T(8,128)(2,1)S(1)} %get-tuple-element.113), channel_id=1, source_target_pairs={{0,8},{4,12},{8,0},{12,4},{16,24},{20,28},{24,16},{28,20},{1,9},{5... | collective-permute-start | bytes 786440 | tf_op jit(solution)/shard_map/ppermute | solution.py:339
  41.3 6.4 %collective-permute-start.5 = (bf16[2,4,128,128]{3,2,1,0:T(8,128)(2,1)S(1)}, bf16[2,4,128,128]{3,2,1,0:T(8,128)(2,1)S(1)}, u32[]{:S(2)}, u32[]{:S(2)}) collective-permute-start(bf16[2,4,128,128]{3,2,1,0:T(8,128)(2,1)S(1)} %get-tuple-element.111), channel_id=1, source_target_pairs={{0,2},{1,3},{2,0},{3,1},{4,6},{5,7},{6,4},{7,5},{8,10},{9,11},{10,... | collective-permute-start | bytes 786440 | tf_op jit(solution)/shard_map/ppermute | solution.py:337
  43.5 8.5 %collective-permute-start.12 = (bf16[2,4,128,128]{3,2,1,0:T(8,128)(2,1)S(1)}, bf16[2,4,128,128]{3,2,1,0:T(8,128)(2,1)S(1)}, u32[]{:S(2)}, u32[]{:S(2)}) collective-permute-start(bf16[2,4,128,128]{3,2,1,0:T(8,128)(2,1)S(1)} %get-tuple-element.124), channel_id=1, source_target_pairs={{0,4},{4,0},{8,12},{12,8},{16,20},{20,16},{24,28},{28,24},{1,5},{5... | collective-permute-start | bytes 786440 | tf_op jit(solution)/shard_map/ppermute | solution.py:339
  45.1 10.6 %collective-permute-start.11 = (bf16[2,4,128,128]{3,2,1,0:T(8,128)(2,1)S(1)}, bf16[2,4,128,128]{3,2,1,0:T(8,128)(2,1)S(1)}, u32[]{:S(2)}, u32[]{:S(2)}) collective-permute-start(bf16[2,4,128,128]{3,2,1,0:T(8,128)(2,1)S(1)} %get-tuple-element.123), channel_id=1, source_target_pairs={{0,8},{4,12},{8,0},{12,4},{16,24},{20,28},{24,16},{28,20},{1,9},{5... | collective-permute-start | bytes 786440 | tf_op jit(solution)/shard_map/ppermute | solution.py:339
  48.4 8.7 %collective-permute-start.9 = (bf16[2,4,128,128]{3,2,1,0:T(8,128)(2,1)S(1)}, bf16[2,4,128,128]{3,2,1,0:T(8,128)(2,1)S(1)}, u32[]{:S(2)}, u32[]{:S(2)}) collective-permute-start(bf16[2,4,128,128]{3,2,1,0:T(8,128)(2,1)S(1)} %get-tuple-element.120), channel_id=1, source_target_pairs={{0,4},{4,0},{8,12},{12,8},{16,20},{20,16},{24,28},{28,24},{1,5},{5... | collective-permute-start | bytes 786440 | tf_op jit(solution)/shard_map/ppermute | solution.py:339
  49.3 7.0 %collective-permute-start.10 = (bf16[1,4,128,128]{3,2,1,0:T(8,128)(2,1)S(1)}, bf16[1,4,128,128]{3,2,1,0:T(8,128)(2,1)S(1)}, u32[]{:S(2)}, u32[]{:S(2)}) collective-permute-start(bf16[1,4,128,128]{3,2,1,0:T(8,128)(2,1)S(1)} %get-tuple-element.121), channel_id=1, source_target_pairs={{0,16},{4,20},{8,24},{12,28},{16,0},{20,4},{24,8},{28,12},{1,17},{... | collective-permute-start | bytes 393224 | tf_op jit(solution)/shard_map/ppermute | solution.py:339
  52.6 12.1 %collective-permute-start.15 = (bf16[2,4,128,128]{3,2,1,0:T(8,128)(2,1)S(1)}, bf16[2,4,128,128]{3,2,1,0:T(8,128)(2,1)S(1)}, u32[]{:S(2)}, u32[]{:S(2)}) collective-permute-start(bf16[2,4,128,128]{3,2,1,0:T(8,128)(2,1)S(1)} %get-tuple-element.133), channel_id=1, source_target_pairs={{0,8},{4,12},{8,0},{12,4},{16,24},{20,28},{24,16},{28,20},{1,9},{5... | collective-permute-start | bytes 786440 | tf_op jit(solution)/shard_map/ppermute | solution.py:339
  57.8 12.1 %collective-permute-start.13 = (bf16[2,4,128,128]{3,2,1,0:T(8,128)(2,1)S(1)}, bf16[2,4,128,128]{3,2,1,0:T(8,128)(2,1)S(1)}, u32[]{:S(2)}, u32[]{:S(2)}) collective-permute-start(bf16[2,4,128,128]{3,2,1,0:T(8,128)(2,1)S(1)} %get-tuple-element.129), channel_id=1, source_target_pairs={{0,8},{4,12},{8,0},{12,4},{16,24},{20,28},{24,16},{28,20},{1,9},{5... | collective-permute-start | bytes 786440 | tf_op jit(solution)/shard_map/ppermute | solution.py:339
  61.0 9.5 %collective-permute-start.17 = (bf16[2,4,128,128]{3,2,1,0:T(8,128)(2,1)S(1)}, bf16[2,4,128,128]{3,2,1,0:T(8,128)(2,1)S(1)}, u32[]{:S(2)}, u32[]{:S(2)}) collective-permute-start(bf16[2,4,128,128]{3,2,1,0:T(8,128)(2,1)S(1)} %get-tuple-element.139), channel_id=1, source_target_pairs={{0,2},{1,3},{2,0},{3,1},{4,6},{5,7},{6,4},{7,5},{8,10},{9,11},{10,... | collective-permute-start | bytes 786440 | tf_op jit(solution)/shard_map/ppermute | solution.py:337
  61.8 7.3 %collective-permute-start.14 = (bf16[1,4,128,128]{3,2,1,0:T(8,128)(2,1)S(1)}, bf16[1,4,128,128]{3,2,1,0:T(8,128)(2,1)S(1)}, u32[]{:S(2)}, u32[]{:S(2)}) collective-permute-start(bf16[1,4,128,128]{3,2,1,0:T(8,128)(2,1)S(1)} %get-tuple-element.131), channel_id=1, source_target_pairs={{0,16},{4,20},{8,24},{12,28},{16,0},{20,4},{24,8},{28,12},{1,17},{... | collective-permute-start | bytes 393224 | tf_op jit(solution)/shard_map/ppermute | solution.py:339
  65.4 8.9 %collective-permute-start.22 = (bf16[1,4,128,128]{3,2,1,0:T(8,128)(2,1)S(1)}, bf16[1,4,128,128]{3,2,1,0:T(8,128)(2,1)S(1)}, u32[]{:S(2)}, u32[]{:S(2)}) collective-permute-start(bf16[1,4,128,128]{3,2,1,0:T(8,128)(2,1)S(1)} %get-tuple-element.145), channel_id=1, source_target_pairs={{0,16},{4,20},{8,24},{12,28},{16,0},{20,4},{24,8},{28,12},{1,17},{... | collective-permute-start | bytes 393224 | tf_op jit(solution)/shard_map/ppermute | solution.py:339
  71.4 5.0 %collective-permute-start.18 = (bf16[1,4,128,128]{3,2,1,0:T(8,128)(2,1)S(1)}, bf16[1,4,128,128]{3,2,1,0:T(8,128)(2,1)S(1)}, u32[]{:S(2)}, u32[]{:S(2)}) collective-permute-start(bf16[1,4,128,128]{3,2,1,0:T(8,128)(2,1)S(1)} %get-tuple-element.141), channel_id=1, source_target_pairs={{0,1},{1,0},{2,3},{3,2},{4,5},{5,4},{6,7},{7,6},{8,9},{9,8},{10,11... | collective-permute-start | bytes 393224 | tf_op jit(solution)/shard_map/ppermute | solution.py:337
  71.5 4.9 %collective-permute-start.19 = (bf16[1,4,128,128]{3,2,1,0:T(8,128)(2,1)S(1)}, bf16[1,4,128,128]{3,2,1,0:T(8,128)(2,1)S(1)}, u32[]{:S(2)}, u32[]{:S(2)}) collective-permute-start(bf16[1,4,128,128]{3,2,1,0:T(8,128)(2,1)S(1)} %get-tuple-element.142), channel_id=1, source_target_pairs={{0,1},{1,0},{2,3},{3,2},{4,5},{5,4},{6,7},{7,6},{8,9},{9,8},{10,11... | collective-permute-start | bytes 393224 | tf_op jit(solution)/shard_map/ppermute | solution.py:337
  72.0 15.6 %collective-permute-start.24 = (bf16[2,4,128,128]{3,2,1,0:T(8,128)(2,1)S(1)}, bf16[2,4,128,128]{3,2,1,0:T(8,128)(2,1)S(1)}, u32[]{:S(2)}, u32[]{:S(2)}) collective-permute-start(bf16[2,4,128,128]{3,2,1,0:T(8,128)(2,1)S(1)} %get-tuple-element.151), channel_id=1, source_target_pairs={{0,2},{1,3},{2,0},{3,1},{4,6},{5,7},{6,4},{7,5},{8,10},{9,11},{10,... | collective-permute-start | bytes 786440 | tf_op jit(solution)/shard_map/ppermute | solution.py:337
  75.0 14.0 %collective-permute-start.29 = (bf16[2,4,128,128]{3,2,1,0:T(8,128)(2,1)S(1)}, bf16[2,4,128,128]{3,2,1,0:T(8,128)(2,1)S(1)}, u32[]{:S(2)}, u32[]{:S(2)}) collective-permute-start(bf16[2,4,128,128]{3,2,1,0:T(8,128)(2,1)S(1)} %get-tuple-element.160), channel_id=1, source_target_pairs={{0,2},{1,3},{2,0},{3,1},{4,6},{5,7},{6,4},{7,5},{8,10},{9,11},{10,... | collective-permute-start | bytes 786440 | tf_op jit(solution)/shard_map/ppermute | solution.py:337
  76.4 9.6 %collective-permute-start.16 = (bf16[1,4,128,128]{3,2,1,0:T(8,128)(2,1)S(1)}, bf16[1,4,128,128]{3,2,1,0:T(8,128)(2,1)S(1)}, u32[]{:S(2)}, u32[]{:S(2)}) collective-permute-start(bf16[1,4,128,128]{3,2,1,0:T(8,128)(2,1)S(1)} %get-tuple-element.137), channel_id=1, source_target_pairs={{0,16},{4,20},{8,24},{12,28},{16,0},{20,4},{24,8},{28,12},{1,17},{... | collective-permute-start | bytes 393224 | tf_op jit(solution)/shard_map/ppermute | solution.py:339
  86.8 12.0 %collective-permute-start.23 = (bf16[2,4,128,128]{3,2,1,0:T(8,128)(2,1)S(1)}, bf16[2,4,128,128]{3,2,1,0:T(8,128)(2,1)S(1)}, u32[]{:S(2)}, u32[]{:S(2)}) collective-permute-start(bf16[2,4,128,128]{3,2,1,0:T(8,128)(2,1)S(1)} %get-tuple-element.149), channel_id=1, source_target_pairs={{0,2},{1,3},{2,0},{3,1},{4,6},{5,7},{6,4},{7,5},{8,10},{9,11},{10,... | collective-permute-start | bytes 786440 | tf_op jit(solution)/shard_map/ppermute | solution.py:337
  90.3 9.6 %collective-permute-start.34 = (bf16[1,4,128,128]{3,2,1,0:T(8,128)(2,1)S(1)}, bf16[1,4,128,128]{3,2,1,0:T(8,128)(2,1)S(1)}, u32[]{:S(2)}, u32[]{:S(2)}) collective-permute-start(bf16[1,4,128,128]{3,2,1,0:T(8,128)(2,1)S(1)} %get-tuple-element.169), channel_id=1, source_target_pairs={{0,1},{1,0},{2,3},{3,2},{4,5},{5,4},{6,7},{7,6},{8,9},{9,8},{10,11... | collective-permute-start | bytes 393224 | tf_op jit(solution)/shard_map/ppermute | solution.py:337
  90.5 9.9 %collective-permute-start.35 = (bf16[1,4,128,128]{3,2,1,0:T(8,128)(2,1)S(1)}, bf16[1,4,128,128]{3,2,1,0:T(8,128)(2,1)S(1)}, u32[]{:S(2)}, u32[]{:S(2)}) collective-permute-start(bf16[1,4,128,128]{3,2,1,0:T(8,128)(2,1)S(1)} %get-tuple-element.170), channel_id=1, source_target_pairs={{0,1},{1,0},{2,3},{3,2},{4,5},{5,4},{6,7},{7,6},{8,9},{9,8},{10,11... | collective-permute-start | bytes 393224 | tf_op jit(solution)/shard_map/ppermute | solution.py:337
  90.9 9.6 %collective-permute-start.36 = (bf16[1,4,128,128]{3,2,1,0:T(8,128)(2,1)S(1)}, bf16[1,4,128,128]{3,2,1,0:T(8,128)(2,1)S(1)}, u32[]{:S(2)}, u32[]{:S(2)}) collective-permute-start(bf16[1,4,128,128]{3,2,1,0:T(8,128)(2,1)S(1)} %get-tuple-element.171), channel_id=1, source_target_pairs={{0,1},{1,0},{2,3},{3,2},{4,5},{5,4},{6,7},{7,6},{8,9},{9,8},{10,11... | collective-permute-start | bytes 393224 | tf_op jit(solution)/shard_map/ppermute | solution.py:337
  91.0 9.9 %collective-permute-start.37 = (bf16[1,4,128,128]{3,2,1,0:T(8,128)(2,1)S(1)}, bf16[1,4,128,128]{3,2,1,0:T(8,128)(2,1)S(1)}, u32[]{:S(2)}, u32[]{:S(2)}) collective-permute-start(bf16[1,4,128,128]{3,2,1,0:T(8,128)(2,1)S(1)} %get-tuple-element.172), channel_id=1, source_target_pairs={{0,1},{1,0},{2,3},{3,2},{4,5},{5,4},{6,7},{7,6},{8,9},{9,8},{10,11... | collective-permute-start | bytes 393224 | tf_op jit(solution)/shard_map/ppermute | solution.py:337
  99.8 8.4 %collective-permute-start.30 = (bf16[1,4,128,128]{3,2,1,0:T(8,128)(2,1)S(1)}, bf16[1,4,128,128]{3,2,1,0:T(8,128)(2,1)S(1)}, u32[]{:S(2)}, u32[]{:S(2)}) collective-permute-start(bf16[1,4,128,128]{3,2,1,0:T(8,128)(2,1)S(1)} %get-tuple-element.164), channel_id=1, source_target_pairs={{0,1},{1,0},{2,3},{3,2},{4,5},{5,4},{6,7},{7,6},{8,9},{9,8},{10,11... | collective-permute-start | bytes 393224 | tf_op jit(solution)/shard_map/ppermute | solution.py:337
  100.0 8.3 %collective-permute-start.31 = (bf16[1,4,128,128]{3,2,1,0:T(8,128)(2,1)S(1)}, bf16[1,4,128,128]{3,2,1,0:T(8,128)(2,1)S(1)}, u32[]{:S(2)}, u32[]{:S(2)}) collective-permute-start(bf16[1,4,128,128]{3,2,1,0:T(8,128)(2,1)S(1)} %get-tuple-element.165), channel_id=1, source_target_pairs={{0,1},{1,0},{2,3},{3,2},{4,5},{5,4},{6,7},{7,6},{8,9},{9,8},{10,11... | collective-permute-start | bytes 393224 | tf_op jit(solution)/shard_map/ppermute | solution.py:337
  100.4 7.9 %collective-permute-start.32 = (bf16[1,4,128,128]{3,2,1,0:T(8,128)(2,1)S(1)}, bf16[1,4,128,128]{3,2,1,0:T(8,128)(2,1)S(1)}, u32[]{:S(2)}, u32[]{:S(2)}) collective-permute-start(bf16[1,4,128,128]{3,2,1,0:T(8,128)(2,1)S(1)} %get-tuple-element.166), channel_id=1, source_target_pairs={{0,1},{1,0},{2,3},{3,2},{4,5},{5,4},{6,7},{7,6},{8,9},{9,8},{10,11... | collective-permute-start | bytes 393224 | tf_op jit(solution)/shard_map/ppermute | solution.py:337
  100.5 7.8 %collective-permute-start.33 = (bf16[1,4,128,128]{3,2,1,0:T(8,128)(2,1)S(1)}, bf16[1,4,128,128]{3,2,1,0:T(8,128)(2,1)S(1)}, u32[]{:S(2)}, u32[]{:S(2)}) collective-permute-start(bf16[1,4,128,128]{3,2,1,0:T(8,128)(2,1)S(1)} %get-tuple-element.167), channel_id=1, source_target_pairs={{0,1},{1,0},{2,3},{3,2},{4,5},{5,4},{6,7},{7,6},{8,9},{9,8},{10,11... | collective-permute-start | bytes 393224 | tf_op jit(solution)/shard_map/ppermute | solution.py:337
  (14 other events, 62.5 us)

commit v5 on v4

--- a/solution.py
+++ b/solution.py
@@ -101,8 +101,36 @@
                 send_ref[j, 1, r - half] = state_b.astype(B16)
 
 
-def grads_kernel(chunk, scaling, place_ref, len_ref, head_ref, mine_ref, *refs):
+def _live(len_ref, first, n, scaling, later):
+    t = lax.broadcasted_iota(jnp.int32, (n, n), later) + first
+    s = lax.broadcasted_iota(jnp.int32, (n, n), 1 - later) + first
+    begin = jnp.zeros((n, n), jnp.int32)
+    total = jnp.int32(0)
+    for k in range(len_ref.shape[0]):
+        total = total + len_ref[k]
+        begin = jnp.where(t >= total, total, begin)
+    return jnp.where((s <= t) & (s >= begin), F32(scaling), F32(0.0))
+
+
+def inner_kernel(scaling, place_ref, len_ref, head_ref, *refs):
+    out = refs[-1]
+    _, heads, n, d = head_ref.shape
+    first = place_ref[0] * n
+    down = _live(len_ref, first, n, scaling, 0)
+    across = _live(len_ref, first, n, scaling, 1)
+    for h in range(heads):
+        query, key, value, grad = (head_ref[i, h] for i in range(4))
+        ts = (_dot(grad, value, 1, 1) * down).astype(B16)
+        st = (_dot(value, grad, 1, 1) * across).astype(B16)
+        sc = (_dot(key, query, 1, 1) * across).astype(B16)
+        out[0, h] = _dot(ts, key, 1, 0)
+        out[1, h] = _dot(st, query, 1, 0)
+        out[2, h] = _dot(sc, grad, 1, 0)
+
+
+def grads_kernel(chunk, scaling, early, place_ref, len_ref, head_ref, mine_ref, *refs):
     got, outs, token_ref = refs[:4], refs[-11:-8], refs[-8]
+    inner_ref = refs[4] if early else None
     wide, slabs, sems = refs[-7:-4], refs[-4:-1], refs[-1]
     token_ref[...] = jnp.zeros(token_ref.shape, token_ref.dtype)
     _, heads, n, d = head_ref.shape
@@ -114,46 +142,37 @@
     lead = jnp.where(row < stop, F32(1.0), F32(0.0))
     last = jnp.where(row >= start, F32(1.0), F32(0.0))
     last16 = last.astype(B16)
-
-    def live(later):
-        t = lax.broadcasted_iota(jnp.int32, (n, n), later) + first
-        s = lax.broadcasted_iota(jnp.int32, (n, n), 1 - later) + first
-        begin = jnp.zeros((n, n), jnp.int32)
-        total = jnp.int32(0)
-        for k in range(len_ref.shape[0]):
-            total = total + len_ref[k]
-            begin = jnp.where(t >= total, total, begin)
-        return jnp.where((s <= t) & (s >= begin), F32(scaling), F32(0.0))
-
-    down, across = live(0), live(1)
     cat = jnp.concatenate
-
-    def query_part(query, key, value, grad, state_a, state_b):
-        x = _dot(grad, cat([value, state_a], axis=0), 1, 1)
-        ts = (x[:, :n] * down).astype(B16)
-        return _dot(ts, key, 1, 0) + x[:, n:] * lead
-
-    def key_part(query, key, value, grad, state_a, state_b):
-        y = _dot(value, cat([grad, state_b], axis=0), 1, 1)
-        st = (y[:, :n] * across).astype(B16)
-        return _dot(st, query, 1, 0) + y[:, n:] * last
-
-    def value_part(query, key, value, grad, state_a, state_b):
-        sc = (_dot(key, query, 1, 1) * across).astype(B16)
-        return _dot(cat([sc, key * last16], axis=1), cat([grad, state_b], axis=0), 1, 0)
-
+    if not early:
+        down = _live(len_ref, first, n, scaling, 0)
+        across = _live(len_ref, first, n, scaling, 1)
+    for r in range(heads):
+        h = r ^ flip
+        if r < half:
+            state_a, state_b = mine_ref[0, r], mine_ref[1, r]
+        else:
+            side, o = divmod(r - half, half // 2)
+            state_a, state_b = got[side][0, o], got[2 + side][0, o]
+        query, key, value, grad = (head_ref[i, h] for i in range(4))
+        at = pl.ds(h, n, stride=heads)
+        if early:
+            wide[0][at, :] = inner_ref[0, h] + _dot(grad, state_a, 1, 1) * lead
+            wide[1][at, :] = inner_ref[1, h] + _dot(value, state_b, 1, 1) * last
+            wide[2][at, :] = inner_ref[2, h] + _dot(key, state_b, 1, 0) * last
+        else:
+            x = _dot(grad, cat([value, state_a], axis=0), 1, 1)
+            y = _dot(value, cat([grad, state_b], axis=0), 1, 1)
+            z = _dot(key, query, 1, 1)
+            ts = (x[:, :n] * down).astype(B16)
+            st = (y[:, :n] * across).astype(B16)
+            sc = (z * across).astype(B16)
+            wide[0][at, :] = _dot(ts, key, 1, 0) + x[:, n:] * lead
+            wide[1][at, :] = _dot(st, query, 1, 0) + y[:, n:] * last
+            wide[2][at, :] = _dot(
+                cat([sc, key * last16], axis=1), cat([grad, state_b], axis=0), 1, 0
+            )
     copies = []
-    for i, part in enumerate((query_part, key_part, value_part)):
-        scr, slab, out = wide[i], slabs[i], outs[i]
-        for r in range(heads):
-            h = r ^ flip
-            if r < half:
-                states = mine_ref[0, r], mine_ref[1, r]
-            else:
-                side, o = divmod(r - half, half // 2)
-                states = got[side][0, o], got[2 + side][0, o]
-            tokens = [head_ref[a, h] for a in range(4)]
-            scr[pl.ds(h, n, stride=heads), :] = part(*tokens, *states)
+    for i, (scr, slab, out) in enumerate(zip(wide, slabs, outs)):
         slab[...] = scr[...].reshape(n, heads, d).astype(B16)
         copy = pltpu.make_async_copy(
             slab, out.at[:, pl.ds(chunk * heads, heads), :], sems.at[i]
@@ -181,7 +200,7 @@
             for level in range(self.head_bits)
         )
         self.place = jnp.stack([device, flip]).astype(jnp.int32)
-        self.index = {}
+        self.index, self.early = {}, {}
         for level in range(self.levels):
             names = ["up_own", "up_got"]
             if level < self.head_bits:
@@ -234,15 +253,26 @@
             self.scalars, *got = got
         return got[:count], got[count : 2 * count], self.swap(got[-1], 0)
 
-    def grads(self, chunk, heads, mine, got, before, after):
+    def inner(self, heads, after):
+        return self.call(
+            functools.partial(inner_kernel, self.scaling),
+            "inner",
+            [self.place, self.lengths, heads, *after],
+            [IN_SMEM] * 2 + [IN_VMEM] + [ANYWHERE] * len(after),
+            jax.ShapeDtypeStruct((3, self.part, self.n, self.d), F32),
+            IN_VMEM,
+            [],
+        )
+
+    def grads(self, chunk, heads, mine, got, inner, before, after):
         n, d, part = self.n, self.d, self.part
         out = jax.ShapeDtypeStruct((n, self.total, d), B16)
         return self.call(
-            functools.partial(grads_kernel, chunk, self.scaling),
+            functools.partial(grads_kernel, chunk, self.scaling, len(inner) > 0),
             "grads",
-            [self.place, self.lengths, heads, mine, *got, *before, *after],
+            [self.place, self.lengths, heads, mine, *got, *inner, *before, *after],
             [IN_SMEM] * 2
-            + [IN_VMEM] * 6
+            + [IN_VMEM] * (6 + len(inner))
             + [IN_HBM] * len(before)
             + [ANYWHERE] * len(after),
             (out, out, out, jax.ShapeDtypeStruct((8, 128), F32)),
@@ -250,8 +280,7 @@
             [pltpu.VMEM((n * part, d), F32)] * 3
             + [pltpu.VMEM((n, part, d), B16)] * 3
             + [pltpu.SemaphoreType.DMA((3,))],
-            cost=5500,
-            input_output_aliases={8 + i: i for i in range(len(before))},
+            input_output_aliases={8 + len(inner) + i: i for i in range(len(before))},
         )
 
     def weights(self, place_ref, len_ref, out):
@@ -325,6 +354,9 @@
         spare = line[-2:] if chunks > 1 else []
         line = line[: len(line) - len(spare)]
         line += [(0, fill), *spare[:-1], (0, final), *spare[-1:]]
+        if chunks > 2:
+            line.insert(2, (0, -1))
+            line.insert(len(line) - 6, (1, -1))
         for chunk in range(1, chunks):
             line += [(chunk, fill)] if chunk == 1 else []
             line += [(chunk + 1, fill)] if chunk + 1 < chunks else []
@@ -451,10 +483,16 @@
 
         def final(before, after):
             *outs, token = self.grads(
-                chunk, here["heads"], here["state"], here["got"], before, after
+                chunk, here["heads"], here["state"], here["got"], here["inner"], before, after
             )
             return outs, token
 
+        def early(after):
+            here["inner"] = (self.inner(here["heads"], after),)
+            return here["inner"][0]
+
+        here["inner"] = ()
+        self.early[chunk] = early
         steps = [functools.partial(up, level) for level in range(bits)]
         steps += [functools.partial(across, level) for level in range(bits, last)]
         steps += [functools.partial(down, level) for level in reversed(range(bits))]
@@ -475,7 +513,9 @@
             stages.append(plan.stages(chunk, keeps[spot], tokens[spot], swapped, spot))
     outs, count = (), len(stages[0])
     for chunk, stage in plan.order(count):
-        if stage + 1 < count:
+        if stage < 0:
+            after = (plan.early[chunk](after),)
+        elif stage + 1 < count:
             after = (stages[chunk][stage](after),)
         else:
             outs, token = stages[chunk][stage](outs, after)

time: 117 us -> 109 us (0.932)
  Pallas kernels: 62.9 us -> 58.8 us
  waiting for transfers between devices: 17.1 us -> 14 us
    pallas_call x30 -> x32, Pallas kernels: 62.9 us -> 58.8 us  [call(): pl.pallas_call(body, in_specs=in_specs, out_specs=out_specs, out_shape=ou...]
    ppermute x26, waiting for transfers between devices: 7.77 us -> 4.12 us  [swap(): return lax.ppermute(x, 'head', moves)]
  transfers between devices with their start and end apart: 38 -> 38, of which waited for: 9 -> 8; matrix products, arithmetic and copies ran while one was open for 0% -> 0% of each run, Pallas kernels for 40% -> 41%
where the time goes in v5:
time: 109 us
  Pallas kernels  58.8 us (54%)
  starting transfers between devices  32.9 us (30%)
  waiting for transfers between devices  14 us (13%)
  local copies, waits for them, and re-layouts  1.26 us (1%)
  between operations  1.17 us (1%)
    pallas_call x32, Pallas kernels, call(): pl.pallas_call(body, in_specs=in_specs, out_specs=out_specs, out_shape=ou...  58.8 us
    ppermute x12, starting transfers between devices, swap(): return lax.ppermute(x, 'seq', [(i, i ^ bit) for i in range(self.seq_size)])  18.2 us
    ppermute x26, starting transfers between devices, swap(): return lax.ppermute(x, 'head', moves)  14.7 us
    ppermute x12, waiting for transfers between devices, swap(): return lax.ppermute(x, 'seq', [(i, i ^ bit) for i in range(self.seq_size)])  9.9 us
    ppermute x26, waiting for transfers between devices, swap(): return lax.ppermute(x, 'head', moves)  4.12 us
  transfers between devices with their start and end apart: 38, of which 8 were waited for; matrix products, arithmetic and copies ran while one was open for 0% of the time, Pallas kernels for 41%

profile of v5, /device:TPU:0, one launch (start us, length us, event | category | flops | bytes accessed | tf_op | source)
XLA Modules:
  0.0 108.7 jit_solution(515136119794130760)
XLA Ops:
  1.2 8.7 %states.2 = (f32[44]{0:T(128)}, f32[2,8,128,128]{3,2,1,0:T(8,128)}, f32[2,8,128,128]{3,2,1,0:T(8,128)}, bf16[4,16,128,128]{3,2,1,0:T(8,128)(2,1)}, bf16[4,16,128...) custom-call(s32[2]{0:T(128)} %pad_add_fusion.place_ref, s32[16]{0:T(128)} %len_ref.15, ...), custom_call_target="tpu_custom_call" | custom-call | flops 1 | bytes 25830000 | tf_op jit(solution)/shard_map/states/pallas_call | solution.py:214
  10.5 1.2 %copy-done = f32[2,8,128,128]{3,2,1,0:T(8,128)S(1)} copy-done((f32[2,8,128,128]{3,2,1,0:T(8,128)S(1)}, f32[2,8,128,128]{3,2,1,0:T(8,128)}, u32[]{:S(2)}) %copy-start) | copy-done | bytes 1048600
  11.7 7.1 %states.3 = (f32[2,8,128,128]{3,2,1,0:T(8,128)S(1)}, f32[2,8,128,128]{3,2,1,0:T(8,128)S(1)}, bf16[4,16,128,128]{3,2,1,0:T(8,128)(2,1)S(1)}, bf16[4,16,128,128]{3...) custom-call(s32[2]{0:T(128)S(1)} %copy-done.7, s32[16]{0:T(128)S(1)} %copy-done.6, bf16[128,64,128]{2,1,0:T(8,128)(2,1)} %refs_0_.3, ...), custom_call_target="tpu_custom_call" | custom-call | flops 1 | bytes 25830000 | tf_op jit(solution)/shard_map/states/pallas_call | solution.py:214
  19.7 3.0 %collective-permute-start.2 = (bf16[2,4,128,128]{3,2,1,0:T(8,128)(2,1)S(1)}, bf16[2,4,128,128]{3,2,1,0:T(8,128)(2,1)S(1)}, u32[]{:S(2)}, u32[]{:S(2)}) collective-permute-start(bf16[2,4,128,128]{3,2,1,0:T(8,128)(2,1)S(1)} %get-tuple-element.101), channel_id=1, source_target_pairs={{0,2},{1,3},{2,0},{3,1},{4,6},{5,7},{6,4},{7,5},{8,10},{9,11},{10,... | collective-permute-start | bytes 786440 | tf_op jit(solution)/shard_map/ppermute | solution.py:369
  23.5 3.7 %inner.2.refs_2_.refs_4_ = f32[3,16,128,128]{3,2,1,0:T(8,128)S(1)} custom-call(s32[2]{0:T(128)S(1)} %copy-done.7, s32[16]{0:T(128)S(1)} %copy-done.6, bf16[4,16,128,128]{3,2,1,0:T(8,128)(2,1)S(1)} %copy-done.1, f32[2,4,128,128]{3,2,1,0:T(8,128)S(1)} %get-tuple-element.104.refs_0_.refs_2_), custom_call_target="tpu_custom_call" | custom-call | flops 1 | bytes 2583000 | tf_op jit(solution)/shard_map/inner/pallas_call | solution.py:214
  27.2 2.7 %collective-permute-done.2.refs_1_.refs_3_ = bf16[2,4,128,128]{3,2,1,0:T(8,128)(2,1)S(1)} collective-permute-done((bf16[2,4,128,128]{3,2,1,0:T(8,128)(2,1)S(1)}, bf16[2,4,128,128]{3,2,1,0:T(8,128)(2,1)S(1)}, u32[]{:S(2)}, u32[]{:S(2)}) %collective-permute-start.2) | collective-permute-done | bytes 262176 | tf_op jit(solution)/shard_map/ppermute | solution.py:369
  30.4 2.2 %collective-permute-start.3 = (bf16[2,4,128,128]{3,2,1,0:T(8,128)(2,1)S(1)}, bf16[2,4,128,128]{3,2,1,0:T(8,128)(2,1)S(1)}, u32[]{:S(2)}, u32[]{:S(2)}) collective-permute-start(bf16[2,4,128,128]{3,2,1,0:T(8,128)(2,1)S(1)} %get-tuple-element.106), channel_id=1, source_target_pairs={{0,4},{4,0},{8,12},{12,8},{16,20},{20,16},{24,28},{28,24},{1,5},{5... | collective-permute-start | bytes 786440 | tf_op jit(solution)/shard_map/ppermute | solution.py:371
  33.3 1.6 %collective-permute-start.8 = (bf16[2,4,128,128]{3,2,1,0:T(8,128)(2,1)S(1)}, bf16[2,4,128,128]{3,2,1,0:T(8,128)(2,1)S(1)}, u32[]{:S(2)}, u32[]{:S(2)}) collective-permute-start(bf16[2,4,128,128]{3,2,1,0:T(8,128)(2,1)S(1)} %get-tuple-element.116), channel_id=1, source_target_pairs={{0,2},{1,3},{2,0},{3,1},{4,6},{5,7},{6,4},{7,5},{8,10},{9,11},{10,... | collective-permute-start | bytes 786440 | tf_op jit(solution)/shard_map/ppermute | solution.py:369
  36.0 2.2 %collective-permute-start.7 = (bf16[2,4,128,128]{3,2,1,0:T(8,128)(2,1)S(1)}, bf16[2,4,128,128]{3,2,1,0:T(8,128)(2,1)S(1)}, u32[]{:S(2)}, u32[]{:S(2)}) collective-permute-start(bf16[2,4,128,128]{3,2,1,0:T(8,128)(2,1)S(1)} %get-tuple-element.115), channel_id=1, source_target_pairs={{0,4},{4,0},{8,12},{12,8},{16,20},{20,16},{24,28},{28,24},{1,5},{5... | collective-permute-start | bytes 786440 | tf_op jit(solution)/shard_map/ppermute | solution.py:371
  38.9 1.6 %collective-permute-start.6 = (bf16[2,4,128,128]{3,2,1,0:T(8,128)(2,1)S(1)}, bf16[2,4,128,128]{3,2,1,0:T(8,128)(2,1)S(1)}, u32[]{:S(2)}, u32[]{:S(2)}) collective-permute-start(bf16[2,4,128,128]{3,2,1,0:T(8,128)(2,1)S(1)} %get-tuple-element.114), channel_id=1, source_target_pairs={{0,8},{4,12},{8,0},{12,4},{16,24},{20,28},{24,16},{28,20},{1,9},{5... | collective-permute-start | bytes 786440 | tf_op jit(solution)/shard_map/ppermute | solution.py:371
  41.2 1.6 %collective-permute-start.5 = (bf16[2,4,128,128]{3,2,1,0:T(8,128)(2,1)S(1)}, bf16[2,4,128,128]{3,2,1,0:T(8,128)(2,1)S(1)}, u32[]{:S(2)}, u32[]{:S(2)}) collective-permute-start(bf16[2,4,128,128]{3,2,1,0:T(8,128)(2,1)S(1)} %get-tuple-element.112), channel_id=1, source_target_pairs={{0,2},{1,3},{2,0},{3,1},{4,6},{5,7},{6,4},{7,5},{8,10},{9,11},{10,... | collective-permute-start | bytes 786440 | tf_op jit(solution)/shard_map/ppermute | solution.py:369
  43.4 0.9 collective-permute-start.12
  45.0 1.1 %collective-permute-start.11 = (bf16[2,4,128,128]{3,2,1,0:T(8,128)(2,1)S(1)}, bf16[2,4,128,128]{3,2,1,0:T(8,128)(2,1)S(1)}, u32[]{:S(2)}, u32[]{:S(2)}) collective-permute-start(bf16[2,4,128,128]{3,2,1,0:T(8,128)(2,1)S(1)} %get-tuple-element.124), channel_id=1, source_target_pairs={{0,8},{4,12},{8,0},{12,4},{16,24},{20,28},{24,16},{28,20},{1,9},{5... | collective-permute-start | bytes 786440 | tf_op jit(solution)/shard_map/ppermute | solution.py:371
  48.2 0.9 collective-permute-start.9
  49.2 2.6 %collective-permute-start.10 = (bf16[1,4,128,128]{3,2,1,0:T(8,128)(2,1)S(1)}, bf16[1,4,128,128]{3,2,1,0:T(8,128)(2,1)S(1)}, u32[]{:S(2)}, u32[]{:S(2)}) collective-permute-start(bf16[1,4,128,128]{3,2,1,0:T(8,128)(2,1)S(1)} %get-tuple-element.122), channel_id=1, source_target_pairs={{0,16},{4,20},{8,24},{12,28},{16,0},{20,4},{24,8},{28,12},{1,17},{... | collective-permute-start | bytes 393224 | tf_op jit(solution)/shard_map/ppermute | solution.py:371
  53.4 2.2 %collective-permute-done.11.refs_1_ = bf16[2,4,128,128]{3,2,1,0:T(8,128)(2,1)S(1)} collective-permute-done((bf16[2,4,128,128]{3,2,1,0:T(8,128)(2,1)S(1)}, bf16[2,4,128,128]{3,2,1,0:T(8,128)(2,1)S(1)}, u32[]{:S(2)}, u32[]{:S(2)}) %collective-permute-start.11) | collective-permute-done | bytes 262176 | tf_op jit(solution)/shard_map/ppermute | solution.py:371
  57.7 3.2 %collective-permute-start.13 = (bf16[2,4,128,128]{3,2,1,0:T(8,128)(2,1)S(1)}, bf16[2,4,128,128]{3,2,1,0:T(8,128)(2,1)S(1)}, u32[]{:S(2)}, u32[]{:S(2)}) collective-permute-start(bf16[2,4,128,128]{3,2,1,0:T(8,128)(2,1)S(1)} %get-tuple-element.130), channel_id=1, source_target_pairs={{0,8},{4,12},{8,0},{12,4},{16,24},{20,28},{24,16},{28,20},{1,9},{5... | collective-permute-start | bytes 786440 | tf_op jit(solution)/shard_map/ppermute | solution.py:371
  62.5 2.2 %collective-permute-done.15.refs_1_ = bf16[2,4,128,128]{3,2,1,0:T(8,128)(2,1)S(1)} collective-permute-done((bf16[2,4,128,128]{3,2,1,0:T(8,128)(2,1)S(1)}, bf16[2,4,128,128]{3,2,1,0:T(8,128)(2,1)S(1)}, u32[]{:S(2)}, u32[]{:S(2)}) %collective-permute-start.15) | collective-permute-done | bytes 262176 | tf_op jit(solution)/shard_map/ppermute | solution.py:371
  65.8 3.5 %inner.3.refs_4_ = f32[3,16,128,128]{3,2,1,0:T(8,128)S(1)} custom-call(s32[2]{0:T(128)S(1)} %copy-done.7, s32[16]{0:T(128)S(1)} %copy-done.6, bf16[4,16,128,128]{3,2,1,0:T(8,128)(2,1)S(1)} %copy-done.2, f32[2,4,128,128]{3,2,1,0:T(8,128)S(1)} %get-tuple-element.136.refs_0_), custom_call_target="tpu_custom_call" | custom-call | flops 1 | bytes 2583000 | tf_op jit(solution)/shard_map/inner/pallas_call | solution.py:214
  70.7 0.9 down.10
  72.1 1.0 collective-permute-start.24
  73.2 1.0 collective-permute-done.22.refs_1_
  74.9 1.4 %collective-permute-start.29 = (bf16[2,4,128,128]{3,2,1,0:T(8,128)(2,1)S(1)}, bf16[2,4,128,128]{3,2,1,0:T(8,128)(2,1)S(1)}, u32[]{:S(2)}, u32[]{:S(2)}) collective-permute-start(bf16[2,4,128,128]{3,2,1,0:T(8,128)(2,1)S(1)} %get-tuple-element.160), channel_id=1, source_target_pairs={{0,2},{1,3},{2,0},{3,1},{4,6},{5,7},{6,4},{7,5},{8,10},{9,11},{10,... | collective-permute-start | bytes 786440 | tf_op jit(solution)/shard_map/ppermute | solution.py:369
  76.3 1.5 %collective-permute-start.16 = (bf16[1,4,128,128]{3,2,1,0:T(8,128)(2,1)S(1)}, bf16[1,4,128,128]{3,2,1,0:T(8,128)(2,1)S(1)}, u32[]{:S(2)}, u32[]{:S(2)}) collective-permute-start(bf16[1,4,128,128]{3,2,1,0:T(8,128)(2,1)S(1)} %get-tuple-element.139), channel_id=1, source_target_pairs={{0,16},{4,20},{8,24},{12,28},{16,0},{20,4},{24,8},{28,12},{1,17},{... | collective-permute-start | bytes 393224 | tf_op jit(solution)/shard_map/ppermute | solution.py:371
  77.8 3.8 %grads.4 = (bf16[128,64,128]{2,1,0:T(8,128)(2,1)}, bf16[128,64,128]{2,1,0:T(8,128)(2,1)}, bf16[128,64,128]{2,1,0:T(8,128)(2,1)}, f32[8,128]{1,0:T(8,128)S(1)}) custom-call(s32[2]{0:T(128)S(1)} %copy-done.7, s32[16]{0:T(128)S(1)} %copy-done.6, bf16[4,16,128,128]{3,2,1,0:T(8,128)(2,1)S(1)} %copy-done.1, ...), custom_call_target="tpu_custom_call" | custom-call | flops 1 | bytes 2583000 | tf_op jit(solution)/shard_map/grads/pallas_call | solution.py:214
  81.6 4.4 %collective-permute-done.16.refs_1_ = bf16[1,4,128,128]{3,2,1,0:T(8,128)(2,1)S(1)} collective-permute-done((bf16[1,4,128,128]{3,2,1,0:T(8,128)(2,1)S(1)}, bf16[1,4,128,128]{3,2,1,0:T(8,128)(2,1)S(1)}, u32[]{:S(2)}, u32[]{:S(2)}) %collective-permute-start.16) | collective-permute-done | bytes 131104 | tf_op jit(solution)/shard_map/ppermute | solution.py:371
  87.4 0.8 down.13
  89.4 0.9 down.14
  91.3 3.7 %grads.5 = (bf16[128,64,128]{2,1,0:T(8,128)(2,1)}, bf16[128,64,128]{2,1,0:T(8,128)(2,1)}, bf16[128,64,128]{2,1,0:T(8,128)(2,1)}, f32[8,128]{1,0:T(8,128)S(1)}) custom-call(s32[2]{0:T(128)S(1)} %copy-done.7, s32[16]{0:T(128)S(1)} %copy-done.6, bf16[4,16,128,128]{3,2,1,0:T(8,128)(2,1)S(1)} %copy-done.2, ...), custom_call_target="tpu_custom_call", output_to_operand_aliasing={{0}: (9, {}), {1}: (10, {}), {2}: (11, {})} | custom-call | flops 1 | bytes 2583000 | tf_op jit(solution)/shard_map/grads/pallas_call | solution.py:214
  95.1 0.8 down.15
  97.1 5.4 %grads.6 = (bf16[128,64,128]{2,1,0:T(8,128)(2,1)}, bf16[128,64,128]{2,1,0:T(8,128)(2,1)}, bf16[128,64,128]{2,1,0:T(8,128)(2,1)}, f32[8,128]{1,0:T(8,128)S(1)}) custom-call(s32[2]{0:T(128)S(1)} %copy-done.7, s32[16]{0:T(128)S(1)} %copy-done.6, ...), custom_call_target="tpu_custom_call", output_to_operand_aliasing={{0}: (8, {}), {1}: (9, {}), {2}: (10, {})} | custom-call | flops 1 | bytes 2583000 | tf_op jit(solution)/shard_map/grads/pallas_call | solution.py:214
  102.5 6.0 %grads.7 = (bf16[128,64,128]{2,1,0:T(8,128)(2,1)}, bf16[128,64,128]{2,1,0:T(8,128)(2,1)}, bf16[128,64,128]{2,1,0:T(8,128)(2,1)}, f32[8,128]{1,0:T(8,128)}) custom-call(s32[2]{0:T(128)S(1)} %copy-done.7, s32[16]{0:T(128)S(1)} %copy-done.6, bf16[4,16,128,128]{3,2,1,0:T(8,128)(2,1)S(1)} %copy-done.4, ...), custom_call_target="tpu_custom_call", output_to_operand_aliasing={{0}: (8, {}), {1}: (9, {}), {2}: (10, {})} | custom-call | flops 1 | bytes 2583000 | tf_op jit(solution)/shard_map/grads/pallas_call | solution.py:214
  (93 shorter events, 23.9 us)
Async XLA Ops:
  10.0 9.0 %collective-permute-start.1 = (bf16[2,2,8,128,128]{4,3,2,1,0:T(8,128)(2,1)}, bf16[2,2,8,128,128]{4,3,2,1,0:T(8,128)(2,1)S(1)}, u32[]{:S(2)}, u32[]{:S(2)}) collective-permute-start(bf16[2,2,8,128,128]{4,3,2,1,0:T(8,128)(2,1)} %get-tuple-element.98), channel_id=1, source_target_pairs={{0,1},{1,0},{2,3},{3,2},{4,5},{5,4},{6,7},{7,6},{8,9},{9,8},{10,11... | collective-permute-start | bytes 3145736 | tf_op jit(solution)/shard_map/ppermute | solution.py:369
  18.9 13.7 %collective-permute-start = (bf16[2,2,8,128,128]{4,3,2,1,0:T(8,128)(2,1)S(1)}, bf16[2,2,8,128,128]{4,3,2,1,0:T(8,128)(2,1)S(1)}, u32[]{:S(2)}, u32[]{:S(2)}) collective-permute-start(bf16[2,2,8,128,128]{4,3,2,1,0:T(8,128)(2,1)S(1)} %get-tuple-element.97), channel_id=1, source_target_pairs={{0,1},{1,0},{2,3},{3,2},{4,5},{5,4},{6,7},{7,6},{8,9},{9,8},{10,11... | collective-permute-start | bytes 3145736 | tf_op jit(solution)/shard_map/ppermute | solution.py:369
  19.7 10.1 %collective-permute-start.2 = (bf16[2,4,128,128]{3,2,1,0:T(8,128)(2,1)S(1)}, bf16[2,4,128,128]{3,2,1,0:T(8,128)(2,1)S(1)}, u32[]{:S(2)}, u32[]{:S(2)}) collective-permute-start(bf16[2,4,128,128]{3,2,1,0:T(8,128)(2,1)S(1)} %get-tuple-element.101), channel_id=1, source_target_pairs={{0,2},{1,3},{2,0},{3,1},{4,6},{5,7},{6,4},{7,5},{8,10},{9,11},{10,... | collective-permute-start | bytes 786440 | tf_op jit(solution)/shard_map/ppermute | solution.py:369
  23.4 12.0 %collective-permute-start.4 = (bf16[2,4,128,128]{3,2,1,0:T(8,128)(2,1)S(1)}, bf16[2,4,128,128]{3,2,1,0:T(8,128)(2,1)S(1)}, u32[]{:S(2)}, u32[]{:S(2)}) collective-permute-start(bf16[2,4,128,128]{3,2,1,0:T(8,128)(2,1)S(1)} %get-tuple-element.107), channel_id=1, source_target_pairs={{0,2},{1,3},{2,0},{3,1},{4,6},{5,7},{6,4},{7,5},{8,10},{9,11},{10,... | collective-permute-start | bytes 786440 | tf_op jit(solution)/shard_map/ppermute | solution.py:369
  30.4 7.8 %collective-permute-start.3 = (bf16[2,4,128,128]{3,2,1,0:T(8,128)(2,1)S(1)}, bf16[2,4,128,128]{3,2,1,0:T(8,128)(2,1)S(1)}, u32[]{:S(2)}, u32[]{:S(2)}) collective-permute-start(bf16[2,4,128,128]{3,2,1,0:T(8,128)(2,1)S(1)} %get-tuple-element.106), channel_id=1, source_target_pairs={{0,4},{4,0},{8,12},{12,8},{16,20},{20,16},{24,28},{28,24},{1,5},{5... | collective-permute-start | bytes 786440 | tf_op jit(solution)/shard_map/ppermute | solution.py:371
  33.3 9.5 %collective-permute-start.8 = (bf16[2,4,128,128]{3,2,1,0:T(8,128)(2,1)S(1)}, bf16[2,4,128,128]{3,2,1,0:T(8,128)(2,1)S(1)}, u32[]{:S(2)}, u32[]{:S(2)}) collective-permute-start(bf16[2,4,128,128]{3,2,1,0:T(8,128)(2,1)S(1)} %get-tuple-element.116), channel_id=1, source_target_pairs={{0,2},{1,3},{2,0},{3,1},{4,6},{5,7},{6,4},{7,5},{8,10},{9,11},{10,... | collective-permute-start | bytes 786440 | tf_op jit(solution)/shard_map/ppermute | solution.py:369
  36.0 8.3 %collective-permute-start.7 = (bf16[2,4,128,128]{3,2,1,0:T(8,128)(2,1)S(1)}, bf16[2,4,128,128]{3,2,1,0:T(8,128)(2,1)S(1)}, u32[]{:S(2)}, u32[]{:S(2)}) collective-permute-start(bf16[2,4,128,128]{3,2,1,0:T(8,128)(2,1)S(1)} %get-tuple-element.115), channel_id=1, source_target_pairs={{0,4},{4,0},{8,12},{12,8},{16,20},{20,16},{24,28},{28,24},{1,5},{5... | collective-permute-start | bytes 786440 | tf_op jit(solution)/shard_map/ppermute | solution.py:371
  38.9 7.2 %collective-permute-start.6 = (bf16[2,4,128,128]{3,2,1,0:T(8,128)(2,1)S(1)}, bf16[2,4,128,128]{3,2,1,0:T(8,128)(2,1)S(1)}, u32[]{:S(2)}, u32[]{:S(2)}) collective-permute-start(bf16[2,4,128,128]{3,2,1,0:T(8,128)(2,1)S(1)} %get-tuple-element.114), channel_id=1, source_target_pairs={{0,8},{4,12},{8,0},{12,4},{16,24},{20,28},{24,16},{28,20},{1,9},{5... | collective-permute-start | bytes 786440 | tf_op jit(solution)/shard_map/ppermute | solution.py:371
  41.2 6.4 %collective-permute-start.5 = (bf16[2,4,128,128]{3,2,1,0:T(8,128)(2,1)S(1)}, bf16[2,4,128,128]{3,2,1,0:T(8,128)(2,1)S(1)}, u32[]{:S(2)}, u32[]{:S(2)}) collective-permute-start(bf16[2,4,128,128]{3,2,1,0:T(8,128)(2,1)S(1)} %get-tuple-element.112), channel_id=1, source_target_pairs={{0,2},{1,3},{2,0},{3,1},{4,6},{5,7},{6,4},{7,5},{8,10},{9,11},{10,... | collective-permute-start | bytes 786440 | tf_op jit(solution)/shard_map/ppermute | solution.py:369
  43.4 8.5 %collective-permute-start.12 = (bf16[2,4,128,128]{3,2,1,0:T(8,128)(2,1)S(1)}, bf16[2,4,128,128]{3,2,1,0:T(8,128)(2,1)S(1)}, u32[]{:S(2)}, u32[]{:S(2)}) collective-permute-start(bf16[2,4,128,128]{3,2,1,0:T(8,128)(2,1)S(1)} %get-tuple-element.125), channel_id=1, source_target_pairs={{0,4},{4,0},{8,12},{12,8},{16,20},{20,16},{24,28},{28,24},{1,5},{5... | collective-permute-start | bytes 786440 | tf_op jit(solution)/shard_map/ppermute | solution.py:371
  45.0 10.6 %collective-permute-start.11 = (bf16[2,4,128,128]{3,2,1,0:T(8,128)(2,1)S(1)}, bf16[2,4,128,128]{3,2,1,0:T(8,128)(2,1)S(1)}, u32[]{:S(2)}, u32[]{:S(2)}) collective-permute-start(bf16[2,4,128,128]{3,2,1,0:T(8,128)(2,1)S(1)} %get-tuple-element.124), channel_id=1, source_target_pairs={{0,8},{4,12},{8,0},{12,4},{16,24},{20,28},{24,16},{28,20},{1,9},{5... | collective-permute-start | bytes 786440 | tf_op jit(solution)/shard_map/ppermute | solution.py:371
  48.2 8.8 %collective-permute-start.9 = (bf16[2,4,128,128]{3,2,1,0:T(8,128)(2,1)S(1)}, bf16[2,4,128,128]{3,2,1,0:T(8,128)(2,1)S(1)}, u32[]{:S(2)}, u32[]{:S(2)}) collective-permute-start(bf16[2,4,128,128]{3,2,1,0:T(8,128)(2,1)S(1)} %get-tuple-element.121), channel_id=1, source_target_pairs={{0,4},{4,0},{8,12},{12,8},{16,20},{20,16},{24,28},{28,24},{1,5},{5... | collective-permute-start | bytes 786440 | tf_op jit(solution)/shard_map/ppermute | solution.py:371
  49.2 7.1 %collective-permute-start.10 = (bf16[1,4,128,128]{3,2,1,0:T(8,128)(2,1)S(1)}, bf16[1,4,128,128]{3,2,1,0:T(8,128)(2,1)S(1)}, u32[]{:S(2)}, u32[]{:S(2)}) collective-permute-start(bf16[1,4,128,128]{3,2,1,0:T(8,128)(2,1)S(1)} %get-tuple-element.122), channel_id=1, source_target_pairs={{0,16},{4,20},{8,24},{12,28},{16,0},{20,4},{24,8},{28,12},{1,17},{... | collective-permute-start | bytes 393224 | tf_op jit(solution)/shard_map/ppermute | solution.py:371
  52.5 12.1 %collective-permute-start.15 = (bf16[2,4,128,128]{3,2,1,0:T(8,128)(2,1)S(1)}, bf16[2,4,128,128]{3,2,1,0:T(8,128)(2,1)S(1)}, u32[]{:S(2)}, u32[]{:S(2)}) collective-permute-start(bf16[2,4,128,128]{3,2,1,0:T(8,128)(2,1)S(1)} %get-tuple-element.135), channel_id=1, source_target_pairs={{0,8},{4,12},{8,0},{12,4},{16,24},{20,28},{24,16},{28,20},{1,9},{5... | collective-permute-start | bytes 786440 | tf_op jit(solution)/shard_map/ppermute | solution.py:371
  57.7 12.3 %collective-permute-start.13 = (bf16[2,4,128,128]{3,2,1,0:T(8,128)(2,1)S(1)}, bf16[2,4,128,128]{3,2,1,0:T(8,128)(2,1)S(1)}, u32[]{:S(2)}, u32[]{:S(2)}) collective-permute-start(bf16[2,4,128,128]{3,2,1,0:T(8,128)(2,1)S(1)} %get-tuple-element.130), channel_id=1, source_target_pairs={{0,8},{4,12},{8,0},{12,4},{16,24},{20,28},{24,16},{28,20},{1,9},{5... | collective-permute-start | bytes 786440 | tf_op jit(solution)/shard_map/ppermute | solution.py:371
  60.9 9.8 %collective-permute-start.17 = (bf16[2,4,128,128]{3,2,1,0:T(8,128)(2,1)S(1)}, bf16[2,4,128,128]{3,2,1,0:T(8,128)(2,1)S(1)}, u32[]{:S(2)}, u32[]{:S(2)}) collective-permute-start(bf16[2,4,128,128]{3,2,1,0:T(8,128)(2,1)S(1)} %get-tuple-element.140), channel_id=1, source_target_pairs={{0,2},{1,3},{2,0},{3,1},{4,6},{5,7},{6,4},{7,5},{8,10},{9,11},{10,... | collective-permute-start | bytes 786440 | tf_op jit(solution)/shard_map/ppermute | solution.py:369
  61.7 7.6 %collective-permute-start.14 = (bf16[1,4,128,128]{3,2,1,0:T(8,128)(2,1)S(1)}, bf16[1,4,128,128]{3,2,1,0:T(8,128)(2,1)S(1)}, u32[]{:S(2)}, u32[]{:S(2)}) collective-permute-start(bf16[1,4,128,128]{3,2,1,0:T(8,128)(2,1)S(1)} %get-tuple-element.132), channel_id=1, source_target_pairs={{0,16},{4,20},{8,24},{12,28},{16,0},{20,4},{24,8},{28,12},{1,17},{... | collective-permute-start | bytes 393224 | tf_op jit(solution)/shard_map/ppermute | solution.py:371
  65.4 8.8 %collective-permute-start.22 = (bf16[1,4,128,128]{3,2,1,0:T(8,128)(2,1)S(1)}, bf16[1,4,128,128]{3,2,1,0:T(8,128)(2,1)S(1)}, u32[]{:S(2)}, u32[]{:S(2)}) collective-permute-start(bf16[1,4,128,128]{3,2,1,0:T(8,128)(2,1)S(1)} %get-tuple-element.146), channel_id=1, source_target_pairs={{0,16},{4,20},{8,24},{12,28},{16,0},{20,4},{24,8},{28,12},{1,17},{... | collective-permute-start | bytes 393224 | tf_op jit(solution)/shard_map/ppermute | solution.py:371
  71.6 4.7 %collective-permute-start.18 = (bf16[1,4,128,128]{3,2,1,0:T(8,128)(2,1)S(1)}, bf16[1,4,128,128]{3,2,1,0:T(8,128)(2,1)S(1)}, u32[]{:S(2)}, u32[]{:S(2)}) collective-permute-start(bf16[1,4,128,128]{3,2,1,0:T(8,128)(2,1)S(1)} %get-tuple-element.142), channel_id=1, source_target_pairs={{0,1},{1,0},{2,3},{3,2},{4,5},{5,4},{6,7},{7,6},{8,9},{9,8},{10,11... | collective-permute-start | bytes 393224 | tf_op jit(solution)/shard_map/ppermute | solution.py:369
  71.6 4.7 %collective-permute-start.19 = (bf16[1,4,128,128]{3,2,1,0:T(8,128)(2,1)S(1)}, bf16[1,4,128,128]{3,2,1,0:T(8,128)(2,1)S(1)}, u32[]{:S(2)}, u32[]{:S(2)}) collective-permute-start(bf16[1,4,128,128]{3,2,1,0:T(8,128)(2,1)S(1)} %get-tuple-element.143), channel_id=1, source_target_pairs={{0,1},{1,0},{2,3},{3,2},{4,5},{5,4},{6,7},{7,6},{8,9},{9,8},{10,11... | collective-permute-start | bytes 393224 | tf_op jit(solution)/shard_map/ppermute | solution.py:369
  72.1 15.3 %collective-permute-start.24 = (bf16[2,4,128,128]{3,2,1,0:T(8,128)(2,1)S(1)}, bf16[2,4,128,128]{3,2,1,0:T(8,128)(2,1)S(1)}, u32[]{:S(2)}, u32[]{:S(2)}) collective-permute-start(bf16[2,4,128,128]{3,2,1,0:T(8,128)(2,1)S(1)} %get-tuple-element.151), channel_id=1, source_target_pairs={{0,2},{1,3},{2,0},{3,1},{4,6},{5,7},{6,4},{7,5},{8,10},{9,11},{10,... | collective-permute-start | bytes 786440 | tf_op jit(solution)/shard_map/ppermute | solution.py:369
  74.9 14.0 %collective-permute-start.29 = (bf16[2,4,128,128]{3,2,1,0:T(8,128)(2,1)S(1)}, bf16[2,4,128,128]{3,2,1,0:T(8,128)(2,1)S(1)}, u32[]{:S(2)}, u32[]{:S(2)}) collective-permute-start(bf16[2,4,128,128]{3,2,1,0:T(8,128)(2,1)S(1)} %get-tuple-element.160), channel_id=1, source_target_pairs={{0,2},{1,3},{2,0},{3,1},{4,6},{5,7},{6,4},{7,5},{8,10},{9,11},{10,... | collective-permute-start | bytes 786440 | tf_op jit(solution)/shard_map/ppermute | solution.py:369
  76.3 9.6 %collective-permute-start.16 = (bf16[1,4,128,128]{3,2,1,0:T(8,128)(2,1)S(1)}, bf16[1,4,128,128]{3,2,1,0:T(8,128)(2,1)S(1)}, u32[]{:S(2)}, u32[]{:S(2)}) collective-permute-start(bf16[1,4,128,128]{3,2,1,0:T(8,128)(2,1)S(1)} %get-tuple-element.139), channel_id=1, source_target_pairs={{0,16},{4,20},{8,24},{12,28},{16,0},{20,4},{24,8},{28,12},{1,17},{... | collective-permute-start | bytes 393224 | tf_op jit(solution)/shard_map/ppermute | solution.py:371
  86.7 8.4 %collective-permute-start.23 = (bf16[2,4,128,128]{3,2,1,0:T(8,128)(2,1)S(1)}, bf16[2,4,128,128]{3,2,1,0:T(8,128)(2,1)S(1)}, u32[]{:S(2)}, u32[]{:S(2)}) collective-permute-start(bf16[2,4,128,128]{3,2,1,0:T(8,128)(2,1)S(1)} %get-tuple-element.150), channel_id=1, source_target_pairs={{0,2},{1,3},{2,0},{3,1},{4,6},{5,7},{6,4},{7,5},{8,10},{9,11},{10,... | collective-permute-start | bytes 786440 | tf_op jit(solution)/shard_map/ppermute | solution.py:369
  90.2 5.9 %collective-permute-start.34 = (bf16[1,4,128,128]{3,2,1,0:T(8,128)(2,1)S(1)}, bf16[1,4,128,128]{3,2,1,0:T(8,128)(2,1)S(1)}, u32[]{:S(2)}, u32[]{:S(2)}) collective-permute-start(bf16[1,4,128,128]{3,2,1,0:T(8,128)(2,1)S(1)} %get-tuple-element.169), channel_id=1, source_target_pairs={{0,1},{1,0},{2,3},{3,2},{4,5},{5,4},{6,7},{7,6},{8,9},{9,8},{10,11... | collective-permute-start | bytes 393224 | tf_op jit(solution)/shard_map/ppermute | solution.py:369
  90.4 6.1 %collective-permute-start.35 = (bf16[1,4,128,128]{3,2,1,0:T(8,128)(2,1)S(1)}, bf16[1,4,128,128]{3,2,1,0:T(8,128)(2,1)S(1)}, u32[]{:S(2)}, u32[]{:S(2)}) collective-permute-start(bf16[1,4,128,128]{3,2,1,0:T(8,128)(2,1)S(1)} %get-tuple-element.170), channel_id=1, source_target_pairs={{0,1},{1,0},{2,3},{3,2},{4,5},{5,4},{6,7},{7,6},{8,9},{9,8},{10,11... | collective-permute-start | bytes 393224 | tf_op jit(solution)/shard_map/ppermute | solution.py:369
  90.8 5.8 %collective-permute-start.36 = (bf16[1,4,128,128]{3,2,1,0:T(8,128)(2,1)S(1)}, bf16[1,4,128,128]{3,2,1,0:T(8,128)(2,1)S(1)}, u32[]{:S(2)}, u32[]{:S(2)}) collective-permute-start(bf16[1,4,128,128]{3,2,1,0:T(8,128)(2,1)S(1)} %get-tuple-element.171), channel_id=1, source_target_pairs={{0,1},{1,0},{2,3},{3,2},{4,5},{5,4},{6,7},{7,6},{8,9},{9,8},{10,11... | collective-permute-start | bytes 393224 | tf_op jit(solution)/shard_map/ppermute | solution.py:369
  90.9 6.1 %collective-permute-start.37 = (bf16[1,4,128,128]{3,2,1,0:T(8,128)(2,1)S(1)}, bf16[1,4,128,128]{3,2,1,0:T(8,128)(2,1)S(1)}, u32[]{:S(2)}, u32[]{:S(2)}) collective-permute-start(bf16[1,4,128,128]{3,2,1,0:T(8,128)(2,1)S(1)} %get-tuple-element.172), channel_id=1, source_target_pairs={{0,1},{1,0},{2,3},{3,2},{4,5},{5,4},{6,7},{7,6},{8,9},{9,8},{10,11... | collective-permute-start | bytes 393224 | tf_op jit(solution)/shard_map/ppermute | solution.py:369
  96.0 6.5 %collective-permute-start.30 = (bf16[1,4,128,128]{3,2,1,0:T(8,128)(2,1)S(1)}, bf16[1,4,128,128]{3,2,1,0:T(8,128)(2,1)S(1)}, u32[]{:S(2)}, u32[]{:S(2)}) collective-permute-start(bf16[1,4,128,128]{3,2,1,0:T(8,128)(2,1)S(1)} %get-tuple-element.164), channel_id=1, source_target_pairs={{0,1},{1,0},{2,3},{3,2},{4,5},{5,4},{6,7},{7,6},{8,9},{9,8},{10,11... | collective-permute-start | bytes 393224 | tf_op jit(solution)/shard_map/ppermute | solution.py:369
  96.1 6.4 %collective-permute-start.31 = (bf16[1,4,128,128]{3,2,1,0:T(8,128)(2,1)S(1)}, bf16[1,4,128,128]{3,2,1,0:T(8,128)(2,1)S(1)}, u32[]{:S(2)}, u32[]{:S(2)}) collective-permute-start(bf16[1,4,128,128]{3,2,1,0:T(8,128)(2,1)S(1)} %get-tuple-element.165), channel_id=1, source_target_pairs={{0,1},{1,0},{2,3},{3,2},{4,5},{5,4},{6,7},{7,6},{8,9},{9,8},{10,11... | collective-permute-start | bytes 393224 | tf_op jit(solution)/shard_map/ppermute | solution.py:369
  96.5 6.0 %collective-permute-start.32 = (bf16[1,4,128,128]{3,2,1,0:T(8,128)(2,1)S(1)}, bf16[1,4,128,128]{3,2,1,0:T(8,128)(2,1)S(1)}, u32[]{:S(2)}, u32[]{:S(2)}) collective-permute-start(bf16[1,4,128,128]{3,2,1,0:T(8,128)(2,1)S(1)} %get-tuple-element.166), channel_id=1, source_target_pairs={{0,1},{1,0},{2,3},{3,2},{4,5},{5,4},{6,7},{7,6},{8,9},{9,8},{10,11... | collective-permute-start | bytes 393224 | tf_op jit(solution)/shard_map/ppermute | solution.py:369
  96.6 5.9 %collective-permute-start.33 = (bf16[1,4,128,128]{3,2,1,0:T(8,128)(2,1)S(1)}, bf16[1,4,128,128]{3,2,1,0:T(8,128)(2,1)S(1)}, u32[]{:S(2)}, u32[]{:S(2)}) collective-permute-start(bf16[1,4,128,128]{3,2,1,0:T(8,128)(2,1)S(1)} %get-tuple-element.167), channel_id=1, source_target_pairs={{0,1},{1,0},{2,3},{3,2},{4,5},{5,4},{6,7},{7,6},{8,9},{9,8},{10,11... | collective-permute-start | bytes 393224 | tf_op jit(solution)/shard_map/ppermute | solution.py:369
  (14 other events, 63.7 us)

commit v6 on v5

--- a/solution.py
+++ b/solution.py
@@ -53,11 +53,12 @@
 
 def states_kernel(chunks, weights, place_ref, len_ref, *refs):
     count = len(chunks)
-    tokens, refs = refs[:4], refs[len(refs) - 2 * count - (weights is not None) - 5 :]
+    tokens, refs = refs[:4], refs[len(refs) - 4 * count - (weights is not None) - 4 :]
     if weights is not None:
         scalar_ref, *refs = refs
-    keeps, head_refs, send_ref = refs[:count], refs[count : 2 * count], refs[2 * count]
-    slab, wide, sems = refs[2 * count + 1], refs[-3:-1], refs[-1]
+    keeps, head_refs = refs[:count], refs[count : 2 * count]
+    sends = refs[2 * count : 4 * count]
+    slab, wide, sems = refs[-4], refs[-3:-1], refs[-1]
     n, _, d = tokens[0].shape
     heads = slab.shape[3]
     half = heads // 2
@@ -97,8 +98,8 @@
                 keeps[j][0, r] = state_a
                 keeps[j][1, r] = state_b
             else:
-                send_ref[j, 0, r - half] = state_a.astype(B16)
-                send_ref[j, 1, r - half] = state_b.astype(B16)
+                sends[2 * j][0, r - half] = state_a.astype(B16)
+                sends[2 * j + 1][0, r - half] = state_b.astype(B16)
 
 
 def _live(len_ref, first, n, scaling, later):
@@ -231,7 +232,7 @@
         first = chunks[0] == 0
         outs = [jax.ShapeDtypeStruct(shape, F32)] * count
         outs += [jax.ShapeDtypeStruct((4, part, n, d), B16)] * count
-        outs += [jax.ShapeDtypeStruct((count, *shape), B16)]
+        outs += [jax.ShapeDtypeStruct((1, *shape[1:]), B16)] * (2 * count)
         specs = [IN_VMEM] * len(outs)
         if first:
             outs = [jax.ShapeDtypeStruct((2 * len(self.index),), F32)] + outs
@@ -251,7 +252,8 @@
         )
         if first:
             self.scalars, *got = got
-        return got[:count], got[count : 2 * count], self.swap(got[-1], 0)
+        moved = [self.swap(x, 0) for x in got[2 * count :]]
+        return got[:count], got[count : 2 * count], moved
 
     def inner(self, heads, after):
         return self.call(
@@ -344,19 +346,23 @@
         )
 
     def order(self, count):
-        chunks = self.chunks
-        line = []
+        chunks, size = self.chunks, max(1, self.chunks // 2)
+        line = [(chunk, 1) for chunk in range(size)]
+        line += [(chunk, 0) for chunk in range(size, chunks)]
         for wave in range(count - 2 + chunks - 1):
             for chunk in reversed(range(chunks)):
-                if 0 <= wave - chunk < count - 2:
-                    line.append((chunk, wave - chunk))
+                one = (chunk, wave - chunk)
+                if 0 < one[1] < count - 2 and one not in line:
+                    line.append(one)
         fill, final = count - 2, count - 1
         spare = line[-2:] if chunks > 1 else []
         line = line[: len(line) - len(spare)]
-        line += [(0, fill), *spare[:-1], (0, final), *spare[-1:]]
+        line += [(0, fill), *spare[:-1], (0, final)]
         if chunks > 2:
-            line.insert(2, (0, -1))
+            line += [(2, -1)]
             line.insert(len(line) - 6, (1, -1))
+            line.insert(line.index((0, count - 3)), (0, -1))
+        line += spare[-1:]
         for chunk in range(1, chunks):
             line += [(chunk, fill)] if chunk == 1 else []
             line += [(chunk + 1, fill)] if chunk + 1 < chunks else []
@@ -370,7 +376,7 @@
         bit = 1 << (level - self.head_bits)
         return lax.ppermute(x, "seq", [(i, i ^ bit) for i in range(self.seq_size)])
 
-    def stages(self, chunk, keep, tokens, swapped, spot):
+    def stages(self, chunk, keep, tokens, swapped):
         d, bits, last = self.d, self.head_bits, self.levels - 1
         own, got, here = [], [], {}
 
@@ -381,16 +387,16 @@
         here["heads"], here["got"] = tokens, swapped
 
         def up(level, after):
-            got.append(here["got"])
+            got.append(here["got"] if level == 0 else [here["got"]])
             heads = own[-1].shape[1]
             half = heads // 2 if level + 1 < bits else heads
-            at = (spot,) if level == 0 else ()
 
             def body(w, ins, outs):
                 for which in range(2):
                     o, g = w("up_own", level, which), w("up_got", level, which)
                     for h in range(heads):
-                        x = o * ins[0][which, h] + g * ins[1][(*at, which, h)].astype(F32)
+                        other = ins[1][which, h] if level else ins[1 + which][0, h]
+                        x = o * ins[0][which, h] + g * other.astype(F32)
                         if h < half:
                             outs[0][which, h] = x
                         if half == heads:
@@ -399,7 +405,7 @@
                             outs[1][which, h - half] = x.astype(B16)
 
             outs = [shaped(half, F32), shaped(half, B16)]
-            keep, send = self.combine("up", body, [own[-1], got[-1]], outs, after)
+            keep, send = self.combine("up", body, [own[-1], *got[-1]], outs, after)
             if half < heads:
                 own.append(keep)
             else:
@@ -444,11 +450,10 @@
 
         def down(level, after):
             top = level == bits - 1
-            ins = [here["state"], here["got"], own[level], got[level]]
+            ins = [here["state"], here["got"], own[level], *got[level]]
             heads = own[level].shape[1]
             half = heads // 2
             factor = self.scaling if level == 0 else 1.0
-            at = (spot,) if level == 0 else ()
 
             def body(w, ins, outs):
                 for which in range(2):
@@ -464,7 +469,8 @@
                             x = ins[0][which, h]
                         else:
                             x = ins[1][which, h - half].astype(F32)
-                        mine = m_in * x + m_got * ins[3][(*at, which, h)].astype(F32)
+                        other = ins[3][which, h] if level else ins[3 + which][0, h]
+                        mine = m_in * x + m_got * other.astype(F32)
                         theirs = s_in * x + s_own * ins[2][which, h]
                         outs[0][which, h] = mine.astype(outs[0].dtype)
                         if level:
@@ -507,10 +513,14 @@
     size = max(1, plan.chunks // 2)
     for begin in range(0, plan.chunks, size):
         chunks = list(range(begin, begin + size))
-        keeps, tokens, swapped = plan.states(chunks, arrays, after)
+        keeps, tokens, moved = plan.states(chunks, arrays, after)
         after = (keeps[0],)
         for spot, chunk in enumerate(chunks):
-            stages.append(plan.stages(chunk, keeps[spot], tokens[spot], swapped, spot))
+            swapped = moved[2 * spot : 2 * spot + 2]
+            stages.append(plan.stages(chunk, keeps[spot], tokens[spot], swapped))
+        if begin == 0:
+            for chunk in chunks:
+                after = (stages[chunk][0](after),)
     outs, count = (), len(stages[0])
     for chunk, stage in plan.order(count):
         if stage < 0:

time: 109 us -> 109 us (level)
  waiting for transfers between devices: 14 us -> 8.33 us
  starting transfers between devices: 32.9 us -> 37.9 us
    ppermute x12, waiting for transfers between devices: 9.9 us -> 3.65 us  [swap(): return lax.ppermute(x, 'seq', [(i, i ^ bit) for i in range(self.seq_size)])]
    ppermute x26 -> x32, starting transfers between devices: 14.7 us -> 17.5 us  [swap(): return lax.ppermute(x, 'head', moves)]
    ppermute x12, starting transfers between devices: 18.2 us -> 20.4 us  [swap(): return lax.ppermute(x, 'seq', [(i, i ^ bit) for i in range(self.seq_size)])]
    ppermute x26 -> x32, waiting for transfers between devices: 4.12 us -> 4.68 us  [swap(): return lax.ppermute(x, 'head', moves)]
    pallas_call x32 -> x33, Pallas kernels: 58.8 us -> 59.4 us  [call(): pl.pallas_call(body, in_specs=in_specs, out_specs=out_specs, out_shape=ou...]
  transfers between devices with their start and end apart: 38 -> 44, of which waited for: 8 -> 6; matrix products, arithmetic and copies ran while one was open for 0% -> 0% of each run, Pallas kernels for 41% -> 41%
where the time goes in v6:
time: 109 us
  Pallas kernels  59.4 us (54%)
  starting transfers between devices  37.9 us (35%)
  waiting for transfers between devices  8.33 us (8%)
  local copies, waits for them, and re-layouts  1.86 us (2%)
  between operations  1.21 us (1%)
    pallas_call x33, Pallas kernels, call(): pl.pallas_call(body, in_specs=in_specs, out_specs=out_specs, out_shape=ou...  59.4 us
    ppermute x12, starting transfers between devices, swap(): return lax.ppermute(x, 'seq', [(i, i ^ bit) for i in range(self.seq_size)])  20.4 us
    ppermute x32, starting transfers between devices, swap(): return lax.ppermute(x, 'head', moves)  17.5 us
    ppermute x32, waiting for transfers between devices, swap(): return lax.ppermute(x, 'head', moves)  4.68 us
    ppermute x12, waiting for transfers between devices, swap(): return lax.ppermute(x, 'seq', [(i, i ^ bit) for i in range(self.seq_size)])  3.65 us
  transfers between devices with their start and end apart: 44, of which 6 were waited for; matrix products, arithmetic and copies ran while one was open for 0% of the time, Pallas kernels for 41%

profile of v6, /device:TPU:0, one launch (start us, length us, event | category | flops | bytes accessed | tf_op | source)
XLA Modules:
  0.0 109.3 jit_solution(9469149207441788975)
XLA Ops:
  1.3 8.6 %states.2 = (f32[44]{0:T(128)}, f32[2,8,128,128]{3,2,1,0:T(8,128)}, f32[2,8,128,128]{3,2,1,0:T(8,128)}, bf16[4,16,128,128]{3,2,1,0:T(8,128)(2,1)}, bf16[4,16,128...) custom-call(s32[2]{0:T(128)} %pad_add_fusion.place_ref, ...), custom_call_target="tpu_custom_call" | custom-call | flops 1 | bytes 25830000 | tf_op jit(solution)/shard_map/states/pallas_call | solution.py:215
  11.0 0.8 collective-permute-done.2.refs_1_.refs_3_
  12.2 1.2 %copy-done = f32[2,8,128,128]{3,2,1,0:T(8,128)S(1)} copy-done((f32[2,8,128,128]{3,2,1,0:T(8,128)S(1)}, f32[2,8,128,128]{3,2,1,0:T(8,128)}, u32[]{:S(2)}) %copy-start) | copy-done | bytes 1048600
  14.7 2.9 %collective-permute-start.9 = (bf16[2,4,128,128]{3,2,1,0:T(8,128)(2,1)S(1)}, bf16[2,4,128,128]{3,2,1,0:T(8,128)(2,1)S(1)}, u32[]{:S(2)}, u32[]{:S(2)}) collective-permute-start(bf16[2,4,128,128]{3,2,1,0:T(8,128)(2,1)S(1)} %get-tuple-element.116), channel_id=1, source_target_pairs={{0,2},{1,3},{2,0},{3,1},{4,6},{5,7},{6,4},{7,5},{8,10},{9,11},{10,... | collective-permute-start | bytes 786440 | tf_op jit(solution)/shard_map/ppermute | solution.py:375
  18.8 6.0 %states.3 = (f32[2,8,128,128]{3,2,1,0:T(8,128)S(1)}, f32[2,8,128,128]{3,2,1,0:T(8,128)S(1)}, bf16[4,16,128,128]{3,2,1,0:T(8,128)(2,1)S(1)}, bf16[4,16,128,128]{3...) custom-call(s32[2]{0:T(128)S(1)} %copy-done.8, ...), custom_call_target="tpu_custom_call" | custom-call | flops 1 | bytes 25830000 | tf_op jit(solution)/shard_map/states/pallas_call | solution.py:215
  26.5 3.3 %collective-permute-done.8.refs_1_.refs_3_ = bf16[2,4,128,128]{3,2,1,0:T(8,128)(2,1)S(1)} collective-permute-done((bf16[2,4,128,128]{3,2,1,0:T(8,128)(2,1)S(1)}, bf16[2,4,128,128]{3,2,1,0:T(8,128)(2,1)S(1)}, u32[]{:S(2)}, u32[]{:S(2)}) %collective-permute-start.8) | collective-permute-done | bytes 262176 | tf_op jit(solution)/shard_map/ppermute | solution.py:375
  29.8 1.8 %collective-permute-start.11 = (bf16[2,4,128,128]{3,2,1,0:T(8,128)(2,1)S(1)}, bf16[2,4,128,128]{3,2,1,0:T(8,128)(2,1)S(1)}, u32[]{:S(2)}, u32[]{:S(2)}) collective-permute-start(bf16[2,4,128,128]{3,2,1,0:T(8,128)(2,1)S(1)} %get-tuple-element.122), channel_id=1, source_target_pairs={{0,4},{4,0},{8,12},{12,8},{16,20},{20,16},{24,28},{28,24},{1,5},{5... | collective-permute-start | bytes 786440 | tf_op jit(solution)/shard_map/ppermute | solution.py:377
  33.3 1.8 %collective-permute-start.14 = (bf16[2,4,128,128]{3,2,1,0:T(8,128)(2,1)S(1)}, bf16[2,4,128,128]{3,2,1,0:T(8,128)(2,1)S(1)}, u32[]{:S(2)}, u32[]{:S(2)}) collective-permute-start(bf16[2,4,128,128]{3,2,1,0:T(8,128)(2,1)S(1)} %get-tuple-element.127), channel_id=1, source_target_pairs={{0,2},{1,3},{2,0},{3,1},{4,6},{5,7},{6,4},{7,5},{8,10},{9,11},{10,... | collective-permute-start | bytes 786440 | tf_op jit(solution)/shard_map/ppermute | solution.py:375
  35.8 3.3 %collective-permute-done.11.refs_1_ = bf16[2,4,128,128]{3,2,1,0:T(8,128)(2,1)S(1)} collective-permute-done((bf16[2,4,128,128]{3,2,1,0:T(8,128)(2,1)S(1)}, bf16[2,4,128,128]{3,2,1,0:T(8,128)(2,1)S(1)}, u32[]{:S(2)}, u32[]{:S(2)}) %collective-permute-start.11) | collective-permute-done | bytes 262176 | tf_op jit(solution)/shard_map/ppermute | solution.py:377
  39.7 2.1 %collective-permute-start.12 = (bf16[2,4,128,128]{3,2,1,0:T(8,128)(2,1)S(1)}, bf16[2,4,128,128]{3,2,1,0:T(8,128)(2,1)S(1)}, u32[]{:S(2)}, u32[]{:S(2)}) collective-permute-start(bf16[2,4,128,128]{3,2,1,0:T(8,128)(2,1)S(1)} %get-tuple-element.124), channel_id=1, source_target_pairs={{0,8},{4,12},{8,0},{12,4},{16,24},{20,28},{24,16},{28,20},{1,9},{5... | collective-permute-start | bytes 786440 | tf_op jit(solution)/shard_map/ppermute | solution.py:377
  41.8 1.5 %collective-permute-start.10 = (bf16[2,4,128,128]{3,2,1,0:T(8,128)(2,1)S(1)}, bf16[2,4,128,128]{3,2,1,0:T(8,128)(2,1)S(1)}, u32[]{:S(2)}, u32[]{:S(2)}) collective-permute-start(bf16[2,4,128,128]{3,2,1,0:T(8,128)(2,1)S(1)} %get-tuple-element.121), channel_id=1, source_target_pairs={{0,2},{1,3},{2,0},{3,1},{4,6},{5,7},{6,4},{7,5},{8,10},{9,11},{10,... | collective-permute-start | bytes 786440 | tf_op jit(solution)/shard_map/ppermute | solution.py:375
  43.9 1.6 %collective-permute-start.18 = (bf16[2,4,128,128]{3,2,1,0:T(8,128)(2,1)S(1)}, bf16[2,4,128,128]{3,2,1,0:T(8,128)(2,1)S(1)}, u32[]{:S(2)}, u32[]{:S(2)}) collective-permute-start(bf16[2,4,128,128]{3,2,1,0:T(8,128)(2,1)S(1)} %get-tuple-element.137), channel_id=1, source_target_pairs={{0,4},{4,0},{8,12},{12,8},{16,20},{20,16},{24,28},{28,24},{1,5},{5... | collective-permute-start | bytes 786440 | tf_op jit(solution)/shard_map/ppermute | solution.py:377
  46.2 0.8 collective-permute-start.17
  48.8 2.4 %collective-permute-start.15 = (bf16[2,4,128,128]{3,2,1,0:T(8,128)(2,1)S(1)}, bf16[2,4,128,128]{3,2,1,0:T(8,128)(2,1)S(1)}, u32[]{:S(2)}, u32[]{:S(2)}) collective-permute-start(bf16[2,4,128,128]{3,2,1,0:T(8,128)(2,1)S(1)} %get-tuple-element.132), channel_id=1, source_target_pairs={{0,4},{4,0},{8,12},{12,8},{16,20},{20,16},{24,28},{28,24},{1,5},{5... | collective-permute-start | bytes 786440 | tf_op jit(solution)/shard_map/ppermute | solution.py:377
  51.2 2.6 %collective-permute-start.16 = (bf16[1,4,128,128]{3,2,1,0:T(8,128)(2,1)S(1)}, bf16[1,4,128,128]{3,2,1,0:T(8,128)(2,1)S(1)}, u32[]{:S(2)}, u32[]{:S(2)}) collective-permute-start(bf16[1,4,128,128]{3,2,1,0:T(8,128)(2,1)S(1)} %get-tuple-element.133), channel_id=1, source_target_pairs={{0,16},{4,20},{8,24},{12,28},{16,0},{20,4},{24,8},{28,12},{1,17},{... | collective-permute-start | bytes 393224 | tf_op jit(solution)/shard_map/ppermute | solution.py:377
  54.4 3.1 %collective-permute-start.21 = (bf16[2,4,128,128]{3,2,1,0:T(8,128)(2,1)S(1)}, bf16[2,4,128,128]{3,2,1,0:T(8,128)(2,1)S(1)}, u32[]{:S(2)}, u32[]{:S(2)}) collective-permute-start(bf16[2,4,128,128]{3,2,1,0:T(8,128)(2,1)S(1)} %get-tuple-element.147), channel_id=1, source_target_pairs={{0,8},{4,12},{8,0},{12,4},{16,24},{20,28},{24,16},{28,20},{1,9},{5... | collective-permute-start | bytes 786440 | tf_op jit(solution)/shard_map/ppermute | solution.py:377
  58.2 3.5 %inner.3.refs_4_ = f32[3,16,128,128]{3,2,1,0:T(8,128)S(1)} custom-call(s32[2]{0:T(128)S(1)} %copy-done.8, s32[16]{0:T(128)S(1)} %copy-done.7, bf16[4,16,128,128]{3,2,1,0:T(8,128)(2,1)S(1)} %copy-done.2, f32[2,4,128,128]{3,2,1,0:T(8,128)S(1)} %get-tuple-element.139.refs_0_), custom_call_target="tpu_custom_call" | custom-call | flops 1 | bytes 2583000 | tf_op jit(solution)/shard_map/inner/pallas_call | solution.py:215
  63.2 1.5 %collective-permute-start.23 = (bf16[2,4,128,128]{3,2,1,0:T(8,128)(2,1)S(1)}, bf16[2,4,128,128]{3,2,1,0:T(8,128)(2,1)S(1)}, u32[]{:S(2)}, u32[]{:S(2)}) collective-permute-start(bf16[2,4,128,128]{3,2,1,0:T(8,128)(2,1)S(1)} %get-tuple-element.153), channel_id=1, source_target_pairs={{0,2},{1,3},{2,0},{3,1},{4,6},{5,7},{6,4},{7,5},{8,10},{9,11},{10,... | collective-permute-start | bytes 786440 | tf_op jit(solution)/shard_map/ppermute | solution.py:375
  64.7 2.7 %collective-permute-start.20 = (bf16[1,4,128,128]{3,2,1,0:T(8,128)(2,1)S(1)}, bf16[1,4,128,128]{3,2,1,0:T(8,128)(2,1)S(1)}, u32[]{:S(2)}, u32[]{:S(2)}) collective-permute-start(bf16[1,4,128,128]{3,2,1,0:T(8,128)(2,1)S(1)} %get-tuple-element.144), channel_id=1, source_target_pairs={{0,16},{4,20},{8,24},{12,28},{16,0},{20,4},{24,8},{28,12},{1,17},{... | collective-permute-start | bytes 393224 | tf_op jit(solution)/shard_map/ppermute | solution.py:377
  68.4 3.5 %inner.4.refs_4_ = f32[3,16,128,128]{3,2,1,0:T(8,128)S(1)} custom-call(s32[2]{0:T(128)S(1)} %copy-done.8, s32[16]{0:T(128)S(1)} %copy-done.7, bf16[4,16,128,128]{3,2,1,0:T(8,128)(2,1)S(1)} %copy-done.3, f32[2,4,128,128]{3,2,1,0:T(8,128)S(1)} %get-tuple-element.148.refs_0_), custom_call_target="tpu_custom_call" | custom-call | flops 1 | bytes 2583000 | tf_op jit(solution)/shard_map/inner/pallas_call | solution.py:215
  71.9 0.7 down.9
  73.4 0.9 down.10
  76.7 1.4 %collective-permute-start.35 = (bf16[2,4,128,128]{3,2,1,0:T(8,128)(2,1)S(1)}, bf16[2,4,128,128]{3,2,1,0:T(8,128)(2,1)S(1)}, u32[]{:S(2)}, u32[]{:S(2)}) collective-permute-start(bf16[2,4,128,128]{3,2,1,0:T(8,128)(2,1)S(1)} %get-tuple-element.173), channel_id=1, source_target_pairs={{0,2},{1,3},{2,0},{3,1},{4,6},{5,7},{6,4},{7,5},{8,10},{9,11},{10,... | collective-permute-start | bytes 786440 | tf_op jit(solution)/shard_map/ppermute | solution.py:375
  78.2 2.7 %collective-permute-start.22 = (bf16[1,4,128,128]{3,2,1,0:T(8,128)(2,1)S(1)}, bf16[1,4,128,128]{3,2,1,0:T(8,128)(2,1)S(1)}, u32[]{:S(2)}, u32[]{:S(2)}) collective-permute-start(bf16[1,4,128,128]{3,2,1,0:T(8,128)(2,1)S(1)} %get-tuple-element.151), channel_id=1, source_target_pairs={{0,16},{4,20},{8,24},{12,28},{16,0},{20,4},{24,8},{28,12},{1,17},{... | collective-permute-start | bytes 393224 | tf_op jit(solution)/shard_map/ppermute | solution.py:377
  80.9 3.7 %grads.4 = (bf16[128,64,128]{2,1,0:T(8,128)(2,1)}, bf16[128,64,128]{2,1,0:T(8,128)(2,1)}, bf16[128,64,128]{2,1,0:T(8,128)(2,1)}, f32[8,128]{1,0:T(8,128)S(1)}) custom-call(s32[2]{0:T(128)S(1)} %copy-done.8, s32[16]{0:T(128)S(1)} %copy-done.7, bf16[4,16,128,128]{3,2,1,0:T(8,128)(2,1)S(1)} %copy-done.2, ...), custom_call_target="tpu_custom_call" | custom-call | flops 1 | bytes 2583000 | tf_op jit(solution)/shard_map/grads/pallas_call | solution.py:215
  84.6 3.5 %inner.5.refs_4_ = f32[3,16,128,128]{3,2,1,0:T(8,128)S(1)} custom-call(s32[2]{0:T(128)S(1)} %copy-done.8, s32[16]{0:T(128)S(1)} %copy-done.7, bf16[4,16,128,128]{3,2,1,0:T(8,128)(2,1)S(1)} %get-tuple-element.152.head_ref, f32[8,128]{1,0:T(8,128)S(1)} %get-tuple-element.161.refs_0_), custom_call_target="tpu_custom_call" | custom-call | flops 1 | bytes 2583000 | tf_op jit(solution)/shard_map/inner/pallas_call | solution.py:215
  89.5 0.8 down.13
  91.4 1.1 down.14
  93.6 3.7 %grads.5 = (bf16[128,64,128]{2,1,0:T(8,128)(2,1)}, bf16[128,64,128]{2,1,0:T(8,128)(2,1)}, bf16[128,64,128]{2,1,0:T(8,128)(2,1)}, f32[8,128]{1,0:T(8,128)S(1)}) custom-call(s32[2]{0:T(128)S(1)} %copy-done.8, s32[16]{0:T(128)S(1)} %copy-done.7, bf16[4,16,128,128]{3,2,1,0:T(8,128)(2,1)S(1)} %copy-done.3, ...), custom_call_target="tpu_custom_call", output_to_operand_aliasing={{0}: (9, {}), {1}: (10, {}), {2}: (11, {})} | custom-call | flops 1 | bytes 2583000 | tf_op jit(solution)/shard_map/grads/pallas_call | solution.py:215
  97.3 0.9 down.15
  99.3 3.7 %grads.6 = (bf16[128,64,128]{2,1,0:T(8,128)(2,1)}, bf16[128,64,128]{2,1,0:T(8,128)(2,1)}, bf16[128,64,128]{2,1,0:T(8,128)(2,1)}, f32[8,128]{1,0:T(8,128)S(1)}) custom-call(s32[2]{0:T(128)S(1)} %copy-done.8, s32[16]{0:T(128)S(1)} %copy-done.7, ...), custom_call_target="tpu_custom_call", output_to_operand_aliasing={{0}: (9, {}), {1}: (10, {}), {2}: (11, {})} | custom-call | flops 1 | bytes 2583000 | tf_op jit(solution)/shard_map/grads/pallas_call | solution.py:215
  103.1 6.0 %grads.7 = (bf16[128,64,128]{2,1,0:T(8,128)(2,1)}, bf16[128,64,128]{2,1,0:T(8,128)(2,1)}, bf16[128,64,128]{2,1,0:T(8,128)(2,1)}, f32[8,128]{1,0:T(8,128)}) custom-call(s32[2]{0:T(128)S(1)} %copy-done.8, s32[16]{0:T(128)S(1)} %copy-done.7, ...), custom_call_target="tpu_custom_call", output_to_operand_aliasing={{0}: (8, {}), {1}: (9, {}), {2}: (10, {})} | custom-call | flops 1 | bytes 2583000 | tf_op jit(solution)/shard_map/grads/pallas_call | solution.py:215
  (108 shorter events, 24.0 us)
Async XLA Ops:
  10.5 7.1 %collective-permute-start = (bf16[1,8,128,128]{3,2,1,0:T(8,128)(2,1)}, bf16[1,8,128,128]{3,2,1,0:T(8,128)(2,1)S(1)}, u32[]{:S(2)}, u32[]{:S(2)}) collective-permute-start(bf16[1,8,128,128]{3,2,1,0:T(8,128)(2,1)} %get-tuple-element.101), channel_id=1, source_target_pairs={{0,1},{1,0},{2,3},{3,2},{4,5},{5,4},{6,7},{7,6},{8,9},{9,8},{10,11... | collective-permute-start | bytes 786440 | tf_op jit(solution)/shard_map/ppermute | solution.py:375
  10.9 6.7 %collective-permute-start.1 = (bf16[1,8,128,128]{3,2,1,0:T(8,128)(2,1)}, bf16[1,8,128,128]{3,2,1,0:T(8,128)(2,1)S(1)}, u32[]{:S(2)}, u32[]{:S(2)}) collective-permute-start(bf16[1,8,128,128]{3,2,1,0:T(8,128)(2,1)} %get-tuple-element.102), channel_id=1, source_target_pairs={{0,1},{1,0},{2,3},{3,2},{4,5},{5,4},{6,7},{7,6},{8,9},{9,8},{10,11... | collective-permute-start | bytes 786440 | tf_op jit(solution)/shard_map/ppermute | solution.py:375
  14.7 10.8 %collective-permute-start.9 = (bf16[2,4,128,128]{3,2,1,0:T(8,128)(2,1)S(1)}, bf16[2,4,128,128]{3,2,1,0:T(8,128)(2,1)S(1)}, u32[]{:S(2)}, u32[]{:S(2)}) collective-permute-start(bf16[2,4,128,128]{3,2,1,0:T(8,128)(2,1)S(1)} %get-tuple-element.116), channel_id=1, source_target_pairs={{0,2},{1,3},{2,0},{3,1},{4,6},{5,7},{6,4},{7,5},{8,10},{9,11},{10,... | collective-permute-start | bytes 786440 | tf_op jit(solution)/shard_map/ppermute | solution.py:375
  18.3 11.5 %collective-permute-start.8 = (bf16[2,4,128,128]{3,2,1,0:T(8,128)(2,1)S(1)}, bf16[2,4,128,128]{3,2,1,0:T(8,128)(2,1)S(1)}, u32[]{:S(2)}, u32[]{:S(2)}) collective-permute-start(bf16[2,4,128,128]{3,2,1,0:T(8,128)(2,1)S(1)} %get-tuple-element.115), channel_id=1, source_target_pairs={{0,2},{1,3},{2,0},{3,1},{4,6},{5,7},{6,4},{7,5},{8,10},{9,11},{10,... | collective-permute-start | bytes 786440 | tf_op jit(solution)/shard_map/ppermute | solution.py:375
  24.8 7.4 %collective-permute-start.6 = (bf16[1,8,128,128]{3,2,1,0:T(8,128)(2,1)S(1)}, bf16[1,8,128,128]{3,2,1,0:T(8,128)(2,1)S(1)}, u32[]{:S(2)}, u32[]{:S(2)}) collective-permute-start(bf16[1,8,128,128]{3,2,1,0:T(8,128)(2,1)S(1)} %get-tuple-element.113), channel_id=1, source_target_pairs={{0,1},{1,0},{2,3},{3,2},{4,5},{5,4},{6,7},{7,6},{8,9},{9,8},{10,11... | collective-permute-start | bytes 786440 | tf_op jit(solution)/shard_map/ppermute | solution.py:375
  24.9 7.7 %collective-permute-start.7 = (bf16[1,8,128,128]{3,2,1,0:T(8,128)(2,1)S(1)}, bf16[1,8,128,128]{3,2,1,0:T(8,128)(2,1)S(1)}, u32[]{:S(2)}, u32[]{:S(2)}) collective-permute-start(bf16[1,8,128,128]{3,2,1,0:T(8,128)(2,1)S(1)} %get-tuple-element.114), channel_id=1, source_target_pairs={{0,1},{1,0},{2,3},{3,2},{4,5},{5,4},{6,7},{7,6},{8,9},{9,8},{10,11... | collective-permute-start | bytes 786440 | tf_op jit(solution)/shard_map/ppermute | solution.py:375
  25.4 9.7 %collective-permute-start.4 = (bf16[1,8,128,128]{3,2,1,0:T(8,128)(2,1)S(1)}, bf16[1,8,128,128]{3,2,1,0:T(8,128)(2,1)S(1)}, u32[]{:S(2)}, u32[]{:S(2)}) collective-permute-start(bf16[1,8,128,128]{3,2,1,0:T(8,128)(2,1)S(1)} %get-tuple-element.110), channel_id=1, source_target_pairs={{0,1},{1,0},{2,3},{3,2},{4,5},{5,4},{6,7},{7,6},{8,9},{9,8},{10,11... | collective-permute-start | bytes 786440 | tf_op jit(solution)/shard_map/ppermute | solution.py:375
  25.5 9.6 %collective-permute-start.5 = (bf16[1,8,128,128]{3,2,1,0:T(8,128)(2,1)S(1)}, bf16[1,8,128,128]{3,2,1,0:T(8,128)(2,1)S(1)}, u32[]{:S(2)}, u32[]{:S(2)}) collective-permute-start(bf16[1,8,128,128]{3,2,1,0:T(8,128)(2,1)S(1)} %get-tuple-element.111), channel_id=1, source_target_pairs={{0,1},{1,0},{2,3},{3,2},{4,5},{5,4},{6,7},{7,6},{8,9},{9,8},{10,11... | collective-permute-start | bytes 786440 | tf_op jit(solution)/shard_map/ppermute | solution.py:375
  29.8 9.2 %collective-permute-start.11 = (bf16[2,4,128,128]{3,2,1,0:T(8,128)(2,1)S(1)}, bf16[2,4,128,128]{3,2,1,0:T(8,128)(2,1)S(1)}, u32[]{:S(2)}, u32[]{:S(2)}) collective-permute-start(bf16[2,4,128,128]{3,2,1,0:T(8,128)(2,1)S(1)} %get-tuple-element.122), channel_id=1, source_target_pairs={{0,4},{4,0},{8,12},{12,8},{16,20},{20,16},{24,28},{28,24},{1,5},{5... | collective-permute-start | bytes 786440 | tf_op jit(solution)/shard_map/ppermute | solution.py:377
  32.3 13.3 %collective-permute-start.13 = (bf16[2,4,128,128]{3,2,1,0:T(8,128)(2,1)S(1)}, bf16[2,4,128,128]{3,2,1,0:T(8,128)(2,1)S(1)}, u32[]{:S(2)}, u32[]{:S(2)}) collective-permute-start(bf16[2,4,128,128]{3,2,1,0:T(8,128)(2,1)S(1)} %get-tuple-element.126), channel_id=1, source_target_pairs={{0,4},{4,0},{8,12},{12,8},{16,20},{20,16},{24,28},{28,24},{1,5},{5... | collective-permute-start | bytes 786440 | tf_op jit(solution)/shard_map/ppermute | solution.py:377
  33.3 10.0 %collective-permute-start.14 = (bf16[2,4,128,128]{3,2,1,0:T(8,128)(2,1)S(1)}, bf16[2,4,128,128]{3,2,1,0:T(8,128)(2,1)S(1)}, u32[]{:S(2)}, u32[]{:S(2)}) collective-permute-start(bf16[2,4,128,128]{3,2,1,0:T(8,128)(2,1)S(1)} %get-tuple-element.127), channel_id=1, source_target_pairs={{0,2},{1,3},{2,0},{3,1},{4,6},{5,7},{6,4},{7,5},{8,10},{9,11},{10,... | collective-permute-start | bytes 786440 | tf_op jit(solution)/shard_map/ppermute | solution.py:375
  39.7 7.6 %collective-permute-start.12 = (bf16[2,4,128,128]{3,2,1,0:T(8,128)(2,1)S(1)}, bf16[2,4,128,128]{3,2,1,0:T(8,128)(2,1)S(1)}, u32[]{:S(2)}, u32[]{:S(2)}) collective-permute-start(bf16[2,4,128,128]{3,2,1,0:T(8,128)(2,1)S(1)} %get-tuple-element.124), channel_id=1, source_target_pairs={{0,8},{4,12},{8,0},{12,4},{16,24},{20,28},{24,16},{28,20},{1,9},{5... | collective-permute-start | bytes 786440 | tf_op jit(solution)/shard_map/ppermute | solution.py:377
  41.8 6.4 %collective-permute-start.10 = (bf16[2,4,128,128]{3,2,1,0:T(8,128)(2,1)S(1)}, bf16[2,4,128,128]{3,2,1,0:T(8,128)(2,1)S(1)}, u32[]{:S(2)}, u32[]{:S(2)}) collective-permute-start(bf16[2,4,128,128]{3,2,1,0:T(8,128)(2,1)S(1)} %get-tuple-element.121), channel_id=1, source_target_pairs={{0,2},{1,3},{2,0},{3,1},{4,6},{5,7},{6,4},{7,5},{8,10},{9,11},{10,... | collective-permute-start | bytes 786440 | tf_op jit(solution)/shard_map/ppermute | solution.py:375
  43.9 9.8 %collective-permute-start.18 = (bf16[2,4,128,128]{3,2,1,0:T(8,128)(2,1)S(1)}, bf16[2,4,128,128]{3,2,1,0:T(8,128)(2,1)S(1)}, u32[]{:S(2)}, u32[]{:S(2)}) collective-permute-start(bf16[2,4,128,128]{3,2,1,0:T(8,128)(2,1)S(1)} %get-tuple-element.137), channel_id=1, source_target_pairs={{0,4},{4,0},{8,12},{12,8},{16,20},{20,16},{24,28},{28,24},{1,5},{5... | collective-permute-start | bytes 786440 | tf_op jit(solution)/shard_map/ppermute | solution.py:377
  46.2 11.3 %collective-permute-start.17 = (bf16[2,4,128,128]{3,2,1,0:T(8,128)(2,1)S(1)}, bf16[2,4,128,128]{3,2,1,0:T(8,128)(2,1)S(1)}, u32[]{:S(2)}, u32[]{:S(2)}) collective-permute-start(bf16[2,4,128,128]{3,2,1,0:T(8,128)(2,1)S(1)} %get-tuple-element.136), channel_id=1, source_target_pairs={{0,8},{4,12},{8,0},{12,4},{16,24},{20,28},{24,16},{28,20},{1,9},{5... | collective-permute-start | bytes 786440 | tf_op jit(solution)/shard_map/ppermute | solution.py:377
  48.8 13.6 %collective-permute-start.15 = (bf16[2,4,128,128]{3,2,1,0:T(8,128)(2,1)S(1)}, bf16[2,4,128,128]{3,2,1,0:T(8,128)(2,1)S(1)}, u32[]{:S(2)}, u32[]{:S(2)}) collective-permute-start(bf16[2,4,128,128]{3,2,1,0:T(8,128)(2,1)S(1)} %get-tuple-element.132), channel_id=1, source_target_pairs={{0,4},{4,0},{8,12},{12,8},{16,20},{20,16},{24,28},{28,24},{1,5},{5... | collective-permute-start | bytes 786440 | tf_op jit(solution)/shard_map/ppermute | solution.py:377
  51.2 10.5 %collective-permute-start.16 = (bf16[1,4,128,128]{3,2,1,0:T(8,128)(2,1)S(1)}, bf16[1,4,128,128]{3,2,1,0:T(8,128)(2,1)S(1)}, u32[]{:S(2)}, u32[]{:S(2)}) collective-permute-start(bf16[1,4,128,128]{3,2,1,0:T(8,128)(2,1)S(1)} %get-tuple-element.133), channel_id=1, source_target_pairs={{0,16},{4,20},{8,24},{12,28},{16,0},{20,4},{24,8},{28,12},{1,17},{... | collective-permute-start | bytes 393224 | tf_op jit(solution)/shard_map/ppermute | solution.py:377
  54.4 13.0 %collective-permute-start.21 = (bf16[2,4,128,128]{3,2,1,0:T(8,128)(2,1)S(1)}, bf16[2,4,128,128]{3,2,1,0:T(8,128)(2,1)S(1)}, u32[]{:S(2)}, u32[]{:S(2)}) collective-permute-start(bf16[2,4,128,128]{3,2,1,0:T(8,128)(2,1)S(1)} %get-tuple-element.147), channel_id=1, source_target_pairs={{0,8},{4,12},{8,0},{12,4},{16,24},{20,28},{24,16},{28,20},{1,9},{5... | collective-permute-start | bytes 786440 | tf_op jit(solution)/shard_map/ppermute | solution.py:377
  63.1 9.6 %collective-permute-start.19 = (bf16[2,4,128,128]{3,2,1,0:T(8,128)(2,1)S(1)}, bf16[2,4,128,128]{3,2,1,0:T(8,128)(2,1)S(1)}, u32[]{:S(2)}, u32[]{:S(2)}) collective-permute-start(bf16[2,4,128,128]{3,2,1,0:T(8,128)(2,1)S(1)} %get-tuple-element.142), channel_id=1, source_target_pairs={{0,8},{4,12},{8,0},{12,4},{16,24},{20,28},{24,16},{28,20},{1,9},{5... | collective-permute-start | bytes 786440 | tf_op jit(solution)/shard_map/ppermute | solution.py:377
  63.2 10.2 %collective-permute-start.23 = (bf16[2,4,128,128]{3,2,1,0:T(8,128)(2,1)S(1)}, bf16[2,4,128,128]{3,2,1,0:T(8,128)(2,1)S(1)}, u32[]{:S(2)}, u32[]{:S(2)}) collective-permute-start(bf16[2,4,128,128]{3,2,1,0:T(8,128)(2,1)S(1)} %get-tuple-element.153), channel_id=1, source_target_pairs={{0,2},{1,3},{2,0},{3,1},{4,6},{5,7},{6,4},{7,5},{8,10},{9,11},{10,... | collective-permute-start | bytes 786440 | tf_op jit(solution)/shard_map/ppermute | solution.py:375
  64.7 7.2 %collective-permute-start.20 = (bf16[1,4,128,128]{3,2,1,0:T(8,128)(2,1)S(1)}, bf16[1,4,128,128]{3,2,1,0:T(8,128)(2,1)S(1)}, u32[]{:S(2)}, u32[]{:S(2)}) collective-permute-start(bf16[1,4,128,128]{3,2,1,0:T(8,128)(2,1)S(1)} %get-tuple-element.144), channel_id=1, source_target_pairs={{0,16},{4,20},{8,24},{12,28},{16,0},{20,4},{24,8},{28,12},{1,17},{... | collective-permute-start | bytes 393224 | tf_op jit(solution)/shard_map/ppermute | solution.py:377
  68.1 7.4 %collective-permute-start.28 = (bf16[1,4,128,128]{3,2,1,0:T(8,128)(2,1)S(1)}, bf16[1,4,128,128]{3,2,1,0:T(8,128)(2,1)S(1)}, u32[]{:S(2)}, u32[]{:S(2)}) collective-permute-start(bf16[1,4,128,128]{3,2,1,0:T(8,128)(2,1)S(1)} %get-tuple-element.159), channel_id=1, source_target_pairs={{0,16},{4,20},{8,24},{12,28},{16,0},{20,4},{24,8},{28,12},{1,17},{... | collective-permute-start | bytes 393224 | tf_op jit(solution)/shard_map/ppermute | solution.py:377
  74.8 14.6 %collective-permute-start.30 = (bf16[2,4,128,128]{3,2,1,0:T(8,128)(2,1)S(1)}, bf16[2,4,128,128]{3,2,1,0:T(8,128)(2,1)S(1)}, u32[]{:S(2)}, u32[]{:S(2)}) collective-permute-start(bf16[2,4,128,128]{3,2,1,0:T(8,128)(2,1)S(1)} %get-tuple-element.164), channel_id=1, source_target_pairs={{0,2},{1,3},{2,0},{3,1},{4,6},{5,7},{6,4},{7,5},{8,10},{9,11},{10,... | collective-permute-start | bytes 786440 | tf_op jit(solution)/shard_map/ppermute | solution.py:375
  75.5 5.4 %collective-permute-start.26 = (bf16[1,4,128,128]{3,2,1,0:T(8,128)(2,1)S(1)}, bf16[1,4,128,128]{3,2,1,0:T(8,128)(2,1)S(1)}, u32[]{:S(2)}, u32[]{:S(2)}) collective-permute-start(bf16[1,4,128,128]{3,2,1,0:T(8,128)(2,1)S(1)} %get-tuple-element.157), channel_id=1, source_target_pairs={{0,1},{1,0},{2,3},{3,2},{4,5},{5,4},{6,7},{7,6},{8,9},{9,8},{10,11... | collective-permute-start | bytes 393224 | tf_op jit(solution)/shard_map/ppermute | solution.py:375
  75.5 5.4 %collective-permute-start.27 = (bf16[1,4,128,128]{3,2,1,0:T(8,128)(2,1)S(1)}, bf16[1,4,128,128]{3,2,1,0:T(8,128)(2,1)S(1)}, u32[]{:S(2)}, u32[]{:S(2)}) collective-permute-start(bf16[1,4,128,128]{3,2,1,0:T(8,128)(2,1)S(1)} %get-tuple-element.158), channel_id=1, source_target_pairs={{0,1},{1,0},{2,3},{3,2},{4,5},{5,4},{6,7},{7,6},{8,9},{9,8},{10,11... | collective-permute-start | bytes 393224 | tf_op jit(solution)/shard_map/ppermute | solution.py:375
  76.7 14.2 %collective-permute-start.35 = (bf16[2,4,128,128]{3,2,1,0:T(8,128)(2,1)S(1)}, bf16[2,4,128,128]{3,2,1,0:T(8,128)(2,1)S(1)}, u32[]{:S(2)}, u32[]{:S(2)}) collective-permute-start(bf16[2,4,128,128]{3,2,1,0:T(8,128)(2,1)S(1)} %get-tuple-element.173), channel_id=1, source_target_pairs={{0,2},{1,3},{2,0},{3,1},{4,6},{5,7},{6,4},{7,5},{8,10},{9,11},{10,... | collective-permute-start | bytes 786440 | tf_op jit(solution)/shard_map/ppermute | solution.py:375
  78.2 9.9 %collective-permute-start.22 = (bf16[1,4,128,128]{3,2,1,0:T(8,128)(2,1)S(1)}, bf16[1,4,128,128]{3,2,1,0:T(8,128)(2,1)S(1)}, u32[]{:S(2)}, u32[]{:S(2)}) collective-permute-start(bf16[1,4,128,128]{3,2,1,0:T(8,128)(2,1)S(1)} %get-tuple-element.151), channel_id=1, source_target_pairs={{0,16},{4,20},{8,24},{12,28},{16,0},{20,4},{24,8},{28,12},{1,17},{... | collective-permute-start | bytes 393224 | tf_op jit(solution)/shard_map/ppermute | solution.py:377
  88.8 8.5 %collective-permute-start.29 = (bf16[2,4,128,128]{3,2,1,0:T(8,128)(2,1)S(1)}, bf16[2,4,128,128]{3,2,1,0:T(8,128)(2,1)S(1)}, u32[]{:S(2)}, u32[]{:S(2)}) collective-permute-start(bf16[2,4,128,128]{3,2,1,0:T(8,128)(2,1)S(1)} %get-tuple-element.163), channel_id=1, source_target_pairs={{0,2},{1,3},{2,0},{3,1},{4,6},{5,7},{6,4},{7,5},{8,10},{9,11},{10,... | collective-permute-start | bytes 786440 | tf_op jit(solution)/shard_map/ppermute | solution.py:375
  92.5 5.9 %collective-permute-start.40 = (bf16[1,4,128,128]{3,2,1,0:T(8,128)(2,1)S(1)}, bf16[1,4,128,128]{3,2,1,0:T(8,128)(2,1)S(1)}, u32[]{:S(2)}, u32[]{:S(2)}) collective-permute-start(bf16[1,4,128,128]{3,2,1,0:T(8,128)(2,1)S(1)} %get-tuple-element.181), channel_id=1, source_target_pairs={{0,1},{1,0},{2,3},{3,2},{4,5},{5,4},{6,7},{7,6},{8,9},{9,8},{10,11... | collective-permute-start | bytes 393224 | tf_op jit(solution)/shard_map/ppermute | solution.py:375
  92.6 6.1 %collective-permute-start.41 = (bf16[1,4,128,128]{3,2,1,0:T(8,128)(2,1)S(1)}, bf16[1,4,128,128]{3,2,1,0:T(8,128)(2,1)S(1)}, u32[]{:S(2)}, u32[]{:S(2)}) collective-permute-start(bf16[1,4,128,128]{3,2,1,0:T(8,128)(2,1)S(1)} %get-tuple-element.182), channel_id=1, source_target_pairs={{0,1},{1,0},{2,3},{3,2},{4,5},{5,4},{6,7},{7,6},{8,9},{9,8},{10,11... | collective-permute-start | bytes 393224 | tf_op jit(solution)/shard_map/ppermute | solution.py:375
  93.1 5.8 %collective-permute-start.42 = (bf16[1,4,128,128]{3,2,1,0:T(8,128)(2,1)S(1)}, bf16[1,4,128,128]{3,2,1,0:T(8,128)(2,1)S(1)}, u32[]{:S(2)}, u32[]{:S(2)}) collective-permute-start(bf16[1,4,128,128]{3,2,1,0:T(8,128)(2,1)S(1)} %get-tuple-element.183), channel_id=1, source_target_pairs={{0,1},{1,0},{2,3},{3,2},{4,5},{5,4},{6,7},{7,6},{8,9},{9,8},{10,11... | collective-permute-start | bytes 393224 | tf_op jit(solution)/shard_map/ppermute | solution.py:375
  93.1 6.1 %collective-permute-start.43 = (bf16[1,4,128,128]{3,2,1,0:T(8,128)(2,1)S(1)}, bf16[1,4,128,128]{3,2,1,0:T(8,128)(2,1)S(1)}, u32[]{:S(2)}, u32[]{:S(2)}) collective-permute-start(bf16[1,4,128,128]{3,2,1,0:T(8,128)(2,1)S(1)} %get-tuple-element.184), channel_id=1, source_target_pairs={{0,1},{1,0},{2,3},{3,2},{4,5},{5,4},{6,7},{7,6},{8,9},{9,8},{10,11... | collective-permute-start | bytes 393224 | tf_op jit(solution)/shard_map/ppermute | solution.py:375
  (21 other events, 76.5 us)

commit v7 on v6

--- a/solution.py
+++ b/solution.py
@@ -361,7 +361,7 @@
         if chunks > 2:
             line += [(2, -1)]
             line.insert(len(line) - 6, (1, -1))
-            line.insert(line.index((0, count - 3)), (0, -1))
+            line.insert(1, (0, -1))
         line += spare[-1:]
         for chunk in range(1, chunks):
             line += [(chunk, fill)] if chunk == 1 else []

time: 109 us -> 114 us (1.046)
  starting transfers between devices: 37.9 us -> 40.4 us
  waiting for transfers between devices: 8.33 us -> 10.2 us
    ppermute x32, waiting for transfers between devices: 4.68 us -> 8.12 us  [swap(): return lax.ppermute(x, 'head', moves)]
    ppermute x12, waiting for transfers between devices: 3.65 us -> 2.05 us  [swap(): return lax.ppermute(x, 'seq', [(i, i ^ bit) for i in range(self.seq_size)])]
    ppermute x12, starting transfers between devices: 20.4 us -> 22 us  [swap(): return lax.ppermute(x, 'seq', [(i, i ^ bit) for i in range(self.seq_size)])]
  transfers between devices with their start and end apart: 44 -> 44, of which waited for: 6 -> 6; matrix products, arithmetic and copies ran while one was open for 0% -> 0% of each run, Pallas kernels for 41% -> 40%
where the time goes in v7:
time: 114 us
  Pallas kernels  59.7 us (52%)
  starting transfers between devices  40.4 us (35%)
  waiting for transfers between devices  10.2 us (9%)
  local copies, waits for them, and re-layouts  1.85 us (2%)
  between operations  1.22 us (1%)
    pallas_call x33, Pallas kernels, call(): pl.pallas_call(body, in_specs=in_specs, out_specs=out_specs, out_shape=ou...  59.7 us
    ppermute x12, starting transfers between devices, swap(): return lax.ppermute(x, 'seq', [(i, i ^ bit) for i in range(self.seq_size)])  22 us
    ppermute x32, starting transfers between devices, swap(): return lax.ppermute(x, 'head', moves)  18.5 us
    ppermute x32, waiting for transfers between devices, swap(): return lax.ppermute(x, 'head', moves)  8.12 us
  transfers between devices with their start and end apart: 44, of which 6 were waited for; matrix products, arithmetic and copies ran while one was open for 0% of the time, Pallas kernels for 40%

profile of v7, /device:TPU:0, one launch (start us, length us, event | category | flops | bytes accessed | tf_op | source)
XLA Modules:
  0.0 114.0 jit_solution(2000228881769888339)
XLA Ops:
  1.3 8.6 %states.2 = (f32[44]{0:T(128)}, f32[2,8,128,128]{3,2,1,0:T(8,128)}, f32[2,8,128,128]{3,2,1,0:T(8,128)}, bf16[4,16,128,128]{3,2,1,0:T(8,128)(2,1)}, bf16[4,16,128...) custom-call(s32[2]{0:T(128)} %pad_add_fusion.place_ref, ...), custom_call_target="tpu_custom_call" | custom-call | flops 1 | bytes 25830000 | tf_op jit(solution)/shard_map/states/pallas_call | solution.py:215
  11.0 0.8 collective-permute-done.2.refs_1_.refs_3_
  12.2 1.2 %copy-done = f32[2,8,128,128]{3,2,1,0:T(8,128)S(1)} copy-done((f32[2,8,128,128]{3,2,1,0:T(8,128)S(1)}, f32[2,8,128,128]{3,2,1,0:T(8,128)}, u32[]{:S(2)}) %copy-start) | copy-done | bytes 1048600
  14.7 2.9 %collective-permute-start.9 = (bf16[2,4,128,128]{3,2,1,0:T(8,128)(2,1)S(1)}, bf16[2,4,128,128]{3,2,1,0:T(8,128)(2,1)S(1)}, u32[]{:S(2)}, u32[]{:S(2)}) collective-permute-start(bf16[2,4,128,128]{3,2,1,0:T(8,128)(2,1)S(1)} %get-tuple-element.117), channel_id=1, source_target_pairs={{0,2},{1,3},{2,0},{3,1},{4,6},{5,7},{6,4},{7,5},{8,10},{9,11},{10,... | collective-permute-start | bytes 786440 | tf_op jit(solution)/shard_map/ppermute | solution.py:375
  18.8 6.0 %states.3 = (f32[2,8,128,128]{3,2,1,0:T(8,128)S(1)}, f32[2,8,128,128]{3,2,1,0:T(8,128)S(1)}, bf16[4,16,128,128]{3,2,1,0:T(8,128)(2,1)S(1)}, bf16[4,16,128,128]{3...) custom-call(s32[2]{0:T(128)S(1)} %copy-done.8, ...), custom_call_target="tpu_custom_call" | custom-call | flops 1 | bytes 25830000 | tf_op jit(solution)/shard_map/states/pallas_call | solution.py:215
  26.6 3.2 %collective-permute-done.8.refs_1_.refs_3_ = bf16[2,4,128,128]{3,2,1,0:T(8,128)(2,1)S(1)} collective-permute-done((bf16[2,4,128,128]{3,2,1,0:T(8,128)(2,1)S(1)}, bf16[2,4,128,128]{3,2,1,0:T(8,128)(2,1)S(1)}, u32[]{:S(2)}, u32[]{:S(2)}) %collective-permute-start.8) | collective-permute-done | bytes 262176 | tf_op jit(solution)/shard_map/ppermute | solution.py:375
  29.8 1.8 %collective-permute-start.11 = (bf16[2,4,128,128]{3,2,1,0:T(8,128)(2,1)S(1)}, bf16[2,4,128,128]{3,2,1,0:T(8,128)(2,1)S(1)}, u32[]{:S(2)}, u32[]{:S(2)}) collective-permute-start(bf16[2,4,128,128]{3,2,1,0:T(8,128)(2,1)S(1)} %get-tuple-element.123), channel_id=1, source_target_pairs={{0,4},{4,0},{8,12},{12,8},{16,20},{20,16},{24,28},{28,24},{1,5},{5... | collective-permute-start | bytes 786440 | tf_op jit(solution)/shard_map/ppermute | solution.py:377
  31.6 3.7 %inner.3.refs_2_.refs_4_ = f32[3,16,128,128]{3,2,1,0:T(8,128)S(1)} custom-call(s32[2]{0:T(128)S(1)} %copy-done.8, s32[16]{0:T(128)S(1)} %copy-done.7, bf16[4,16,128,128]{3,2,1,0:T(8,128)(2,1)S(1)} %copy-done.2, f32[2,4,128,128]{3,2,1,0:T(8,128)S(1)} %get-tuple-element.118.refs_0_), custom_call_target="tpu_custom_call" | custom-call | flops 1 | bytes 2583000 | tf_op jit(solution)/shard_map/inner/pallas_call | solution.py:215
  36.9 1.8 %collective-permute-start.14 = (bf16[2,4,128,128]{3,2,1,0:T(8,128)(2,1)S(1)}, bf16[2,4,128,128]{3,2,1,0:T(8,128)(2,1)S(1)}, u32[]{:S(2)}, u32[]{:S(2)}) collective-permute-start(bf16[2,4,128,128]{3,2,1,0:T(8,128)(2,1)S(1)} %get-tuple-element.128), channel_id=1, source_target_pairs={{0,2},{1,3},{2,0},{3,1},{4,6},{5,7},{6,4},{7,5},{8,10},{9,11},{10,... | collective-permute-start | bytes 786440 | tf_op jit(solution)/shard_map/ppermute | solution.py:375
  40.1 1.6 %collective-permute-start.12 = (bf16[2,4,128,128]{3,2,1,0:T(8,128)(2,1)S(1)}, bf16[2,4,128,128]{3,2,1,0:T(8,128)(2,1)S(1)}, u32[]{:S(2)}, u32[]{:S(2)}) collective-permute-start(bf16[2,4,128,128]{3,2,1,0:T(8,128)(2,1)S(1)} %get-tuple-element.125), channel_id=1, source_target_pairs={{0,8},{4,12},{8,0},{12,4},{16,24},{20,28},{24,16},{28,20},{1,9},{5... | collective-permute-start | bytes 786440 | tf_op jit(solution)/shard_map/ppermute | solution.py:377
  42.3 3.7 %collective-permute-done.14.refs_1_.refs_3_ = bf16[2,4,128,128]{3,2,1,0:T(8,128)(2,1)S(1)} collective-permute-done((bf16[2,4,128,128]{3,2,1,0:T(8,128)(2,1)S(1)}, bf16[2,4,128,128]{3,2,1,0:T(8,128)(2,1)S(1)}, u32[]{:S(2)}, u32[]{:S(2)}) %collective-permute-start.14) | collective-permute-done | bytes 262176 | tf_op jit(solution)/shard_map/ppermute | solution.py:375
  46.6 1.4 %collective-permute-start.18 = (bf16[2,4,128,128]{3,2,1,0:T(8,128)(2,1)S(1)}, bf16[2,4,128,128]{3,2,1,0:T(8,128)(2,1)S(1)}, u32[]{:S(2)}, u32[]{:S(2)}) collective-permute-start(bf16[2,4,128,128]{3,2,1,0:T(8,128)(2,1)S(1)} %get-tuple-element.137), channel_id=1, source_target_pairs={{0,4},{4,0},{8,12},{12,8},{16,20},{20,16},{24,28},{28,24},{1,5},{5... | collective-permute-start | bytes 786440 | tf_op jit(solution)/shard_map/ppermute | solution.py:377
  48.7 2.3 %collective-permute-start.17 = (bf16[2,4,128,128]{3,2,1,0:T(8,128)(2,1)S(1)}, bf16[2,4,128,128]{3,2,1,0:T(8,128)(2,1)S(1)}, u32[]{:S(2)}, u32[]{:S(2)}) collective-permute-start(bf16[2,4,128,128]{3,2,1,0:T(8,128)(2,1)S(1)} %get-tuple-element.136), channel_id=1, source_target_pairs={{0,8},{4,12},{8,0},{12,4},{16,24},{20,28},{24,16},{28,20},{1,9},{5... | collective-permute-start | bytes 786440 | tf_op jit(solution)/shard_map/ppermute | solution.py:377
  52.9 2.6 %collective-permute-start.16 = (bf16[1,4,128,128]{3,2,1,0:T(8,128)(2,1)S(1)}, bf16[1,4,128,128]{3,2,1,0:T(8,128)(2,1)S(1)}, u32[]{:S(2)}, u32[]{:S(2)}) collective-permute-start(bf16[1,4,128,128]{3,2,1,0:T(8,128)(2,1)S(1)} %get-tuple-element.134), channel_id=1, source_target_pairs={{0,16},{4,20},{8,24},{12,28},{16,0},{20,4},{24,8},{28,12},{1,17},{... | collective-permute-start | bytes 393224 | tf_op jit(solution)/shard_map/ppermute | solution.py:377
  56.2 2.3 %collective-permute-start.21 = (bf16[2,4,128,128]{3,2,1,0:T(8,128)(2,1)S(1)}, bf16[2,4,128,128]{3,2,1,0:T(8,128)(2,1)S(1)}, u32[]{:S(2)}, u32[]{:S(2)}) collective-permute-start(bf16[2,4,128,128]{3,2,1,0:T(8,128)(2,1)S(1)} %get-tuple-element.147), channel_id=1, source_target_pairs={{0,8},{4,12},{8,0},{12,4},{16,24},{20,28},{24,16},{28,20},{1,9},{5... | collective-permute-start | bytes 786440 | tf_op jit(solution)/shard_map/ppermute | solution.py:377
  61.1 3.5 %collective-permute-start.19 = (bf16[2,4,128,128]{3,2,1,0:T(8,128)(2,1)S(1)}, bf16[2,4,128,128]{3,2,1,0:T(8,128)(2,1)S(1)}, u32[]{:S(2)}, u32[]{:S(2)}) collective-permute-start(bf16[2,4,128,128]{3,2,1,0:T(8,128)(2,1)S(1)} %get-tuple-element.142), channel_id=1, source_target_pairs={{0,8},{4,12},{8,0},{12,4},{16,24},{20,28},{24,16},{28,20},{1,9},{5... | collective-permute-start | bytes 786440 | tf_op jit(solution)/shard_map/ppermute | solution.py:377
  64.6 1.9 %collective-permute-start.23 = (bf16[2,4,128,128]{3,2,1,0:T(8,128)(2,1)S(1)}, bf16[2,4,128,128]{3,2,1,0:T(8,128)(2,1)S(1)}, u32[]{:S(2)}, u32[]{:S(2)}) collective-permute-start(bf16[2,4,128,128]{3,2,1,0:T(8,128)(2,1)S(1)} %get-tuple-element.153), channel_id=1, source_target_pairs={{0,2},{1,3},{2,0},{3,1},{4,6},{5,7},{6,4},{7,5},{8,10},{9,11},{10,... | collective-permute-start | bytes 786440 | tf_op jit(solution)/shard_map/ppermute | solution.py:375
  66.5 2.8 %collective-permute-start.20 = (bf16[1,4,128,128]{3,2,1,0:T(8,128)(2,1)S(1)}, bf16[1,4,128,128]{3,2,1,0:T(8,128)(2,1)S(1)}, u32[]{:S(2)}, u32[]{:S(2)}) collective-permute-start(bf16[1,4,128,128]{3,2,1,0:T(8,128)(2,1)S(1)} %get-tuple-element.144), channel_id=1, source_target_pairs={{0,16},{4,20},{8,24},{12,28},{16,0},{20,4},{24,8},{28,12},{1,17},{... | collective-permute-start | bytes 393224 | tf_op jit(solution)/shard_map/ppermute | solution.py:377
  70.0 2.3 %collective-permute-start.28 = (bf16[1,4,128,128]{3,2,1,0:T(8,128)(2,1)S(1)}, bf16[1,4,128,128]{3,2,1,0:T(8,128)(2,1)S(1)}, u32[]{:S(2)}, u32[]{:S(2)}) collective-permute-start(bf16[1,4,128,128]{3,2,1,0:T(8,128)(2,1)S(1)} %get-tuple-element.159), channel_id=1, source_target_pairs={{0,16},{4,20},{8,24},{12,28},{16,0},{20,4},{24,8},{28,12},{1,17},{... | collective-permute-start | bytes 393224 | tf_op jit(solution)/shard_map/ppermute | solution.py:377
  72.3 3.5 %inner.4.refs_4_ = f32[3,16,128,128]{3,2,1,0:T(8,128)S(1)} custom-call(s32[2]{0:T(128)S(1)} %copy-done.8, s32[16]{0:T(128)S(1)} %copy-done.7, bf16[4,16,128,128]{3,2,1,0:T(8,128)(2,1)S(1)} %copy-done.3, f32[2,4,128,128]{3,2,1,0:T(8,128)S(1)} %get-tuple-element.148.refs_0_), custom_call_target="tpu_custom_call" | custom-call | flops 1 | bytes 2583000 | tf_op jit(solution)/shard_map/inner/pallas_call | solution.py:215
  77.3 0.9 down.10
  78.7 2.4 %collective-permute-start.30 = (bf16[2,4,128,128]{3,2,1,0:T(8,128)(2,1)S(1)}, bf16[2,4,128,128]{3,2,1,0:T(8,128)(2,1)S(1)}, u32[]{:S(2)}, u32[]{:S(2)}) collective-permute-start(bf16[2,4,128,128]{3,2,1,0:T(8,128)(2,1)S(1)} %get-tuple-element.164), channel_id=1, source_target_pairs={{0,2},{1,3},{2,0},{3,1},{4,6},{5,7},{6,4},{7,5},{8,10},{9,11},{10,... | collective-permute-start | bytes 786440 | tf_op jit(solution)/shard_map/ppermute | solution.py:375
  82.9 3.8 %grads.4 = (bf16[128,64,128]{2,1,0:T(8,128)(2,1)}, bf16[128,64,128]{2,1,0:T(8,128)(2,1)}, bf16[128,64,128]{2,1,0:T(8,128)(2,1)}, f32[8,128]{1,0:T(8,128)S(1)}) custom-call(s32[2]{0:T(128)S(1)} %copy-done.8, s32[16]{0:T(128)S(1)} %copy-done.7, bf16[4,16,128,128]{3,2,1,0:T(8,128)(2,1)S(1)} %copy-done.2, ...), custom_call_target="tpu_custom_call" | custom-call | flops 1 | bytes 2583000 | tf_op jit(solution)/shard_map/grads/pallas_call | solution.py:215
  86.7 3.5 %inner.5.refs_4_ = f32[3,16,128,128]{3,2,1,0:T(8,128)S(1)} custom-call(s32[2]{0:T(128)S(1)} %copy-done.8, s32[16]{0:T(128)S(1)} %copy-done.7, bf16[4,16,128,128]{3,2,1,0:T(8,128)(2,1)S(1)} %get-tuple-element.152.head_ref, f32[8,128]{1,0:T(8,128)S(1)} %get-tuple-element.161.refs_0_), custom_call_target="tpu_custom_call" | custom-call | flops 1 | bytes 2583000 | tf_op jit(solution)/shard_map/inner/pallas_call | solution.py:215
  90.1 1.5 %collective-permute-done.22.refs_1_ = bf16[1,4,128,128]{3,2,1,0:T(8,128)(2,1)S(1)} collective-permute-done((bf16[1,4,128,128]{3,2,1,0:T(8,128)(2,1)S(1)}, bf16[1,4,128,128]{3,2,1,0:T(8,128)(2,1)S(1)}, u32[]{:S(2)}, u32[]{:S(2)}) %collective-permute-start.22) | collective-permute-done | bytes 131104 | tf_op jit(solution)/shard_map/ppermute | solution.py:377
  92.4 1.7 %collective-permute-start.29 = (bf16[2,4,128,128]{3,2,1,0:T(8,128)(2,1)S(1)}, bf16[2,4,128,128]{3,2,1,0:T(8,128)(2,1)S(1)}, u32[]{:S(2)}, u32[]{:S(2)}) collective-permute-start(bf16[2,4,128,128]{3,2,1,0:T(8,128)(2,1)S(1)} %get-tuple-element.163), channel_id=1, source_target_pairs={{0,2},{1,3},{2,0},{3,1},{4,6},{5,7},{6,4},{7,5},{8,10},{9,11},{10,... | collective-permute-start | bytes 786440 | tf_op jit(solution)/shard_map/ppermute | solution.py:375
  94.1 0.8 down.13
  96.1 1.1 down.14
  98.2 3.8 %grads.5 = (bf16[128,64,128]{2,1,0:T(8,128)(2,1)}, bf16[128,64,128]{2,1,0:T(8,128)(2,1)}, bf16[128,64,128]{2,1,0:T(8,128)(2,1)}, f32[8,128]{1,0:T(8,128)S(1)}) custom-call(s32[2]{0:T(128)S(1)} %copy-done.8, s32[16]{0:T(128)S(1)} %copy-done.7, bf16[4,16,128,128]{3,2,1,0:T(8,128)(2,1)S(1)} %copy-done.3, ...), custom_call_target="tpu_custom_call", output_to_operand_aliasing={{0}: (9, {}), {1}: (10, {}), {2}: (11, {})} | custom-call | flops 1 | bytes 2583000 | tf_op jit(solution)/shard_map/grads/pallas_call | solution.py:215
  102.0 0.9 down.15
  104.0 3.7 %grads.6 = (bf16[128,64,128]{2,1,0:T(8,128)(2,1)}, bf16[128,64,128]{2,1,0:T(8,128)(2,1)}, bf16[128,64,128]{2,1,0:T(8,128)(2,1)}, f32[8,128]{1,0:T(8,128)S(1)}) custom-call(s32[2]{0:T(128)S(1)} %copy-done.8, s32[16]{0:T(128)S(1)} %copy-done.7, ...), custom_call_target="tpu_custom_call", output_to_operand_aliasing={{0}: (9, {}), {1}: (10, {}), {2}: (11, {})} | custom-call | flops 1 | bytes 2583000 | tf_op jit(solution)/shard_map/grads/pallas_call | solution.py:215
  107.8 6.0 %grads.7 = (bf16[128,64,128]{2,1,0:T(8,128)(2,1)}, bf16[128,64,128]{2,1,0:T(8,128)(2,1)}, bf16[128,64,128]{2,1,0:T(8,128)(2,1)}, f32[8,128]{1,0:T(8,128)}) custom-call(s32[2]{0:T(128)S(1)} %copy-done.8, s32[16]{0:T(128)S(1)} %copy-done.7, ...), custom_call_target="tpu_custom_call", output_to_operand_aliasing={{0}: (8, {}), {1}: (9, {}), {2}: (10, {})} | custom-call | flops 1 | bytes 2583000 | tf_op jit(solution)/shard_map/grads/pallas_call | solution.py:215
  (108 shorter events, 24.7 us)
Async XLA Ops:
  10.5 7.1 %collective-permute-start = (bf16[1,8,128,128]{3,2,1,0:T(8,128)(2,1)}, bf16[1,8,128,128]{3,2,1,0:T(8,128)(2,1)S(1)}, u32[]{:S(2)}, u32[]{:S(2)}) collective-permute-start(bf16[1,8,128,128]{3,2,1,0:T(8,128)(2,1)} %get-tuple-element.101), channel_id=1, source_target_pairs={{0,1},{1,0},{2,3},{3,2},{4,5},{5,4},{6,7},{7,6},{8,9},{9,8},{10,11... | collective-permute-start | bytes 786440 | tf_op jit(solution)/shard_map/ppermute | solution.py:375
  10.9 6.7 %collective-permute-start.1 = (bf16[1,8,128,128]{3,2,1,0:T(8,128)(2,1)}, bf16[1,8,128,128]{3,2,1,0:T(8,128)(2,1)S(1)}, u32[]{:S(2)}, u32[]{:S(2)}) collective-permute-start(bf16[1,8,128,128]{3,2,1,0:T(8,128)(2,1)} %get-tuple-element.102), channel_id=1, source_target_pairs={{0,1},{1,0},{2,3},{3,2},{4,5},{5,4},{6,7},{7,6},{8,9},{9,8},{10,11... | collective-permute-start | bytes 786440 | tf_op jit(solution)/shard_map/ppermute | solution.py:375
  14.7 10.8 %collective-permute-start.9 = (bf16[2,4,128,128]{3,2,1,0:T(8,128)(2,1)S(1)}, bf16[2,4,128,128]{3,2,1,0:T(8,128)(2,1)S(1)}, u32[]{:S(2)}, u32[]{:S(2)}) collective-permute-start(bf16[2,4,128,128]{3,2,1,0:T(8,128)(2,1)S(1)} %get-tuple-element.117), channel_id=1, source_target_pairs={{0,2},{1,3},{2,0},{3,1},{4,6},{5,7},{6,4},{7,5},{8,10},{9,11},{10,... | collective-permute-start | bytes 786440 | tf_op jit(solution)/shard_map/ppermute | solution.py:375
  18.3 11.5 %collective-permute-start.8 = (bf16[2,4,128,128]{3,2,1,0:T(8,128)(2,1)S(1)}, bf16[2,4,128,128]{3,2,1,0:T(8,128)(2,1)S(1)}, u32[]{:S(2)}, u32[]{:S(2)}) collective-permute-start(bf16[2,4,128,128]{3,2,1,0:T(8,128)(2,1)S(1)} %get-tuple-element.115), channel_id=1, source_target_pairs={{0,2},{1,3},{2,0},{3,1},{4,6},{5,7},{6,4},{7,5},{8,10},{9,11},{10,... | collective-permute-start | bytes 786440 | tf_op jit(solution)/shard_map/ppermute | solution.py:375
  24.9 11.0 %collective-permute-start.6 = (bf16[1,8,128,128]{3,2,1,0:T(8,128)(2,1)S(1)}, bf16[1,8,128,128]{3,2,1,0:T(8,128)(2,1)S(1)}, u32[]{:S(2)}, u32[]{:S(2)}) collective-permute-start(bf16[1,8,128,128]{3,2,1,0:T(8,128)(2,1)S(1)} %get-tuple-element.113), channel_id=1, source_target_pairs={{0,1},{1,0},{2,3},{3,2},{4,5},{5,4},{6,7},{7,6},{8,9},{9,8},{10,11... | collective-permute-start | bytes 786440 | tf_op jit(solution)/shard_map/ppermute | solution.py:375
  25.0 11.3 %collective-permute-start.7 = (bf16[1,8,128,128]{3,2,1,0:T(8,128)(2,1)S(1)}, bf16[1,8,128,128]{3,2,1,0:T(8,128)(2,1)S(1)}, u32[]{:S(2)}, u32[]{:S(2)}) collective-permute-start(bf16[1,8,128,128]{3,2,1,0:T(8,128)(2,1)S(1)} %get-tuple-element.114), channel_id=1, source_target_pairs={{0,1},{1,0},{2,3},{3,2},{4,5},{5,4},{6,7},{7,6},{8,9},{9,8},{10,11... | collective-permute-start | bytes 786440 | tf_op jit(solution)/shard_map/ppermute | solution.py:375
  25.5 13.3 %collective-permute-start.4 = (bf16[1,8,128,128]{3,2,1,0:T(8,128)(2,1)S(1)}, bf16[1,8,128,128]{3,2,1,0:T(8,128)(2,1)S(1)}, u32[]{:S(2)}, u32[]{:S(2)}) collective-permute-start(bf16[1,8,128,128]{3,2,1,0:T(8,128)(2,1)S(1)} %get-tuple-element.110), channel_id=1, source_target_pairs={{0,1},{1,0},{2,3},{3,2},{4,5},{5,4},{6,7},{7,6},{8,9},{9,8},{10,11... | collective-permute-start | bytes 786440 | tf_op jit(solution)/shard_map/ppermute | solution.py:375
  25.5 13.2 %collective-permute-start.5 = (bf16[1,8,128,128]{3,2,1,0:T(8,128)(2,1)S(1)}, bf16[1,8,128,128]{3,2,1,0:T(8,128)(2,1)S(1)}, u32[]{:S(2)}, u32[]{:S(2)}) collective-permute-start(bf16[1,8,128,128]{3,2,1,0:T(8,128)(2,1)S(1)} %get-tuple-element.111), channel_id=1, source_target_pairs={{0,1},{1,0},{2,3},{3,2},{4,5},{5,4},{6,7},{7,6},{8,9},{9,8},{10,11... | collective-permute-start | bytes 786440 | tf_op jit(solution)/shard_map/ppermute | solution.py:375
  29.8 9.6 %collective-permute-start.11 = (bf16[2,4,128,128]{3,2,1,0:T(8,128)(2,1)S(1)}, bf16[2,4,128,128]{3,2,1,0:T(8,128)(2,1)S(1)}, u32[]{:S(2)}, u32[]{:S(2)}) collective-permute-start(bf16[2,4,128,128]{3,2,1,0:T(8,128)(2,1)S(1)} %get-tuple-element.123), channel_id=1, source_target_pairs={{0,4},{4,0},{8,12},{12,8},{16,20},{20,16},{24,28},{28,24},{1,5},{5... | collective-permute-start | bytes 786440 | tf_op jit(solution)/shard_map/ppermute | solution.py:377
  35.9 12.1 %collective-permute-start.13 = (bf16[2,4,128,128]{3,2,1,0:T(8,128)(2,1)S(1)}, bf16[2,4,128,128]{3,2,1,0:T(8,128)(2,1)S(1)}, u32[]{:S(2)}, u32[]{:S(2)}) collective-permute-start(bf16[2,4,128,128]{3,2,1,0:T(8,128)(2,1)S(1)} %get-tuple-element.127), channel_id=1, source_target_pairs={{0,4},{4,0},{8,12},{12,8},{16,20},{20,16},{24,28},{28,24},{1,5},{5... | collective-permute-start | bytes 786440 | tf_op jit(solution)/shard_map/ppermute | solution.py:377
  36.9 9.0 %collective-permute-start.14 = (bf16[2,4,128,128]{3,2,1,0:T(8,128)(2,1)S(1)}, bf16[2,4,128,128]{3,2,1,0:T(8,128)(2,1)S(1)}, u32[]{:S(2)}, u32[]{:S(2)}) collective-permute-start(bf16[2,4,128,128]{3,2,1,0:T(8,128)(2,1)S(1)} %get-tuple-element.128), channel_id=1, source_target_pairs={{0,2},{1,3},{2,0},{3,1},{4,6},{5,7},{6,4},{7,5},{8,10},{9,11},{10,... | collective-permute-start | bytes 786440 | tf_op jit(solution)/shard_map/ppermute | solution.py:375
  40.1 10.9 %collective-permute-start.12 = (bf16[2,4,128,128]{3,2,1,0:T(8,128)(2,1)S(1)}, bf16[2,4,128,128]{3,2,1,0:T(8,128)(2,1)S(1)}, u32[]{:S(2)}, u32[]{:S(2)}) collective-permute-start(bf16[2,4,128,128]{3,2,1,0:T(8,128)(2,1)S(1)} %get-tuple-element.125), channel_id=1, source_target_pairs={{0,8},{4,12},{8,0},{12,4},{16,24},{20,28},{24,16},{28,20},{1,9},{5... | collective-permute-start | bytes 786440 | tf_op jit(solution)/shard_map/ppermute | solution.py:377
  41.8 10.0 %collective-permute-start.10 = (bf16[2,4,128,128]{3,2,1,0:T(8,128)(2,1)S(1)}, bf16[2,4,128,128]{3,2,1,0:T(8,128)(2,1)S(1)}, u32[]{:S(2)}, u32[]{:S(2)}) collective-permute-start(bf16[2,4,128,128]{3,2,1,0:T(8,128)(2,1)S(1)} %get-tuple-element.122), channel_id=1, source_target_pairs={{0,2},{1,3},{2,0},{3,1},{4,6},{5,7},{6,4},{7,5},{8,10},{9,11},{10,... | collective-permute-start | bytes 786440 | tf_op jit(solution)/shard_map/ppermute | solution.py:375
  46.6 8.9 %collective-permute-start.18 = (bf16[2,4,128,128]{3,2,1,0:T(8,128)(2,1)S(1)}, bf16[2,4,128,128]{3,2,1,0:T(8,128)(2,1)S(1)}, u32[]{:S(2)}, u32[]{:S(2)}) collective-permute-start(bf16[2,4,128,128]{3,2,1,0:T(8,128)(2,1)S(1)} %get-tuple-element.137), channel_id=1, source_target_pairs={{0,4},{4,0},{8,12},{12,8},{16,20},{20,16},{24,28},{28,24},{1,5},{5... | collective-permute-start | bytes 786440 | tf_op jit(solution)/shard_map/ppermute | solution.py:377
  48.7 9.8 %collective-permute-start.17 = (bf16[2,4,128,128]{3,2,1,0:T(8,128)(2,1)S(1)}, bf16[2,4,128,128]{3,2,1,0:T(8,128)(2,1)S(1)}, u32[]{:S(2)}, u32[]{:S(2)}) collective-permute-start(bf16[2,4,128,128]{3,2,1,0:T(8,128)(2,1)S(1)} %get-tuple-element.136), channel_id=1, source_target_pairs={{0,8},{4,12},{8,0},{12,4},{16,24},{20,28},{24,16},{28,20},{1,9},{5... | collective-permute-start | bytes 786440 | tf_op jit(solution)/shard_map/ppermute | solution.py:377
  52.3 8.1 %collective-permute-start.15 = (bf16[2,4,128,128]{3,2,1,0:T(8,128)(2,1)S(1)}, bf16[2,4,128,128]{3,2,1,0:T(8,128)(2,1)S(1)}, u32[]{:S(2)}, u32[]{:S(2)}) collective-permute-start(bf16[2,4,128,128]{3,2,1,0:T(8,128)(2,1)S(1)} %get-tuple-element.133), channel_id=1, source_target_pairs={{0,4},{4,0},{8,12},{12,8},{16,20},{20,16},{24,28},{28,24},{1,5},{5... | collective-permute-start | bytes 786440 | tf_op jit(solution)/shard_map/ppermute | solution.py:377
  52.9 6.8 %collective-permute-start.16 = (bf16[1,4,128,128]{3,2,1,0:T(8,128)(2,1)S(1)}, bf16[1,4,128,128]{3,2,1,0:T(8,128)(2,1)S(1)}, u32[]{:S(2)}, u32[]{:S(2)}) collective-permute-start(bf16[1,4,128,128]{3,2,1,0:T(8,128)(2,1)S(1)} %get-tuple-element.134), channel_id=1, source_target_pairs={{0,16},{4,20},{8,24},{12,28},{16,0},{20,4},{24,8},{28,12},{1,17},{... | collective-permute-start | bytes 393224 | tf_op jit(solution)/shard_map/ppermute | solution.py:377
  56.2 13.1 %collective-permute-start.21 = (bf16[2,4,128,128]{3,2,1,0:T(8,128)(2,1)S(1)}, bf16[2,4,128,128]{3,2,1,0:T(8,128)(2,1)S(1)}, u32[]{:S(2)}, u32[]{:S(2)}) collective-permute-start(bf16[2,4,128,128]{3,2,1,0:T(8,128)(2,1)S(1)} %get-tuple-element.147), channel_id=1, source_target_pairs={{0,8},{4,12},{8,0},{12,4},{16,24},{20,28},{24,16},{28,20},{1,9},{5... | collective-permute-start | bytes 786440 | tf_op jit(solution)/shard_map/ppermute | solution.py:377
  61.1 15.5 %collective-permute-start.19 = (bf16[2,4,128,128]{3,2,1,0:T(8,128)(2,1)S(1)}, bf16[2,4,128,128]{3,2,1,0:T(8,128)(2,1)S(1)}, u32[]{:S(2)}, u32[]{:S(2)}) collective-permute-start(bf16[2,4,128,128]{3,2,1,0:T(8,128)(2,1)S(1)} %get-tuple-element.142), channel_id=1, source_target_pairs={{0,8},{4,12},{8,0},{12,4},{16,24},{20,28},{24,16},{28,20},{1,9},{5... | collective-permute-start | bytes 786440 | tf_op jit(solution)/shard_map/ppermute | solution.py:377
  64.6 12.7 %collective-permute-start.23 = (bf16[2,4,128,128]{3,2,1,0:T(8,128)(2,1)S(1)}, bf16[2,4,128,128]{3,2,1,0:T(8,128)(2,1)S(1)}, u32[]{:S(2)}, u32[]{:S(2)}) collective-permute-start(bf16[2,4,128,128]{3,2,1,0:T(8,128)(2,1)S(1)} %get-tuple-element.153), channel_id=1, source_target_pairs={{0,2},{1,3},{2,0},{3,1},{4,6},{5,7},{6,4},{7,5},{8,10},{9,11},{10,... | collective-permute-start | bytes 786440 | tf_op jit(solution)/shard_map/ppermute | solution.py:375
  66.5 9.3 %collective-permute-start.20 = (bf16[1,4,128,128]{3,2,1,0:T(8,128)(2,1)S(1)}, bf16[1,4,128,128]{3,2,1,0:T(8,128)(2,1)S(1)}, u32[]{:S(2)}, u32[]{:S(2)}) collective-permute-start(bf16[1,4,128,128]{3,2,1,0:T(8,128)(2,1)S(1)} %get-tuple-element.144), channel_id=1, source_target_pairs={{0,16},{4,20},{8,24},{12,28},{16,0},{20,4},{24,8},{28,12},{1,17},{... | collective-permute-start | bytes 393224 | tf_op jit(solution)/shard_map/ppermute | solution.py:377
  70.0 11.2 %collective-permute-start.28 = (bf16[1,4,128,128]{3,2,1,0:T(8,128)(2,1)S(1)}, bf16[1,4,128,128]{3,2,1,0:T(8,128)(2,1)S(1)}, u32[]{:S(2)}, u32[]{:S(2)}) collective-permute-start(bf16[1,4,128,128]{3,2,1,0:T(8,128)(2,1)S(1)} %get-tuple-element.159), channel_id=1, source_target_pairs={{0,16},{4,20},{8,24},{12,28},{16,0},{20,4},{24,8},{28,12},{1,17},{... | collective-permute-start | bytes 393224 | tf_op jit(solution)/shard_map/ppermute | solution.py:377
  78.7 15.4 %collective-permute-start.30 = (bf16[2,4,128,128]{3,2,1,0:T(8,128)(2,1)S(1)}, bf16[2,4,128,128]{3,2,1,0:T(8,128)(2,1)S(1)}, u32[]{:S(2)}, u32[]{:S(2)}) collective-permute-start(bf16[2,4,128,128]{3,2,1,0:T(8,128)(2,1)S(1)} %get-tuple-element.164), channel_id=1, source_target_pairs={{0,2},{1,3},{2,0},{3,1},{4,6},{5,7},{6,4},{7,5},{8,10},{9,11},{10,... | collective-permute-start | bytes 786440 | tf_op jit(solution)/shard_map/ppermute | solution.py:375
  82.4 13.2 %collective-permute-start.35 = (bf16[2,4,128,128]{3,2,1,0:T(8,128)(2,1)S(1)}, bf16[2,4,128,128]{3,2,1,0:T(8,128)(2,1)S(1)}, u32[]{:S(2)}, u32[]{:S(2)}) collective-permute-start(bf16[2,4,128,128]{3,2,1,0:T(8,128)(2,1)S(1)} %get-tuple-element.173), channel_id=1, source_target_pairs={{0,2},{1,3},{2,0},{3,1},{4,6},{5,7},{6,4},{7,5},{8,10},{9,11},{10,... | collective-permute-start | bytes 786440 | tf_op jit(solution)/shard_map/ppermute | solution.py:375
  82.5 9.2 %collective-permute-start.22 = (bf16[1,4,128,128]{3,2,1,0:T(8,128)(2,1)S(1)}, bf16[1,4,128,128]{3,2,1,0:T(8,128)(2,1)S(1)}, u32[]{:S(2)}, u32[]{:S(2)}) collective-permute-start(bf16[1,4,128,128]{3,2,1,0:T(8,128)(2,1)S(1)} %get-tuple-element.151), channel_id=1, source_target_pairs={{0,16},{4,20},{8,24},{12,28},{16,0},{20,4},{24,8},{28,12},{1,17},{... | collective-permute-start | bytes 393224 | tf_op jit(solution)/shard_map/ppermute | solution.py:377
  92.4 9.6 %collective-permute-start.29 = (bf16[2,4,128,128]{3,2,1,0:T(8,128)(2,1)S(1)}, bf16[2,4,128,128]{3,2,1,0:T(8,128)(2,1)S(1)}, u32[]{:S(2)}, u32[]{:S(2)}) collective-permute-start(bf16[2,4,128,128]{3,2,1,0:T(8,128)(2,1)S(1)} %get-tuple-element.163), channel_id=1, source_target_pairs={{0,2},{1,3},{2,0},{3,1},{4,6},{5,7},{6,4},{7,5},{8,10},{9,11},{10,... | collective-permute-start | bytes 786440 | tf_op jit(solution)/shard_map/ppermute | solution.py:375
  97.1 5.9 %collective-permute-start.40 = (bf16[1,4,128,128]{3,2,1,0:T(8,128)(2,1)S(1)}, bf16[1,4,128,128]{3,2,1,0:T(8,128)(2,1)S(1)}, u32[]{:S(2)}, u32[]{:S(2)}) collective-permute-start(bf16[1,4,128,128]{3,2,1,0:T(8,128)(2,1)S(1)} %get-tuple-element.181), channel_id=1, source_target_pairs={{0,1},{1,0},{2,3},{3,2},{4,5},{5,4},{6,7},{7,6},{8,9},{9,8},{10,11... | collective-permute-start | bytes 393224 | tf_op jit(solution)/shard_map/ppermute | solution.py:375
  97.3 6.2 %collective-permute-start.41 = (bf16[1,4,128,128]{3,2,1,0:T(8,128)(2,1)S(1)}, bf16[1,4,128,128]{3,2,1,0:T(8,128)(2,1)S(1)}, u32[]{:S(2)}, u32[]{:S(2)}) collective-permute-start(bf16[1,4,128,128]{3,2,1,0:T(8,128)(2,1)S(1)} %get-tuple-element.182), channel_id=1, source_target_pairs={{0,1},{1,0},{2,3},{3,2},{4,5},{5,4},{6,7},{7,6},{8,9},{9,8},{10,11... | collective-permute-start | bytes 393224 | tf_op jit(solution)/shard_map/ppermute | solution.py:375
  97.7 5.8 %collective-permute-start.42 = (bf16[1,4,128,128]{3,2,1,0:T(8,128)(2,1)S(1)}, bf16[1,4,128,128]{3,2,1,0:T(8,128)(2,1)S(1)}, u32[]{:S(2)}, u32[]{:S(2)}) collective-permute-start(bf16[1,4,128,128]{3,2,1,0:T(8,128)(2,1)S(1)} %get-tuple-element.183), channel_id=1, source_target_pairs={{0,1},{1,0},{2,3},{3,2},{4,5},{5,4},{6,7},{7,6},{8,9},{9,8},{10,11... | collective-permute-start | bytes 393224 | tf_op jit(solution)/shard_map/ppermute | solution.py:375
  97.8 6.2 %collective-permute-start.43 = (bf16[1,4,128,128]{3,2,1,0:T(8,128)(2,1)S(1)}, bf16[1,4,128,128]{3,2,1,0:T(8,128)(2,1)S(1)}, u32[]{:S(2)}, u32[]{:S(2)}) collective-permute-start(bf16[1,4,128,128]{3,2,1,0:T(8,128)(2,1)S(1)} %get-tuple-element.184), channel_id=1, source_target_pairs={{0,1},{1,0},{2,3},{3,2},{4,5},{5,4},{6,7},{7,6},{8,9},{9,8},{10,11... | collective-permute-start | bytes 393224 | tf_op jit(solution)/shard_map/ppermute | solution.py:375
  102.9 4.9 %collective-permute-start.36 = (bf16[1,4,128,128]{3,2,1,0:T(8,128)(2,1)S(1)}, bf16[1,4,128,128]{3,2,1,0:T(8,128)(2,1)S(1)}, u32[]{:S(2)}, u32[]{:S(2)}) collective-permute-start(bf16[1,4,128,128]{3,2,1,0:T(8,128)(2,1)S(1)} %get-tuple-element.177), channel_id=1, source_target_pairs={{0,1},{1,0},{2,3},{3,2},{4,5},{5,4},{6,7},{7,6},{8,9},{9,8},{10,11... | collective-permute-start | bytes 393224 | tf_op jit(solution)/shard_map/ppermute | solution.py:375
  103.0 4.7 %collective-permute-start.37 = (bf16[1,4,128,128]{3,2,1,0:T(8,128)(2,1)S(1)}, bf16[1,4,128,128]{3,2,1,0:T(8,128)(2,1)S(1)}, u32[]{:S(2)}, u32[]{:S(2)}) collective-permute-start(bf16[1,4,128,128]{3,2,1,0:T(8,128)(2,1)S(1)} %get-tuple-element.178), channel_id=1, source_target_pairs={{0,1},{1,0},{2,3},{3,2},{4,5},{5,4},{6,7},{7,6},{8,9},{9,8},{10,11... | collective-permute-start | bytes 393224 | tf_op jit(solution)/shard_map/ppermute | solution.py:375
  (21 other events, 82.2 us)
